TPU v7x, 32 devices: a whole 2x2x4 slice. The times are simulated.
32 devices in a mesh: freq: 4 (over z), lat: 2 (over x), lon: 4 (over y, core).
Axes of the slice: x: 2, y: 2, z: 4, core: 2. Of those that a mesh axis runs over, the one named last changes fastest.
Arguments:
- direction: float32 [3, 32, 256, 2048], P(None, 'freq', 'lat', 'lon'), may hold values from -6 to 6
- base_flow: float32 [2, 32, 256, 2048], P(None, 'freq', 'lat', 'lon'), may hold values from -2 to 2
- water_depth: float32 [256, 2048], P('lat', 'lon'), may hold values from 0.5 to 2
- drag_factor: float32 [256, 2048], P('lat', 'lon'), may hold values from 0.2 to 2
- wet_mask: int32 [256, 2048], P('lat', 'lon'), may hold values 0 or 1
Outputs:
- result: float32 [3, 32, 256, 2048], P(None, 'freq', 'lat', 'lon')
All inputs are finite; a program needn't handle non-finite values. No bound on the sum of `wet_mask` on one device may be relied on, other than what follows from the above.
Results may differ from a plain program's by a relative error of at most 0.000071.
Values sent between devices are 32-bit elements; how exact they have to be, the bound alone decides.
No kernel may reach another device: no remote copies, remote signals or barrier semaphores. Data moves between devices by JAX's collectives and lax.ppermute only.
A program may use at most 128 MiB of HBM per device.

v0:
```python
import math

import jax
import jax.numpy as jnp
from jax import lax
from jax.sharding import PartitionSpec as P

NCON = 16
NTIME = 256


LINEAR_DRAG = 0.5
GRAVITY = 1.0
OMEGA_STEP = 0.25
SPEED_SOFT = 0.01


def extended_2(block, sides, width):
    for axis, dim in sides:
        count = lax.axis_size(axis)
        forward = [(i, i + 1) for i in range(count - 1)]
        forward.append((count - 1, 0))
        backward = [(target, source) for source, target in forward]
        low = lax.ppermute(
            lax.slice_in_dim(block, block.shape[dim] - width, None, axis=dim), axis, forward
        )
        high = lax.ppermute(lax.slice_in_dim(block, 0, width, axis=dim), axis, backward)
        block = jnp.concatenate([low, block, high], axis=dim)
    return block


def samples_table(sample_count, constituents):
    sample_index = jnp.arange(sample_count, dtype=jnp.int32)
    harmonic = jnp.arange(1, constituents + 1, dtype=jnp.int32)
    wrapped_turns = sample_index[:, None] * harmonic[None, :] % sample_count
    phase_angle = wrapped_turns.astype(jnp.float32) * (2.0 * math.pi / sample_count)
    table = jnp.stack([jnp.cos(phase_angle), jnp.sin(phase_angle)], axis=2)
    return table.reshape(sample_count, 2 * constituents)


def rotation_of(row_index, total_rows):
    return 0.5 + (row_index.astype(jnp.float32) + 0.5) / total_rows


def tendency(values, angular):
    cos_sin = values.reshape((values.shape[0] // 2, 2) + values.shape[1:])
    moved = jnp.stack([angular * cos_sin[:, 1], -angular * cos_sin[:, 0]], axis=1)
    return moved.reshape(values.shape)


def linear_residual(extended, tile_rows, tile_cols, angular, rotation):

    def neighbour(plane, row_step, col_step):
        return extended[
            plane,
            :,
            1 + row_step : 1 + row_step + tile_rows,
            1 + col_step : 1 + col_step + tile_cols,
        ]

    height = neighbour(0, 0, 0)
    east = neighbour(1, 0, 0)
    north = neighbour(2, 0, 0)
    res_height = (
        tendency(height, angular)
        + neighbour(3, 0, 0)
        - neighbour(3, 0, -1)
        + neighbour(4, 0, 0)
        - neighbour(4, -1, 0)
    )
    north_mean = 0.25 * (north + neighbour(2, 0, 1) + neighbour(2, -1, 0) + neighbour(2, -1, 1))
    east_mean = 0.25 * (east + neighbour(1, 0, -1) + neighbour(1, 1, 0) + neighbour(1, 1, -1))
    res_east = (
        tendency(east, angular)
        + LINEAR_DRAG * east
        - rotation * north_mean
        + GRAVITY * (neighbour(0, 0, 1) - height)
    )
    res_north = (
        tendency(north, angular)
        + LINEAR_DRAG * north
        + rotation * east_mean
        + GRAVITY * (neighbour(0, 1, 0) - height)
    )
    return jnp.stack([res_height, res_east, res_north])


def friction_row(row_block, drag_row, table):
    highest = lax.Precision.HIGHEST
    series = jnp.einsum("tc,fcn->ftn", table, row_block, precision=highest)
    base_east, base_north, step_east, step_north = (series[0], series[1], series[2], series[3])
    magnitude = jnp.sqrt(base_east * base_east + base_north * base_north + SPEED_SOFT)
    projected = (base_east * step_east + base_north * step_north) / magnitude
    force_east = drag_row * (magnitude * step_east + base_east * projected)
    force_north = drag_row * (magnitude * step_north + base_north * projected)
    forces = jnp.stack([force_east, force_north])
    analysed = jnp.einsum("tc,ftn->fcn", table, forces, precision=highest) * (2.0 / table.shape[0])
    drag_rate = drag_row * jnp.mean(magnitude, axis=0)
    return (analysed, drag_rate)


def precondition(residual, angular, rotation, drag_rate):
    shaped = residual.reshape((3, residual.shape[1] // 2, 2) + residual.shape[2:])
    cos_part = shaped[:, :, 0]
    sin_part = shaped[:, :, 1]
    height_cos = -sin_part[0] / angular
    height_sin = cos_part[0] / angular
    real_rate = drag_rate + LINEAR_DRAG
    det_real = real_rate * real_rate - angular * angular + rotation * rotation
    det_imag = 2.0 * real_rate * angular
    det_norm = det_real * det_real + det_imag * det_imag
    inv_real = det_real / det_norm
    inv_imag = -det_imag / det_norm
    east_re = cos_part[1]
    east_im = -sin_part[1]
    north_re = cos_part[2]
    north_im = -sin_part[2]
    num_east_re = real_rate * east_re - angular * east_im + rotation * north_re
    num_east_im = real_rate * east_im + angular * east_re + rotation * north_im
    num_north_re = -rotation * east_re + real_rate * north_re - angular * north_im
    num_north_im = -rotation * east_im + real_rate * north_im + angular * north_re
    east_out_re = num_east_re * inv_real - num_east_im * inv_imag
    east_out_im = num_east_re * inv_imag + num_east_im * inv_real
    north_out_re = num_north_re * inv_real - num_north_im * inv_imag
    north_out_im = num_north_re * inv_imag + num_north_im * inv_real
    cosines = jnp.stack([height_cos, east_out_re, north_out_re])
    sines = jnp.stack([height_sin, -east_out_im, -north_out_im])
    return jnp.stack([cosines, sines], axis=2).reshape(residual.shape)


def local(direction, base_flow, water_depth, drag_factor, wet_mask):
    local_coefs = direction.shape[1]
    tile_rows = direction.shape[2]
    tile_cols = direction.shape[3]
    groups = lax.axis_size("freq")
    member = lax.axis_index("freq")
    band_rows = tile_rows // groups
    lat_place = lax.axis_index("lat")
    lat_count = lax.axis_size("lat")
    total_rows = tile_rows * lat_count
    wet_cells = wet_mask.astype(jnp.float32)
    height = direction[0] * wet_cells
    east = direction[1] * wet_cells
    north = direction[2] * wet_cells
    planes = jnp.stack([height, east, north, water_depth * east, water_depth * north])
    extended = extended_2(planes, (("lat", 2), ("lon", 3)), 1)
    rim_keep = jnp.ones((tile_rows + 2,), jnp.float32)
    rim_keep = rim_keep.at[0].set(jnp.where(lat_place == 0, 0.0, 1.0))
    rim_keep = rim_keep.at[tile_rows + 1].set(jnp.where(lat_place == lat_count - 1, 0.0, 1.0))
    extended = extended * rim_keep[:, None]
    local_count = local_coefs // 2
    first_con = member * local_count
    angular_local = OMEGA_STEP * (first_con + jnp.arange(local_count, dtype=jnp.int32) + 1).astype(
        jnp.float32
    )
    row_global = lat_place * tile_rows + jnp.arange(tile_rows, dtype=jnp.int32)
    rotation = rotation_of(row_global, total_rows)
    linear_part = linear_residual(
        extended, tile_rows, tile_cols, angular_local[:, None, None], rotation[:, None]
    )
    table = samples_table(NTIME, NCON)
    flows = jnp.concatenate([base_flow, jnp.stack([east, north])], axis=0)
    band_start = member * band_rows
    drag_band = lax.dynamic_slice_in_dim(drag_factor, band_start, band_rows, 0)
    flows_band, linear_band = (
        lax.all_to_all(flows, "freq", split_axis=2, concat_axis=1, tiled=True),
        lax.all_to_all(linear_part, "freq", split_axis=2, concat_axis=1, tiled=True),
    )
    mask_band = lax.dynamic_slice_in_dim(wet_cells, band_start, band_rows, 0)
    rotation_band = rotation_of(
        lat_place * tile_rows + band_start + jnp.arange(band_rows, dtype=jnp.int32), total_rows
    )
    angular_all = OMEGA_STEP * jnp.arange(1, NCON + 1, dtype=jnp.float32)

    def finish_row(items):
        row_block, linear_row, drag_row, mask_row, rotation_row = items
        friction, drag_rate = friction_row(row_block, drag_row, table)
        residual = (
            linear_row + jnp.concatenate([jnp.zeros_like(friction[:1]), friction], axis=0)
        ) * mask_row
        return precondition(residual, angular_all[:, None], rotation_row, drag_rate)

    band_result = lax.map(
        finish_row,
        (
            jnp.moveaxis(flows_band, 2, 0),
            jnp.moveaxis(linear_band, 2, 0),
            drag_band,
            mask_band,
            rotation_band,
        ),
    )
    band_result = jnp.moveaxis(band_result, 0, 2)
    return lax.all_to_all(band_result, "freq", split_axis=1, concat_axis=2, tiled=True)


def solution(mesh):
    placed = (
        P(None, "freq", "lat", "lon"),
        P(None, "freq", "lat", "lon"),
        P("lat", "lon"),
        P("lat", "lon"),
        P("lat", "lon"),
    )
    return jax.shard_map(
        local, mesh=mesh, in_specs=placed, out_specs=P(None, "freq", "lat", "lon"), check_vma=False
    )
```

profile of v0, /device:TPU:12, one launch (start us, length us, event | category | flops | bytes accessed | tf_op | source)
XLA Modules:
  0.0 1069.2 jit_solution(100319029989826023)
XLA Ops:
  24.1 4.9 pad_maximum_fusion.5
  40.4 12.1 %maximum_multiply_fusion = f32[5,8,130,514]{3,1,2,0:T(8,128)S(1)} fusion(f32[5,8,130,1]{3,1,2,0:T(8,128)} %copy.85, f32[5,8,1,512]{3,1,2,0:T(8,128)S(1)} %collective-permute-done.1, f32[5,8,128,512]{3,1,2,0:T(8,128)} %copy-done.1, f32[5,8,1,512]{3,1,2,0:T(8,128)S(1)} %collective-permute-done, f32[5,8,130,1]{3,1,2,0:T(8,128)S(1)} %copy.84, ...), kind=kLoop, calls=%fused_computation.57 | loop fusion | flops 13364000 | bytes 21382920 | tf_op jit(solution)/shard_map/mul | solution.py:150
  52.5 4.8 copy-done
  69.3 10.9 %slice_subtract_fusion.2 = (f32[1,8,128,512]{3,1,2,0:T(8,128)}, f32[1,8,128,512]{3,1,2,0:T(8,128)}, f32[1,8,128,512]{3,1,2,0:T(8,128)}) fusion(f32[5,8,130,514]{3,1,2,0:T(8,128)} %copy-done, f32[1,8,128,512]{3,1,2,0:T(8,128)S(1)} %reshape.1279), kind=kLoop, calls=%fused_computation.79 | loop fusion | flops 2097152 | bytes 20971520 | tf_op jit(solution)/shard_map/sub | solution.py:65
  86.5 6.6 slice_multiply_fusion.2
  99.0 4.7 pad_maximum_fusion.7
  107.4 14.0 %fusion.27 = (f32[1,8,128,512]{3,1,2,0:T(8,128)S(1)}, f32[1,8,128,512]{3,1,2,0:T(8,128)S(1)}) fusion(f32[5,8,130,514]{3,1,2,0:T(8,128)} %copy-done, f32[1,8,128,512]{3,1,2,0:T(8,128)} %reshape.1280, f32[128]{0:T(128)S(1)} %add_multiply_fusion.3, f32[1,8,128,512]{3,1,2,0:T(8,128)S(1)} %reshape.1281), kind=kLoop, calls=%fused_computation.73 | loop fusion | flops 9437184 | bytes 31457792 | tf_op jit(solution)/shard_map/add | solution.py:74
  125.6 5.7 all-to-all-start
  131.2 4.8 copy.88
  139.9 127.0 %all-to-all-done = f32[3,8,128,512]{3,1,0,2:T(8,128)} async-done(((f32[3,8,128,512]{3,1,0,2:T(8,128)}), f32[3,8,128,512]{3,1,0,2:T(8,128)}, u32[]{:S(2)}, u32[]{:S(2)}) %all-to-all-start) | async-done | bytes 6291488 | tf_op jit(solution)/shard_map/all_to_all | solution.py:167
  267.0 9.0 all-to-all-start.1
  277.1 6.5 copy.182
  283.6 172.3 %all-to-all-done.1 = f32[4,8,128,512]{3,1,0,2:T(8,128)} async-done(((f32[4,8,128,512]{3,1,0,2:T(8,128)}), f32[4,8,128,512]{3,1,0,2:T(8,128)}, u32[]{:S(2)}, u32[]{:S(2)}) %all-to-all-start.1) | async-done | bytes 8388640 | tf_op jit(solution)/shard_map/all_to_all | solution.py:166
  455.9 8.1 copy.181
  464.0 458.5 %while.15 = (s32[]{:T(128)}, f32[32,3,32,512]{3,0,1,2:T(8,128)}, f32[32,3,32,512]{3,2,1,0:T(8,128)}, f32[32,512]{1,0:T(8,128)S(1)}, f32[32,4,32,512]{3,2,1,0:T(8...) while((s32[]{:T(128)}, f32[32,3,32,512]{3,0,1,2:T(8,128)}, ...), condition=%wide.region_2.3_spmd.clone.clone, body=%wide.region_0.0_spmd.clone.clone.sunk | while | flops 305752128 | bytes 11770913 | solution.py:183
  473.4 5.0 dynamic_update_slice.8
  487.7 5.0 dynamic_update_slice.8
  502.0 5.0 dynamic_update_slice.8
  516.4 5.0 dynamic_update_slice.8
  530.7 5.0 dynamic_update_slice.8
  545.0 5.0 dynamic_update_slice.8
  559.4 5.0 dynamic_update_slice.8
  573.7 5.0 dynamic_update_slice.8
  588.0 5.0 dynamic_update_slice.8
  602.3 5.0 dynamic_update_slice.8
  616.7 5.0 dynamic_update_slice.8
  631.0 5.0 dynamic_update_slice.8
  645.3 5.0 dynamic_update_slice.8
  659.6 5.0 dynamic_update_slice.8
  674.0 5.0 dynamic_update_slice.8
  688.3 5.0 dynamic_update_slice.8
  702.6 5.0 dynamic_update_slice.8
  717.0 5.0 dynamic_update_slice.8
  731.3 5.0 dynamic_update_slice.8
  745.6 5.0 dynamic_update_slice.8
  759.9 5.0 dynamic_update_slice.8
  774.3 5.0 dynamic_update_slice.8
  788.6 5.0 dynamic_update_slice.8
  802.9 5.0 dynamic_update_slice.8
  817.2 5.0 dynamic_update_slice.8
  831.6 5.0 dynamic_update_slice.8
  845.9 5.0 dynamic_update_slice.8
  860.2 5.0 dynamic_update_slice.8
  874.5 5.0 dynamic_update_slice.8
  888.9 5.0 dynamic_update_slice.8
  903.2 5.0 dynamic_update_slice.8
  917.5 5.0 dynamic_update_slice.8
  922.5 143.1 %all_to_all.54 = f32[3,32,32,512]{3,2,0,1:T(8,128)S(1)} all-to-all(f32[3,32,32,512]{3,2,0,1:T(8,128)} %bitcast.165), channel_id=1, replica_groups=mesh['freq'=4,'lat'=2,'lon'=4] {'freq'}, dimensions={1} | all-to-all | bytes 12582912 | tf_op jit(solution)/shard_map/all_to_all | solution.py:194
  (697 shorter events, 312.2 us)
Async XLA Ops:
  8.4 2.7 copy-start.5
  13.8 4.0 copy-start.1
  17.8 5.3 collective-permute-start
  19.4 4.7 collective-permute-start.1
  32.3 3.5 collective-permute-start.2
  33.9 3.5 collective-permute-start.3
  52.5 4.8 copy-start
  107.4 14.0 %copy-start.2 = (f32[1,8,128,512]{3,1,2,0:T(8,128)S(1)}, f32[1,8,128,512]{3,1,2,0:T(8,128)}, u32[]{:S(2)}) copy-start(f32[1,8,128,512]{3,1,2,0:T(8,128)} %get-tuple-element.227) | copy-start | bytes 6291460
  125.6 141.4 %all-to-all-start = ((f32[3,8,128,512]{3,1,0,2:T(8,128)}), f32[3,8,128,512]{3,1,0,2:T(8,128)}, u32[]{:S(2)}, u32[]{:S(2)}) async-start(f32[3,8,128,512]{3,1,0,2:T(8,128)} %copy.86), calls=%async_computation | async-start | bytes 12582912 | tf_op jit(solution)/shard_map/all_to_all | solution.py:167
  131.2 4.8 copy-start.3
  131.2 4.8 copy-start.4
  267.0 188.9 %all-to-all-start.1 = ((f32[4,8,128,512]{3,1,0,2:T(8,128)}), f32[4,8,128,512]{3,1,0,2:T(8,128)}, u32[]{:S(2)}, u32[]{:S(2)}) async-start(f32[4,8,128,512]{3,1,0,2:T(8,128)} %pad_maximum_fusion.1), calls=%async_computation.1 | async-start | bytes 16777216 | tf_op jit(solution)/shard_map/all_to_all | solution.py:166
where the time goes:
time: 1090 us; the launch traced here: 1070 us
  waiting for transfers between devices  304 us (28%)
  local copies, waits for them, and re-layouts  268 us (25%)
  other arithmetic  157 us (14%)
  blocking collectives  143 us (13%)
  matrix products  116 us (11%)
  loops' own time  62.9 us (6%)
  starting transfers between devices  18.6 us (2%)
    dynamic_update_slice x96, local copies, waits for them, and re-layouts, local(): lax.map(finish_row, (jnp.moveaxis(flows_band, 2, 0), jnp.moveaxis(linear_...  172 us
    all_to_all x1, waiting for transfers between devices, local(): lax.all_to_all(flows, 'freq', split_axis=2, concat_axis=1, tiled=True)  172 us
    all_to_all x1, blocking collectives, local(): lax.all_to_all(band_result, 'freq', split_axis=1, concat_axis=2, tiled=True)  143 us
    all_to_all x1, waiting for transfers between devices, local(): lax.all_to_all(linear_part, 'freq', split_axis=2, concat_axis=1, tiled=True)  127 us
    dot_general x32, matrix products, friction_row(): series = jnp.einsum('tc,fcn->ftn', table, row_block, precision=highest)  92.3 us
    another operation x1, loops' own time, local(): lax.map(finish_row, (jnp.moveaxis(flows_band, 2, 0), jnp.moveaxis(linear_...  62.9 us
    mul x32, other arithmetic, finish_row(): (linear_row + jnp.concatenate([jnp.zeros_like(friction[:1]), friction], a...  30.8 us
    dot_general x32, matrix products, friction_row(): jnp.einsum('tc,ftn->fcn', table, forces, precision=highest)  23.4 us
  transfers between devices with their start and end apart: 6, of which 5 were waited for; matrix products, arithmetic and copies ran while one was open for 2% of the time, Pallas kernels for 0%

commit v1 on v0

v1 whole, which is shorter than its diff:
```python
import math

import jax
import jax.numpy as jnp
import ml_dtypes
import numpy as np
from jax import lax
from jax.experimental import pallas as pl
from jax.experimental.pallas import tpu as pltpu
from jax.sharding import PartitionSpec as P

NCON = 16
NTIME = 256
LANES = 128
SUB = 8

LINEAR_DRAG = 0.5
GRAVITY = 1.0
OMEGA_STEP = 0.25
SPEED_SOFT = 0.01
CHUNKS = 4
VMEM_BYTES = 48 * 1024 * 1024


def split_table():
    sample = np.arange(NTIME)[:, None]
    harmonic = np.arange(1, NCON + 1)[None, :]
    phase = (sample * harmonic % NTIME) * (2.0 * math.pi / NTIME)
    table = np.stack([np.cos(phase), np.sin(phase)], axis=2).reshape(NTIME, 2 * NCON)
    table = table.astype(np.float32)
    high = table.astype(ml_dtypes.bfloat16)
    low = (table - high.astype(np.float32)).astype(ml_dtypes.bfloat16)
    return high, low


def split_value(value):
    high = value.astype(jnp.bfloat16)
    low = (value - high.astype(jnp.float32)).astype(jnp.bfloat16)
    return high, low


def friction_kernel(groups, coefs, synth_ref, analyse_ref, flows_ref, out_ref):
    width = 2 * LANES
    columns = 2 * NCON

    def body(step, carry):
        tile = step * 2
        loaded = []
        for source in range(groups):
            pair = [flows_ref[source, tile], flows_ref[source, tile + 1]]
            loaded.append(jnp.concatenate(pair, axis=1))
        series = []
        for field in range(4):
            rows = slice(field * coefs, (field + 1) * coefs)
            values = jnp.concatenate([part[rows] for part in loaded], axis=0)
            high, low = split_value(values)
            operand = jnp.concatenate([high, low, high], axis=0)
            series.append(
                jnp.dot(synth_ref[...], operand, preferred_element_type=jnp.float32)
            )
        base_east, base_north, step_east, step_north = series
        square = base_east * base_east + base_north * base_north + SPEED_SOFT
        inverse = lax.rsqrt(square)
        speed = square * inverse
        projected = (base_east * step_east + base_north * step_north) * inverse
        forces = (
            speed * step_east + base_east * projected,
            speed * step_north + base_north * projected,
        )
        mean = jnp.sum(speed, axis=0, keepdims=True) * (1.0 / NTIME)
        analysed = []
        for force in forces:
            high, low = split_value(force)
            both = jnp.dot(analyse_ref[...], high, preferred_element_type=jnp.float32)
            rest = jnp.dot(
                analyse_ref[:columns, :], low, preferred_element_type=jnp.float32
            )
            analysed.append(both[:columns] + both[columns:] + rest)
        for part in range(2):
            lanes = slice(part * LANES, (part + 1) * LANES)
            for target in range(groups):
                rows = slice(target * coefs, (target + 1) * coefs)
                block = jnp.concatenate(
                    [analysed[0][rows, lanes], analysed[1][rows, lanes]], axis=0
                )
                start = pl.multiple_of((tile + part) * 2 * coefs, SUB)
                out_ref[target, 0, pl.ds(start, 2 * coefs), :] = block
                out_ref[target, 0, pl.ds(SUB * 2 * coefs + tile + part, 1), :] = mean[:, lanes]
        return carry

    lax.fori_loop(0, SUB // 2, body, 0)


def friction_call(flows, groups, coefs):
    tiles = flows.shape[1]
    rows = flows.shape[2]
    high, low = split_table()
    synth = np.concatenate([high, high, low], axis=1)
    scale = 2.0 / NTIME
    analyse = np.concatenate([high.T, low.T], axis=0).astype(np.float32) * scale
    analyse = analyse.astype(ml_dtypes.bfloat16)
    out_rows = SUB * (2 * coefs + 1)
    cells = groups * tiles * LANES
    return pl.pallas_call(
        lambda *refs: friction_kernel(groups, coefs, *refs),
        out_shape=jax.ShapeDtypeStruct((groups, tiles // SUB, out_rows, LANES), jnp.float32),
        grid=(tiles // SUB,),
        in_specs=[
            pl.BlockSpec(synth.shape, lambda i: (0, 0)),
            pl.BlockSpec(analyse.shape, lambda i: (0, 0)),
            pl.BlockSpec((groups, SUB, rows, LANES), lambda i: (0, i, 0, 0)),
        ],
        out_specs=pl.BlockSpec((groups, 1, out_rows, LANES), lambda i: (0, i, 0, 0)),
        compiler_params=pltpu.CompilerParams(vmem_limit_bytes=VMEM_BYTES),
        cost_estimate=pl.CostEstimate(
            flops=2 * cells * NTIME * 96 * 6 // 4, bytes_accessed=cells * 128, transcendentals=0
        ),
        name="friction",
    )(jnp.asarray(synth), jnp.asarray(analyse), flows)


def finish_kernel(coefs, lane_tiles, scalars_ref, first_block, refs):
    direction_ref, wet_ref, depth_ref, drag_ref, edge_ref, slab_ref, back_ref, out_ref = refs
    columns = lane_tiles * LANES
    wet = wet_ref[...].astype(jnp.float32)
    depth = depth_ref[...]
    drag = drag_ref[...]
    lane = lax.broadcasted_iota(jnp.int32, (SUB, columns), 1)
    sub = lax.broadcasted_iota(jnp.int32, (SUB, columns), 0)
    block = (first_block + pl.program_id(0)) * SUB
    row = (block + sub).astype(jnp.float32)
    rotation = 0.5 + (row + scalars_ref[0] + 0.5) * scalars_ref[1]

    def wide(slab):
        return jnp.concatenate([slab] * lane_tiles, axis=1)

    def west(value, slab):
        return jnp.where(lane == 0, wide(slab), pltpu.roll(value, 1, 1))

    def east_of(value, slab):
        return jnp.where(lane == columns - 1, wide(slab), pltpu.roll(value, columns - 1, 1))

    def above(value, edge):
        return jnp.where(sub == 0, edge, pltpu.roll(value, 1, 0))

    def below(value, edge):
        return jnp.where(sub == SUB - 1, edge, pltpu.roll(value, SUB - 1, 0))

    group_tiles = []
    for lane_tile in range(lane_tiles):
        rows = []
        for r in range(SUB):
            tile = r * lane_tiles + lane_tile
            start = (tile % SUB) * 2 * coefs
            rows.append(back_ref[tile // SUB, start : start + 2 * coefs, :])
        group_tiles.append(jnp.swapaxes(jnp.stack(rows, axis=0), 0, 1))
    friction = [
        jnp.concatenate([part[index] for part in group_tiles], axis=1) * drag
        for index in range(2 * coefs)
    ]
    speed = []
    for lane_tile in range(lane_tiles):
        rows = []
        for r in range(SUB):
            tile = r * lane_tiles + lane_tile
            at = SUB * 2 * coefs + tile % SUB
            rows.append(back_ref[tile // SUB, at : at + 1, :])
        speed.append(jnp.concatenate(rows, axis=0))
    real_rate = drag * jnp.concatenate(speed, axis=1) + LINEAR_DRAG

    for k in range(coefs // 2):
        angular = scalars_ref[2 + k]
        residual = []
        planes = []
        for part in range(2):
            c = 2 * k + part
            planes.append([direction_ref[p, c] * wet for p in range(3)])
        for part in range(2):
            c = 2 * k + part
            height, east, north = planes[part]
            other = planes[1 - part]
            signed = angular if part == 0 else -angular
            east_flux = depth * east
            north_flux = depth * north
            north_up = above(north, edge_ref[0, 0, c : c + 1])
            flux_up = above(north_flux, edge_ref[0, 1, c : c + 1])
            height_down = below(height, edge_ref[0, 2, c : c + 1])
            east_down = below(east, edge_ref[0, 3, c : c + 1])
            res_height = (
                signed * other[0]
                + east_flux
                - west(east_flux, slab_ref[2, c])
                + north_flux
                - flux_up
            )
            north_mean = 0.25 * (
                north
                + east_of(north, slab_ref[4, c])
                + north_up
                + east_of(north_up, slab_ref[5, c])
            )
            east_mean = 0.25 * (
                east
                + west(east, slab_ref[0, c])
                + east_down
                + west(east_down, slab_ref[1, c])
            )
            res_east = (
                signed * other[1]
                + LINEAR_DRAG * east
                - rotation * north_mean
                + GRAVITY * (east_of(height, slab_ref[3, c]) - height)
            )
            res_north = (
                signed * other[2]
                + LINEAR_DRAG * north
                + rotation * east_mean
                + GRAVITY * (height_down - height)
            )
            residual.append(
                (
                    res_height * wet,
                    (res_east + friction[c]) * wet,
                    (res_north + friction[coefs + c]) * wet,
                )
            )
        cos_part, sin_part = residual
        inverse_angular = 1.0 / (angular + jnp.zeros((SUB, columns), jnp.float32))
        out_ref[0, 2 * k] = -sin_part[0] * inverse_angular
        out_ref[0, 2 * k + 1] = cos_part[0] * inverse_angular
        det_real = real_rate * real_rate - angular * angular + rotation * rotation
        det_imag = 2.0 * real_rate * angular
        inverse_norm = 1.0 / (det_real * det_real + det_imag * det_imag)
        inv_real = det_real * inverse_norm
        inv_imag = -det_imag * inverse_norm
        east_re, north_re = cos_part[1], cos_part[2]
        east_im, north_im = -sin_part[1], -sin_part[2]
        num_east_re = real_rate * east_re - angular * east_im + rotation * north_re
        num_east_im = real_rate * east_im + angular * east_re + rotation * north_im
        num_north_re = -rotation * east_re + real_rate * north_re - angular * north_im
        num_north_im = -rotation * east_im + real_rate * north_im + angular * north_re
        out_ref[1, 2 * k] = num_east_re * inv_real - num_east_im * inv_imag
        out_ref[1, 2 * k + 1] = -(num_east_re * inv_imag + num_east_im * inv_real)
        out_ref[2, 2 * k] = num_north_re * inv_real - num_north_im * inv_imag
        out_ref[2, 2 * k + 1] = -(num_north_re * inv_imag + num_north_im * inv_real)


def finish_call(scalars, direction, wet_mask, depth, drag, edges, slabs, back, result, start, blocks):
    coefs = direction.shape[1]
    columns = direction.shape[3]
    lane_tiles = columns // LANES

    def kernel(scalars_ref, *refs):
        if result is not None:
            refs = refs[:7] + refs[8:]
        finish_kernel(coefs, lane_tiles, scalars_ref, start, refs)

    flat = pl.BlockSpec((SUB, columns), lambda i: (start + i, 0))
    planes = pl.BlockSpec((3, coefs, SUB, columns), lambda i: (0, 0, start + i, 0))
    in_specs = [
        pl.BlockSpec(memory_space=pltpu.SMEM),
        planes,
        flat,
        flat,
        flat,
        pl.BlockSpec((1, 4, coefs, columns), lambda i: (start + i, 0, 0, 0)),
        pl.BlockSpec((6, coefs, SUB, LANES), lambda i: (0, 0, start + i, 0)),
        pl.BlockSpec((lane_tiles,) + back.shape[1:], lambda i: (i, 0, 0)),
    ]
    operands = [scalars, direction, wet_mask, depth, drag, edges, slabs, back]
    aliases = {}
    if result is not None:
        in_specs.append(pl.BlockSpec(memory_space=pl.ANY))
        operands.append(result)
        aliases = {8: 0}
    return pl.pallas_call(
        kernel,
        out_shape=jax.ShapeDtypeStruct(direction.shape, jnp.float32),
        grid=(blocks,),
        in_specs=in_specs,
        out_specs=planes,
        input_output_aliases=aliases,
        compiler_params=pltpu.CompilerParams(vmem_limit_bytes=VMEM_BYTES),
        cost_estimate=pl.CostEstimate(
            flops=0, bytes_accessed=blocks * SUB * columns * coefs * 36, transcendentals=0
        ),
        name="finish",
    )(*operands)


def shifted(block, axis, step, wrap):
    count = lax.axis_size(axis)
    pairs = [
        (i, (i + step) % count) for i in range(count) if wrap or 0 <= i + step < count
    ]
    return lax.ppermute(block, axis, pairs)


def halo(direction, wet, depth):
    height, east, north = direction[0], direction[1], direction[2]
    rows = direction.shape[2]
    last = north[:, SUB - 1 :: SUB] * wet[SUB - 1 :: SUB]
    up = jnp.stack([last, last * depth[SUB - 1 :: SUB]])
    first = wet[::SUB]
    down = jnp.stack([height[:, ::SUB] * first, east[:, ::SUB] * first])
    from_above = shifted(up[:, :, -1:], "lat", 1, False)
    from_below = shifted(down[:, :, :1], "lat", -1, False)
    up = jnp.concatenate([from_above, up[:, :, :-1]], axis=2)
    down = jnp.concatenate([down[:, :, 1:], from_below], axis=2)
    edges = jnp.moveaxis(jnp.concatenate([up, down], axis=0), 2, 0)
    wet_last = wet[:, -1]
    east_col = east[:, :, -1] * wet_last
    east_below = jnp.concatenate([east_col[:, 1:], from_below[1, :, :, -1]], axis=1)
    north_col = north[:, :, 0] * wet[:, 0]
    north_above = jnp.concatenate([from_above[0, :, :, 0], north_col[:, :-1]], axis=1)
    to_right = jnp.stack([east_col, east_below, east_col * depth[:, -1]])
    to_left = jnp.stack([height[:, :, 0] * wet[:, 0], north_col, north_above])
    cols = jnp.concatenate(
        [shifted(to_right, "lon", 1, True), shifted(to_left, "lon", -1, True)], axis=0
    )
    slabs = jnp.broadcast_to(cols[:, :, :, None], cols.shape + (LANES,))
    return edges, slabs


def exchange(block):
    return lax.all_to_all(block, "freq", split_axis=0, concat_axis=0, tiled=True)


def local(direction, base_flow, water_depth, drag_factor, wet_mask):
    coefs, tile_rows, tile_cols = direction.shape[1:]
    groups = lax.axis_size("freq")
    member = lax.axis_index("freq")
    lat_place = lax.axis_index("lat")
    total_rows = tile_rows * lax.axis_size("lat")
    lane_tiles = tile_cols // LANES
    wet = wet_mask.astype(jnp.float32)
    angular = OMEGA_STEP * (
        member * (coefs // 2) + jnp.arange(coefs // 2, dtype=jnp.int32) + 1
    ).astype(jnp.float32)
    row_start = (lat_place * tile_rows).astype(jnp.float32)
    scalars = jnp.concatenate(
        [jnp.stack([row_start, jnp.float32(1.0 / total_rows)]), angular]
    )
    edges, slabs = halo(direction, wet, water_depth)
    rows = tile_rows // CHUNKS
    band = rows // groups
    result = None
    for chunk in range(CHUNKS):
        span = slice(chunk * rows, (chunk + 1) * rows)
        flows = jnp.concatenate([base_flow[:, :, span], direction[1:, :, span]], axis=0)
        flows = flows.reshape(4, coefs, groups, band, lane_tiles, LANES)
        flows = flows.transpose(2, 3, 4, 0, 1, 5)
        flows = flows.reshape(groups, band * lane_tiles, 4 * coefs, LANES)
        flows = exchange(flows)
        back = friction_call(flows, groups, coefs)
        back = exchange(back)
        back = back.reshape((-1,) + back.shape[2:])
        result = finish_call(
            scalars, direction, wet_mask, water_depth, drag_factor, edges, slabs, back,
            result, chunk * rows // SUB, rows // SUB,
        )
    return result


def solution(mesh):
    placed = (
        P(None, "freq", "lat", "lon"),
        P(None, "freq", "lat", "lon"),
        P("lat", "lon"),
        P("lat", "lon"),
        P("lat", "lon"),
    )
    return jax.shard_map(
        local, mesh=mesh, in_specs=placed, out_specs=P(None, "freq", "lat", "lon"), check_vma=False
    )
```

time: 1090 us -> 364 us (0.33); the launches traced: 1070 us -> 358 us
  local copies, waits for them, and re-layouts: 268 us -> 54.1 us
  other arithmetic: 157 us -> 7.25 us
  blocking collectives: 143 us -> 0 us
  waiting for transfers between devices: 304 us -> 179 us
  matrix products: 116 us -> 0 us
  loops' own time: 62.9 us -> 0 us
  Pallas kernels: 0 us -> 56.3 us
  starting transfers between devices: 18.6 us -> 60.7 us
    dynamic_update_slice x96 -> x0, local copies, waits for them, and re-layouts: 172 us -> none  [local(): lax.map(finish_row, (jnp.moveaxis(flows_band, 2, 0), jnp.moveaxis(linear_...]
    all_to_all x1 -> x0, blocking collectives: 143 us -> none  [local(): lax.all_to_all(band_result, 'freq', split_axis=1, concat_axis=2, tiled=True)]
    all_to_all x2 -> x8, waiting for transfers between devices: 299 us -> 178 us  [exchange(): lax.all_to_all(block, 'freq', split_axis=0, concat_axis=0, tiled=True)]
    dot_general x64 -> x0, matrix products: 116 us -> none  [the longest x32 92.3 us: friction_row(): series = jnp.einsum('tc,fcn->ftn', table, row_block, precision=highest)]
    mul x167 -> x5, other arithmetic: 71.1 us -> 0.02 us  [the longest x1 0.01 us: local(): OMEGA_STEP * (member * (coefs // 2) + jnp.arange(coefs // 2, dtype=jnp.in...]
    another operation x1 -> x0, loops' own time: 62.9 us -> none  [local(): lax.map(finish_row, (jnp.moveaxis(flows_band, 2, 0), jnp.moveaxis(linear_...]
    pallas_call x0 -> x8, Pallas kernels: none -> 56.3 us  [the longest x4 38.1 us: friction_call(): pl.pallas_call(lambda *refs: friction_kernel(groups, coefs, *refs), out_s...]
    all_to_all x2 -> x8, starting transfers between devices: 14.7 us -> 53.1 us  [exchange(): lax.all_to_all(block, 'freq', split_axis=0, concat_axis=0, tiled=True)]
  transfers between devices with their start and end apart: 6 -> 12, of which waited for: 5 -> 9; matrix products, arithmetic and copies ran while one was open for 2% -> 12% of each run, Pallas kernels for 0% -> 14%
where the time goes in v1:
time: 364 us; the launch traced here: 358 us
  waiting for transfers between devices  179 us (49%)
  starting transfers between devices  60.7 us (17%)
  Pallas kernels  56.3 us (15%)
  local copies, waits for them, and re-layouts  54.1 us (15%)
  other arithmetic  7.25 us (2%)
    all_to_all x8, waiting for transfers between devices, exchange(): lax.all_to_all(block, 'freq', split_axis=0, concat_axis=0, tiled=True)  178 us
    all_to_all x8, starting transfers between devices, exchange(): lax.all_to_all(block, 'freq', split_axis=0, concat_axis=0, tiled=True)  53.1 us
    pallas_call x4, Pallas kernels, friction_call(): pl.pallas_call(lambda *refs: friction_kernel(groups, coefs, *refs), out_s...  38.1 us
    pallas_call x4, Pallas kernels, finish_call(): pl.pallas_call(kernel, out_shape=jax.ShapeDtypeStruct(direction.shape, jn...  18.2 us
    reshape x4, local copies, waits for them, and re-layouts, local(): flows = flows.reshape(4, coefs, groups, band, lane_tiles, LANES)  13.5 us
    unnamed x45, local copies, waits for them, and re-layouts  12.5 us
    ppermute x4, starting transfers between devices, shifted(): return lax.ppermute(block, axis, pairs)  7.58 us
  transfers between devices with their start and end apart: 12, of which 9 were waited for; matrix products, arithmetic and copies ran while one was open for 12% of the time, Pallas kernels for 14%

profile of v1, /device:TPU:12, one launch (start us, length us, event | category | flops | bytes accessed | tf_op | source)
XLA Modules:
  0.0 357.9 jit_solution(2032552458825850743)
XLA Ops:
  0.0 3.9 %fusion.7 = (f32[2,8,32,512]{3,2,1,0:T(8,128)S(1)}, f32[2,8,32,512]{3,2,1,0:T(8,128)S(1)}, f32[2,8,32,512]{3,2,1,0:T(8,128)}, f32[2,8,32,512]{3,2,1,0:T(8,128)S(1)}) fusion(f32[2,8,128,512]{3,2,1,0:T(8,128)} %param.14), kind=kLoop, calls=%fused_computation.41 | loop fusion | bytes 8388608 | tf_op jit(solution)/shard_map/slice | solution.py:350
  4.4 1.9 fusion.5
  6.3 1.9 maximum_bitcast_fusion.2
  8.3 2.5 copy.74
  10.8 5.3 %all-to-all-start.4 = ((f32[4,32,32,128]{3,2,1,0:T(8,128)}), f32[4,32,32,128]{3,2,1,0:T(8,128)S(1)}, u32[]{:S(2)}, u32[]{:S(2)}) async-start(f32[4,32,32,128]{3,2,1,0:T(8,128)} %bitcast.72), calls=%async_computation.4 | async-start | bytes 4194304 | tf_op jit(solution)/shard_map/all_to_all | solution.py:326
  16.1 4.2 %copy.75 = f32[4,8,4,8,4,128]{5,1,0,4,3,2:T(8,128)} copy(f32[4,8,4,8,4,128]{5,3,4,2,1,0:T(8,128)} %get-tuple-element.32) | data formatting | bytes 4194304 | tf_op jit(solution)/shard_map/reshape | solution.py:351
  20.3 40.8 %all-to-all-done.4.refs_2_ = f32[4,32,32,128]{3,2,1,0:T(8,128)S(1)} async-done(((f32[4,32,32,128]{3,2,1,0:T(8,128)}), f32[4,32,32,128]{3,2,1,0:T(8,128)S(1)}, u32[]{:S(2)}, u32[]{:S(2)}) %all-to-all-start.4) | async-done | bytes 2097184 | tf_op jit(solution)/shard_map/all_to_all | solution.py:326
  61.1 1.4 copy-done.15
  62.4 7.7 %all-to-all-start.6 = ((f32[4,32,32,128]{3,2,1,0:T(8,128)}), f32[4,32,32,128]{3,2,1,0:T(8,128)}, u32[]{:S(2)}, u32[]{:S(2)}) async-start(f32[4,32,32,128]{3,2,1,0:T(8,128)} %bitcast.69), calls=%async_computation.6 | async-start | bytes 4194304 | tf_op jit(solution)/shard_map/all_to_all | solution.py:326
  70.1 3.7 %maximum_bitcast_fusion = (f32[4,8,4,8,4,128]{5,3,4,2,1,0:T(8,128)S(1)}, f32[4,8,4,8,4,128]{5,3,4,2,1,0:T(8,128)}) fusion(f32[2,8,32,512]{3,2,1,0:T(8,128)} %get-tuple-element.12, f32[2,8,32,512]{3,2,1,0:T(8,128)} %get-tuple-element.18, f32[2,8,32,512]{3,2,1,0:T(8,128)} %get-tuple-element.11, f32[2,8,32,512]{3,2,1,0:T(8,128)S(1)} %get-tuple-element.17), kind=kLoop, calls=%fused_computation | loop fusion | flops 1048576 | bytes 8388608 | tf_op jit(solution)/shard_map/reshape | solution.py:351
  73.8 2.6 copy.72
  76.4 38.1 %all-to-all-done.6.refs_2_ = f32[4,32,32,128]{3,2,1,0:T(8,128)} async-done(((f32[4,32,32,128]{3,2,1,0:T(8,128)}), f32[4,32,32,128]{3,2,1,0:T(8,128)}, u32[]{:S(2)}, u32[]{:S(2)}) %all-to-all-start.6) | async-done | bytes 2097184 | tf_op jit(solution)/shard_map/all_to_all | solution.py:326
  114.6 7.0 %all-to-all-start = ((f32[4,32,32,128]{3,2,1,0:T(8,128)}), f32[4,32,32,128]{3,2,1,0:T(8,128)S(1)}, u32[]{:S(2)}, u32[]{:S(2)}) async-start(f32[4,32,32,128]{3,2,1,0:T(8,128)} %bitcast.70), calls=%async_computation | async-start | bytes 4194304 | tf_op jit(solution)/shard_map/all_to_all | solution.py:326
  121.5 4.1 %copy.73 = f32[4,8,4,8,4,128]{5,1,0,4,3,2:T(8,128)} copy(f32[4,8,4,8,4,128]{5,3,4,2,1,0:T(8,128)} %get-tuple-element.30) | data formatting | bytes 4194304 | tf_op jit(solution)/shard_map/reshape | solution.py:351
  125.7 40.3 %all-to-all-done.refs_2_ = f32[4,32,32,128]{3,2,1,0:T(8,128)S(1)} async-done(((f32[4,32,32,128]{3,2,1,0:T(8,128)}), f32[4,32,32,128]{3,2,1,0:T(8,128)S(1)}, u32[]{:S(2)}, u32[]{:S(2)}) %all-to-all-start) | async-done | bytes 2097184 | tf_op jit(solution)/shard_map/all_to_all | solution.py:326
  165.9 1.4 copy-done.13
  167.3 7.7 %all-to-all-start.2 = ((f32[4,32,32,128]{3,2,1,0:T(8,128)}), f32[4,32,32,128]{3,2,1,0:T(8,128)}, u32[]{:S(2)}, u32[]{:S(2)}) async-start(f32[4,32,32,128]{3,2,1,0:T(8,128)} %bitcast.71), calls=%async_computation.2 | async-start | bytes 4194304 | tf_op jit(solution)/shard_map/all_to_all | solution.py:326
  175.0 1.6 copy-done.16
  176.6 9.1 %friction.6 = f32[4,4,136,128]{3,2,1,0:T(8,128)} custom-call(bf16[256,96]{1,0:T(8,128)(2,1)S(1)} %copy-done.17, bf16[64,256]{1,0:T(8,128)(2,1)S(1)} %copy-done.18, f32[4,32,32,128]{3,2,1,0:T(8,128)S(1)} %copy-done.16), custom_call_target="tpu_custom_call" | custom-call | flops 1207959552 | bytes 2097152 | tf_op jit(solution)/shard_map/friction/pallas_call | solution.py:104
  185.6 33.7 %all-to-all-done.2.refs_2_ = f32[4,32,32,128]{3,2,1,0:T(8,128)} async-done(((f32[4,32,32,128]{3,2,1,0:T(8,128)}), f32[4,32,32,128]{3,2,1,0:T(8,128)}, u32[]{:S(2)}, u32[]{:S(2)}) %all-to-all-start.2) | async-done | bytes 2097184 | tf_op jit(solution)/shard_map/all_to_all | solution.py:326
  219.4 6.9 %all-to-all-start.5 = ((f32[4,4,136,128]{3,2,1,0:T(8,128)}), f32[4,4,136,128]{3,2,1,0:T(8,128)S(1)}, u32[]{:S(2)}, u32[]{:S(2)}) async-start(f32[4,4,136,128]{3,2,1,0:T(8,128)} %friction.6), calls=%async_computation.5 | async-start | bytes 2228224 | tf_op jit(solution)/shard_map/all_to_all | solution.py:326
  226.2 10.0 %friction.7 = f32[4,4,136,128]{3,2,1,0:T(8,128)} custom-call(bf16[256,96]{1,0:T(8,128)(2,1)S(1)} %copy-done.17, bf16[64,256]{1,0:T(8,128)(2,1)S(1)} %copy-done.18, f32[4,32,32,128]{3,2,1,0:T(8,128)} %all-to-all-done.6.refs_2_), custom_call_target="tpu_custom_call" | custom-call | flops 1207959552 | bytes 2097152 | tf_op jit(solution)/shard_map/friction/pallas_call | solution.py:104
  236.2 13.4 %all-to-all-done.5 = f32[4,4,136,128]{3,2,1,0:T(8,128)S(1)} async-done(((f32[4,4,136,128]{3,2,1,0:T(8,128)}), f32[4,4,136,128]{3,2,1,0:T(8,128)S(1)}, u32[]{:S(2)}, u32[]{:S(2)}) %all-to-all-start.5) | async-done | bytes 1114144 | tf_op jit(solution)/shard_map/all_to_all | solution.py:326
  249.6 6.8 %all-to-all-start.7 = ((f32[4,4,136,128]{3,2,1,0:T(8,128)}), f32[4,4,136,128]{3,2,1,0:T(8,128)S(1)}, u32[]{:S(2)}, u32[]{:S(2)}) async-start(f32[4,4,136,128]{3,2,1,0:T(8,128)} %friction.7), calls=%async_computation.7 | async-start | bytes 2228224 | tf_op jit(solution)/shard_map/all_to_all | solution.py:326
  256.4 5.8 %fusion.6 = (f32[1,8,128,512]{3,2,1,0:T(8,128)}, f32[1,8,128,512]{3,2,1,0:T(8,128)}, f32[1,8,128,512]{3,2,1,0:T(8,128)}) fusion(f32[3,8,128,512]{3,2,1,0:T(8,128)} %refs_0_.11), kind=kLoop, calls=%fused_computation.40 | loop fusion | bytes 12582912 | tf_op jit(solution)/shard_map/slice | solution.py:300
  262.2 10.0 %friction.5 = f32[4,4,136,128]{3,2,1,0:T(8,128)} custom-call(bf16[256,96]{1,0:T(8,128)(2,1)S(1)} %copy-done.17, bf16[64,256]{1,0:T(8,128)(2,1)S(1)} %copy-done.18, f32[4,32,32,128]{3,2,1,0:T(8,128)} %all-to-all-done.2.refs_2_), custom_call_target="tpu_custom_call" | custom-call | flops 1207959552 | bytes 2097152 | tf_op jit(solution)/shard_map/friction/pallas_call | solution.py:104
  272.1 7.6 %all-to-all-done.7 = f32[4,4,136,128]{3,2,1,0:T(8,128)S(1)} async-done(((f32[4,4,136,128]{3,2,1,0:T(8,128)}), f32[4,4,136,128]{3,2,1,0:T(8,128)S(1)}, u32[]{:S(2)}, u32[]{:S(2)}) %all-to-all-start.7) | async-done | bytes 1114144 | tf_op jit(solution)/shard_map/all_to_all | solution.py:326
  279.7 6.8 %all-to-all-start.3 = ((f32[4,4,136,128]{3,2,1,0:T(8,128)}), f32[4,4,136,128]{3,2,1,0:T(8,128)S(1)}, u32[]{:S(2)}, u32[]{:S(2)}) async-start(f32[4,4,136,128]{3,2,1,0:T(8,128)} %friction.5), calls=%async_computation.3 | async-start | bytes 2228224 | tf_op jit(solution)/shard_map/all_to_all | solution.py:326
  286.5 6.7 %copy_bitcast_fusion = (f32[8,128,512]{2,0,1:T(8,128)}, f32[8,128,512]{2,0,1:T(8,128)}) fusion(f32[1,8,128,512]{3,2,1,0:T(8,128)} %get-tuple-element.15, f32[1,8,128,512]{3,2,1,0:T(8,128)} %get-tuple-element.13), kind=kLoop, calls=%fused_computation.4 | loop fusion | bytes 8388608 | tf_op jit(solution)/shard_map/squeeze | solution.py:300
  293.3 1.1 multiply_bitcast_fusion.1
  294.4 1.3 collective-permute-start.1
  296.8 2.8 copy.82
  299.7 4.5 %collective-permute-start = (f32[2,8,1,512]{3,1,0,2:T(8,128)S(1)}, f32[2,8,1,512]{3,1,0,2:T(8,128)S(1)}, u32[]{:S(2)}, u32[]{:S(2)}) collective-permute-start(f32[2,8,1,512]{3,1,0,2:T(8,128)S(1)} %pad_maximum_fusion.2), channel_id=1, source_target_pairs={{0,4},{1,5},{2,6},{3,7},{8,12},{9,13},{10,14},{11,15},{16,20},{17,... | collective-permute-start | bytes 98312 | tf_op jit(solution)/shard_map/ppermute | solution.py:296
  304.2 1.2 slice.127
  305.5 1.9 slice.130
  308.5 1.2 copy.68
  309.7 1.2 copy.69
  312.1 1.6 copy-done.14
  313.7 9.1 %friction.4 = f32[4,4,136,128]{3,2,1,0:T(8,128)} custom-call(bf16[256,96]{1,0:T(8,128)(2,1)S(1)} %copy-done.17, bf16[64,256]{1,0:T(8,128)(2,1)S(1)} %copy-done.18, f32[4,32,32,128]{3,2,1,0:T(8,128)S(1)} %copy-done.14), custom_call_target="tpu_custom_call" | custom-call | flops 1207959552 | bytes 2097152 | tf_op jit(solution)/shard_map/friction/pallas_call | solution.py:104
  322.8 5.1 %all-to-all-start.1 = ((f32[4,4,136,128]{3,2,1,0:T(8,128)}), f32[4,4,136,128]{3,2,1,0:T(8,128)}, u32[]{:S(2)}, u32[]{:S(2)}) async-start(f32[4,4,136,128]{3,2,1,0:T(8,128)} %friction.4), calls=%async_computation.1 | async-start | bytes 2228224 | tf_op jit(solution)/shard_map/all_to_all | solution.py:326
  328.3 1.7 collective-permute-start.3
  330.2 1.1 collective-permute-done.2
  332.4 4.5 %finish.4.refs_7_ = f32[3,8,128,512]{3,2,1,0:T(8,128)} custom-call(f32[6]{0:T(128)S(1)} %pad_maximum_fusion.6.scalars_ref, f32[3,8,128,512]{3,2,1,0:T(8,128)} %refs_0_.11, s32[128,512]{1,0:T(8,128)S(1)} %copy-done.2, f32[128,512]{1,0:T(8,128)S(1)} %copy-done.3, f32[128,512]{1,0:T(8,128)S(1)} %copy-done.11, f32[16,4,8,512]{3,2,1,0:T(8,128)S(1)} %fusion.2.refs_4_, ...), custom_call_target="tpu_custom_call" | custom-call | bytes 4718592 | tf_op jit(solution)/shard_map/finish/pallas_call | solution.py:276
  336.9 4.5 %finish.5.refs_7_ = f32[3,8,128,512]{3,2,1,0:T(8,128)} custom-call(f32[6]{0:T(128)S(1)} %pad_maximum_fusion.6.scalars_ref, f32[3,8,128,512]{3,2,1,0:T(8,128)} %refs_0_.11, s32[128,512]{1,0:T(8,128)S(1)} %copy-done.2, f32[128,512]{1,0:T(8,128)S(1)} %copy-done.3, f32[128,512]{1,0:T(8,128)S(1)} %copy-done.11, ...), custom_call_target="tpu_custom_call", output_to_operand_aliasing={{}: (8, {})} | custom-call | bytes 4718592 | tf_op jit(solution)/shard_map/finish/pallas_call | solution.py:276
  341.5 4.5 %finish.6.refs_7_ = f32[3,8,128,512]{3,2,1,0:T(8,128)} custom-call(f32[6]{0:T(128)S(1)} %pad_maximum_fusion.6.scalars_ref, f32[3,8,128,512]{3,2,1,0:T(8,128)} %refs_0_.11, s32[128,512]{1,0:T(8,128)S(1)} %copy-done.2, f32[128,512]{1,0:T(8,128)S(1)} %copy-done.3, f32[128,512]{1,0:T(8,128)S(1)} %copy-done.11, ...), custom_call_target="tpu_custom_call", output_to_operand_aliasing={{}: (8, {})} | custom-call | bytes 4718592 | tf_op jit(solution)/shard_map/finish/pallas_call | solution.py:276
  345.9 4.2 %all-to-all-done.1 = f32[4,4,136,128]{3,2,1,0:T(8,128)} async-done(((f32[4,4,136,128]{3,2,1,0:T(8,128)}), f32[4,4,136,128]{3,2,1,0:T(8,128)}, u32[]{:S(2)}, u32[]{:S(2)}) %all-to-all-start.1) | async-done | bytes 1114144 | tf_op jit(solution)/shard_map/all_to_all | solution.py:326
  350.1 1.2 copy-done.1
  353.2 4.6 %finish.7 = f32[3,8,128,512]{3,2,1,0:T(8,128)} custom-call(f32[6]{0:T(128)S(1)} %pad_maximum_fusion.6.scalars_ref, f32[3,8,128,512]{3,2,1,0:T(8,128)} %refs_0_.11, s32[128,512]{1,0:T(8,128)S(1)} %copy-done.2, f32[128,512]{1,0:T(8,128)S(1)} %copy-done.4, f32[128,512]{1,0:T(8,128)S(1)} %copy-done.12, ...), custom_call_target="tpu_custom_call", output_to_operand_aliasing={{}: (8, {})} | custom-call | bytes 4718592 | tf_op jit(solution)/shard_map/finish/pallas_call | solution.py:276
  (71 shorter events, 7.3 us)
Async XLA Ops:
  0.0 4.4 %copy-start.19 = (f32[3,8,128,512]{3,2,1,0:T(8,128)S(1)}, f32[3,8,128,512]{3,2,1,0:T(8,128)}, u32[]{:S(2)}) copy-start(f32[3,8,128,512]{3,2,1,0:T(8,128)} %refs_0_.11) | copy-start | bytes 18874372
  10.8 50.2 %all-to-all-start.4 = ((f32[4,32,32,128]{3,2,1,0:T(8,128)}), f32[4,32,32,128]{3,2,1,0:T(8,128)S(1)}, u32[]{:S(2)}, u32[]{:S(2)}) async-start(f32[4,32,32,128]{3,2,1,0:T(8,128)} %bitcast.72), calls=%async_computation.4 | async-start | bytes 4194304 | tf_op jit(solution)/shard_map/all_to_all | solution.py:326
  61.0 1.4 copy-start.15
  62.4 52.1 %all-to-all-start.6 = ((f32[4,32,32,128]{3,2,1,0:T(8,128)}), f32[4,32,32,128]{3,2,1,0:T(8,128)}, u32[]{:S(2)}, u32[]{:S(2)}) async-start(f32[4,32,32,128]{3,2,1,0:T(8,128)} %bitcast.69), calls=%async_computation.6 | async-start | bytes 4194304 | tf_op jit(solution)/shard_map/all_to_all | solution.py:326
  114.6 51.4 %all-to-all-start = ((f32[4,32,32,128]{3,2,1,0:T(8,128)}), f32[4,32,32,128]{3,2,1,0:T(8,128)S(1)}, u32[]{:S(2)}, u32[]{:S(2)}) async-start(f32[4,32,32,128]{3,2,1,0:T(8,128)} %bitcast.70), calls=%async_computation | async-start | bytes 4194304 | tf_op jit(solution)/shard_map/all_to_all | solution.py:326
  165.9 1.4 copy-start.13
  165.9 9.0 %copy-start.17 = (bf16[256,96]{1,0:T(8,128)(2,1)S(1)}, bf16[256,96]{1,0:T(8,128)(2,1)}, u32[]{:S(2)}) copy-start(bf16[256,96]{1,0:T(8,128)(2,1)} %constant.24.clone.refs_0_) | copy-start | bytes 147460
  165.9 9.0 %copy-start.18 = (bf16[64,256]{1,0:T(8,128)(2,1)S(1)}, bf16[64,256]{1,0:T(8,128)(2,1)}, u32[]{:S(2)}) copy-start(bf16[64,256]{1,0:T(8,128)(2,1)} %constant.25.clone.refs_1_) | copy-start | bytes 98308
  167.3 52.1 %all-to-all-start.2 = ((f32[4,32,32,128]{3,2,1,0:T(8,128)}), f32[4,32,32,128]{3,2,1,0:T(8,128)}, u32[]{:S(2)}, u32[]{:S(2)}) async-start(f32[4,32,32,128]{3,2,1,0:T(8,128)} %bitcast.71), calls=%async_computation.2 | async-start | bytes 4194304 | tf_op jit(solution)/shard_map/all_to_all | solution.py:326
  175.0 1.6 copy-start.16
  219.4 30.2 %all-to-all-start.5 = ((f32[4,4,136,128]{3,2,1,0:T(8,128)}), f32[4,4,136,128]{3,2,1,0:T(8,128)S(1)}, u32[]{:S(2)}, u32[]{:S(2)}) async-start(f32[4,4,136,128]{3,2,1,0:T(8,128)} %friction.6), calls=%async_computation.5 | async-start | bytes 2228224 | tf_op jit(solution)/shard_map/all_to_all | solution.py:326
  249.6 12.6 %copy-start.5 = (f32[4,4,136,128]{3,2,1,0:T(8,128)}, f32[4,4,136,128]{3,2,1,0:T(8,128)S(1)}, u32[]{:S(2)}) copy-start(f32[4,4,136,128]{3,2,1,0:T(8,128)S(1)} %all-to-all-done.5) | copy-start | bytes 3342340
  249.6 30.1 %all-to-all-start.7 = ((f32[4,4,136,128]{3,2,1,0:T(8,128)}), f32[4,4,136,128]{3,2,1,0:T(8,128)S(1)}, u32[]{:S(2)}, u32[]{:S(2)}) async-start(f32[4,4,136,128]{3,2,1,0:T(8,128)} %friction.7), calls=%async_computation.7 | async-start | bytes 2228224 | tf_op jit(solution)/shard_map/all_to_all | solution.py:326
  279.7 13.5 %copy-start.7 = (f32[4,4,136,128]{3,2,1,0:T(8,128)}, f32[4,4,136,128]{3,2,1,0:T(8,128)S(1)}, u32[]{:S(2)}) copy-start(f32[4,4,136,128]{3,2,1,0:T(8,128)S(1)} %all-to-all-done.7) | copy-start | bytes 3342340
  279.7 43.1 %all-to-all-start.3 = ((f32[4,4,136,128]{3,2,1,0:T(8,128)}), f32[4,4,136,128]{3,2,1,0:T(8,128)S(1)}, u32[]{:S(2)}, u32[]{:S(2)}) async-start(f32[4,4,136,128]{3,2,1,0:T(8,128)} %friction.5), calls=%async_computation.3 | async-start | bytes 2228224 | tf_op jit(solution)/shard_map/all_to_all | solution.py:326
  286.5 6.7 %copy-start.2 = (s32[128,512]{1,0:T(8,128)S(1)}, s32[128,512]{1,0:T(8,128)}, u32[]{:S(2)}) copy-start(s32[128,512]{1,0:T(8,128)} %refs_1_.11) | copy-start | bytes 786436
  293.2 6.3 %copy-start.20 = (f32[128,512]{1,0:T(8,128)}, f32[128,512]{1,0:T(8,128)S(1)}, u32[]{:S(2)}) copy-start(f32[128,512]{1,0:T(8,128)S(1)} %convert_element_type.11) | copy-start | bytes 786436
  294.4 33.6 %collective-permute-start.1 = (f32[2,8,1,512]{3,1,0,2:T(8,128)S(1)}, f32[2,8,1,512]{3,1,0,2:T(8,128)S(1)}, u32[]{:S(2)}, u32[]{:S(2)}) collective-permute-start(f32[2,8,1,512]{3,1,0,2:T(8,128)S(1)} %pad_maximum_fusion.1), channel_id=1, source_target_pairs={{4,0},{5,1},{6,2},{7,3},{12,8},{13,9},{14,10},{15,11},{20,16},{21,... | collective-permute-start | bytes 98312 | tf_op jit(solution)/shard_map/ppermute | solution.py:296
  299.7 28.6 %collective-permute-start = (f32[2,8,1,512]{3,1,0,2:T(8,128)S(1)}, f32[2,8,1,512]{3,1,0,2:T(8,128)S(1)}, u32[]{:S(2)}, u32[]{:S(2)}) collective-permute-start(f32[2,8,1,512]{3,1,0,2:T(8,128)S(1)} %pad_maximum_fusion.2), channel_id=1, source_target_pairs={{0,4},{1,5},{2,6},{3,7},{8,12},{9,13},{10,14},{11,15},{16,20},{17,... | collective-permute-start | bytes 98312 | tf_op jit(solution)/shard_map/ppermute | solution.py:296
  305.5 5.5 %copy-start.21 = (f32[128,512]{1,0:T(8,128)S(1)}, f32[128,512]{1,0:T(8,128)}, u32[]{:S(2)}) copy-start(f32[128,512]{1,0:T(8,128)} %copy-done.20) | copy-start | bytes 786436
  312.1 1.6 copy-start.14
  322.8 7.3 %copy-start.9 = (f32[4,4,136,128]{3,2,1,0:T(8,128)}, f32[4,4,136,128]{3,2,1,0:T(8,128)S(1)}, u32[]{:S(2)}) copy-start(f32[4,4,136,128]{3,2,1,0:T(8,128)S(1)} %all-to-all-done.3) | copy-start | bytes 3342340
  322.8 27.3 %all-to-all-start.1 = ((f32[4,4,136,128]{3,2,1,0:T(8,128)}), f32[4,4,136,128]{3,2,1,0:T(8,128)}, u32[]{:S(2)}, u32[]{:S(2)}) async-start(f32[4,4,136,128]{3,2,1,0:T(8,128)} %friction.4), calls=%async_computation.1 | async-start | bytes 2228224 | tf_op jit(solution)/shard_map/all_to_all | solution.py:326
  328.2 3.1 collective-permute-start.2
  328.3 3.1 collective-permute-start.3
  330.1 11.3 %copy-start = (f32[16,4,8,512]{3,2,1,0:T(8,128)}, f32[16,4,8,512]{3,2,1,0:T(8,128)S(1)}, u32[]{:S(2)}) copy-start(f32[16,4,8,512]{3,2,1,0:T(8,128)S(1)} %fusion.2.refs_4_) | copy-start | bytes 3145732
  330.2 2.2 copy-start.3
  330.2 2.2 copy-start.8
  330.2 2.2 copy-start.11
  332.4 4.6 %copy-start.6 = (f32[4,4,136,128]{3,2,1,0:T(8,128)S(1)}, f32[4,4,136,128]{3,2,1,0:T(8,128)}, u32[]{:S(2)}) copy-start(f32[4,4,136,128]{3,2,1,0:T(8,128)} %copy-done.5) | copy-start | bytes 3342340
  336.9 4.6 %copy-start.10 = (f32[4,4,136,128]{3,2,1,0:T(8,128)S(1)}, f32[4,4,136,128]{3,2,1,0:T(8,128)}, u32[]{:S(2)}) copy-start(f32[4,4,136,128]{3,2,1,0:T(8,128)} %copy-done.9) | copy-start | bytes 3342340
  350.1 1.2 copy-start.1
  351.3 0.9 copy-start.4
  352.3 0.9 copy-start.12

commit v2 on v1

--- a/solution.py
+++ b/solution.py
@@ -18,7 +18,6 @@
 GRAVITY = 1.0
 OMEGA_STEP = 0.25
 SPEED_SOFT = 0.01
-CHUNKS = 4
 VMEM_BYTES = 48 * 1024 * 1024
 
 
@@ -39,15 +38,15 @@
     return high, low
 
 
-def friction_kernel(groups, coefs, synth_ref, analyse_ref, flows_ref, out_ref):
-    width = 2 * LANES
+def friction_kernel(groups, coefs, place_ref, synth_ref, analyse_ref, *refs):
+    flow_refs, out_refs = refs[:groups], refs[groups:]
     columns = 2 * NCON
 
     def body(step, carry):
         tile = step * 2
         loaded = []
         for source in range(groups):
-            pair = [flows_ref[source, tile], flows_ref[source, tile + 1]]
+            pair = [flow_refs[source][tile], flow_refs[source][tile + 1]]
             loaded.append(jnp.concatenate(pair, axis=1))
         series = []
         for field in range(4):
@@ -56,7 +55,7 @@
             high, low = split_value(values)
             operand = jnp.concatenate([high, low, high], axis=0)
             series.append(
-                jnp.dot(synth_ref[...], operand, preferred_element_type=jnp.float32)
+                jnp.dot(synth_ref[0], operand, preferred_element_type=jnp.float32)
             )
         base_east, base_north, step_east, step_north = series
         square = base_east * base_east + base_north * base_north + SPEED_SOFT
@@ -71,9 +70,9 @@
         analysed = []
         for force in forces:
             high, low = split_value(force)
-            both = jnp.dot(analyse_ref[...], high, preferred_element_type=jnp.float32)
+            both = jnp.dot(analyse_ref[0], high, preferred_element_type=jnp.float32)
             rest = jnp.dot(
-                analyse_ref[:columns, :], low, preferred_element_type=jnp.float32
+                analyse_ref[0, :columns, :], low, preferred_element_type=jnp.float32
             )
             analysed.append(both[:columns] + both[columns:] + rest)
         for part in range(2):
@@ -84,42 +83,58 @@
                     [analysed[0][rows, lanes], analysed[1][rows, lanes]], axis=0
                 )
                 start = pl.multiple_of((tile + part) * 2 * coefs, SUB)
-                out_ref[target, 0, pl.ds(start, 2 * coefs), :] = block
-                out_ref[target, 0, pl.ds(SUB * 2 * coefs + tile + part, 1), :] = mean[:, lanes]
+                out_refs[target][0, pl.ds(start, 2 * coefs), :] = block
+                at = SUB * 2 * coefs + tile + part
+                out_refs[target][0, pl.ds(at, 1), :] = mean[:, lanes]
         return carry
 
     lax.fori_loop(0, SUB // 2, body, 0)
 
 
-def friction_call(flows, groups, coefs):
-    tiles = flows.shape[1]
-    rows = flows.shape[2]
+def placed_tables(groups, coefs):
     high, low = split_table()
-    synth = np.concatenate([high, high, low], axis=1)
-    scale = 2.0 / NTIME
-    analyse = np.concatenate([high.T, low.T], axis=0).astype(np.float32) * scale
-    analyse = analyse.astype(ml_dtypes.bfloat16)
+    synth, analyse = [], []
+    for member in range(groups):
+        sources = [(member - step) % groups for step in range(groups)]
+        targets = [(member + step) % groups for step in range(groups)]
+        source = np.concatenate([np.arange(coefs) + m * coefs for m in sources])
+        target = np.concatenate([np.arange(coefs) + m * coefs for m in targets])
+        synth.append(np.concatenate([high[:, source], high[:, source], low[:, source]], axis=1))
+        both = np.concatenate([high[:, target].T, low[:, target].T], axis=0)
+        analyse.append((both.astype(np.float32) * (2.0 / NTIME)).astype(ml_dtypes.bfloat16))
+    return np.stack(synth), np.stack(analyse)
+
+
+def friction_call(place, flows, coefs):
+    groups = len(flows)
+    tiles, rows = flows[0].shape[:2]
+    synth, analyse = placed_tables(groups, coefs)
     out_rows = SUB * (2 * coefs + 1)
     cells = groups * tiles * LANES
+    grid_spec = pltpu.PrefetchScalarGridSpec(
+        num_scalar_prefetch=1,
+        grid=(tiles // SUB,),
+        in_specs=[
+            pl.BlockSpec((1,) + synth.shape[1:], lambda i, place: (place[0], 0, 0)),
+            pl.BlockSpec((1,) + analyse.shape[1:], lambda i, place: (place[0], 0, 0)),
+        ]
+        + [pl.BlockSpec((SUB, rows, LANES), lambda i, place: (i, 0, 0))] * groups,
+        out_specs=[pl.BlockSpec((1, out_rows, LANES), lambda i, place: (i, 0, 0))] * groups,
+    )
+    out = jax.ShapeDtypeStruct((tiles // SUB, out_rows, LANES), jnp.float32)
     return pl.pallas_call(
         lambda *refs: friction_kernel(groups, coefs, *refs),
-        out_shape=jax.ShapeDtypeStruct((groups, tiles // SUB, out_rows, LANES), jnp.float32),
-        grid=(tiles // SUB,),
-        in_specs=[
-            pl.BlockSpec(synth.shape, lambda i: (0, 0)),
-            pl.BlockSpec(analyse.shape, lambda i: (0, 0)),
-            pl.BlockSpec((groups, SUB, rows, LANES), lambda i: (0, i, 0, 0)),
-        ],
-        out_specs=pl.BlockSpec((groups, 1, out_rows, LANES), lambda i: (0, i, 0, 0)),
+        out_shape=[out] * groups,
+        grid_spec=grid_spec,
         compiler_params=pltpu.CompilerParams(vmem_limit_bytes=VMEM_BYTES),
         cost_estimate=pl.CostEstimate(
-            flops=2 * cells * NTIME * 96 * 6 // 4, bytes_accessed=cells * 128, transcendentals=0
+            flops=cells * NTIME * 512, bytes_accessed=cells * 128, transcendentals=0
         ),
         name="friction",
-    )(jnp.asarray(synth), jnp.asarray(analyse), flows)
-
-
-def finish_kernel(coefs, lane_tiles, scalars_ref, first_block, refs):
+    )(place, jnp.asarray(synth), jnp.asarray(analyse), *flows)
+
+
+def finish_kernel(coefs, lane_tiles, blocks_ref, scalars_ref, refs):
     direction_ref, wet_ref, depth_ref, drag_ref, edge_ref, slab_ref, back_ref, out_ref = refs
     columns = lane_tiles * LANES
     wet = wet_ref[...].astype(jnp.float32)
@@ -127,7 +142,7 @@
     drag = drag_ref[...]
     lane = lax.broadcasted_iota(jnp.int32, (SUB, columns), 1)
     sub = lax.broadcasted_iota(jnp.int32, (SUB, columns), 0)
-    block = (first_block + pl.program_id(0)) * SUB
+    block = blocks_ref[pl.program_id(0)] * SUB
     row = (block + sub).astype(jnp.float32)
     rotation = 0.5 + (row + scalars_ref[0] + 0.5) * scalars_ref[1]
 
@@ -245,44 +260,45 @@
         out_ref[2, 2 * k + 1] = -(num_north_re * inv_imag + num_north_im * inv_real)
 
 
-def finish_call(scalars, direction, wet_mask, depth, drag, edges, slabs, back, result, start, blocks):
+def finish_call(blocks, scalars, direction, wet_mask, depth, drag, edges, slabs, back, result):
     coefs = direction.shape[1]
     columns = direction.shape[3]
     lane_tiles = columns // LANES
 
-    def kernel(scalars_ref, *refs):
+    def kernel(blocks_ref, scalars_ref, *refs):
         if result is not None:
             refs = refs[:7] + refs[8:]
-        finish_kernel(coefs, lane_tiles, scalars_ref, start, refs)
-
-    flat = pl.BlockSpec((SUB, columns), lambda i: (start + i, 0))
-    planes = pl.BlockSpec((3, coefs, SUB, columns), lambda i: (0, 0, start + i, 0))
+        finish_kernel(coefs, lane_tiles, blocks_ref, scalars_ref, refs)
+
+    flat = pl.BlockSpec((SUB, columns), lambda i, at: (at[i], 0))
+    planes = pl.BlockSpec((3, coefs, SUB, columns), lambda i, at: (0, 0, at[i], 0))
     in_specs = [
         pl.BlockSpec(memory_space=pltpu.SMEM),
         planes,
         flat,
         flat,
         flat,
-        pl.BlockSpec((1, 4, coefs, columns), lambda i: (start + i, 0, 0, 0)),
-        pl.BlockSpec((6, coefs, SUB, LANES), lambda i: (0, 0, start + i, 0)),
-        pl.BlockSpec((lane_tiles,) + back.shape[1:], lambda i: (i, 0, 0)),
+        pl.BlockSpec((1, 4, coefs, columns), lambda i, at: (at[i], 0, 0, 0)),
+        pl.BlockSpec((6, coefs, SUB, LANES), lambda i, at: (0, 0, at[i], 0)),
+        pl.BlockSpec((lane_tiles,) + back.shape[1:], lambda i, at: (i, 0, 0)),
     ]
-    operands = [scalars, direction, wet_mask, depth, drag, edges, slabs, back]
+    operands = [blocks, scalars, direction, wet_mask, depth, drag, edges, slabs, back]
     aliases = {}
     if result is not None:
         in_specs.append(pl.BlockSpec(memory_space=pl.ANY))
         operands.append(result)
-        aliases = {8: 0}
+        aliases = {9: 0}
+    count = blocks.shape[0]
     return pl.pallas_call(
         kernel,
         out_shape=jax.ShapeDtypeStruct(direction.shape, jnp.float32),
-        grid=(blocks,),
-        in_specs=in_specs,
-        out_specs=planes,
+        grid_spec=pltpu.PrefetchScalarGridSpec(
+            num_scalar_prefetch=1, grid=(count,), in_specs=in_specs, out_specs=planes
+        ),
         input_output_aliases=aliases,
         compiler_params=pltpu.CompilerParams(vmem_limit_bytes=VMEM_BYTES),
         cost_estimate=pl.CostEstimate(
-            flops=0, bytes_accessed=blocks * SUB * columns * coefs * 36, transcendentals=0
+            flops=0, bytes_accessed=count * SUB * columns * coefs * 36, transcendentals=0
         ),
         name="finish",
     )(*operands)
@@ -322,10 +338,6 @@
     return edges, slabs
 
 
-def exchange(block):
-    return lax.all_to_all(block, "freq", split_axis=0, concat_axis=0, tiled=True)
-
-
 def local(direction, base_flow, water_depth, drag_factor, wet_mask):
     coefs, tile_rows, tile_cols = direction.shape[1:]
     groups = lax.axis_size("freq")
@@ -342,22 +354,30 @@
         [jnp.stack([row_start, jnp.float32(1.0 / total_rows)]), angular]
     )
     edges, slabs = halo(direction, wet, water_depth)
-    rows = tile_rows // CHUNKS
-    band = rows // groups
+    place = jnp.reshape(member, (1,)).astype(jnp.int32)
+    chunks = tile_rows // (groups * SUB)
+    steps = jnp.arange(groups, dtype=jnp.int32)
+    sources = (member - steps) % groups
     result = None
-    for chunk in range(CHUNKS):
-        span = slice(chunk * rows, (chunk + 1) * rows)
-        flows = jnp.concatenate([base_flow[:, :, span], direction[1:, :, span]], axis=0)
-        flows = flows.reshape(4, coefs, groups, band, lane_tiles, LANES)
-        flows = flows.transpose(2, 3, 4, 0, 1, 5)
-        flows = flows.reshape(groups, band * lane_tiles, 4 * coefs, LANES)
-        flows = exchange(flows)
-        back = friction_call(flows, groups, coefs)
-        back = exchange(back)
-        back = back.reshape((-1,) + back.shape[2:])
+    for chunk in range(chunks):
+        flows = []
+        for step in range(groups):
+            target = (member + step) % groups
+            start = (chunk * groups + target) * SUB
+            base = lax.dynamic_slice_in_dim(base_flow, start, SUB, 2)
+            moving = lax.dynamic_slice_in_dim(direction[1:], start, SUB, 2)
+            block = jnp.concatenate([base, moving], axis=0)
+            block = block.reshape(4, coefs, SUB, lane_tiles, LANES).transpose(2, 3, 0, 1, 4)
+            block = block.reshape(SUB * lane_tiles, 4 * coefs, LANES)
+            flows.append(block if step == 0 else shifted(block, "freq", step, True))
+        back = friction_call(place, flows, coefs)
+        back = [
+            block if step == 0 else shifted(block, "freq", step, True)
+            for step, block in enumerate(back)
+        ]
         result = finish_call(
-            scalars, direction, wet_mask, water_depth, drag_factor, edges, slabs, back,
-            result, chunk * rows // SUB, rows // SUB,
+            chunk * groups + sources, scalars, direction, wet_mask, water_depth, drag_factor,
+            edges, slabs, jnp.concatenate(back, axis=0), result,
         )
     return result
 

time: 364 us -> 304 us (0.84); the launches traced: 358 us -> 302 us
  waiting for transfers between devices: 179 us -> 135 us
  local copies, waits for them, and re-layouts: 54.1 us -> 45.5 us
  starting transfers between devices: 60.7 us -> 53.9 us
  other arithmetic: 7.25 us -> 13.8 us
    all_to_all x8 -> x0, waiting for transfers between devices: 178 us -> none  [exchange(): lax.all_to_all(block, 'freq', split_axis=0, concat_axis=0, tiled=True)]
    ppermute x4 -> x28, waiting for transfers between devices: 1.27 us -> 135 us  [shifted(): return lax.ppermute(block, axis, pairs)]
    all_to_all x8 -> x0, starting transfers between devices: 53.1 us -> none  [exchange(): lax.all_to_all(block, 'freq', split_axis=0, concat_axis=0, tiled=True)]
    ppermute x4 -> x28, starting transfers between devices: 7.58 us -> 53.9 us  [shifted(): return lax.ppermute(block, axis, pairs)]
    dynamic_slice x0 -> x1, local copies, waits for them, and re-layouts: none -> 6.36 us  [local(): moving = lax.dynamic_slice_in_dim(direction[1:], start, SUB, 2)]
    reshape x2 -> x16, other arithmetic: 5.64 us -> 11.7 us  [local(): block.reshape(4, coefs, SUB, lane_tiles, LANES).transpose(2, 3, 0, 1, 4)]
    unnamed x45 -> x99, local copies, waits for them, and re-layouts: 12.5 us -> 6.56 us
    pallas_call x4, Pallas kernels: 38.1 us -> 33.4 us  [friction_call(): pl.pallas_call(lambda *refs: friction_kernel(groups, coefs, *refs), out_s...]
  transfers between devices with their start and end apart: 12 -> 28, of which waited for: 9 -> 15; matrix products, arithmetic and copies ran while one was open for 12% -> 14% of each run, Pallas kernels for 14% -> 16%
where the time goes in v2:
time: 304 us; the launch traced here: 302 us
  waiting for transfers between devices  135 us (44%)
  starting transfers between devices  53.9 us (18%)
  Pallas kernels  53.4 us (18%)
  local copies, waits for them, and re-layouts  45.5 us (15%)
  other arithmetic  13.8 us (5%)
    ppermute x28, waiting for transfers between devices, shifted(): return lax.ppermute(block, axis, pairs)  135 us
    ppermute x28, starting transfers between devices, shifted(): return lax.ppermute(block, axis, pairs)  53.9 us
    pallas_call x4, Pallas kernels, friction_call(): pl.pallas_call(lambda *refs: friction_kernel(groups, coefs, *refs), out_s...  33.4 us
    pallas_call x4, Pallas kernels, finish_call(): pl.pallas_call(kernel, out_shape=jax.ShapeDtypeStruct(direction.shape, jn...  20 us
    reshape x16, local copies, waits for them, and re-layouts, local(): block.reshape(4, coefs, SUB, lane_tiles, LANES).transpose(2, 3, 0, 1, 4)  11.7 us
    reshape x16, other arithmetic, local(): block.reshape(4, coefs, SUB, lane_tiles, LANES).transpose(2, 3, 0, 1, 4)  11.7 us
    unnamed x99, local copies, waits for them, and re-layouts  6.56 us
    dynamic_slice x1, local copies, waits for them, and re-layouts, local(): moving = lax.dynamic_slice_in_dim(direction[1:], start, SUB, 2)  6.36 us
  transfers between devices with their start and end apart: 28, of which 15 were waited for; matrix products, arithmetic and copies ran while one was open for 14% of the time, Pallas kernels for 16%

profile of v2, /device:TPU:12, one launch (start us, length us, event | category | flops | bytes accessed | tf_op | source)
XLA Modules:
  0.0 301.8 jit_solution(5249339899215950821)
XLA Ops:
  0.0 4.8 %slice.111 = f32[2,8,128,512]{3,2,1,0:T(8,128)} slice(f32[3,8,128,512]{3,2,1,0:T(8,128)} %refs_0_.7), slice={[1:3], [0:8], [0:128], [0:512]} | slice | bytes 8388608 | tf_op jit(solution)/shard_map/slice | solution.py:368
  4.8 6.4 %constant_dynamic-slice_fusion = (f32[2,8,8,512]{3,2,1,0:T(8,128)}, f32[2,8,8,512]{3,2,1,0:T(8,128)}, f32[2,8,8,512]{3,2,1,0:T(8,128)}, f32[2,8,8,512]{3,2,1,0:T...) fusion(f32[2,8,128,512]{3,2,1,0:T(8,128)} %slice.111, ...), kind=kLoop, calls=%fused_computation.43 | loop fusion | bytes 16777280 | tf_op jit(solution)/shard_map/dynamic_slice | solution.py:368
  12.3 1.6 collective-permute-start.4
  15.1 1.6 collective-permute-start.10
  17.8 1.2 collective-permute-start.11
  19.1 2.9 fusion.6
  22.0 4.7 %copy_bitcast_fusion = (f32[8,128,512]{2,0,1:T(8,128)S(1)}, f32[8,128,512]{2,0,1:T(8,128)S(1)}) fusion(f32[1,8,128,512]{3,2,1,0:T(8,128)} %get-tuple-element.43, f32[1,8,128,512]{3,2,1,0:T(8,128)} %get-tuple-element.41), kind=kLoop, calls=%fused_computation | loop fusion | bytes 8388608 | tf_op jit(solution)/shard_map/squeeze | solution.py:316
  26.7 1.3 copy-done.6
  28.7 1.3 collective-permute-start.1
  30.0 2.8 copy.130
  33.0 4.5 %collective-permute-start = (f32[2,8,1,512]{3,1,0,2:T(8,128)S(1)}, f32[2,8,1,512]{3,1,0,2:T(8,128)S(1)}, u32[]{:S(2)}, u32[]{:S(2)}) collective-permute-start(f32[2,8,1,512]{3,1,0,2:T(8,128)S(1)} %pad_maximum_fusion.6), channel_id=1, source_target_pairs={{0,4},{1,5},{2,6},{3,7},{8,12},{9,13},{10,14},{11,15},{16,20},{17,... | collective-permute-start | bytes 98312 | tf_op jit(solution)/shard_map/ppermute | solution.py:312
  38.3 2.0 slice.114
  40.3 1.9 slice.117
  42.3 1.2 copy.101
  43.5 1.2 copy.104
  44.8 1.3 broadcast_multiply_fusion
  58.4 1.7 collective-permute-start.3
  62.3 1.1 copy.121
  65.1 1.6 collective-permute-start.22
  66.6 3.5 %collective-permute-start.23 = (f32[32,32,128]{2,1,0:T(8,128)}, f32[32,32,128]{2,1,0:T(8,128)}, u32[]{:S(2)}, u32[]{:S(2)}) collective-permute-start(f32[32,32,128]{2,1,0:T(8,128)} %bitcast.65), channel_id=1, source_target_pairs={{0,16},{8,24},{16,0},{24,8},{1,17},{9,25},{17,1},{25,9},{2,18},{10... | collective-permute-start | bytes 1572872 | tf_op jit(solution)/shard_map/ppermute | solution.py:312
  70.4 1.4 copy.120
  76.8 25.2 %collective-permute-done.12.refs_6_ = f32[32,32,128]{2,1,0:T(8,128)S(1)} collective-permute-done((f32[32,32,128]{2,1,0:T(8,128)}, f32[32,32,128]{2,1,0:T(8,128)S(1)}, u32[]{:S(2)}, u32[]{:S(2)}) %collective-permute-start.12) | collective-permute-done | bytes 524320 | tf_op jit(solution)/shard_map/ppermute | solution.py:312
  102.0 33.8 %collective-permute-done.23.refs_5_ = f32[32,32,128]{2,1,0:T(8,128)} collective-permute-done((f32[32,32,128]{2,1,0:T(8,128)}, f32[32,32,128]{2,1,0:T(8,128)}, u32[]{:S(2)}, u32[]{:S(2)}) %collective-permute-start.23) | collective-permute-done | bytes 524320 | tf_op jit(solution)/shard_map/ppermute | solution.py:312
  135.8 12.7 %collective-permute-start.18 = (f32[32,32,128]{2,1,0:T(8,128)S(1)}, f32[32,32,128]{2,1,0:T(8,128)S(1)}, u32[]{:S(2)}, u32[]{:S(2)}) collective-permute-start(f32[32,32,128]{2,1,0:T(8,128)S(1)} %bitcast.130), channel_id=1, source_target_pairs={{0,24},{8,0},{16,8},{24,16},{1,25},{9,1},{17,9},{25,17},{2,26},{10... | collective-permute-start | bytes 1572872 | tf_op jit(solution)/shard_map/ppermute | solution.py:312
  148.5 9.9 %collective-permute-done.24.refs_6_ = f32[32,32,128]{2,1,0:T(8,128)} collective-permute-done((f32[32,32,128]{2,1,0:T(8,128)}, f32[32,32,128]{2,1,0:T(8,128)}, u32[]{:S(2)}, u32[]{:S(2)}) %collective-permute-start.24) | collective-permute-done | bytes 524320 | tf_op jit(solution)/shard_map/ppermute | solution.py:312
  158.4 8.1 %friction.5 = (f32[4,136,128]{2,1,0:T(8,128)S(1)}, f32[4,136,128]{2,1,0:T(8,128)S(1)}, f32[4,136,128]{2,1,0:T(8,128)S(1)}, f32[4,136,128]{2,1,0:T(8,128)S(1)}) custom-call(s32[1]{0:T(128)} %bitcast.20.refs_0_, bf16[4,256,96]{2,1,0:T(8,128)(2,1)S(1)} %copy-done.3, bf16[4,64,256]{2,1,0:T(8,128)(2,1)S(1)} %copy-done.4, f32[32,32,128]{2,1,0:T(8,128)S(1)} %bitcast.126, ...), custom_call_target="tpu_custom_call" | custom-call | flops 2147483648 | bytes 2097152 | tf_op jit(solution)/shard_map/friction/pallas_call | solution.py:125
  166.5 9.1 %friction.7 = (f32[4,136,128]{2,1,0:T(8,128)S(1)}, f32[4,136,128]{2,1,0:T(8,128)S(1)}, f32[4,136,128]{2,1,0:T(8,128)S(1)}, f32[4,136,128]{2,1,0:T(8,128)S(1)}) custom-call(s32[1]{0:T(128)} %bitcast.20.refs_0_, bf16[4,256,96]{2,1,0:T(8,128)(2,1)S(1)} %copy-done.3, bf16[4,64,256]{2,1,0:T(8,128)(2,1)S(1)} %copy-done.4, f32[32,32,128]{2,1,0:T(8,128)S(1)} %bitcast.125, ...), custom_call_target="tpu_custom_call" | custom-call | flops 2147483648 | bytes 2097152 | tf_op jit(solution)/shard_map/friction/pallas_call | solution.py:125
  175.6 3.3 %collective-permute-done.5.refs_5_ = f32[32,32,128]{2,1,0:T(8,128)S(1)} collective-permute-done((f32[32,32,128]{2,1,0:T(8,128)S(1)}, f32[32,32,128]{2,1,0:T(8,128)S(1)}, u32[]{:S(2)}, u32[]{:S(2)}) %collective-permute-start.5) | collective-permute-done | bytes 524320 | tf_op jit(solution)/shard_map/ppermute | solution.py:312
  179.0 11.2 %collective-permute-done.16.refs_4_ = f32[32,32,128]{2,1,0:T(8,128)S(1)} collective-permute-done((f32[32,32,128]{2,1,0:T(8,128)S(1)}, f32[32,32,128]{2,1,0:T(8,128)S(1)}, u32[]{:S(2)}, u32[]{:S(2)}) %collective-permute-start.16) | collective-permute-done | bytes 524320 | tf_op jit(solution)/shard_map/ppermute | solution.py:312
  190.2 2.5 collective-permute-start.25
  192.7 14.8 %collective-permute-done.17.refs_5_ = f32[32,32,128]{2,1,0:T(8,128)S(1)} collective-permute-done((f32[32,32,128]{2,1,0:T(8,128)S(1)}, f32[32,32,128]{2,1,0:T(8,128)S(1)}, u32[]{:S(2)}, u32[]{:S(2)}) %collective-permute-start.17) | collective-permute-done | bytes 524320 | tf_op jit(solution)/shard_map/ppermute | solution.py:312
  207.5 3.4 %collective-permute-start.26 = (f32[4,136,128]{2,1,0:T(8,128)S(1)}, f32[4,136,128]{2,1,0:T(8,128)S(1)}, u32[]{:S(2)}, u32[]{:S(2)}) collective-permute-start(f32[4,136,128]{2,1,0:T(8,128)S(1)} %get-tuple-element.35), channel_id=1, source_target_pairs={{0,16},{8,24},{16,0},{24,8},{1,17},{9,25},{17,1},{25,9},{2,18},{10... | collective-permute-start | bytes 835592 | tf_op jit(solution)/shard_map/ppermute | solution.py:312
  210.8 8.1 %friction.6 = (f32[4,136,128]{2,1,0:T(8,128)S(1)}, f32[4,136,128]{2,1,0:T(8,128)S(1)}, f32[4,136,128]{2,1,0:T(8,128)S(1)}, f32[4,136,128]{2,1,0:T(8,128)S(1)}) custom-call(s32[1]{0:T(128)} %bitcast.20.refs_0_, bf16[4,256,96]{2,1,0:T(8,128)(2,1)S(1)} %copy-done.3, bf16[4,64,256]{2,1,0:T(8,128)(2,1)S(1)} %copy-done.4, f32[32,32,128]{2,1,0:T(8,128)S(1)} %bitcast.124, ...), custom_call_target="tpu_custom_call" | custom-call | flops 2147483648 | bytes 2097152 | tf_op jit(solution)/shard_map/friction/pallas_call | solution.py:125
  218.9 2.3 collective-permute-done.6.refs_6_
  221.2 1.6 collective-permute-start.20
  222.8 14.5 %collective-permute-done.25 = f32[4,136,128]{2,1,0:T(8,128)S(1)} collective-permute-done((f32[4,136,128]{2,1,0:T(8,128)S(1)}, f32[4,136,128]{2,1,0:T(8,128)S(1)}, u32[]{:S(2)}, u32[]{:S(2)}) %collective-permute-start.25) | collective-permute-done | bytes 278560 | tf_op jit(solution)/shard_map/ppermute | solution.py:312
  237.3 8.1 %friction.4 = (f32[4,136,128]{2,1,0:T(8,128)S(1)}, f32[4,136,128]{2,1,0:T(8,128)S(1)}, f32[4,136,128]{2,1,0:T(8,128)S(1)}, f32[4,136,128]{2,1,0:T(8,128)S(1)}) custom-call(s32[1]{0:T(128)} %bitcast.20.refs_0_, bf16[4,256,96]{2,1,0:T(8,128)(2,1)S(1)} %copy-done.3, bf16[4,64,256]{2,1,0:T(8,128)(2,1)S(1)} %copy-done.4, f32[32,32,128]{2,1,0:T(8,128)S(1)} %bitcast.123, ...), custom_call_target="tpu_custom_call" | custom-call | flops 2147483648 | bytes 2097152 | tf_op jit(solution)/shard_map/friction/pallas_call | solution.py:125
  246.2 3.4 %collective-permute-start.14 = (f32[4,136,128]{2,1,0:T(8,128)S(1)}, f32[4,136,128]{2,1,0:T(8,128)S(1)}, u32[]{:S(2)}, u32[]{:S(2)}) collective-permute-start(f32[4,136,128]{2,1,0:T(8,128)S(1)} %get-tuple-element.27), channel_id=1, source_target_pairs={{0,16},{8,24},{16,0},{24,8},{1,17},{9,25},{17,1},{25,9},{2,18},{10... | collective-permute-start | bytes 835592 | tf_op jit(solution)/shard_map/ppermute | solution.py:312
  250.7 5.0 %finish.4.refs_7_ = f32[3,8,128,512]{3,2,1,0:T(8,128)} custom-call(s32[4]{0:T(128)S(1)} %and_select_fusion.blocks_ref, f32[6]{0:T(128)S(1)} %pad_maximum_fusion.10.scalars_ref, f32[3,8,128,512]{3,2,1,0:T(8,128)} %refs_0_.7, s32[128,512]{1,0:T(8,128)S(1)} %copy-done, f32[128,512]{1,0:T(8,128)S(1)} %copy-done.1, f32[128,512]{1,0:T(8,128)S(1)} %copy-done.2, ...), custom_call_target="tpu_custom_call" | custom-call | bytes 4718592 | tf_op jit(solution)/shard_map/finish/pallas_call | solution.py:292
  255.7 5.5 %collective-permute-done.19 = f32[4,136,128]{2,1,0:T(8,128)S(1)} collective-permute-done((f32[4,136,128]{2,1,0:T(8,128)S(1)}, f32[4,136,128]{2,1,0:T(8,128)S(1)}, u32[]{:S(2)}, u32[]{:S(2)}) %collective-permute-start.19) | collective-permute-done | bytes 278560 | tf_op jit(solution)/shard_map/ppermute | solution.py:312
  261.2 2.5 collective-permute-start.7
  263.7 6.3 %collective-permute-done.20 = f32[4,136,128]{2,1,0:T(8,128)S(1)} collective-permute-done((f32[4,136,128]{2,1,0:T(8,128)S(1)}, f32[4,136,128]{2,1,0:T(8,128)S(1)}, u32[]{:S(2)}, u32[]{:S(2)}) %collective-permute-start.20) | collective-permute-done | bytes 278560 | tf_op jit(solution)/shard_map/ppermute | solution.py:312
  270.0 9.5 %collective-permute-start.8 = (f32[4,136,128]{2,1,0:T(8,128)S(1)}, f32[4,136,128]{2,1,0:T(8,128)S(1)}, u32[]{:S(2)}, u32[]{:S(2)}) collective-permute-start(f32[4,136,128]{2,1,0:T(8,128)S(1)} %get-tuple-element.23), channel_id=1, source_target_pairs={{0,16},{8,24},{16,0},{24,8},{1,17},{9,25},{17,1},{25,9},{2,18},{10... | collective-permute-start | bytes 835592 | tf_op jit(solution)/shard_map/ppermute | solution.py:312
  279.6 5.0 %finish.5.refs_7_ = f32[3,8,128,512]{3,2,1,0:T(8,128)} custom-call(s32[4]{0:T(128)S(1)} %broadcast_add_fusion.2.blocks_ref, f32[6]{0:T(128)S(1)} %pad_maximum_fusion.10.scalars_ref, f32[3,8,128,512]{3,2,1,0:T(8,128)} %refs_0_.7, s32[128,512]{1,0:T(8,128)S(1)} %copy-done, f32[128,512]{1,0:T(8,128)S(1)} %copy-done.1, ...), custom_call_target="tpu_custom_call", output_to_operand_aliasing={{}: (9, {})} | custom-call | bytes 4718592 | tf_op jit(solution)/shard_map/finish/pallas_call | solution.py:292
  285.0 1.9 collective-permute-done.15
  287.0 5.0 %finish.6.refs_7_ = f32[3,8,128,512]{3,2,1,0:T(8,128)} custom-call(s32[4]{0:T(128)S(1)} %get-tuple-element.82.blocks_ref, f32[6]{0:T(128)S(1)} %pad_maximum_fusion.10.scalars_ref, f32[3,8,128,512]{3,2,1,0:T(8,128)} %refs_0_.7, s32[128,512]{1,0:T(8,128)S(1)} %copy-done, f32[128,512]{1,0:T(8,128)S(1)} %copy-done.1, ...), custom_call_target="tpu_custom_call", output_to_operand_aliasing={{}: (9, {})} | custom-call | bytes 4718592 | tf_op jit(solution)/shard_map/finish/pallas_call | solution.py:292
  292.0 4.1 %collective-permute-done.8 = f32[4,136,128]{2,1,0:T(8,128)S(1)} collective-permute-done((f32[4,136,128]{2,1,0:T(8,128)S(1)}, f32[4,136,128]{2,1,0:T(8,128)S(1)}, u32[]{:S(2)}, u32[]{:S(2)}) %collective-permute-start.8) | collective-permute-done | bytes 278560 | tf_op jit(solution)/shard_map/ppermute | solution.py:312
  296.7 5.0 %finish.7 = f32[3,8,128,512]{3,2,1,0:T(8,128)} custom-call(s32[4]{0:T(128)S(1)} %get-tuple-element.83.blocks_ref, f32[6]{0:T(128)S(1)} %pad_maximum_fusion.10.scalars_ref, f32[3,8,128,512]{3,2,1,0:T(8,128)} %refs_0_.7, s32[128,512]{1,0:T(8,128)S(1)} %copy-done, f32[128,512]{1,0:T(8,128)S(1)} %copy-done.1, ...), custom_call_target="tpu_custom_call", output_to_operand_aliasing={{}: (9, {})} | custom-call | bytes 4718592 | tf_op jit(solution)/shard_map/finish/pallas_call | solution.py:292
  (190 shorter events, 29.6 us)
Async XLA Ops:
  11.2 7.9 %copy-start.5 = (f32[3,8,128,512]{3,2,1,0:T(8,128)S(1)}, f32[3,8,128,512]{3,2,1,0:T(8,128)}, u32[]{:S(2)}) copy-start(f32[3,8,128,512]{3,2,1,0:T(8,128)} %refs_0_.7) | copy-start | bytes 18874372
  12.3 54.3 %collective-permute-start.4 = (f32[32,32,128]{2,1,0:T(8,128)}, f32[32,32,128]{2,1,0:T(8,128)S(1)}, u32[]{:S(2)}, u32[]{:S(2)}) collective-permute-start(f32[32,32,128]{2,1,0:T(8,128)} %bitcast.26), channel_id=1, source_target_pairs={{0,8},{8,16},{16,24},{24,0},{1,9},{9,17},{17,25},{25,1},{2,10},{10... | collective-permute-start | bytes 1572872 | tf_op jit(solution)/shard_map/ppermute | solution.py:312
  15.1 55.1 %collective-permute-start.10 = (f32[32,32,128]{2,1,0:T(8,128)}, f32[32,32,128]{2,1,0:T(8,128)S(1)}, u32[]{:S(2)}, u32[]{:S(2)}) collective-permute-start(f32[32,32,128]{2,1,0:T(8,128)} %bitcast.38), channel_id=1, source_target_pairs={{0,8},{8,16},{16,24},{24,0},{1,9},{9,17},{17,25},{25,1},{2,10},{10... | collective-permute-start | bytes 1572872 | tf_op jit(solution)/shard_map/ppermute | solution.py:312
  17.8 4.1 %copy-start = (s32[128,512]{1,0:T(8,128)S(1)}, s32[128,512]{1,0:T(8,128)}, u32[]{:S(2)}) copy-start(s32[128,512]{1,0:T(8,128)} %refs_1_.11) | copy-start | bytes 786436
  17.8 58.3 %collective-permute-start.11 = (f32[32,32,128]{2,1,0:T(8,128)}, f32[32,32,128]{2,1,0:T(8,128)S(1)}, u32[]{:S(2)}, u32[]{:S(2)}) collective-permute-start(f32[32,32,128]{2,1,0:T(8,128)} %bitcast.41), channel_id=1, source_target_pairs={{0,16},{8,24},{16,0},{24,8},{1,17},{9,25},{17,1},{25,9},{2,18},{10... | collective-permute-start | bytes 1572872 | tf_op jit(solution)/shard_map/ppermute | solution.py:312
  26.7 2.0 copy-start.7
  26.7 3.3 %copy-start.1 = (f32[128,512]{1,0:T(8,128)S(1)}, f32[128,512]{1,0:T(8,128)}, u32[]{:S(2)}) copy-start(f32[128,512]{1,0:T(8,128)} %refs_2_.11) | copy-start | bytes 786436
  28.7 4.2 %copy-start.8 = (f32[1,8,16,512]{3,1,0,2:T(8,128)}, f32[1,8,16,512]{3,1,0,2:T(8,128)S(1)}, u32[]{:S(2)}) copy-start(f32[1,8,16,512]{3,1,0,2:T(8,128)S(1)} %get-tuple-element.79) | copy-start | bytes 786436
  28.7 29.4 %collective-permute-start.1 = (f32[2,8,1,512]{3,1,0,2:T(8,128)S(1)}, f32[2,8,1,512]{3,1,0,2:T(8,128)S(1)}, u32[]{:S(2)}, u32[]{:S(2)}) collective-permute-start(f32[2,8,1,512]{3,1,0,2:T(8,128)S(1)} %pad_maximum_fusion.5), channel_id=1, source_target_pairs={{4,0},{5,1},{6,2},{7,3},{12,8},{13,9},{14,10},{15,11},{20,16},{21,... | collective-permute-start | bytes 98312 | tf_op jit(solution)/shard_map/ppermute | solution.py:312
  32.9 9.3 %copy-start.10 = (f32[1,8,16,512]{3,1,0,2:T(8,128)}, f32[1,8,16,512]{3,1,0,2:T(8,128)S(1)}, u32[]{:S(2)}) copy-start(f32[1,8,16,512]{3,1,0,2:T(8,128)S(1)} %get-tuple-element.76) | copy-start | bytes 786436
  32.9 9.3 %copy-start.12 = (f32[1,8,16,512]{3,1,0,2:T(8,128)}, f32[1,8,16,512]{3,1,0,2:T(8,128)S(1)}, u32[]{:S(2)}) copy-start(f32[1,8,16,512]{3,1,0,2:T(8,128)S(1)} %get-tuple-element.77) | copy-start | bytes 786436
  33.0 25.3 %collective-permute-start = (f32[2,8,1,512]{3,1,0,2:T(8,128)S(1)}, f32[2,8,1,512]{3,1,0,2:T(8,128)S(1)}, u32[]{:S(2)}, u32[]{:S(2)}) collective-permute-start(f32[2,8,1,512]{3,1,0,2:T(8,128)S(1)} %pad_maximum_fusion.6), channel_id=1, source_target_pairs={{0,4},{1,5},{2,6},{3,7},{8,12},{9,13},{10,14},{11,15},{16,20},{17,... | collective-permute-start | bytes 98312 | tf_op jit(solution)/shard_map/ppermute | solution.py:312
  38.3 6.5 %copy-start.48 = (f32[128]{0:T(128)}, f32[128]{0:T(128)S(1)}, u32[]{:S(2)}) copy-start(f32[128]{0:T(128)S(1)} %get-tuple-element.37) | copy-start | bytes 1540
  42.3 4.0 %copy-start.47 = (f32[128]{0:T(128)S(1)}, f32[128]{0:T(128)}, u32[]{:S(2)}) copy-start(f32[128]{0:T(128)} %get-tuple-element.38) | copy-start | bytes 1540
  46.2 2.3 copy-start.44
  46.2 2.3 copy-start.45
  47.4 2.0 copy-start.42
  47.4 2.0 copy-start.43
  56.3 2.0 copy-start.46
  58.3 6.3 %collective-permute-start.2 = (f32[3,8,128]{2,1,0:T(8,128)S(1)}, f32[3,8,128]{2,1,0:T(8,128)S(1)}, u32[]{:S(2)}, u32[]{:S(2)}) collective-permute-start(f32[3,8,128]{2,1,0:T(8,128)S(1)} %pad_maximum_fusion.8), channel_id=1, source_target_pairs={{0,1},{1,2},{2,3},{3,0},{4,5},{5,6},{6,7},{7,4},{8,9},{9,10},{10,1... | collective-permute-start | bytes 36872 | tf_op jit(solution)/shard_map/ppermute | solution.py:312
  58.4 6.7 %collective-permute-start.3 = (f32[3,8,128]{2,1,0:T(8,128)S(1)}, f32[3,8,128]{2,1,0:T(8,128)S(1)}, u32[]{:S(2)}, u32[]{:S(2)}) collective-permute-start(f32[3,8,128]{2,1,0:T(8,128)S(1)} %pad_maximum_fusion.9), channel_id=1, source_target_pairs={{0,3},{1,0},{2,1},{3,2},{4,7},{5,4},{6,5},{7,6},{8,11},{9,8},{10,9... | collective-permute-start | bytes 36872 | tf_op jit(solution)/shard_map/ppermute | solution.py:312
  60.1 2.2 copy-start.22
  61.2 2.3 copy-start.23
  64.6 37.4 %collective-permute-start.12 = (f32[32,32,128]{2,1,0:T(8,128)}, f32[32,32,128]{2,1,0:T(8,128)S(1)}, u32[]{:S(2)}, u32[]{:S(2)}) collective-permute-start(f32[32,32,128]{2,1,0:T(8,128)} %bitcast.44), channel_id=1, source_target_pairs={{0,24},{8,0},{16,8},{24,16},{1,25},{9,1},{17,9},{25,17},{2,26},{10... | collective-permute-start | bytes 1572872 | tf_op jit(solution)/shard_map/ppermute | solution.py:312
  65.1 36.9 %collective-permute-start.22 = (f32[32,32,128]{2,1,0:T(8,128)}, f32[32,32,128]{2,1,0:T(8,128)S(1)}, u32[]{:S(2)}, u32[]{:S(2)}) collective-permute-start(f32[32,32,128]{2,1,0:T(8,128)} %bitcast.62), channel_id=1, source_target_pairs={{0,8},{8,16},{16,24},{24,0},{1,9},{9,17},{17,25},{25,1},{2,10},{10... | collective-permute-start | bytes 1572872 | tf_op jit(solution)/shard_map/ppermute | solution.py:312
  66.6 69.2 %collective-permute-start.23 = (f32[32,32,128]{2,1,0:T(8,128)}, f32[32,32,128]{2,1,0:T(8,128)}, u32[]{:S(2)}, u32[]{:S(2)}) collective-permute-start(f32[32,32,128]{2,1,0:T(8,128)} %bitcast.65), channel_id=1, source_target_pairs={{0,16},{8,24},{16,0},{24,8},{1,17},{9,25},{17,1},{25,9},{2,18},{10... | collective-permute-start | bytes 1572872 | tf_op jit(solution)/shard_map/ppermute | solution.py:312
  70.1 88.3 %collective-permute-start.24 = (f32[32,32,128]{2,1,0:T(8,128)}, f32[32,32,128]{2,1,0:T(8,128)}, u32[]{:S(2)}, u32[]{:S(2)}) collective-permute-start(f32[32,32,128]{2,1,0:T(8,128)} %bitcast.68), channel_id=1, source_target_pairs={{0,24},{8,0},{16,8},{24,16},{1,25},{9,1},{17,9},{25,17},{2,26},{10... | collective-permute-start | bytes 1572872 | tf_op jit(solution)/shard_map/ppermute | solution.py:312
  75.5 73.0 %copy-start.11 = (f32[1,8,16,512]{3,1,0,2:T(8,128)S(1)}, f32[1,8,16,512]{3,1,0,2:T(8,128)}, u32[]{:S(2)}) copy-start(f32[1,8,16,512]{3,1,0,2:T(8,128)} %copy-done.10) | copy-start | bytes 786436
  75.5 73.0 %copy-start.13 = (f32[1,8,16,512]{3,1,0,2:T(8,128)S(1)}, f32[1,8,16,512]{3,1,0,2:T(8,128)}, u32[]{:S(2)}) copy-start(f32[1,8,16,512]{3,1,0,2:T(8,128)} %copy-done.12) | copy-start | bytes 786436
  76.1 82.3 %copy-start.3 = (bf16[4,256,96]{2,1,0:T(8,128)(2,1)S(1)}, bf16[4,256,96]{2,1,0:T(8,128)(2,1)}, u32[]{:S(2)}) copy-start(bf16[4,256,96]{2,1,0:T(8,128)(2,1)} %constant.91.clone.refs_1_) | copy-start | bytes 589828
  76.1 82.3 %copy-start.4 = (bf16[4,64,256]{2,1,0:T(8,128)(2,1)S(1)}, bf16[4,64,256]{2,1,0:T(8,128)(2,1)}, u32[]{:S(2)}) copy-start(bf16[4,64,256]{2,1,0:T(8,128)(2,1)} %constant.92.clone.refs_2_) | copy-start | bytes 393220
  76.1 102.8 %collective-permute-start.5 = (f32[32,32,128]{2,1,0:T(8,128)S(1)}, f32[32,32,128]{2,1,0:T(8,128)S(1)}, u32[]{:S(2)}, u32[]{:S(2)}) collective-permute-start(f32[32,32,128]{2,1,0:T(8,128)S(1)} %bitcast.133), channel_id=1, source_target_pairs={{0,16},{8,24},{16,0},{24,8},{1,17},{9,25},{17,1},{25,9},{2,18},{10... | collective-permute-start | bytes 1572872 | tf_op jit(solution)/shard_map/ppermute | solution.py:312
  102.0 88.2 %collective-permute-start.16 = (f32[32,32,128]{2,1,0:T(8,128)S(1)}, f32[32,32,128]{2,1,0:T(8,128)S(1)}, u32[]{:S(2)}, u32[]{:S(2)}) collective-permute-start(f32[32,32,128]{2,1,0:T(8,128)S(1)} %bitcast.132), channel_id=1, source_target_pairs={{0,8},{8,16},{16,24},{24,0},{1,9},{9,17},{17,25},{25,1},{2,10},{10... | collective-permute-start | bytes 1572872 | tf_op jit(solution)/shard_map/ppermute | solution.py:312
  102.0 105.5 %collective-permute-start.17 = (f32[32,32,128]{2,1,0:T(8,128)S(1)}, f32[32,32,128]{2,1,0:T(8,128)S(1)}, u32[]{:S(2)}, u32[]{:S(2)}) collective-permute-start(f32[32,32,128]{2,1,0:T(8,128)S(1)} %bitcast.131), channel_id=1, source_target_pairs={{0,16},{8,24},{16,0},{24,8},{1,17},{9,25},{17,1},{25,9},{2,18},{10... | collective-permute-start | bytes 1572872 | tf_op jit(solution)/shard_map/ppermute | solution.py:312
  135.8 75.0 %collective-permute-start.18 = (f32[32,32,128]{2,1,0:T(8,128)S(1)}, f32[32,32,128]{2,1,0:T(8,128)S(1)}, u32[]{:S(2)}, u32[]{:S(2)}) collective-permute-start(f32[32,32,128]{2,1,0:T(8,128)S(1)} %bitcast.130), channel_id=1, source_target_pairs={{0,24},{8,0},{16,8},{24,16},{1,25},{9,1},{17,9},{25,17},{2,26},{10... | collective-permute-start | bytes 1572872 | tf_op jit(solution)/shard_map/ppermute | solution.py:312
  158.4 62.8 %collective-permute-start.6 = (f32[32,32,128]{2,1,0:T(8,128)S(1)}, f32[32,32,128]{2,1,0:T(8,128)S(1)}, u32[]{:S(2)}, u32[]{:S(2)}) collective-permute-start(f32[32,32,128]{2,1,0:T(8,128)S(1)} %bitcast.129), channel_id=1, source_target_pairs={{0,24},{8,0},{16,8},{24,16},{1,25},{9,1},{17,9},{25,17},{2,26},{10... | collective-permute-start | bytes 1572872 | tf_op jit(solution)/shard_map/ppermute | solution.py:312
  179.0 42.3 %collective-permute-start.13 = (f32[4,136,128]{2,1,0:T(8,128)S(1)}, f32[4,136,128]{2,1,0:T(8,128)S(1)}, u32[]{:S(2)}, u32[]{:S(2)}) collective-permute-start(f32[4,136,128]{2,1,0:T(8,128)S(1)} %get-tuple-element.26), channel_id=1, source_target_pairs={{0,8},{8,16},{16,24},{24,0},{1,9},{9,17},{17,25},{25,1},{2,10},{10... | collective-permute-start | bytes 835592 | tf_op jit(solution)/shard_map/ppermute | solution.py:312
  190.2 47.1 %collective-permute-start.25 = (f32[4,136,128]{2,1,0:T(8,128)S(1)}, f32[4,136,128]{2,1,0:T(8,128)S(1)}, u32[]{:S(2)}, u32[]{:S(2)}) collective-permute-start(f32[4,136,128]{2,1,0:T(8,128)S(1)} %get-tuple-element.34), channel_id=1, source_target_pairs={{0,8},{8,16},{16,24},{24,0},{1,9},{9,17},{17,25},{25,1},{2,10},{10... | collective-permute-start | bytes 835592 | tf_op jit(solution)/shard_map/ppermute | solution.py:312
  207.5 38.8 %collective-permute-start.26 = (f32[4,136,128]{2,1,0:T(8,128)S(1)}, f32[4,136,128]{2,1,0:T(8,128)S(1)}, u32[]{:S(2)}, u32[]{:S(2)}) collective-permute-start(f32[4,136,128]{2,1,0:T(8,128)S(1)} %get-tuple-element.35), channel_id=1, source_target_pairs={{0,16},{8,24},{16,0},{24,8},{1,17},{9,25},{17,1},{25,9},{2,18},{10... | collective-permute-start | bytes 835592 | tf_op jit(solution)/shard_map/ppermute | solution.py:312
  210.8 38.8 %collective-permute-start.27 = (f32[4,136,128]{2,1,0:T(8,128)S(1)}, f32[4,136,128]{2,1,0:T(8,128)S(1)}, u32[]{:S(2)}, u32[]{:S(2)}) collective-permute-start(f32[4,136,128]{2,1,0:T(8,128)S(1)} %get-tuple-element.36), channel_id=1, source_target_pairs={{0,24},{8,0},{16,8},{24,16},{1,25},{9,1},{17,9},{25,17},{2,26},{10... | collective-permute-start | bytes 835592 | tf_op jit(solution)/shard_map/ppermute | solution.py:312
  221.2 40.0 %collective-permute-start.19 = (f32[4,136,128]{2,1,0:T(8,128)S(1)}, f32[4,136,128]{2,1,0:T(8,128)S(1)}, u32[]{:S(2)}, u32[]{:S(2)}) collective-permute-start(f32[4,136,128]{2,1,0:T(8,128)S(1)} %get-tuple-element.30), channel_id=1, source_target_pairs={{0,8},{8,16},{16,24},{24,0},{1,9},{9,17},{17,25},{25,1},{2,10},{10... | collective-permute-start | bytes 835592 | tf_op jit(solution)/shard_map/ppermute | solution.py:312
  221.2 48.8 %collective-permute-start.20 = (f32[4,136,128]{2,1,0:T(8,128)S(1)}, f32[4,136,128]{2,1,0:T(8,128)S(1)}, u32[]{:S(2)}, u32[]{:S(2)}) collective-permute-start(f32[4,136,128]{2,1,0:T(8,128)S(1)} %get-tuple-element.31), channel_id=1, source_target_pairs={{0,16},{8,24},{16,0},{24,8},{1,17},{9,25},{17,1},{25,9},{2,18},{10... | collective-permute-start | bytes 835592 | tf_op jit(solution)/shard_map/ppermute | solution.py:312
  237.3 42.2 %collective-permute-start.21 = (f32[4,136,128]{2,1,0:T(8,128)S(1)}, f32[4,136,128]{2,1,0:T(8,128)S(1)}, u32[]{:S(2)}, u32[]{:S(2)}) collective-permute-start(f32[4,136,128]{2,1,0:T(8,128)S(1)} %get-tuple-element.32), channel_id=1, source_target_pairs={{0,24},{8,0},{16,8},{24,16},{1,25},{9,1},{17,9},{25,17},{2,26},{10... | collective-permute-start | bytes 835592 | tf_op jit(solution)/shard_map/ppermute | solution.py:312
  246.2 38.7 %collective-permute-start.14 = (f32[4,136,128]{2,1,0:T(8,128)S(1)}, f32[4,136,128]{2,1,0:T(8,128)S(1)}, u32[]{:S(2)}, u32[]{:S(2)}) collective-permute-start(f32[4,136,128]{2,1,0:T(8,128)S(1)} %get-tuple-element.27), channel_id=1, source_target_pairs={{0,16},{8,24},{16,0},{24,8},{1,17},{9,25},{17,1},{25,9},{2,18},{10... | collective-permute-start | bytes 835592 | tf_op jit(solution)/shard_map/ppermute | solution.py:312
  249.6 37.2 %collective-permute-start.15 = (f32[4,136,128]{2,1,0:T(8,128)S(1)}, f32[4,136,128]{2,1,0:T(8,128)S(1)}, u32[]{:S(2)}, u32[]{:S(2)}) collective-permute-start(f32[4,136,128]{2,1,0:T(8,128)S(1)} %get-tuple-element.28), channel_id=1, source_target_pairs={{0,24},{8,0},{16,8},{24,16},{1,25},{9,1},{17,9},{25,17},{2,26},{10... | collective-permute-start | bytes 835592 | tf_op jit(solution)/shard_map/ppermute | solution.py:312
  261.2 30.8 %collective-permute-start.7 = (f32[4,136,128]{2,1,0:T(8,128)S(1)}, f32[4,136,128]{2,1,0:T(8,128)S(1)}, u32[]{:S(2)}, u32[]{:S(2)}) collective-permute-start(f32[4,136,128]{2,1,0:T(8,128)S(1)} %get-tuple-element.22), channel_id=1, source_target_pairs={{0,8},{8,16},{16,24},{24,0},{1,9},{9,17},{17,25},{25,1},{2,10},{10... | collective-permute-start | bytes 835592 | tf_op jit(solution)/shard_map/ppermute | solution.py:312
  270.0 26.0 %collective-permute-start.8 = (f32[4,136,128]{2,1,0:T(8,128)S(1)}, f32[4,136,128]{2,1,0:T(8,128)S(1)}, u32[]{:S(2)}, u32[]{:S(2)}) collective-permute-start(f32[4,136,128]{2,1,0:T(8,128)S(1)} %get-tuple-element.23), channel_id=1, source_target_pairs={{0,16},{8,24},{16,0},{24,8},{1,17},{9,25},{17,1},{25,9},{2,18},{10... | collective-permute-start | bytes 835592 | tf_op jit(solution)/shard_map/ppermute | solution.py:312
  279.5 17.1 %collective-permute-start.9 = (f32[4,136,128]{2,1,0:T(8,128)S(1)}, f32[4,136,128]{2,1,0:T(8,128)S(1)}, u32[]{:S(2)}, u32[]{:S(2)}) collective-permute-start(f32[4,136,128]{2,1,0:T(8,128)S(1)} %get-tuple-element.24), channel_id=1, source_target_pairs={{0,24},{8,0},{16,8},{24,16},{1,25},{9,1},{17,9},{25,17},{2,26},{10... | collective-permute-start | bytes 835592 | tf_op jit(solution)/shard_map/ppermute | solution.py:312
  (29 other events, 44.1 us)

commit v3 on v2

--- a/solution.py
+++ b/solution.py
@@ -19,6 +19,9 @@
 OMEGA_STEP = 0.25
 SPEED_SOFT = 0.01
 VMEM_BYTES = 48 * 1024 * 1024
+CHUNK_SHARES = (24, 25, 26, 22)
+SHARE_UNITS = 128
+LOOP_TILES = 8
 
 
 def split_table():
@@ -38,16 +41,15 @@
     return high, low
 
 
-def friction_kernel(groups, coefs, place_ref, synth_ref, analyse_ref, *refs):
+def friction_kernel(groups, coefs, tiles, place_ref, synth_ref, analyse_ref, *refs):
     flow_refs, out_refs = refs[:groups], refs[groups:]
     columns = 2 * NCON
 
-    def body(step, carry):
-        tile = step * 2
+    def block(tile, count):
         loaded = []
         for source in range(groups):
-            pair = [flow_refs[source][tile], flow_refs[source][tile + 1]]
-            loaded.append(jnp.concatenate(pair, axis=1))
+            parts = [flow_refs[source][tile + i] for i in range(count)]
+            loaded.append(jnp.concatenate(parts, axis=1))
         series = []
         for field in range(4):
             rows = slice(field * coefs, (field + 1) * coefs)
@@ -75,20 +77,25 @@
                 analyse_ref[0, :columns, :], low, preferred_element_type=jnp.float32
             )
             analysed.append(both[:columns] + both[columns:] + rest)
-        for part in range(2):
+        for part in range(count):
             lanes = slice(part * LANES, (part + 1) * LANES)
             for target in range(groups):
                 rows = slice(target * coefs, (target + 1) * coefs)
-                block = jnp.concatenate(
+                values = jnp.concatenate(
                     [analysed[0][rows, lanes], analysed[1][rows, lanes]], axis=0
                 )
                 start = pl.multiple_of((tile + part) * 2 * coefs, SUB)
-                out_refs[target][0, pl.ds(start, 2 * coefs), :] = block
-                at = SUB * 2 * coefs + tile + part
-                out_refs[target][0, pl.ds(at, 1), :] = mean[:, lanes]
+                out_refs[target][pl.ds(start, 2 * coefs), :] = values
+                at = tiles * 2 * coefs + tile + part
+                out_refs[target][pl.ds(at, 1), :] = mean[:, lanes]
+
+    def body(step, carry):
+        block(step * 2, 2)
         return carry
 
-    lax.fori_loop(0, SUB // 2, body, 0)
+    lax.fori_loop(0, tiles // 2, body, 0)
+    if tiles % 2:
+        block(tiles - 1, 1)
 
 
 def placed_tables(groups, coefs):
@@ -105,26 +112,29 @@
     return np.stack(synth), np.stack(analyse)
 
 
+def piece_rows(tiles, coefs):
+    return tiles * 2 * coefs + -(-tiles // SUB) * SUB
+
+
 def friction_call(place, flows, coefs):
     groups = len(flows)
-    tiles, rows = flows[0].shape[:2]
+    tiles = flows[0].shape[0]
     synth, analyse = placed_tables(groups, coefs)
-    out_rows = SUB * (2 * coefs + 1)
     cells = groups * tiles * LANES
+    out_shape = (piece_rows(tiles, coefs), LANES)
     grid_spec = pltpu.PrefetchScalarGridSpec(
         num_scalar_prefetch=1,
-        grid=(tiles // SUB,),
+        grid=(1,),
         in_specs=[
             pl.BlockSpec((1,) + synth.shape[1:], lambda i, place: (place[0], 0, 0)),
             pl.BlockSpec((1,) + analyse.shape[1:], lambda i, place: (place[0], 0, 0)),
         ]
-        + [pl.BlockSpec((SUB, rows, LANES), lambda i, place: (i, 0, 0))] * groups,
-        out_specs=[pl.BlockSpec((1, out_rows, LANES), lambda i, place: (i, 0, 0))] * groups,
+        + [pl.BlockSpec(flows[0].shape, lambda i, place: (0, 0, 0))] * groups,
+        out_specs=[pl.BlockSpec(out_shape, lambda i, place: (0, 0))] * groups,
     )
-    out = jax.ShapeDtypeStruct((tiles // SUB, out_rows, LANES), jnp.float32)
     return pl.pallas_call(
-        lambda *refs: friction_kernel(groups, coefs, *refs),
-        out_shape=[out] * groups,
+        lambda *refs: friction_kernel(groups, coefs, tiles, *refs),
+        out_shape=[jax.ShapeDtypeStruct(out_shape, jnp.float32)] * groups,
         grid_spec=grid_spec,
         compiler_params=pltpu.CompilerParams(vmem_limit_bytes=VMEM_BYTES),
         cost_estimate=pl.CostEstimate(
@@ -134,15 +144,200 @@
     )(place, jnp.asarray(synth), jnp.asarray(analyse), *flows)
 
 
-def finish_kernel(coefs, lane_tiles, blocks_ref, scalars_ref, refs):
-    direction_ref, wet_ref, depth_ref, drag_ref, edge_ref, slab_ref, back_ref, out_ref = refs
+def index_kernel(wet_ref, index_ref, place_ref, offset_ref, scratch):
+    blocks = scratch.shape[0]
+    rows, cols = wet_ref.shape
+    at = 0
+    for row in range(0, rows, SUB):
+        for col in range(0, cols, LANES):
+            part = wet_ref[row : row + SUB, col : col + LANES]
+            scratch[at : at + SUB, :] = jnp.where(part != 0, 1.0, 0.0)
+            at += SUB
+    wet = scratch[...].astype(jnp.bfloat16)
+    earlier = lax.broadcasted_iota(jnp.int32, (LANES, LANES), 0)
+    later = lax.broadcasted_iota(jnp.int32, (LANES, LANES), 1)
+    before = jnp.where(earlier < later, 1.0, 0.0).astype(jnp.bfloat16)
+    ones = jnp.ones((LANES, LANES), jnp.bfloat16)
+    rank = jnp.dot(wet, before, preferred_element_type=jnp.float32)
+    count = jnp.dot(wet, ones, preferred_element_type=jnp.float32)
+    low = lax.broadcasted_iota(jnp.int32, (blocks, blocks), 0)
+    high = lax.broadcasted_iota(jnp.int32, (blocks, blocks), 1)
+    summing = jnp.where(high < low, 1.0, 0.0).astype(jnp.bfloat16)
+    offset = jnp.dot(summing, count.astype(jnp.bfloat16), preferred_element_type=jnp.float32)
+    lane = lax.broadcasted_iota(jnp.int32, (blocks, LANES), 1)
+    rank = rank.astype(jnp.int32)
+    held = jnp.where(scratch[...] > 0.5, lane + LANES * (lane - rank), 0)
+    for bit in range(7):
+        step = 1 << bit
+        coming = pltpu.roll(held, LANES - step, 1)
+        moves = (coming >> (7 + bit)) & 1
+        stays = 1 - ((held >> (7 + bit)) & 1)
+        held = jnp.where(moves == 1, coming, held * stays)
+    source = held & (LANES - 1)
+    shift = offset.astype(jnp.int32) & (LANES - 1)
+    index_ref[...] = jnp.take_along_axis(
+        source, (lane - shift) & (LANES - 1), axis=1, mode="promise_in_bounds"
+    )
+    place_ref[...] = shift + rank
+    eye = jnp.where(earlier == later, 1.0, 0.0)
+    cubes = offset.reshape(blocks // LANES, LANES, LANES)
+    table = jnp.sum(cubes * eye[None], axis=1)
+    total = offset[blocks - 1 : blocks] + count[blocks - 1 : blocks]
+    offset_ref[: blocks // LANES, :] = table.astype(jnp.int32)
+    offset_ref[blocks // LANES : blocks // LANES + 1, :] = total.astype(jnp.int32)
+
+
+def index_call(wet_mask):
+    rows, cols = wet_mask.shape
+    blocks = rows * cols // LANES
+    table = -(-(blocks // LANES + 1) // SUB) * SUB
+    return pl.pallas_call(
+        index_kernel,
+        out_shape=[
+            jax.ShapeDtypeStruct((blocks, LANES), jnp.int32),
+            jax.ShapeDtypeStruct((blocks, LANES), jnp.int32),
+            jax.ShapeDtypeStruct((table, LANES), jnp.int32),
+        ],
+        scratch_shapes=[pltpu.VMEM((blocks, LANES), jnp.float32)],
+        compiler_params=pltpu.CompilerParams(vmem_limit_bytes=VMEM_BYTES),
+        name="index",
+    )(wet_mask)
+
+
+def pack_kernel(groups, coefs, tiles, params_ref, offset_ref, index_ref, base_ref, step_ref, *refs):
+    out_refs = refs[:groups]
+    held, stage, in_sem, out_sem = refs[groups:]
+    columns = held.shape[-1]
+    lane_tiles = columns // LANES
+    per_block = SUB * lane_tiles
+    row_blocks = index_ref.shape[0] // per_block
+    count = groups * tiles
+    first_tile = params_ref[1]
+    low = first_tile * LANES
+    high = low + count * LANES
+
+    def offset_of(block):
+        return offset_ref[block // LANES, block % LANES]
+
+    begin = jnp.int32(0)
+    end = jnp.int32(0)
+    for block in range(row_blocks):
+        begin += (offset_of((block + 1) * per_block) <= low).astype(jnp.int32)
+        end += (offset_of(block * per_block) < high).astype(jnp.int32)
+    end = jnp.maximum(end, begin)
+
+    def copies(block):
+        slot = block % 2
+        rows = pl.ds(pl.multiple_of(block * SUB, SUB), SUB)
+        return (
+            pltpu.make_async_copy(
+                base_ref.at[:, :, rows, :], held.at[slot, pl.ds(0, 2)], in_sem.at[slot, 0]
+            ),
+            pltpu.make_async_copy(
+                step_ref.at[pl.ds(1, 2), :, rows, :], held.at[slot, pl.ds(2, 2)], in_sem.at[slot, 1]
+            ),
+        )
+
+    @pl.when(begin < end)
+    def _():
+        for copy in copies(begin):
+            copy.start()
+
+    lane = lax.broadcasted_iota(jnp.int32, (coefs, LANES), 1)
+
+    def place_of(offset):
+        return jnp.clip((offset >> 7) - first_tile + 1, 0, count + 1)
+
+    def body(block, current):
+        @pl.when(block + 1 < end)
+        def _():
+            for copy in copies(block + 1):
+                copy.start()
+
+        for copy in copies(block):
+            copy.wait()
+        slot = block % 2
+        for lane_tile in range(lane_tiles):
+            lanes = slice(lane_tile * LANES, (lane_tile + 1) * LANES)
+            turned = [
+                jnp.swapaxes(held[slot, field, :, :, lanes], 0, 1) for field in range(4)
+            ]
+            start = block * per_block + lane_tile * SUB
+            index = index_ref[pl.ds(pl.multiple_of(start, SUB), SUB), :]
+            for r in range(SUB):
+                offset = offset_of(start + r)
+                following = offset_of(start + r + 1)
+                shift = offset & (LANES - 1)
+                crossing = (following >> 7) > (offset >> 7)
+                source = jnp.broadcast_to(index[r : r + 1], (coefs, LANES))
+                to = place_of(offset)
+                renewed = []
+                for field in range(4):
+                    got = jnp.take_along_axis(
+                        turned[field][r], source, axis=1, mode="promise_in_bounds"
+                    )
+                    full = jnp.where(lane >= shift, got, current[field])
+                    stage[to, field * coefs : (field + 1) * coefs, :] = full
+                    renewed.append(jnp.where(crossing, got, full))
+                current = tuple(renewed)
+        return current
+
+    zero = jnp.zeros((coefs, LANES), jnp.float32)
+    current = lax.fori_loop(begin, end, body, (zero,) * 4)
+    last = place_of(offset_of(end * per_block))
+    for field in range(4):
+        stage[last, field * coefs : (field + 1) * coefs, :] = current[field]
+    outs = []
+    for step in range(groups):
+        member = lax.rem(params_ref[0] + step, groups)
+        outs.append(
+            pltpu.make_async_copy(
+                stage.at[pl.ds(1 + member * tiles, tiles)], out_refs[step], out_sem.at[step]
+            )
+        )
+    for copy in outs:
+        copy.start()
+    for copy in outs:
+        copy.wait()
+
+
+def pack_call(params, offset, index, base_flow, direction, groups, tiles):
+    coefs, _, columns = direction.shape[1:]
+    shape = (tiles, 4 * coefs, LANES)
+    anywhere = pl.BlockSpec(memory_space=pl.ANY)
+    grid_spec = pltpu.PrefetchScalarGridSpec(
+        num_scalar_prefetch=2,
+        grid=(1,),
+        in_specs=[pl.BlockSpec(index.shape, lambda i, p, o: (0, 0)), anywhere, anywhere],
+        out_specs=[anywhere] * groups,
+        scratch_shapes=[
+            pltpu.VMEM((2, 4, coefs, SUB, columns), jnp.float32),
+            pltpu.VMEM((groups * tiles + 2, 4 * coefs, LANES), jnp.float32),
+            pltpu.SemaphoreType.DMA((2, 2)),
+            pltpu.SemaphoreType.DMA((groups,)),
+        ],
+    )
+    return pl.pallas_call(
+        lambda *refs: pack_kernel(groups, coefs, tiles, *refs),
+        out_shape=[jax.ShapeDtypeStruct(shape, jnp.float32)] * groups,
+        grid_spec=grid_spec,
+        compiler_params=pltpu.CompilerParams(vmem_limit_bytes=VMEM_BYTES),
+        cost_estimate=pl.CostEstimate(
+            flops=0, bytes_accessed=groups * tiles * coefs * 4096, transcendentals=0
+        ),
+        name="pack",
+    )(params, offset, index, base_flow, direction)
+
+
+def finish_kernel(coefs, lane_tiles, row_block, first_ref, offset_ref, table_ref, scalars_ref, back, refs):
+    (direction_ref, wet_ref, depth_ref, drag_ref, edge_ref, slab_ref, cell_ref, out_ref) = refs
     columns = lane_tiles * LANES
     wet = wet_ref[...].astype(jnp.float32)
     depth = depth_ref[...]
     drag = drag_ref[...]
     lane = lax.broadcasted_iota(jnp.int32, (SUB, columns), 1)
     sub = lax.broadcasted_iota(jnp.int32, (SUB, columns), 0)
-    block = blocks_ref[pl.program_id(0)] * SUB
+    block = row_block * SUB
     row = (block + sub).astype(jnp.float32)
     rotation = 0.5 + (row + scalars_ref[0] + 0.5) * scalars_ref[1]
 
@@ -161,27 +356,46 @@
     def below(value, edge):
         return jnp.where(sub == SUB - 1, edge, pltpu.roll(value, SUB - 1, 0))
 
-    group_tiles = []
+    def gathered(here, after, index, over):
+        first = jnp.take_along_axis(here, index, axis=1, mode="promise_in_bounds")
+        second = jnp.take_along_axis(after, index, axis=1, mode="promise_in_bounds")
+        return jnp.where(over, second, first)
+
+    spread = []
+    speed = []
     for lane_tile in range(lane_tiles):
+        places = cell_ref[lane_tile * SUB : (lane_tile + 1) * SUB, :]
         rows = []
+        speeds = [[], []]
         for r in range(SUB):
-            tile = r * lane_tiles + lane_tile
-            start = (tile % SUB) * 2 * coefs
-            rows.append(back_ref[tile // SUB, start : start + 2 * coefs, :])
-        group_tiles.append(jnp.swapaxes(jnp.stack(rows, axis=0), 0, 1))
+            at = (row_block * lane_tiles + lane_tile) * SUB + r
+            tile = offset_ref[at // LANES, at % LANES] >> 7
+            found = []
+            for which in range(2):
+                start = pl.multiple_of(table_ref[first_ref[1] * 2, tile + which], SUB)
+                found.append(back[pl.ds(start, 2 * coefs), :])
+                start = table_ref[first_ref[1] * 2 + 1, tile + which]
+                speeds[which].append(back[pl.ds(start, 1), :])
+            place = jnp.broadcast_to(places[r : r + 1], (2 * coefs, LANES))
+            rows.append(gathered(found[0], found[1], place & (LANES - 1), place >= LANES))
+        spread.append(jnp.swapaxes(jnp.stack(rows, axis=0), 0, 1))
+        speed.append(
+            gathered(
+                jnp.concatenate(speeds[0], axis=0),
+                jnp.concatenate(speeds[1], axis=0),
+                places & (LANES - 1),
+                places >= LANES,
+            )
+        )
+    is_wet = wet > 0.5
     friction = [
-        jnp.concatenate([part[index] for part in group_tiles], axis=1) * drag
+        jnp.where(
+            is_wet, jnp.concatenate([part[index] for part in spread], axis=1) * drag, 0.0
+        )
         for index in range(2 * coefs)
     ]
-    speed = []
-    for lane_tile in range(lane_tiles):
-        rows = []
-        for r in range(SUB):
-            tile = r * lane_tiles + lane_tile
-            at = SUB * 2 * coefs + tile % SUB
-            rows.append(back_ref[tile // SUB, at : at + 1, :])
-        speed.append(jnp.concatenate(rows, axis=0))
-    real_rate = drag * jnp.concatenate(speed, axis=1) + LINEAR_DRAG
+    speed = jnp.where(is_wet, jnp.concatenate(speed, axis=1), 0.0)
+    real_rate = drag * speed + LINEAR_DRAG
 
     for k in range(coefs // 2):
         angular = scalars_ref[2 + k]
@@ -260,45 +474,70 @@
         out_ref[2, 2 * k + 1] = -(num_north_re * inv_imag + num_north_im * inv_real)
 
 
-def finish_call(blocks, scalars, direction, wet_mask, depth, drag, edges, slabs, back, result):
+def finish_call(first, offset, table, scalars, arrays, pieces, rows, result):
+    direction, columns = arrays[0], arrays[0].shape[3]
     coefs = direction.shape[1]
-    columns = direction.shape[3]
     lane_tiles = columns // LANES
-
-    def kernel(blocks_ref, scalars_ref, *refs):
-        if result is not None:
-            refs = refs[:7] + refs[8:]
-        finish_kernel(coefs, lane_tiles, blocks_ref, scalars_ref, refs)
-
-    flat = pl.BlockSpec((SUB, columns), lambda i, at: (at[i], 0))
-    planes = pl.BlockSpec((3, coefs, SUB, columns), lambda i, at: (0, 0, at[i], 0))
-    in_specs = [
-        pl.BlockSpec(memory_space=pltpu.SMEM),
-        planes,
-        flat,
-        flat,
-        flat,
-        pl.BlockSpec((1, 4, coefs, columns), lambda i, at: (at[i], 0, 0, 0)),
-        pl.BlockSpec((6, coefs, SUB, LANES), lambda i, at: (0, 0, at[i], 0)),
-        pl.BlockSpec((lane_tiles,) + back.shape[1:], lambda i, at: (i, 0, 0)),
-    ]
-    operands = [blocks, scalars, direction, wet_mask, depth, drag, edges, slabs, back]
-    aliases = {}
-    if result is not None:
-        in_specs.append(pl.BlockSpec(memory_space=pl.ANY))
+    shares = 1 if result is not None else 0
+
+    def kernel(first_ref, offset_ref, table_ref, scalars_ref, *refs):
+        array_refs = refs[:7]
+        piece_refs = refs[7 + shares : -3]
+        out_ref, back, sem = refs[-3:]
+        first = first_ref[0]
+        copies = []
+        at = 0
+        for n, piece in enumerate(piece_refs):
+            rows = piece.shape[0]
+            copies.append(pltpu.make_async_copy(piece, back.at[pl.ds(at, rows)], sem.at[n]))
+            at += rows
+        for copy in copies:
+            copy.start()
+        for copy in copies:
+            copy.wait()
+
+        def body(*block_refs):
+            finish_kernel(
+                coefs, lane_tiles, first + pl.program_id(0), first_ref, offset_ref, table_ref,
+                scalars_ref, back, block_refs,
+            )
+
+        flat = pl.BlockSpec((SUB, columns), lambda i: (first + i, 0))
+        planes = pl.BlockSpec((3, coefs, SUB, columns), lambda i: (0, 0, first + i, 0))
+        pltpu.emit_pipeline(
+            body,
+            grid=(first_ref[2],),
+            in_specs=[
+                planes,
+                flat,
+                flat,
+                flat,
+                pl.BlockSpec((1, 4, coefs, columns), lambda i: (first + i, 0, 0, 0)),
+                pl.BlockSpec((6, coefs, SUB, LANES), lambda i: (0, 0, first + i, 0)),
+                pl.BlockSpec((SUB * lane_tiles, LANES), lambda i: (first + i, 0)),
+            ],
+            out_specs=[planes],
+        )(*array_refs, out_ref)
+
+    anywhere = pl.BlockSpec(memory_space=pl.ANY)
+    scalar = pl.BlockSpec(memory_space=pltpu.SMEM)
+    operands = [first, offset, table, scalars] + list(arrays)
+    if shares:
         operands.append(result)
-        aliases = {9: 0}
-    count = blocks.shape[0]
+    operands += pieces
     return pl.pallas_call(
         kernel,
         out_shape=jax.ShapeDtypeStruct(direction.shape, jnp.float32),
-        grid_spec=pltpu.PrefetchScalarGridSpec(
-            num_scalar_prefetch=1, grid=(count,), in_specs=in_specs, out_specs=planes
-        ),
-        input_output_aliases=aliases,
+        in_specs=[scalar] * 4 + [anywhere] * (7 + shares + len(pieces)),
+        out_specs=anywhere,
+        scratch_shapes=[
+            pltpu.VMEM((rows, LANES), jnp.float32),
+            pltpu.SemaphoreType.DMA((len(pieces),)),
+        ],
+        input_output_aliases={11: 0} if shares else {},
         compiler_params=pltpu.CompilerParams(vmem_limit_bytes=VMEM_BYTES),
         cost_estimate=pl.CostEstimate(
-            flops=0, bytes_accessed=count * SUB * columns * coefs * 36, transcendentals=0
+            flops=0, bytes_accessed=8 * SUB * columns * coefs * 36, transcendentals=0
         ),
         name="finish",
     )(*operands)
@@ -338,6 +577,31 @@
     return edges, slabs
 
 
+def spread_out(blocks):
+    return [
+        block if step == 0 else shifted(block, "freq", step, True)
+        for step, block in enumerate(blocks)
+    ]
+
+
+def tile_table(groups, coefs, chunk_tiles, steps, blocks):
+    places = list(chunk_tiles) + [LOOP_TILES] * steps
+    table = np.zeros((2 * groups, blocks + LANES), np.int32)
+    for member in range(groups):
+        tile = 0
+        row = 0
+        for tiles in places:
+            for band in range(groups):
+                start = row + (member - band) % groups * piece_rows(tiles, coefs)
+                for i in range(tiles):
+                    if tile < blocks:
+                        table[2 * member, tile] = start + i * 2 * coefs
+                        table[2 * member + 1, tile] = start + tiles * 2 * coefs + i
+                    tile += 1
+            row += groups * piece_rows(tiles, coefs)
+    return table
+
+
 def local(direction, base_flow, water_depth, drag_factor, wet_mask):
     coefs, tile_rows, tile_cols = direction.shape[1:]
     groups = lax.axis_size("freq")
@@ -355,30 +619,61 @@
     )
     edges, slabs = halo(direction, wet, water_depth)
     place = jnp.reshape(member, (1,)).astype(jnp.int32)
-    chunks = tile_rows // (groups * SUB)
-    steps = jnp.arange(groups, dtype=jnp.int32)
-    sources = (member - steps) % groups
+    blocks = tile_rows * lane_tiles
+    row_blocks = tile_rows // SUB
+    chunk_tiles = [share * blocks // (groups * SHARE_UNITS) for share in CHUNK_SHARES]
+    fixed = groups * sum(chunk_tiles)
+    steps = -(-(blocks - fixed) // (groups * LOOP_TILES))
+    table = jnp.asarray(tile_table(groups, coefs, chunk_tiles, steps, blocks))
+    index, cells, offset = index_call(wet_mask)
+    offsets = offset.reshape(-1)
+    ends = offsets[SUB * lane_tiles : blocks + 1 : SUB * lane_tiles]
+
+    def through(first_tile, tiles):
+        params = jnp.stack([place[0], jnp.asarray(first_tile, jnp.int32)])
+        flows = pack_call(params, offset, index, base_flow, direction, groups, tiles)
+        back = friction_call(place, spread_out(flows), coefs)
+        return spread_out(back)
+
+    largest = lax.pmax(offsets[blocks], ("lat", "lon"))
+    loop_cells = groups * LOOP_TILES * LANES
+    loops = jnp.maximum(largest - fixed * LANES + loop_cells - 1, 0) // loop_cells
+
+    def more(state):
+        done, held = state
+        back = through(fixed + done * groups * LOOP_TILES, LOOP_TILES)
+        held = lax.dynamic_update_slice_in_dim(
+            held, jnp.concatenate(back, axis=0)[None], done, 0
+        )
+        return done + 1, held
+
+    rows = groups * piece_rows(LOOP_TILES, coefs)
+    extra = jnp.zeros((steps, rows, LANES), jnp.float32)
+    _, extra = lax.while_loop(lambda state: state[0] < loops, more, (jnp.int32(0), extra))
+
+    arrays = (direction, wet_mask, water_depth, drag_factor, edges, slabs, cells)
+    pieces = []
+    back_rows = rows * steps + groups * sum(piece_rows(tiles, coefs) for tiles in chunk_tiles)
     result = None
-    for chunk in range(chunks):
-        flows = []
-        for step in range(groups):
-            target = (member + step) % groups
-            start = (chunk * groups + target) * SUB
-            base = lax.dynamic_slice_in_dim(base_flow, start, SUB, 2)
-            moving = lax.dynamic_slice_in_dim(direction[1:], start, SUB, 2)
-            block = jnp.concatenate([base, moving], axis=0)
-            block = block.reshape(4, coefs, SUB, lane_tiles, LANES).transpose(2, 3, 0, 1, 4)
-            block = block.reshape(SUB * lane_tiles, 4 * coefs, LANES)
-            flows.append(block if step == 0 else shifted(block, "freq", step, True))
-        back = friction_call(place, flows, coefs)
-        back = [
-            block if step == 0 else shifted(block, "freq", step, True)
-            for step, block in enumerate(back)
-        ]
+    begin = jnp.int32(0)
+    tile = 0
+    for chunk, tiles in enumerate(chunk_tiles):
+        pieces += through(tile, tiles)
+        tile += groups * tiles
+        if chunk == len(chunk_tiles) - 1:
+            end = jnp.int32(row_blocks)
+            pieces.append(extra.reshape(-1, LANES))
+        elif chunk == len(chunk_tiles) - 2:
+            end = jnp.sum((ends <= tile * LANES).astype(jnp.int32))
+        else:
+            continue
+        start = jnp.minimum(begin, row_blocks - 1)
+        count = jnp.maximum(end - start, 1)
+        first = jnp.stack([start, place[0], count])
         result = finish_call(
-            chunk * groups + sources, scalars, direction, wet_mask, water_depth, drag_factor,
-            edges, slabs, jnp.concatenate(back, axis=0), result,
+            first, offset, table, scalars, arrays, list(pieces), back_rows, result
         )
+        begin = end
     return result
 
 

time: 304 us -> 282 us (0.928)
  Pallas kernels: 53.4 us -> 86.2 us
  waiting for transfers between devices: 135 us -> 109 us
  local copies, waits for them, and re-layouts: 45.5 us -> 30.6 us
  starting transfers between devices: 53.9 us -> 39.3 us
  other arithmetic: 13.8 us -> 3.27 us
  blocking collectives: 0 us -> 8 us
    ppermute x28, waiting for transfers between devices: 135 us -> 109 us  [shifted(): return lax.ppermute(block, axis, pairs)]
    pallas_call x4 -> x9, Pallas kernels: 33.4 us -> 53.2 us  [the longest x4 26.9 us: friction_call(): pl.pallas_call(lambda *refs: friction_kernel(groups, coefs, tiles, *refs)...]
    ppermute x28, starting transfers between devices: 53.9 us -> 39.3 us  [shifted(): return lax.ppermute(block, axis, pairs)]
    pallas_call x4 -> x2, Pallas kernels: 20 us -> 32.9 us  [finish_call(): pl.pallas_call(kernel, out_shape=jax.ShapeDtypeStruct(direction.shape, jn...]
    reshape x16 -> x0, local copies, waits for them, and re-layouts: 11.7 us -> none  [local(): block.reshape(4, coefs, SUB, lane_tiles, LANES).transpose(2, 3, 0, 1, 4)]
    reshape x16 -> x0, other arithmetic: 11.7 us -> none  [local(): block.reshape(4, coefs, SUB, lane_tiles, LANES).transpose(2, 3, 0, 1, 4)]
    pmax x0 -> x1, blocking collectives: none -> 8 us  [local(): largest = lax.pmax(offsets[blocks], ('lat', 'lon'))]
    dynamic_slice x1 -> x0, local copies, waits for them, and re-layouts: 6.36 us -> none  [local(): moving = lax.dynamic_slice_in_dim(direction[1:], start, SUB, 2)]
  transfers between devices with their start and end apart: 28 -> 28, of which waited for: 15 -> 13; matrix products, arithmetic and copies ran while one was open for 14% -> 9% of each run, Pallas kernels for 16% -> 24%
where the time goes in v3:
time: 282 us; the launch traced here: 279 us
  waiting for transfers between devices  109 us (39%)
  Pallas kernels  86.2 us (31%)
  starting transfers between devices  39.3 us (14%)
  local copies, waits for them, and re-layouts  30.6 us (11%)
  blocking collectives  8 us (3%)
  other arithmetic  3.27 us (1%)
    ppermute x28, waiting for transfers between devices, shifted(): return lax.ppermute(block, axis, pairs)  109 us
    ppermute x28, starting transfers between devices, shifted(): return lax.ppermute(block, axis, pairs)  39.3 us
    pallas_call x2, Pallas kernels, finish_call(): pl.pallas_call(kernel, out_shape=jax.ShapeDtypeStruct(direction.shape, jn...  32.9 us
    pallas_call x4, Pallas kernels, friction_call(): pl.pallas_call(lambda *refs: friction_kernel(groups, coefs, tiles, *refs)...  26.9 us
    pallas_call x4, Pallas kernels, pack_call(): pl.pallas_call(lambda *refs: pack_kernel(groups, coefs, tiles, *refs), ou...  25.3 us
    unnamed x75, local copies, waits for them, and re-layouts  11 us
    pmax x1, blocking collectives, local(): largest = lax.pmax(offsets[blocks], ('lat', 'lon'))  8 us
    slice x1, local copies, waits for them, and re-layouts, halo(): height, east, north = (direction[0], direction[1], direction[2])  5.8 us
  transfers between devices with their start and end apart: 28, of which 13 were waited for; matrix products, arithmetic and copies ran while one was open for 9% of the time, Pallas kernels for 24%

profile of v3, /device:TPU:12, one launch (start us, length us, event | category | flops | bytes accessed | tf_op | source)
XLA Modules:
  0.0 279.2 jit_solution(6732650165122005763)
XLA Ops:
  2.0 6.3 %pack.8 = (f32[24,32,128]{2,1,0:T(8,128)S(1)}, f32[24,32,128]{2,1,0:T(8,128)}, f32[24,32,128]{2,1,0:T(8,128)}, f32[24,32,128]{2,1,0:T(8,128)}) custom-call(s32[2]{0:T(128)S(1)} %pad_add_fusion.3.refs_0_, s32[8,128]{1,0:T(8,128)S(1)} %get-tuple-element.355.refs_1_.offset_ref, s32[512,128]{1,0:T(8,128)S(1)} %get-tuple-element.356.refs_2_, ...), custom_call_target="tpu_custom_call" | custom-call | bytes 3145728 | tf_op jit(solution)/shard_map/pack/pallas_call | solution.py:320
  9.1 1.6 collective-permute-start.10
  10.7 1.2 collective-permute-start.11
  12.5 8.0 %pmax.7 = s32[]{:T(128)} all-reduce(s32[]{:T(128)} %bitcast.25), channel_id=1, replica_groups=mesh['freq'=4,'lat'=2,'lon'=4] {'lat','lon'}, use_global_device_ids=true, to_apply=%region_1.2 | all-reduce | flops 1 | bytes 8 | tf_op jit(solution)/shard_map/pmax | solution.py:638
  21.1 1.1 broadcast_in_dim.20
  22.2 1.9 collective-permute-start.12
  24.1 5.8 %fusion.7 = (f32[1,8,128,512]{3,2,1,0:T(8,128)}, f32[1,8,128,512]{3,2,1,0:T(8,128)}, f32[1,8,128,512]{3,2,1,0:T(8,128)}) fusion(f32[3,8,128,512]{3,2,1,0:T(8,128)} %get-tuple-element.443), kind=kLoop, calls=%fused_computation.46 | loop fusion | bytes 12582912 | tf_op jit(solution)/shard_map/slice | solution.py:555
  30.0 4.7 %copy_bitcast_fusion = (f32[8,128,512]{2,0,1:T(8,128)S(1)}, f32[8,128,512]{2,0,1:T(8,128)S(1)}) fusion(f32[1,8,128,512]{3,2,1,0:T(8,128)} %get-tuple-element.273, f32[1,8,128,512]{3,2,1,0:T(8,128)} %get-tuple-element.271), kind=kLoop, calls=%fused_computation.3 | loop fusion | bytes 8388608 | tf_op jit(solution)/shard_map/squeeze | solution.py:555
  34.7 1.3 copy-done.18
  36.7 1.3 collective-permute-start.7
  38.4 1.2 slice.103
  39.7 1.9 slice.106
  42.4 1.2 copy.57
  43.7 2.8 %copy.67 = f32[1,8,128,512]{3,1,2,0:T(8,128)S(1)} copy(f32[1,8,128,512]{3,2,1,0:T(8,128)} %get-tuple-element.272) | data formatting | bytes 4194304
  46.5 1.3 copy-done.17
  48.1 1.0 fusion.5
  49.2 6.3 %pack.9 = (f32[25,32,128]{2,1,0:T(8,128)S(1)}, f32[25,32,128]{2,1,0:T(8,128)}, f32[25,32,128]{2,1,0:T(8,128)}, f32[25,32,128]{2,1,0:T(8,128)}) custom-call(s32[2]{0:T(128)S(1)} %pad_add_fusion.4.refs_0_, s32[8,128]{1,0:T(8,128)S(1)} %get-tuple-element.449, s32[512,128]{1,0:T(8,128)S(1)} %get-tuple-element.445, f32[2,8,128,512]{3,2,1,0:T(8,128)} %get-tuple-element.444, ...), custom_call_target="tpu_custom_call" | custom-call | bytes 3276800 | tf_op jit(solution)/shard_map/pack/pallas_call | solution.py:320
  56.4 4.5 %collective-permute-start.6 = (f32[2,8,1,512]{3,1,0,2:T(8,128)S(1)}, f32[2,8,1,512]{3,1,0,2:T(8,128)S(1)}, u32[]{:S(2)}, u32[]{:S(2)}) collective-permute-start(f32[2,8,1,512]{3,1,0,2:T(8,128)S(1)} %pad_maximum_fusion.2), channel_id=1, source_target_pairs={{0,4},{1,5},{2,6},{3,7},{8,12},{9,13},{10,14},{11,15},{16,20},{17,... | collective-permute-start | bytes 98312 | tf_op jit(solution)/shard_map/ppermute | solution.py:551
  61.4 1.2 collective-permute-done.6
  62.6 3.1 %collective-permute-done.8 = f32[3,8,128]{2,1,0:T(8,128)S(1)} collective-permute-done((f32[3,8,128]{2,1,0:T(8,128)S(1)}, f32[3,8,128]{2,1,0:T(8,128)S(1)}, u32[]{:S(2)}, u32[]{:S(2)}) %collective-permute-start.8) | collective-permute-done | bytes 12320 | tf_op jit(solution)/shard_map/ppermute | solution.py:551
  65.8 7.0 %pack.10 = (f32[26,32,128]{2,1,0:T(8,128)S(1)}, f32[26,32,128]{2,1,0:T(8,128)}, f32[26,32,128]{2,1,0:T(8,128)S(1)}, f32[26,32,128]{2,1,0:T(8,128)S(1)}) custom-call(s32[2]{0:T(128)S(1)} %pad_add_fusion.5.refs_0_, s32[8,128]{1,0:T(8,128)S(1)} %get-tuple-element.449, s32[512,128]{1,0:T(8,128)} %copy-done.15, f32[2,8,128,512]{3,2,1,0:T(8,128)} %get-tuple-element.444, ...), custom_call_target="tpu_custom_call" | custom-call | bytes 3407872 | tf_op jit(solution)/shard_map/pack/pallas_call | solution.py:320
  72.8 2.4 collective-permute-start.17
  76.7 2.0 collective-permute-start.22
  78.7 2.5 collective-permute-start.23
  83.3 5.7 %pack.11 = (f32[22,32,128]{2,1,0:T(8,128)S(1)}, f32[22,32,128]{2,1,0:T(8,128)S(1)}, f32[22,32,128]{2,1,0:T(8,128)S(1)}, f32[22,32,128]{2,1,0:T(8,128)S(1)}) custom-call(s32[2]{0:T(128)S(1)} %pad_add_fusion.6.refs_0_, s32[8,128]{1,0:T(8,128)S(1)} %get-tuple-element.449, s32[512,128]{1,0:T(8,128)} %copy-done.15, f32[2,8,128,512]{3,2,1,0:T(8,128)} %get-tuple-element.444, ...), custom_call_target="tpu_custom_call" | custom-call | bytes 2883584 | tf_op jit(solution)/shard_map/pack/pallas_call | solution.py:320
  89.9 11.7 %collective-permute-done.17.refs_5_ = f32[25,32,128]{2,1,0:T(8,128)} collective-permute-done((f32[25,32,128]{2,1,0:T(8,128)}, f32[25,32,128]{2,1,0:T(8,128)}, u32[]{:S(2)}, u32[]{:S(2)}) %collective-permute-start.17) | collective-permute-done | bytes 409632 | tf_op jit(solution)/shard_map/ppermute | solution.py:551
  101.6 20.5 %collective-permute-done.18.refs_6_ = f32[25,32,128]{2,1,0:T(8,128)} collective-permute-done((f32[25,32,128]{2,1,0:T(8,128)}, f32[25,32,128]{2,1,0:T(8,128)}, u32[]{:S(2)}, u32[]{:S(2)}) %collective-permute-start.18) | collective-permute-done | bytes 409632 | tf_op jit(solution)/shard_map/ppermute | solution.py:551
  122.0 22.2 %collective-permute-done.22.refs_4_ = f32[26,32,128]{2,1,0:T(8,128)S(1)} collective-permute-done((f32[26,32,128]{2,1,0:T(8,128)}, f32[26,32,128]{2,1,0:T(8,128)S(1)}, u32[]{:S(2)}, u32[]{:S(2)}) %collective-permute-start.22) | collective-permute-done | bytes 426016 | tf_op jit(solution)/shard_map/ppermute | solution.py:551
  144.3 7.1 %friction.8 = (f32[408,128]{1,0:T(8,128)S(1)}, f32[408,128]{1,0:T(8,128)S(1)}, f32[408,128]{1,0:T(8,128)S(1)}, f32[408,128]{1,0:T(8,128)S(1)}) custom-call(s32[1]{0:T(128)} %bitcast.2.refs_0_, bf16[4,256,96]{2,1,0:T(8,128)(2,1)S(1)} %copy-done.30, bf16[4,64,256]{2,1,0:T(8,128)(2,1)S(1)} %copy-done.33, f32[24,32,128]{2,1,0:T(8,128)S(1)} %copy-done.10, ...), custom_call_target="tpu_custom_call" | custom-call | flops 1610612736 | bytes 1572864 | tf_op jit(solution)/shard_map/friction/pallas_call | solution.py:135
  151.4 1.8 collective-permute-done.23.refs_5_
  153.9 1.7 collective-permute-done.24.refs_6_
  155.6 1.1 collective-permute-start.14
  156.6 7.6 %friction.9 = (f32[432,128]{1,0:T(8,128)S(1)}, f32[432,128]{1,0:T(8,128)S(1)}, f32[432,128]{1,0:T(8,128)S(1)}, f32[432,128]{1,0:T(8,128)S(1)}) custom-call(s32[1]{0:T(128)} %bitcast.2.refs_0_, bf16[4,256,96]{2,1,0:T(8,128)(2,1)S(1)} %copy-done.30, bf16[4,64,256]{2,1,0:T(8,128)(2,1)S(1)} %copy-done.33, f32[25,32,128]{2,1,0:T(8,128)S(1)} %copy-done.6, ...), custom_call_target="tpu_custom_call" | custom-call | flops 1677721600 | bytes 1638400 | tf_op jit(solution)/shard_map/friction/pallas_call | solution.py:135
  164.3 6.6 %friction.10 = (f32[448,128]{1,0:T(8,128)S(1)}, f32[448,128]{1,0:T(8,128)S(1)}, f32[448,128]{1,0:T(8,128)S(1)}, f32[448,128]{1,0:T(8,128)S(1)}) custom-call(s32[1]{0:T(128)} %bitcast.2.refs_0_, bf16[4,256,96]{2,1,0:T(8,128)(2,1)S(1)} %copy-done.30, bf16[4,64,256]{2,1,0:T(8,128)(2,1)S(1)} %copy-done.33, f32[26,32,128]{2,1,0:T(8,128)S(1)} %get-tuple-element.188.refs_3_, ...), custom_call_target="tpu_custom_call" | custom-call | flops 1744830464 | bytes 1703936 | tf_op jit(solution)/shard_map/friction/pallas_call | solution.py:135
  170.9 2.1 collective-permute-start.15
  173.2 11.5 %collective-permute-done.30.refs_6_ = f32[22,32,128]{2,1,0:T(8,128)S(1)} collective-permute-done((f32[22,32,128]{2,1,0:T(8,128)S(1)}, f32[22,32,128]{2,1,0:T(8,128)S(1)}, u32[]{:S(2)}, u32[]{:S(2)}) %collective-permute-start.30) | collective-permute-done | bytes 360480 | tf_op jit(solution)/shard_map/ppermute | solution.py:551
  184.7 1.0 collective-permute-start.21
  185.7 10.4 %collective-permute-done.14.refs_9_.refs_10_ = f32[408,128]{1,0:T(8,128)S(1)} collective-permute-done((f32[408,128]{1,0:T(8,128)S(1)}, f32[408,128]{1,0:T(8,128)S(1)}, u32[]{:S(2)}, u32[]{:S(2)}) %collective-permute-start.14) | collective-permute-done | bytes 208928 | tf_op jit(solution)/shard_map/ppermute | solution.py:551
  196.3 5.6 %friction.11 = (f32[376,128]{1,0:T(8,128)S(1)}, f32[376,128]{1,0:T(8,128)S(1)}, f32[376,128]{1,0:T(8,128)S(1)}, f32[376,128]{1,0:T(8,128)S(1)}) custom-call(s32[1]{0:T(128)} %bitcast.2.refs_0_, bf16[4,256,96]{2,1,0:T(8,128)(2,1)S(1)} %copy-done.31, bf16[4,64,256]{2,1,0:T(8,128)(2,1)S(1)} %copy-done.34, f32[22,32,128]{2,1,0:T(8,128)S(1)} %get-tuple-element.196.refs_3_, ...), custom_call_target="tpu_custom_call" | custom-call | flops 1476395008 | bytes 1441792 | tf_op jit(solution)/shard_map/friction/pallas_call | solution.py:135
  201.9 4.0 %collective-permute-start.31 = (f32[376,128]{1,0:T(8,128)S(1)}, f32[376,128]{1,0:T(8,128)S(1)}, u32[]{:S(2)}, u32[]{:S(2)}) collective-permute-start(f32[376,128]{1,0:T(8,128)S(1)} %get-tuple-element.201), channel_id=1, source_target_pairs={{0,8},{8,16},{16,24},{24,0},{1,9},{9,17},{17,25},{25,1},{2,10},{10... | collective-permute-start | bytes 577544 | tf_op jit(solution)/shard_map/ppermute | solution.py:551
  206.3 11.5 %collective-permute-start.33 = (f32[376,128]{1,0:T(8,128)S(1)}, f32[376,128]{1,0:T(8,128)S(1)}, u32[]{:S(2)}, u32[]{:S(2)}) collective-permute-start(f32[376,128]{1,0:T(8,128)S(1)} %get-tuple-element.203), channel_id=1, source_target_pairs={{0,24},{8,0},{16,8},{24,16},{1,25},{9,1},{17,9},{25,17},{2,26},{10... | collective-permute-start | bytes 577544 | tf_op jit(solution)/shard_map/ppermute | solution.py:551
  217.8 3.3 %collective-permute-done.21.refs_14_.refs_15_ = f32[432,128]{1,0:T(8,128)S(1)} collective-permute-done((f32[432,128]{1,0:T(8,128)S(1)}, f32[432,128]{1,0:T(8,128)S(1)}, u32[]{:S(2)}, u32[]{:S(2)}) %collective-permute-start.21) | collective-permute-done | bytes 221216 | tf_op jit(solution)/shard_map/ppermute | solution.py:551
  221.1 1.0 collective-permute-start.27
  222.2 19.6 %collective-permute-done.26.refs_17_.refs_18_ = f32[448,128]{1,0:T(8,128)S(1)} collective-permute-done((f32[448,128]{1,0:T(8,128)S(1)}, f32[448,128]{1,0:T(8,128)S(1)}, u32[]{:S(2)}, u32[]{:S(2)}) %collective-permute-start.26) | collective-permute-done | bytes 229408 | tf_op jit(solution)/shard_map/ppermute | solution.py:551
  241.8 2.1 collective-permute-done.27.refs_18_.refs_19_
  243.9 2.1 broadcast_in_dim.9.refs_5_
  246.0 20.7 %finish.2.refs_7_ = f32[3,8,128,512]{3,2,1,0:T(8,128)} custom-call(s32[3]{0:T(128)S(1)} %get-tuple-element.281.first_ref, s32[8,128]{1,0:T(8,128)S(1)} %get-tuple-element.449, s32[8,640]{1,0:T(8,128)S(1)} %copy-done.4, f32[6]{0:T(128)S(1)} %pad_maximum_fusion.6.scalars_ref, f32[3,8,128,512]{3,2,1,0:T(8,128)S(1)} %bitcast.59, s32[128,512]{1,0:T(8,128)S(1)} %copy-done.1, ...), custom_call_target="tpu_custom_call" | custom-call | bytes 9437184 | tf_op jit(solution)/shard_map/finish/pallas_call | solution.py:528
  266.8 12.2 %finish.3 = f32[3,8,128,512]{3,2,1,0:T(8,128)} custom-call(s32[3]{0:T(128)S(1)} %get-tuple-element.280.first_ref, s32[8,128]{1,0:T(8,128)S(1)} %get-tuple-element.449, s32[8,640]{1,0:T(8,128)S(1)} %copy-done.4, f32[6]{0:T(128)S(1)} %pad_maximum_fusion.6.scalars_ref, f32[3,8,128,512]{3,2,1,0:T(8,128)S(1)} %bitcast.59, ...), custom_call_target="tpu_custom_call", output_to_operand_aliasing={{}: (11, {})} | custom-call | bytes 9437184 | tf_op jit(solution)/shard_map/finish/pallas_call | solution.py:528
  (140 shorter events, 12.0 us)
Async XLA Ops:
  2.0 20.2 %copy-start.29 = (bf16[4,256,96]{2,1,0:T(8,128)(2,1)S(1)}, bf16[4,256,96]{2,1,0:T(8,128)(2,1)}, u32[]{:S(2)}) copy-start(bf16[4,256,96]{2,1,0:T(8,128)(2,1)} %constant.95.clone.refs_1_) | copy-start | bytes 589828
  2.0 20.2 %copy-start.32 = (bf16[4,64,256]{2,1,0:T(8,128)(2,1)S(1)}, bf16[4,64,256]{2,1,0:T(8,128)(2,1)}, u32[]{:S(2)}) copy-start(bf16[4,64,256]{2,1,0:T(8,128)(2,1)} %constant.96.clone.refs_2_) | copy-start | bytes 393220
  9.1 66.1 %collective-permute-start.10 = (f32[24,32,128]{2,1,0:T(8,128)}, f32[24,32,128]{2,1,0:T(8,128)S(1)}, u32[]{:S(2)}, u32[]{:S(2)}) collective-permute-start(f32[24,32,128]{2,1,0:T(8,128)} %get-tuple-element.173), channel_id=1, source_target_pairs={{0,8},{8,16},{16,24},{24,0},{1,9},{9,17},{17,25},{25,1},{2,10},{10... | collective-permute-start | bytes 1179656 | tf_op jit(solution)/shard_map/ppermute | solution.py:551
  10.7 65.3 %collective-permute-start.11 = (f32[24,32,128]{2,1,0:T(8,128)}, f32[24,32,128]{2,1,0:T(8,128)S(1)}, u32[]{:S(2)}, u32[]{:S(2)}) collective-permute-start(f32[24,32,128]{2,1,0:T(8,128)} %get-tuple-element.174), channel_id=1, source_target_pairs={{0,16},{8,24},{16,0},{24,8},{1,17},{9,25},{17,1},{25,9},{2,18},{10... | collective-permute-start | bytes 1179656 | tf_op jit(solution)/shard_map/ppermute | solution.py:551
  22.2 27.0 %copy-start.15 = (s32[512,128]{1,0:T(8,128)}, s32[512,128]{1,0:T(8,128)S(1)}, u32[]{:S(2)}) copy-start(s32[512,128]{1,0:T(8,128)S(1)} %get-tuple-element.445) | copy-start | bytes 786436
  22.2 56.5 %collective-permute-start.12 = (f32[24,32,128]{2,1,0:T(8,128)}, f32[24,32,128]{2,1,0:T(8,128)}, u32[]{:S(2)}, u32[]{:S(2)}) collective-permute-start(f32[24,32,128]{2,1,0:T(8,128)} %get-tuple-element.175), channel_id=1, source_target_pairs={{0,24},{8,0},{16,8},{24,16},{1,25},{9,1},{17,9},{25,17},{2,26},{10... | collective-permute-start | bytes 1179656 | tf_op jit(solution)/shard_map/ppermute | solution.py:551
  36.7 24.2 %collective-permute-start.7 = (f32[2,8,1,512]{3,1,0,2:T(8,128)S(1)}, f32[2,8,1,512]{3,1,0,2:T(8,128)S(1)}, u32[]{:S(2)}, u32[]{:S(2)}) collective-permute-start(f32[2,8,1,512]{3,1,0,2:T(8,128)S(1)} %pad_maximum_fusion.1), channel_id=1, source_target_pairs={{4,0},{5,1},{6,2},{7,3},{12,8},{13,9},{14,10},{15,11},{20,16},{21,... | collective-permute-start | bytes 98312 | tf_op jit(solution)/shard_map/ppermute | solution.py:551
  56.4 6.1 %collective-permute-start.6 = (f32[2,8,1,512]{3,1,0,2:T(8,128)S(1)}, f32[2,8,1,512]{3,1,0,2:T(8,128)S(1)}, u32[]{:S(2)}, u32[]{:S(2)}) collective-permute-start(f32[2,8,1,512]{3,1,0,2:T(8,128)S(1)} %pad_maximum_fusion.2), channel_id=1, source_target_pairs={{0,4},{1,5},{2,6},{3,7},{8,12},{9,13},{10,14},{11,15},{16,20},{17,... | collective-permute-start | bytes 98312 | tf_op jit(solution)/shard_map/ppermute | solution.py:551
  61.1 20.1 %collective-permute-start.16 = (f32[25,32,128]{2,1,0:T(8,128)}, f32[25,32,128]{2,1,0:T(8,128)S(1)}, u32[]{:S(2)}, u32[]{:S(2)}) collective-permute-start(f32[25,32,128]{2,1,0:T(8,128)} %get-tuple-element.181), channel_id=1, source_target_pairs={{0,8},{8,16},{16,24},{24,0},{1,9},{9,17},{17,25},{25,1},{2,10},{10... | collective-permute-start | bytes 1228808 | tf_op jit(solution)/shard_map/ppermute | solution.py:551
  62.6 3.1 %collective-permute-start.8 = (f32[3,8,128]{2,1,0:T(8,128)S(1)}, f32[3,8,128]{2,1,0:T(8,128)S(1)}, u32[]{:S(2)}, u32[]{:S(2)}) collective-permute-start(f32[3,8,128]{2,1,0:T(8,128)S(1)} %pad_maximum_fusion.4), channel_id=1, source_target_pairs={{0,1},{1,2},{2,3},{3,0},{4,5},{5,6},{6,7},{7,4},{8,9},{9,10},{10,1... | collective-permute-start | bytes 36872 | tf_op jit(solution)/shard_map/ppermute | solution.py:551
  65.7 7.1 %collective-permute-start.9 = (f32[3,8,128]{2,1,0:T(8,128)S(1)}, f32[3,8,128]{2,1,0:T(8,128)S(1)}, u32[]{:S(2)}, u32[]{:S(2)}) collective-permute-start(f32[3,8,128]{2,1,0:T(8,128)S(1)} %pad_maximum_fusion.5), channel_id=1, source_target_pairs={{0,3},{1,0},{2,1},{3,2},{4,7},{5,4},{6,5},{7,6},{8,11},{9,8},{10,9... | collective-permute-start | bytes 36872 | tf_op jit(solution)/shard_map/ppermute | solution.py:551
  72.8 28.7 %collective-permute-start.17 = (f32[25,32,128]{2,1,0:T(8,128)}, f32[25,32,128]{2,1,0:T(8,128)}, u32[]{:S(2)}, u32[]{:S(2)}) collective-permute-start(f32[25,32,128]{2,1,0:T(8,128)} %get-tuple-element.182), channel_id=1, source_target_pairs={{0,16},{8,24},{16,0},{24,8},{1,17},{9,25},{17,1},{25,9},{2,18},{10... | collective-permute-start | bytes 1228808 | tf_op jit(solution)/shard_map/ppermute | solution.py:551
  76.0 46.1 %collective-permute-start.18 = (f32[25,32,128]{2,1,0:T(8,128)}, f32[25,32,128]{2,1,0:T(8,128)}, u32[]{:S(2)}, u32[]{:S(2)}) collective-permute-start(f32[25,32,128]{2,1,0:T(8,128)} %get-tuple-element.183), channel_id=1, source_target_pairs={{0,24},{8,0},{16,8},{24,16},{1,25},{9,1},{17,9},{25,17},{2,26},{10... | collective-permute-start | bytes 1228808 | tf_op jit(solution)/shard_map/ppermute | solution.py:551
  76.7 67.5 %collective-permute-start.22 = (f32[26,32,128]{2,1,0:T(8,128)}, f32[26,32,128]{2,1,0:T(8,128)S(1)}, u32[]{:S(2)}, u32[]{:S(2)}) collective-permute-start(f32[26,32,128]{2,1,0:T(8,128)} %get-tuple-element.189), channel_id=1, source_target_pairs={{0,8},{8,16},{16,24},{24,0},{1,9},{9,17},{17,25},{25,1},{2,10},{10... | collective-permute-start | bytes 1277960 | tf_op jit(solution)/shard_map/ppermute | solution.py:551
  78.7 74.5 %collective-permute-start.23 = (f32[26,32,128]{2,1,0:T(8,128)S(1)}, f32[26,32,128]{2,1,0:T(8,128)S(1)}, u32[]{:S(2)}, u32[]{:S(2)}) collective-permute-start(f32[26,32,128]{2,1,0:T(8,128)S(1)} %get-tuple-element.190), channel_id=1, source_target_pairs={{0,16},{8,24},{16,0},{24,8},{1,17},{9,25},{17,1},{25,9},{2,18},{10... | collective-permute-start | bytes 1277960 | tf_op jit(solution)/shard_map/ppermute | solution.py:551
  82.0 73.5 %collective-permute-start.24 = (f32[26,32,128]{2,1,0:T(8,128)S(1)}, f32[26,32,128]{2,1,0:T(8,128)S(1)}, u32[]{:S(2)}, u32[]{:S(2)}) collective-permute-start(f32[26,32,128]{2,1,0:T(8,128)S(1)} %get-tuple-element.191), channel_id=1, source_target_pairs={{0,24},{8,0},{16,8},{24,16},{1,25},{9,1},{17,9},{25,17},{2,26},{10... | collective-permute-start | bytes 1277960 | tf_op jit(solution)/shard_map/ppermute | solution.py:551
  83.2 61.0 %copy-start.10 = (f32[24,32,128]{2,1,0:T(8,128)S(1)}, f32[24,32,128]{2,1,0:T(8,128)}, u32[]{:S(2)}) copy-start(f32[24,32,128]{2,1,0:T(8,128)} %copy-done.9) | copy-start | bytes 1179652
  83.2 61.0 %copy-start.12 = (f32[24,32,128]{2,1,0:T(8,128)S(1)}, f32[24,32,128]{2,1,0:T(8,128)}, u32[]{:S(2)}) copy-start(f32[24,32,128]{2,1,0:T(8,128)} %copy-done.11) | copy-start | bytes 1179652
  83.3 61.0 %copy-start.14 = (f32[24,32,128]{2,1,0:T(8,128)S(1)}, f32[24,32,128]{2,1,0:T(8,128)}, u32[]{:S(2)}) copy-start(f32[24,32,128]{2,1,0:T(8,128)} %copy-done.13) | copy-start | bytes 1179652
  83.3 61.0 %copy-start.30 = (bf16[4,256,96]{2,1,0:T(8,128)(2,1)S(1)}, bf16[4,256,96]{2,1,0:T(8,128)(2,1)}, u32[]{:S(2)}) copy-start(bf16[4,256,96]{2,1,0:T(8,128)(2,1)} %constant.95.clone.refs_1_) | copy-start | bytes 589828
  83.3 61.0 %copy-start.33 = (bf16[4,64,256]{2,1,0:T(8,128)(2,1)S(1)}, bf16[4,64,256]{2,1,0:T(8,128)(2,1)}, u32[]{:S(2)}) copy-start(bf16[4,64,256]{2,1,0:T(8,128)(2,1)} %constant.96.clone.refs_2_) | copy-start | bytes 393220
  101.6 69.3 %collective-permute-start.28 = (f32[22,32,128]{2,1,0:T(8,128)S(1)}, f32[22,32,128]{2,1,0:T(8,128)S(1)}, u32[]{:S(2)}, u32[]{:S(2)}) collective-permute-start(f32[22,32,128]{2,1,0:T(8,128)S(1)} %get-tuple-element.197), channel_id=1, source_target_pairs={{0,8},{8,16},{16,24},{24,0},{1,9},{9,17},{17,25},{25,1},{2,10},{10... | collective-permute-start | bytes 1081352 | tf_op jit(solution)/shard_map/ppermute | solution.py:551
  122.0 51.1 %collective-permute-start.29 = (f32[22,32,128]{2,1,0:T(8,128)S(1)}, f32[22,32,128]{2,1,0:T(8,128)S(1)}, u32[]{:S(2)}, u32[]{:S(2)}) collective-permute-start(f32[22,32,128]{2,1,0:T(8,128)S(1)} %get-tuple-element.198), channel_id=1, source_target_pairs={{0,16},{8,24},{16,0},{24,8},{1,17},{9,25},{17,1},{25,9},{2,18},{10... | collective-permute-start | bytes 1081352 | tf_op jit(solution)/shard_map/ppermute | solution.py:551
  144.2 40.5 %collective-permute-start.30 = (f32[22,32,128]{2,1,0:T(8,128)S(1)}, f32[22,32,128]{2,1,0:T(8,128)S(1)}, u32[]{:S(2)}, u32[]{:S(2)}) collective-permute-start(f32[22,32,128]{2,1,0:T(8,128)S(1)} %get-tuple-element.199), channel_id=1, source_target_pairs={{0,24},{8,0},{16,8},{24,16},{1,25},{9,1},{17,9},{25,17},{2,26},{10... | collective-permute-start | bytes 1081352 | tf_op jit(solution)/shard_map/ppermute | solution.py:551
  144.3 12.4 %copy-start.6 = (f32[25,32,128]{2,1,0:T(8,128)S(1)}, f32[25,32,128]{2,1,0:T(8,128)}, u32[]{:S(2)}) copy-start(f32[25,32,128]{2,1,0:T(8,128)} %copy-done.5) | copy-start | bytes 1228804
  144.3 12.4 %copy-start.8 = (f32[25,32,128]{2,1,0:T(8,128)S(1)}, f32[25,32,128]{2,1,0:T(8,128)}, u32[]{:S(2)}) copy-start(f32[25,32,128]{2,1,0:T(8,128)} %copy-done.7) | copy-start | bytes 1228804
  153.2 31.5 %collective-permute-start.13 = (f32[408,128]{1,0:T(8,128)S(1)}, f32[408,128]{1,0:T(8,128)S(1)}, u32[]{:S(2)}, u32[]{:S(2)}) collective-permute-start(f32[408,128]{1,0:T(8,128)S(1)} %get-tuple-element.177), channel_id=1, source_target_pairs={{0,8},{8,16},{16,24},{24,0},{1,9},{9,17},{17,25},{25,1},{2,10},{10... | collective-permute-start | bytes 626696 | tf_op jit(solution)/shard_map/ppermute | solution.py:551
  155.6 40.6 %collective-permute-start.14 = (f32[408,128]{1,0:T(8,128)S(1)}, f32[408,128]{1,0:T(8,128)S(1)}, u32[]{:S(2)}, u32[]{:S(2)}) collective-permute-start(f32[408,128]{1,0:T(8,128)S(1)} %get-tuple-element.178), channel_id=1, source_target_pairs={{0,16},{8,24},{16,0},{24,8},{1,17},{9,25},{17,1},{25,9},{2,18},{10... | collective-permute-start | bytes 626696 | tf_op jit(solution)/shard_map/ppermute | solution.py:551
  164.3 31.9 %copy-start.31 = (bf16[4,256,96]{2,1,0:T(8,128)(2,1)S(1)}, bf16[4,256,96]{2,1,0:T(8,128)(2,1)}, u32[]{:S(2)}) copy-start(bf16[4,256,96]{2,1,0:T(8,128)(2,1)} %constant.95.clone.refs_1_) | copy-start | bytes 589828
  164.3 31.9 %copy-start.34 = (bf16[4,64,256]{2,1,0:T(8,128)(2,1)S(1)}, bf16[4,64,256]{2,1,0:T(8,128)(2,1)}, u32[]{:S(2)}) copy-start(bf16[4,64,256]{2,1,0:T(8,128)(2,1)} %constant.96.clone.refs_2_) | copy-start | bytes 393220
  164.3 81.7 %slice-start = ((s8[6291456]{0:T(1024)(128)(4,1)}), s8[2097152]{0:T(1024)(128)(4,1)S(1)}, s32[]{:S(2)}) async-start(s8[6291456]{0:T(1024)(128)(4,1)} %bitcast.58), calls=%async_computation | async-start | bytes 4194304
  170.9 30.9 %collective-permute-start.15 = (f32[408,128]{1,0:T(8,128)S(1)}, f32[408,128]{1,0:T(8,128)S(1)}, u32[]{:S(2)}, u32[]{:S(2)}) collective-permute-start(f32[408,128]{1,0:T(8,128)S(1)} %get-tuple-element.179), channel_id=1, source_target_pairs={{0,24},{8,0},{16,8},{24,16},{1,25},{9,1},{17,9},{25,17},{2,26},{10... | collective-permute-start | bytes 626696 | tf_op jit(solution)/shard_map/ppermute | solution.py:551
  173.2 32.7 %collective-permute-start.19 = (f32[432,128]{1,0:T(8,128)S(1)}, f32[432,128]{1,0:T(8,128)S(1)}, u32[]{:S(2)}, u32[]{:S(2)}) collective-permute-start(f32[432,128]{1,0:T(8,128)S(1)} %get-tuple-element.185), channel_id=1, source_target_pairs={{0,8},{8,16},{16,24},{24,0},{1,9},{9,17},{17,25},{25,1},{2,10},{10... | collective-permute-start | bytes 663560 | tf_op jit(solution)/shard_map/ppermute | solution.py:551
  184.7 21.6 %collective-permute-start.20 = (f32[432,128]{1,0:T(8,128)S(1)}, f32[432,128]{1,0:T(8,128)S(1)}, u32[]{:S(2)}, u32[]{:S(2)}) collective-permute-start(f32[432,128]{1,0:T(8,128)S(1)} %get-tuple-element.186), channel_id=1, source_target_pairs={{0,16},{8,24},{16,0},{24,8},{1,17},{9,25},{17,1},{25,9},{2,18},{10... | collective-permute-start | bytes 663560 | tf_op jit(solution)/shard_map/ppermute | solution.py:551
  184.7 36.3 %collective-permute-start.21 = (f32[432,128]{1,0:T(8,128)S(1)}, f32[432,128]{1,0:T(8,128)S(1)}, u32[]{:S(2)}, u32[]{:S(2)}) collective-permute-start(f32[432,128]{1,0:T(8,128)S(1)} %get-tuple-element.187), channel_id=1, source_target_pairs={{0,24},{8,0},{16,8},{24,16},{1,25},{9,1},{17,9},{25,17},{2,26},{10... | collective-permute-start | bytes 663560 | tf_op jit(solution)/shard_map/ppermute | solution.py:551
  196.1 24.9 %collective-permute-start.25 = (f32[448,128]{1,0:T(8,128)S(1)}, f32[448,128]{1,0:T(8,128)S(1)}, u32[]{:S(2)}, u32[]{:S(2)}) collective-permute-start(f32[448,128]{1,0:T(8,128)S(1)} %get-tuple-element.193), channel_id=1, source_target_pairs={{0,8},{8,16},{16,24},{24,0},{1,9},{9,17},{17,25},{25,1},{2,10},{10... | collective-permute-start | bytes 688136 | tf_op jit(solution)/shard_map/ppermute | solution.py:551
  196.2 25.9 %copy-start.25 = (f32[1,8,16,512]{3,1,0,2:T(8,128)S(1)}, f32[1,8,16,512]{3,1,0,2:T(8,128)}, u32[]{:S(2)}) copy-start(f32[1,8,16,512]{3,1,0,2:T(8,128)} %copy-done.24) | copy-start | bytes 786436
  196.2 25.9 %copy-start.27 = (f32[1,8,16,512]{3,1,0,2:T(8,128)S(1)}, f32[1,8,16,512]{3,1,0,2:T(8,128)}, u32[]{:S(2)}) copy-start(f32[1,8,16,512]{3,1,0,2:T(8,128)} %copy-done.26) | copy-start | bytes 786436
  196.2 25.8 %copy-start.28 = (f32[2,8,15,512]{3,1,0,2:T(8,128)S(1)}, f32[2,8,15,512]{3,1,0,2:T(8,128)}, u32[]{:S(2)}) copy-start(f32[2,8,15,512]{3,1,0,2:T(8,128)} %fusion.4) | copy-start | bytes 1474564
  196.2 49.8 %slice-start.1 = ((s8[6291456]{0:T(1024)(128)(4,1)}), s8[4194304]{0:T(1024)(128)(4,1)S(1)}, s32[]{:S(2)}) async-start(s8[6291456]{0:T(1024)(128)(4,1)} %bitcast.58), calls=%async_computation.1 | async-start | bytes 8388608
  201.9 64.9 %collective-permute-start.31 = (f32[376,128]{1,0:T(8,128)S(1)}, f32[376,128]{1,0:T(8,128)S(1)}, u32[]{:S(2)}, u32[]{:S(2)}) collective-permute-start(f32[376,128]{1,0:T(8,128)S(1)} %get-tuple-element.201), channel_id=1, source_target_pairs={{0,8},{8,16},{16,24},{24,0},{1,9},{9,17},{17,25},{25,1},{2,10},{10... | collective-permute-start | bytes 577544 | tf_op jit(solution)/shard_map/ppermute | solution.py:551
  205.8 60.9 %collective-permute-start.32 = (f32[376,128]{1,0:T(8,128)S(1)}, f32[376,128]{1,0:T(8,128)S(1)}, u32[]{:S(2)}, u32[]{:S(2)}) collective-permute-start(f32[376,128]{1,0:T(8,128)S(1)} %get-tuple-element.202), channel_id=1, source_target_pairs={{0,16},{8,24},{16,0},{24,8},{1,17},{9,25},{17,1},{25,9},{2,18},{10... | collective-permute-start | bytes 577544 | tf_op jit(solution)/shard_map/ppermute | solution.py:551
  206.3 60.5 %collective-permute-start.33 = (f32[376,128]{1,0:T(8,128)S(1)}, f32[376,128]{1,0:T(8,128)S(1)}, u32[]{:S(2)}, u32[]{:S(2)}) collective-permute-start(f32[376,128]{1,0:T(8,128)S(1)} %get-tuple-element.203), channel_id=1, source_target_pairs={{0,24},{8,0},{16,8},{24,16},{1,25},{9,1},{17,9},{25,17},{2,26},{10... | collective-permute-start | bytes 577544 | tf_op jit(solution)/shard_map/ppermute | solution.py:551
  221.1 20.8 %collective-permute-start.26 = (f32[448,128]{1,0:T(8,128)S(1)}, f32[448,128]{1,0:T(8,128)S(1)}, u32[]{:S(2)}, u32[]{:S(2)}) collective-permute-start(f32[448,128]{1,0:T(8,128)S(1)} %get-tuple-element.194), channel_id=1, source_target_pairs={{0,16},{8,24},{16,0},{24,8},{1,17},{9,25},{17,1},{25,9},{2,18},{10... | collective-permute-start | bytes 688136 | tf_op jit(solution)/shard_map/ppermute | solution.py:551
  221.1 22.8 %collective-permute-start.27 = (f32[448,128]{1,0:T(8,128)S(1)}, f32[448,128]{1,0:T(8,128)S(1)}, u32[]{:S(2)}, u32[]{:S(2)}) collective-permute-start(f32[448,128]{1,0:T(8,128)S(1)} %get-tuple-element.195), channel_id=1, source_target_pairs={{0,24},{8,0},{16,8},{24,16},{1,25},{9,1},{17,9},{25,17},{2,26},{10... | collective-permute-start | bytes 688136 | tf_op jit(solution)/shard_map/ppermute | solution.py:551
  222.2 23.8 %copy-start.3 = (f32[128,512]{1,0:T(8,128)S(1)}, f32[128,512]{1,0:T(8,128)}, u32[]{:S(2)}) copy-start(f32[128,512]{1,0:T(8,128)} %refs_3_.11) | copy-start | bytes 786436
  222.2 23.8 %copy-start.4 = (s32[8,640]{1,0:T(8,128)S(1)}, s32[8,640]{1,0:T(8,128)}, u32[]{:S(2)}) copy-start(s32[8,640]{1,0:T(8,128)} %constant.94.clone.table_ref) | copy-start | bytes 61444
  246.0 20.7 %copy-start.16 = (f32[4,544,128]{2,1,0:T(8,128)S(1)}, f32[4,544,128]{2,1,0:T(8,128)}, u32[]{:S(2)}) copy-start(f32[4,544,128]{2,1,0:T(8,128)} %get-tuple-element.204) | copy-start | bytes 3342340
  (17 other events, 63.4 us)

commit v4 on v3

--- a/solution.py
+++ b/solution.py
@@ -19,7 +19,7 @@
 OMEGA_STEP = 0.25
 SPEED_SOFT = 0.01
 VMEM_BYTES = 48 * 1024 * 1024
-CHUNK_SHARES = (24, 25, 26, 22)
+CHUNK_SHARES = (14, 50, 33)
 SHARE_UNITS = 128
 LOOP_TILES = 8
 
@@ -42,7 +42,8 @@
 
 
 def friction_kernel(groups, coefs, tiles, place_ref, synth_ref, analyse_ref, *refs):
-    flow_refs, out_refs = refs[:groups], refs[groups:]
+    flow_refs, out_refs, token_ref = refs[:groups], refs[groups:-1], refs[-1]
+    token_ref[...] = jnp.zeros_like(token_ref)
     columns = 2 * NCON
 
     def block(tile, count):
@@ -130,11 +131,13 @@
             pl.BlockSpec((1,) + analyse.shape[1:], lambda i, place: (place[0], 0, 0)),
         ]
         + [pl.BlockSpec(flows[0].shape, lambda i, place: (0, 0, 0))] * groups,
-        out_specs=[pl.BlockSpec(out_shape, lambda i, place: (0, 0))] * groups,
+        out_specs=[pl.BlockSpec(out_shape, lambda i, place: (0, 0))] * groups
+        + [pl.BlockSpec((SUB, LANES), lambda i, place: (0, 0))],
     )
     return pl.pallas_call(
         lambda *refs: friction_kernel(groups, coefs, tiles, *refs),
-        out_shape=[jax.ShapeDtypeStruct(out_shape, jnp.float32)] * groups,
+        out_shape=[jax.ShapeDtypeStruct(out_shape, jnp.float32)] * groups
+        + [jax.ShapeDtypeStruct((SUB, LANES), jnp.int32)],
         grid_spec=grid_spec,
         compiler_params=pltpu.CompilerParams(vmem_limit_bytes=VMEM_BYTES),
         cost_estimate=pl.CostEstimate(
@@ -206,7 +209,8 @@
 
 def pack_kernel(groups, coefs, tiles, params_ref, offset_ref, index_ref, base_ref, step_ref, *refs):
     out_refs = refs[:groups]
-    held, stage, in_sem, out_sem = refs[groups:]
+    token_ref, held, stage, in_sem, out_sem = refs[groups:]
+    token_ref[...] = jnp.zeros_like(token_ref)
     columns = held.shape[-1]
     lane_tiles = columns // LANES
     per_block = SUB * lane_tiles
@@ -309,7 +313,7 @@
         num_scalar_prefetch=2,
         grid=(1,),
         in_specs=[pl.BlockSpec(index.shape, lambda i, p, o: (0, 0)), anywhere, anywhere],
-        out_specs=[anywhere] * groups,
+        out_specs=[anywhere] * groups + [pl.BlockSpec((SUB, LANES), lambda i, p, o: (0, 0))],
         scratch_shapes=[
             pltpu.VMEM((2, 4, coefs, SUB, columns), jnp.float32),
             pltpu.VMEM((groups * tiles + 2, 4 * coefs, LANES), jnp.float32),
@@ -319,7 +323,8 @@
     )
     return pl.pallas_call(
         lambda *refs: pack_kernel(groups, coefs, tiles, *refs),
-        out_shape=[jax.ShapeDtypeStruct(shape, jnp.float32)] * groups,
+        out_shape=[jax.ShapeDtypeStruct(shape, jnp.float32)] * groups
+        + [jax.ShapeDtypeStruct((SUB, LANES), jnp.int32)],
         grid_spec=grid_spec,
         compiler_params=pltpu.CompilerParams(vmem_limit_bytes=VMEM_BYTES),
         cost_estimate=pl.CostEstimate(
@@ -329,32 +334,152 @@
     )(params, offset, index, base_flow, direction)
 
 
+def prepare_kernel(coefs, scalars_ref, *refs):
+    (here_ref, prev_ref, next_ref, wet_ref, wet_prev_ref, wet_next_ref, depth_ref, depth_prev_ref,
+     above_ref, below_ref, slab_ref, out_ref) = refs
+    columns = here_ref.shape[-1]
+    row_block = pl.program_id(0)
+    at_top = row_block == 0
+    at_bottom = row_block == pl.num_programs(0) - 1
+    wet = wet_ref[...].astype(jnp.float32)
+    wet_prev = wet_prev_ref[SUB - 1 :, :].astype(jnp.float32)
+    wet_next = wet_next_ref[:1, :].astype(jnp.float32)
+    depth = depth_ref[...]
+    depth_prev = depth_prev_ref[SUB - 1 :, :]
+    lane = lax.broadcasted_iota(jnp.int32, (SUB, columns), 1)
+    sub = lax.broadcasted_iota(jnp.int32, (SUB, columns), 0)
+    row = (row_block * SUB + sub).astype(jnp.float32)
+    rotation = 0.5 + (row + scalars_ref[0] + 0.5) * scalars_ref[1]
+
+    def wide(slab):
+        return jnp.concatenate([slab] * (columns // LANES), axis=1)
+
+    def west(value, slab):
+        return jnp.where(lane == 0, wide(slab), pltpu.roll(value, 1, 1))
+
+    def east_of(value, slab):
+        return jnp.where(lane == columns - 1, wide(slab), pltpu.roll(value, columns - 1, 1))
+
+    def above(value, edge):
+        return jnp.where(sub == 0, edge, pltpu.roll(value, 1, 0))
+
+    def below(value, edge):
+        return jnp.where(sub == SUB - 1, edge, pltpu.roll(value, SUB - 1, 0))
+
+    for k in range(coefs // 2):
+        angular = scalars_ref[2 + k]
+        inverse_angular = 1.0 / (angular + jnp.zeros((SUB, columns), jnp.float32))
+        planes = [
+            [here_ref[p, 2 * k + part] * wet for p in range(3)] for part in range(2)
+        ]
+        for part in range(2):
+            c = 2 * k + part
+            height, east, north = planes[part]
+            other = planes[1 - part]
+            signed = angular if part == 0 else -angular
+            east_flux = depth * east
+            north_flux = depth * north
+            north_edge = prev_ref[0, c, SUB - 1 :, :] * wet_prev
+            flux_edge = jnp.where(at_top, above_ref[1, c : c + 1], north_edge * depth_prev)
+            north_edge = jnp.where(at_top, above_ref[0, c : c + 1], north_edge)
+            height_edge = jnp.where(
+                at_bottom, below_ref[0, c : c + 1], next_ref[0, c, :1, :] * wet_next
+            )
+            east_edge = jnp.where(
+                at_bottom, below_ref[1, c : c + 1], next_ref[1, c, :1, :] * wet_next
+            )
+            north_up = above(north, north_edge)
+            east_down = below(east, east_edge)
+            res_height = (
+                signed * other[0]
+                + east_flux
+                - west(east_flux, slab_ref[2, c])
+                + north_flux
+                - above(north_flux, flux_edge)
+            )
+            north_mean = 0.25 * (
+                north
+                + east_of(north, slab_ref[4, c])
+                + north_up
+                + east_of(north_up, slab_ref[5, c])
+            )
+            east_mean = 0.25 * (
+                east
+                + west(east, slab_ref[0, c])
+                + east_down
+                + west(east_down, slab_ref[1, c])
+            )
+            res_east = (
+                signed * other[1]
+                + LINEAR_DRAG * east
+                - rotation * north_mean
+                + GRAVITY * (east_of(height, slab_ref[3, c]) - height)
+            )
+            res_north = (
+                signed * other[2]
+                + LINEAR_DRAG * north
+                + rotation * east_mean
+                + GRAVITY * (below(height, height_edge) - height)
+            )
+            if part == 0:
+                out_ref[0, c + 1] = res_height * wet * inverse_angular
+            else:
+                out_ref[0, c - 1] = -res_height * wet * inverse_angular
+            out_ref[1, c] = res_east * wet
+            out_ref[2, c] = res_north * wet
+
+
+def prepare_call(scalars, direction, wet_mask, depth, above, below, slabs):
+    _, coefs, rows, columns = direction.shape
+    last = rows // SUB - 1
+
+    def before(i):
+        return jnp.maximum(i - 1, 0)
+
+    def after(i):
+        return jnp.minimum(i + 1, last)
+
+    planes = pl.BlockSpec((3, coefs, SUB, columns), lambda i: (0, 0, i, 0))
+    flat = (SUB, columns)
+    edge = pl.BlockSpec((2, coefs, columns), lambda i: (0, 0, 0))
+    return pl.pallas_call(
+        lambda *refs: prepare_kernel(coefs, *refs),
+        out_shape=jax.ShapeDtypeStruct(direction.shape, jnp.float32),
+        grid=(rows // SUB,),
+        in_specs=[
+            pl.BlockSpec(memory_space=pltpu.SMEM),
+            planes,
+            pl.BlockSpec((1, coefs, SUB, columns), lambda i: (2, 0, before(i), 0)),
+            pl.BlockSpec((2, coefs, SUB, columns), lambda i: (0, 0, after(i), 0)),
+            pl.BlockSpec(flat, lambda i: (i, 0)),
+            pl.BlockSpec(flat, lambda i: (before(i), 0)),
+            pl.BlockSpec(flat, lambda i: (after(i), 0)),
+            pl.BlockSpec(flat, lambda i: (i, 0)),
+            pl.BlockSpec(flat, lambda i: (before(i), 0)),
+            edge,
+            edge,
+            pl.BlockSpec((6, coefs, SUB, LANES), lambda i: (0, 0, i, 0)),
+        ],
+        out_specs=planes,
+        compiler_params=pltpu.CompilerParams(vmem_limit_bytes=VMEM_BYTES),
+        cost_estimate=pl.CostEstimate(
+            flops=0, bytes_accessed=rows * columns * coefs * 48, transcendentals=0
+        ),
+        name="prepare",
+    )(
+        scalars, direction, direction, direction, wet_mask, wet_mask, wet_mask, depth, depth,
+        above, below, slabs,
+    )
+
+
 def finish_kernel(coefs, lane_tiles, row_block, first_ref, offset_ref, table_ref, scalars_ref, back, refs):
-    (direction_ref, wet_ref, depth_ref, drag_ref, edge_ref, slab_ref, cell_ref, out_ref) = refs
+    wet_ref, drag_ref, cell_ref, east_ref, north_ref, east_out, north_out = refs
     columns = lane_tiles * LANES
     wet = wet_ref[...].astype(jnp.float32)
-    depth = depth_ref[...]
     drag = drag_ref[...]
-    lane = lax.broadcasted_iota(jnp.int32, (SUB, columns), 1)
     sub = lax.broadcasted_iota(jnp.int32, (SUB, columns), 0)
-    block = row_block * SUB
-    row = (block + sub).astype(jnp.float32)
+    row = (row_block * SUB + sub).astype(jnp.float32)
     rotation = 0.5 + (row + scalars_ref[0] + 0.5) * scalars_ref[1]
-
-    def wide(slab):
-        return jnp.concatenate([slab] * lane_tiles, axis=1)
-
-    def west(value, slab):
-        return jnp.where(lane == 0, wide(slab), pltpu.roll(value, 1, 1))
-
-    def east_of(value, slab):
-        return jnp.where(lane == columns - 1, wide(slab), pltpu.roll(value, columns - 1, 1))
-
-    def above(value, edge):
-        return jnp.where(sub == 0, edge, pltpu.roll(value, 1, 0))
-
-    def below(value, edge):
-        return jnp.where(sub == SUB - 1, edge, pltpu.roll(value, SUB - 1, 0))
 
     def gathered(here, after, index, over):
         first = jnp.take_along_axis(here, index, axis=1, mode="promise_in_bounds")
@@ -396,105 +521,38 @@
     ]
     speed = jnp.where(is_wet, jnp.concatenate(speed, axis=1), 0.0)
     real_rate = drag * speed + LINEAR_DRAG
-
     for k in range(coefs // 2):
         angular = scalars_ref[2 + k]
-        residual = []
-        planes = []
-        for part in range(2):
-            c = 2 * k + part
-            planes.append([direction_ref[p, c] * wet for p in range(3)])
-        for part in range(2):
-            c = 2 * k + part
-            height, east, north = planes[part]
-            other = planes[1 - part]
-            signed = angular if part == 0 else -angular
-            east_flux = depth * east
-            north_flux = depth * north
-            north_up = above(north, edge_ref[0, 0, c : c + 1])
-            flux_up = above(north_flux, edge_ref[0, 1, c : c + 1])
-            height_down = below(height, edge_ref[0, 2, c : c + 1])
-            east_down = below(east, edge_ref[0, 3, c : c + 1])
-            res_height = (
-                signed * other[0]
-                + east_flux
-                - west(east_flux, slab_ref[2, c])
-                + north_flux
-                - flux_up
-            )
-            north_mean = 0.25 * (
-                north
-                + east_of(north, slab_ref[4, c])
-                + north_up
-                + east_of(north_up, slab_ref[5, c])
-            )
-            east_mean = 0.25 * (
-                east
-                + west(east, slab_ref[0, c])
-                + east_down
-                + west(east_down, slab_ref[1, c])
-            )
-            res_east = (
-                signed * other[1]
-                + LINEAR_DRAG * east
-                - rotation * north_mean
-                + GRAVITY * (east_of(height, slab_ref[3, c]) - height)
-            )
-            res_north = (
-                signed * other[2]
-                + LINEAR_DRAG * north
-                + rotation * east_mean
-                + GRAVITY * (height_down - height)
-            )
-            residual.append(
-                (
-                    res_height * wet,
-                    (res_east + friction[c]) * wet,
-                    (res_north + friction[coefs + c]) * wet,
-                )
-            )
-        cos_part, sin_part = residual
-        inverse_angular = 1.0 / (angular + jnp.zeros((SUB, columns), jnp.float32))
-        out_ref[0, 2 * k] = -sin_part[0] * inverse_angular
-        out_ref[0, 2 * k + 1] = cos_part[0] * inverse_angular
+        cos_at, sin_at = 2 * k, 2 * k + 1
         det_real = real_rate * real_rate - angular * angular + rotation * rotation
         det_imag = 2.0 * real_rate * angular
         inverse_norm = 1.0 / (det_real * det_real + det_imag * det_imag)
         inv_real = det_real * inverse_norm
         inv_imag = -det_imag * inverse_norm
-        east_re, north_re = cos_part[1], cos_part[2]
-        east_im, north_im = -sin_part[1], -sin_part[2]
+        east_re = east_ref[0, cos_at] + friction[cos_at]
+        east_im = -(east_ref[0, sin_at] + friction[sin_at])
+        north_re = north_ref[0, cos_at] + friction[coefs + cos_at]
+        north_im = -(north_ref[0, sin_at] + friction[coefs + sin_at])
         num_east_re = real_rate * east_re - angular * east_im + rotation * north_re
         num_east_im = real_rate * east_im + angular * east_re + rotation * north_im
         num_north_re = -rotation * east_re + real_rate * north_re - angular * north_im
         num_north_im = -rotation * east_im + real_rate * north_im + angular * north_re
-        out_ref[1, 2 * k] = num_east_re * inv_real - num_east_im * inv_imag
-        out_ref[1, 2 * k + 1] = -(num_east_re * inv_imag + num_east_im * inv_real)
-        out_ref[2, 2 * k] = num_north_re * inv_real - num_north_im * inv_imag
-        out_ref[2, 2 * k + 1] = -(num_north_re * inv_imag + num_north_im * inv_real)
+        east_out[0, cos_at] = num_east_re * inv_real - num_east_im * inv_imag
+        east_out[0, sin_at] = -(num_east_re * inv_imag + num_east_im * inv_real)
+        north_out[0, cos_at] = num_north_re * inv_real - num_north_im * inv_imag
+        north_out[0, sin_at] = -(num_north_re * inv_imag + num_north_im * inv_real)
 
 
 def finish_call(first, offset, table, scalars, arrays, pieces, rows, result):
-    direction, columns = arrays[0], arrays[0].shape[3]
-    coefs = direction.shape[1]
+    _, coefs, _, columns = result.shape
     lane_tiles = columns // LANES
-    shares = 1 if result is not None else 0
 
     def kernel(first_ref, offset_ref, table_ref, scalars_ref, *refs):
-        array_refs = refs[:7]
-        piece_refs = refs[7 + shares : -3]
+        array_refs = refs[:3]
+        piece_refs = refs[4:-3]
         out_ref, back, sem = refs[-3:]
         first = first_ref[0]
-        copies = []
-        at = 0
-        for n, piece in enumerate(piece_refs):
-            rows = piece.shape[0]
-            copies.append(pltpu.make_async_copy(piece, back.at[pl.ds(at, rows)], sem.at[n]))
-            at += rows
-        for copy in copies:
-            copy.start()
-        for copy in copies:
-            copy.wait()
+        count = first_ref[2]
 
         def body(*block_refs):
             finish_kernel(
@@ -502,39 +560,44 @@
                 scalars_ref, back, block_refs,
             )
 
-        flat = pl.BlockSpec((SUB, columns), lambda i: (first + i, 0))
-        planes = pl.BlockSpec((3, coefs, SUB, columns), lambda i: (0, 0, first + i, 0))
-        pltpu.emit_pipeline(
-            body,
-            grid=(first_ref[2],),
-            in_specs=[
-                planes,
-                flat,
-                flat,
-                flat,
-                pl.BlockSpec((1, 4, coefs, columns), lambda i: (first + i, 0, 0, 0)),
-                pl.BlockSpec((6, coefs, SUB, LANES), lambda i: (0, 0, first + i, 0)),
-                pl.BlockSpec((SUB * lane_tiles, LANES), lambda i: (first + i, 0)),
-            ],
-            out_specs=[planes],
-        )(*array_refs, out_ref)
+        @pl.when(count > 0)
+        def _():
+            copies = []
+            at = 0
+            for n, piece in enumerate(piece_refs):
+                rows = piece.shape[0]
+                copies.append(
+                    pltpu.make_async_copy(piece, back.at[pl.ds(at, rows)], sem.at[n])
+                )
+                at += rows
+            for copy in copies:
+                copy.start()
+            for copy in copies:
+                copy.wait()
+            flat = pl.BlockSpec((SUB, columns), lambda i: (first + i, 0))
+            east = pl.BlockSpec((1, coefs, SUB, columns), lambda i: (1, 0, first + i, 0))
+            north = pl.BlockSpec((1, coefs, SUB, columns), lambda i: (2, 0, first + i, 0))
+            cells = pl.BlockSpec((SUB * lane_tiles, LANES), lambda i: (first + i, 0))
+            pltpu.emit_pipeline(
+                body,
+                grid=(count,),
+                in_specs=[flat, flat, cells, east, north],
+                out_specs=[east, north],
+            )(*array_refs, out_ref, out_ref, out_ref, out_ref)
 
     anywhere = pl.BlockSpec(memory_space=pl.ANY)
     scalar = pl.BlockSpec(memory_space=pltpu.SMEM)
-    operands = [first, offset, table, scalars] + list(arrays)
-    if shares:
-        operands.append(result)
-    operands += pieces
+    operands = [first, offset, table, scalars] + list(arrays) + [result] + pieces
     return pl.pallas_call(
         kernel,
-        out_shape=jax.ShapeDtypeStruct(direction.shape, jnp.float32),
-        in_specs=[scalar] * 4 + [anywhere] * (7 + shares + len(pieces)),
+        out_shape=jax.ShapeDtypeStruct(result.shape, jnp.float32),
+        in_specs=[scalar] * 4 + [anywhere] * (4 + len(pieces)),
         out_specs=anywhere,
         scratch_shapes=[
             pltpu.VMEM((rows, LANES), jnp.float32),
             pltpu.SemaphoreType.DMA((len(pieces),)),
         ],
-        input_output_aliases={11: 0} if shares else {},
+        input_output_aliases={7: 0},
         compiler_params=pltpu.CompilerParams(vmem_limit_bytes=VMEM_BYTES),
         cost_estimate=pl.CostEstimate(
             flops=0, bytes_accessed=8 * SUB * columns * coefs * 36, transcendentals=0
@@ -553,28 +616,20 @@
 
 def halo(direction, wet, depth):
     height, east, north = direction[0], direction[1], direction[2]
-    rows = direction.shape[2]
-    last = north[:, SUB - 1 :: SUB] * wet[SUB - 1 :: SUB]
-    up = jnp.stack([last, last * depth[SUB - 1 :: SUB]])
-    first = wet[::SUB]
-    down = jnp.stack([height[:, ::SUB] * first, east[:, ::SUB] * first])
-    from_above = shifted(up[:, :, -1:], "lat", 1, False)
-    from_below = shifted(down[:, :, :1], "lat", -1, False)
-    up = jnp.concatenate([from_above, up[:, :, :-1]], axis=2)
-    down = jnp.concatenate([down[:, :, 1:], from_below], axis=2)
-    edges = jnp.moveaxis(jnp.concatenate([up, down], axis=0), 2, 0)
-    wet_last = wet[:, -1]
-    east_col = east[:, :, -1] * wet_last
-    east_below = jnp.concatenate([east_col[:, 1:], from_below[1, :, :, -1]], axis=1)
+    last = north[:, -1] * wet[-1]
+    above = shifted(jnp.stack([last, last * depth[-1]]), "lat", 1, False)
+    below = shifted(direction[:2, :, 0] * wet[0], "lat", -1, False)
+    east_col = east[:, :, -1] * wet[:, -1]
+    east_below = jnp.concatenate([east_col[:, 1:], below[1, :, -1:]], axis=1)
     north_col = north[:, :, 0] * wet[:, 0]
-    north_above = jnp.concatenate([from_above[0, :, :, 0], north_col[:, :-1]], axis=1)
+    north_above = jnp.concatenate([above[0, :, :1], north_col[:, :-1]], axis=1)
     to_right = jnp.stack([east_col, east_below, east_col * depth[:, -1]])
     to_left = jnp.stack([height[:, :, 0] * wet[:, 0], north_col, north_above])
     cols = jnp.concatenate(
         [shifted(to_right, "lon", 1, True), shifted(to_left, "lon", -1, True)], axis=0
     )
     slabs = jnp.broadcast_to(cols[:, :, :, None], cols.shape + (LANES,))
-    return edges, slabs
+    return above, below, slabs
 
 
 def spread_out(blocks):
@@ -609,7 +664,6 @@
     lat_place = lax.axis_index("lat")
     total_rows = tile_rows * lax.axis_size("lat")
     lane_tiles = tile_cols // LANES
-    wet = wet_mask.astype(jnp.float32)
     angular = OMEGA_STEP * (
         member * (coefs // 2) + jnp.arange(coefs // 2, dtype=jnp.int32) + 1
     ).astype(jnp.float32)
@@ -617,7 +671,6 @@
     scalars = jnp.concatenate(
         [jnp.stack([row_start, jnp.float32(1.0 / total_rows)]), angular]
     )
-    edges, slabs = halo(direction, wet, water_depth)
     place = jnp.reshape(member, (1,)).astype(jnp.int32)
     blocks = tile_rows * lane_tiles
     row_blocks = tile_rows // SUB
@@ -629,19 +682,43 @@
     offsets = offset.reshape(-1)
     ends = offsets[SUB * lane_tiles : blocks + 1 : SUB * lane_tiles]
 
-    def through(first_tile, tiles):
-        params = jnp.stack([place[0], jnp.asarray(first_tile, jnp.int32)])
-        flows = pack_call(params, offset, index, base_flow, direction, groups, tiles)
-        back = friction_call(place, spread_out(flows), coefs)
-        return spread_out(back)
-
-    largest = lax.pmax(offsets[blocks], ("lat", "lon"))
+    def packed(first_tile, tiles, token):
+        params = jnp.stack([place[0], first_tile + token])
+        *flows, token = pack_call(
+            params, offset, index, base_flow, direction, groups, tiles
+        )
+        return spread_out(flows), token[0, 0]
+
+    def through(flows):
+        *back, token = friction_call(place, flows, coefs)
+        return spread_out(back), token[0, 0]
+
+    flows = []
+    backs = []
+    tile = 0
+    token = jnp.int32(0)
+    for chunk, tiles in enumerate(chunk_tiles):
+        flow, token = packed(tile, tiles, token)
+        flows.append(flow)
+        if chunk >= 1:
+            back, token_back = through(flows[chunk - 1])
+            backs.append(back)
+            if chunk == 1:
+                token = token + token_back
+        tile += groups * tiles
+    backs.append(through(flows[-1])[0])
+    later_mask = wet_mask + token
+    wet = later_mask.astype(jnp.float32)
+    above, below, slabs = halo(direction, wet, water_depth)
+    result = prepare_call(scalars, direction, later_mask, water_depth, above, below, slabs)
+
+    largest = lax.pmax(offsets[blocks] + token, ("lat", "lon"))
     loop_cells = groups * LOOP_TILES * LANES
     loops = jnp.maximum(largest - fixed * LANES + loop_cells - 1, 0) // loop_cells
 
     def more(state):
         done, held = state
-        back = through(fixed + done * groups * LOOP_TILES, LOOP_TILES)
+        back = through(packed(fixed + done * groups * LOOP_TILES, LOOP_TILES, 0)[0])[0]
         held = lax.dynamic_update_slice_in_dim(
             held, jnp.concatenate(back, axis=0)[None], done, 0
         )
@@ -651,14 +728,13 @@
     extra = jnp.zeros((steps, rows, LANES), jnp.float32)
     _, extra = lax.while_loop(lambda state: state[0] < loops, more, (jnp.int32(0), extra))
 
-    arrays = (direction, wet_mask, water_depth, drag_factor, edges, slabs, cells)
+    arrays = (wet_mask, drag_factor, cells)
     pieces = []
     back_rows = rows * steps + groups * sum(piece_rows(tiles, coefs) for tiles in chunk_tiles)
-    result = None
     begin = jnp.int32(0)
     tile = 0
     for chunk, tiles in enumerate(chunk_tiles):
-        pieces += through(tile, tiles)
+        pieces += backs[chunk]
         tile += groups * tiles
         if chunk == len(chunk_tiles) - 1:
             end = jnp.int32(row_blocks)
@@ -667,9 +743,7 @@
             end = jnp.sum((ends <= tile * LANES).astype(jnp.int32))
         else:
             continue
-        start = jnp.minimum(begin, row_blocks - 1)
-        count = jnp.maximum(end - start, 1)
-        first = jnp.stack([start, place[0], count])
+        first = jnp.stack([begin, place[0], end - begin])
         result = finish_call(
             first, offset, table, scalars, arrays, list(pieces), back_rows, result
         )

time: 282 us -> 256 us (0.908)
  waiting for transfers between devices: 109 us -> 85.6 us
  Pallas kernels: 86.2 us -> 79.9 us
    ppermute x28 -> x22, waiting for transfers between devices: 109 us -> 85.6 us  [shifted(): return lax.ppermute(block, axis, pairs)]
    pallas_call x4 -> x3, Pallas kernels: 25.3 us -> 16.4 us  [pack_call(): pl.pallas_call(lambda *refs: pack_kernel(groups, coefs, tiles, *refs), ou...]
    unnamed x75 -> x43, local copies, waits for them, and re-layouts: 11 us -> 17 us
    squeeze x3 -> x2, local copies, waits for them, and re-layouts: 4.77 us -> 0.07 us  [the longest x1 0.07 us: halo(): east_below = jnp.concatenate([east_col[:, 1:], below[1, :, -1:]], axis=1)]
    pallas_call x4 -> x3, Pallas kernels: 26.9 us -> 30.2 us  [friction_call(): pl.pallas_call(lambda *refs: friction_kernel(groups, coefs, tiles, *refs)...]
    ppermute x28 -> x22, starting transfers between devices: 39.3 us -> 40.6 us  [shifted(): return lax.ppermute(block, axis, pairs)]
    pallas_call x2 -> x3, Pallas kernels: 32.9 us -> 32.3 us  [the longest x2 22.3 us: finish_call(): pl.pallas_call(kernel, out_shape=jax.ShapeDtypeStruct(result.shape, jnp.f...]
  transfers between devices with their start and end apart: 28 -> 22, of which waited for: 13 -> 6; matrix products, arithmetic and copies ran while one was open for 9% -> 11% of each run, Pallas kernels for 24% -> 25%
where the time goes in v4:
time: 256 us; the launch traced here: 255 us
  waiting for transfers between devices  85.6 us (33%)
  Pallas kernels  79.9 us (31%)
  starting transfers between devices  40.6 us (16%)
  local copies, waits for them, and re-layouts  31 us (12%)
  blocking collectives  7.9 us (3%)
  other arithmetic  5.13 us (2%)
  between operations  4.85 us (2%)
    ppermute x22, waiting for transfers between devices, shifted(): return lax.ppermute(block, axis, pairs)  85.6 us
    ppermute x22, starting transfers between devices, shifted(): return lax.ppermute(block, axis, pairs)  40.6 us
    pallas_call x3, Pallas kernels, friction_call(): pl.pallas_call(lambda *refs: friction_kernel(groups, coefs, tiles, *refs)...  30.2 us
    pallas_call x2, Pallas kernels, finish_call(): pl.pallas_call(kernel, out_shape=jax.ShapeDtypeStruct(result.shape, jnp.f...  22.3 us
    unnamed x43, local copies, waits for them, and re-layouts  17 us
    pallas_call x3, Pallas kernels, pack_call(): pl.pallas_call(lambda *refs: pack_kernel(groups, coefs, tiles, *refs), ou...  16.4 us
    pallas_call x1, Pallas kernels, prepare_call(): pl.pallas_call(lambda *refs: prepare_kernel(coefs, *refs), out_shape=jax....  10 us
    pmax x1, blocking collectives, local(): largest = lax.pmax(offsets[blocks] + token, ('lat', 'lon'))  7.9 us
  transfers between devices with their start and end apart: 22, of which 6 were waited for; matrix products, arithmetic and copies ran while one was open for 11% of the time, Pallas kernels for 25%

profile of v4, /device:TPU:12, one launch (start us, length us, event | category | flops | bytes accessed | tf_op | source)
XLA Modules:
  0.0 255.0 jit_solution(6931708891639298449)
XLA Ops:
  0.0 0.9 copy-done
  1.0 1.0 index.1
  2.0 6.1 %pack.7 = (f32[14,32,128]{2,1,0:T(8,128)S(1)}, f32[14,32,128]{2,1,0:T(8,128)S(1)}, f32[14,32,128]{2,1,0:T(8,128)S(1)}, f32[14,32,128]{2,1,0:T(8,128)S(1)}, s32[8,128]{1,0:T(8,128)S(1)}) custom-call(s32[2]{0:T(128)S(1)} %pad_add_fusion.3.refs_0_, s32[8,128]{1,0:T(8,128)S(1)} %get-tuple-element.347.refs_1_.offset_ref, ...), custom_call_target="tpu_custom_call" | custom-call | bytes 1835008 | tf_op jit(solution)/shard_map/pack/pallas_call | solution.py:324
  8.1 1.6 collective-permute-start.6
  9.8 1.2 collective-permute-start.7
  11.0 1.8 collective-permute-start.8
  14.0 6.5 %pack.8 = (f32[50,32,128]{2,1,0:T(8,128)S(1)}, f32[50,32,128]{2,1,0:T(8,128)}, f32[50,32,128]{2,1,0:T(8,128)}, f32[50,32,128]{2,1,0:T(8,128)}, s32[8,128]{1,0:T(8,128)S(1)}) custom-call(s32[2]{0:T(128)S(1)} %pad_add_fusion.4.refs_0_, s32[8,128]{1,0:T(8,128)S(1)} %get-tuple-element.347.refs_1_.offset_ref, s32[512,128]{1,0:T(8,128)S(1)} %get-tuple-element.348.refs_2_, ...), custom_call_target="tpu_custom_call" | custom-call | bytes 6553600 | tf_op jit(solution)/shard_map/pack/pallas_call | solution.py:324
  21.9 3.5 %collective-permute-start.17 = (f32[50,32,128]{2,1,0:T(8,128)}, f32[50,32,128]{2,1,0:T(8,128)}, u32[]{:S(2)}, u32[]{:S(2)}) collective-permute-start(f32[50,32,128]{2,1,0:T(8,128)} %get-tuple-element.182), channel_id=1, source_target_pairs={{0,16},{8,24},{16,0},{24,8},{1,17},{9,25},{17,1},{25,9},{2,18},{10... | collective-permute-start | bytes 2457608 | tf_op jit(solution)/shard_map/ppermute | solution.py:614
  25.4 5.1 %collective-permute-done.7.refs_5_ = f32[14,32,128]{2,1,0:T(8,128)S(1)} collective-permute-done((f32[14,32,128]{2,1,0:T(8,128)S(1)}, f32[14,32,128]{2,1,0:T(8,128)S(1)}, u32[]{:S(2)}, u32[]{:S(2)}) %collective-permute-start.7) | collective-permute-done | bytes 229408 | tf_op jit(solution)/shard_map/ppermute | solution.py:614
  30.6 35.8 %collective-permute-done.8.refs_6_ = f32[14,32,128]{2,1,0:T(8,128)S(1)} collective-permute-done((f32[14,32,128]{2,1,0:T(8,128)S(1)}, f32[14,32,128]{2,1,0:T(8,128)S(1)}, u32[]{:S(2)}, u32[]{:S(2)}) %collective-permute-start.8) | collective-permute-done | bytes 229408 | tf_op jit(solution)/shard_map/ppermute | solution.py:614
  66.4 5.0 %friction.7 = (f32[240,128]{1,0:T(8,128)S(1)}, f32[240,128]{1,0:T(8,128)S(1)}, f32[240,128]{1,0:T(8,128)}, f32[240,128]{1,0:T(8,128)S(1)}, s32[8,128]{1,0:T(8,128)S(1)}) custom-call(s32[1]{0:T(128)} %bitcast.2.refs_0_, bf16[4,256,96]{2,1,0:T(8,128)(2,1)} %constant.93.clone.refs_1_, bf16[4,64,256]{2,1,0:T(8,128)(2,1)} %constant.94.clone.refs_2_, ...), custom_call_target="tpu_custom_call" | custom-call | flops 939524096 | bytes 917504 | tf_op jit(solution)/shard_map/friction/pallas_call | solution.py:137
  73.4 3.8 %pack.9 = (f32[33,32,128]{2,1,0:T(8,128)S(1)}, f32[33,32,128]{2,1,0:T(8,128)S(1)}, f32[33,32,128]{2,1,0:T(8,128)S(1)}, f32[33,32,128]{2,1,0:T(8,128)S(1)}, s32[8,128]{1,0:T(8,128)S(1)}) custom-call(s32[2]{0:T(128)S(1)} %pad_add_fusion.5.refs_0_, s32[8,128]{1,0:T(8,128)S(1)} %get-tuple-element.347.refs_1_.offset_ref, ...), custom_call_target="tpu_custom_call" | custom-call | bytes 4325376 | tf_op jit(solution)/shard_map/pack/pallas_call | solution.py:324
  77.2 0.8 copy-done.7
  78.0 0.9 copy-done.8
  78.8 0.8 copy-done.9
  81.5 7.9 %pmax.7 = s32[]{:T(128)} all-reduce(s32[]{:T(128)S(6)} %add.54), channel_id=1, replica_groups=mesh['freq'=4,'lat'=2,'lon'=4] {'lat','lon'}, use_global_device_ids=true, to_apply=%region_1.2 | all-reduce | flops 1 | bytes 8 | tf_op jit(solution)/shard_map/pmax | solution.py:715
  90.0 1.1 broadcast_in_dim.16
  91.1 1.0 slice.82
  92.1 5.8 %fusion.7 = (f32[1,8,128,512]{3,2,1,0:T(8,128)}, f32[1,8,128,512]{3,2,1,0:T(8,128)}, f32[1,8,128,512]{3,2,1,0:T(8,128)}) fusion(f32[3,8,128,512]{3,2,1,0:T(8,128)} %get-tuple-element.425), kind=kLoop, calls=%fused_computation.38 | loop fusion | bytes 12582912 | tf_op jit(solution)/shard_map/slice | solution.py:618
  97.9 2.9 %copy.32 = f32[1,8,128,512]{2,1,3,0:T(8,128)} copy(f32[1,8,128,512]{3,2,1,0:T(8,128)} %get-tuple-element.267) | data formatting | bytes 4194304
  100.8 2.8 %copy.38 = f32[1,8,128,512]{3,1,2,0:T(8,128)S(1)} copy(f32[1,8,128,512]{3,2,1,0:T(8,128)} %get-tuple-element.268) | data formatting | bytes 4194304
  103.6 1.3 copy-done.17
  104.9 0.9 slice.105
  105.8 1.2 copy.27
  107.0 3.0 %copy.33 = f32[1,8,128,512]{2,1,3,0:T(8,128)} copy(f32[1,8,128,512]{3,2,1,0:T(8,128)} %get-tuple-element.269) | data formatting | bytes 4194304
  110.9 1.3 collective-permute-start.10
  112.2 0.7 bitcast_multiply_fusion.2
  114.3 0.7 broadcast_multiply_fusion
  115.1 4.5 %collective-permute-start.9 = (f32[2,8,512]{2,1,0:T(8,128)S(1)}, f32[2,8,512]{2,1,0:T(8,128)S(1)}, u32[]{:S(2)}, u32[]{:S(2)}) collective-permute-start(f32[2,8,512]{2,1,0:T(8,128)S(1)} %pad_maximum_fusion), channel_id=1, source_target_pairs={{0,4},{1,5},{2,6},{3,7},{8,12},{9,13},{10,14},{11,15},{16,20},{17,... | collective-permute-start | bytes 98312 | tf_op jit(solution)/shard_map/ppermute | solution.py:614
  119.8 2.0 collective-permute-start.22
  122.3 0.9 copy-done.5
  123.2 2.5 collective-permute-start.24
  125.7 1.7 collective-permute-start.12
  127.4 1.1 copy-done.6
  128.6 14.9 %friction.8 = (f32[856,128]{1,0:T(8,128)S(1)}, f32[856,128]{1,0:T(8,128)}, f32[856,128]{1,0:T(8,128)S(1)}, f32[856,128]{1,0:T(8,128)S(1)}, s32[8,128]{1,0:T(8,128)}) custom-call(s32[1]{0:T(128)} %bitcast.2.refs_0_, bf16[4,256,96]{2,1,0:T(8,128)(2,1)} %constant.93.clone.refs_1_, bf16[4,64,256]{2,1,0:T(8,128)(2,1)} %constant.94.clone.refs_2_, ...), custom_call_target="tpu_custom_call" | custom-call | flops 3355443200 | bytes 3276800 | tf_op jit(solution)/shard_map/friction/pallas_call | solution.py:137
  143.5 0.8 copy-done.10
  144.2 0.7 copy-done.11
  146.9 30.8 %collective-permute-done.13.refs_5_ = f32[240,128]{1,0:T(8,128)S(1)} collective-permute-done((f32[240,128]{1,0:T(8,128)S(1)}, f32[240,128]{1,0:T(8,128)S(1)}, u32[]{:S(2)}, u32[]{:S(2)}) %collective-permute-start.13) | collective-permute-done | bytes 122912 | tf_op jit(solution)/shard_map/ppermute | solution.py:614
  178.0 15.6 %collective-permute-start.15 = (f32[240,128]{1,0:T(8,128)S(1)}, f32[240,128]{1,0:T(8,128)S(1)}, u32[]{:S(2)}, u32[]{:S(2)}) collective-permute-start(f32[240,128]{1,0:T(8,128)S(1)} %get-tuple-element.179), channel_id=1, source_target_pairs={{0,24},{8,0},{16,8},{24,16},{1,25},{9,1},{17,9},{25,17},{2,26},{10... | collective-permute-start | bytes 368648 | tf_op jit(solution)/shard_map/ppermute | solution.py:614
  193.7 10.2 %friction.9 = (f32[568,128]{1,0:T(8,128)S(1)}, f32[568,128]{1,0:T(8,128)S(1)}, f32[568,128]{1,0:T(8,128)S(1)}, f32[568,128]{1,0:T(8,128)S(1)}, s32[8,128]{1,0:T(8,128)}) custom-call(s32[1]{0:T(128)} %bitcast.2.refs_0_, bf16[4,256,96]{2,1,0:T(8,128)(2,1)} %constant.93.clone.refs_1_, bf16[4,64,256]{2,1,0:T(8,128)(2,1)} %constant.94.clone.refs_2_, ...), custom_call_target="tpu_custom_call" | custom-call | flops 2214592512 | bytes 2162688 | tf_op jit(solution)/shard_map/friction/pallas_call | solution.py:137
  204.0 1.9 collective-permute-start.25
  205.9 4.2 %collective-permute-done.15.refs_7_ = f32[240,128]{1,0:T(8,128)S(1)} collective-permute-done((f32[240,128]{1,0:T(8,128)S(1)}, f32[240,128]{1,0:T(8,128)S(1)}, u32[]{:S(2)}, u32[]{:S(2)}) %collective-permute-start.15) | collective-permute-done | bytes 122912 | tf_op jit(solution)/shard_map/ppermute | solution.py:614
  211.8 0.9 broadcast_in_dim.15.refs_11_
  212.8 10.0 %prepare.1.refs_3_ = f32[3,8,128,512]{3,2,1,0:T(8,128)} custom-call(f32[6]{0:T(128)S(1)} %pad_maximum_fusion.4.refs_0_.scalars_ref, f32[3,8,128,512]{3,2,1,0:T(8,128)S(1)} %bitcast.59, f32[3,8,128,512]{3,2,1,0:T(8,128)S(1)} %bitcast.59, f32[3,8,128,512]{3,2,1,0:T(8,128)S(1)} %bitcast.59, s32[128,512]{1,0:T(8,128)S(1)} %get-tuple-element.266.refs_4_.refs_5_.refs_6_, ...), custom_call_target="tpu_custom_call" | custom-call | bytes 25165824 | tf_op jit(solution)/shard_map/prepare/pallas_call | solution.py:445
  222.8 5.9 %collective-permute-done.20.refs_10_ = f32[856,128]{1,0:T(8,128)S(1)} collective-permute-done((f32[856,128]{1,0:T(8,128)}, f32[856,128]{1,0:T(8,128)S(1)}, u32[]{:S(2)}, u32[]{:S(2)}) %collective-permute-start.20) | collective-permute-done | bytes 438304 | tf_op jit(solution)/shard_map/ppermute | solution.py:614
  228.7 3.7 %collective-permute-done.21.refs_11_ = f32[856,128]{1,0:T(8,128)S(1)} collective-permute-done((f32[856,128]{1,0:T(8,128)}, f32[856,128]{1,0:T(8,128)S(1)}, u32[]{:S(2)}, u32[]{:S(2)}) %collective-permute-start.21) | collective-permute-done | bytes 438304 | tf_op jit(solution)/shard_map/ppermute | solution.py:614
  232.4 12.7 %finish.2.refs_3_ = f32[3,8,128,512]{3,2,1,0:T(8,128)} custom-call(s32[3]{0:T(128)S(1)} %get-tuple-element.275.first_ref, s32[8,128]{1,0:T(8,128)S(1)} %get-tuple-element.429, s32[8,640]{1,0:T(8,128)S(1)} %copy-done.4, f32[6]{0:T(128)S(1)} %pad_maximum_fusion.4.refs_0_.scalars_ref, s32[128,512]{1,0:T(8,128)S(1)} %copy-done.1, ...), custom_call_target="tpu_custom_call", output_to_operand_aliasing={{}: (7, {})} | custom-call | bytes 9437184 | tf_op jit(solution)/shard_map/finish/pallas_call | solution.py:591
  245.2 9.7 %finish.3 = f32[3,8,128,512]{3,2,1,0:T(8,128)} custom-call(s32[3]{0:T(128)S(1)} %get-tuple-element.274.first_ref, s32[8,128]{1,0:T(8,128)S(1)} %get-tuple-element.429, s32[8,640]{1,0:T(8,128)S(1)} %copy-done.4, f32[6]{0:T(128)S(1)} %pad_maximum_fusion.4.refs_0_.scalars_ref, s32[128,512]{1,0:T(8,128)S(1)} %copy-done.1, ...), custom_call_target="tpu_custom_call", output_to_operand_aliasing={{}: (7, {})} | custom-call | bytes 9437184 | tf_op jit(solution)/shard_map/finish/pallas_call | solution.py:591
  (90 shorter events, 9.8 us)
Async XLA Ops:
  0.0 0.9 copy-start
  2.0 12.0 %copy-start.14 = (f32[3,8,128,512]{3,2,1,0:T(8,128)S(1)}, f32[3,8,128,512]{3,2,1,0:T(8,128)}, u32[]{:S(2)}) copy-start(f32[3,8,128,512]{3,2,1,0:T(8,128)} %refs_3_.7) | copy-start | bytes 18874372
  2.0 12.0 %copy-start.15 = (f32[2,8,128,512]{3,2,1,0:T(8,128)S(1)}, f32[2,8,128,512]{3,2,1,0:T(8,128)}, u32[]{:S(2)}) copy-start(f32[2,8,128,512]{3,2,1,0:T(8,128)} %refs_3_.6) | copy-start | bytes 12582916
  8.1 17.3 %collective-permute-start.6 = (f32[14,32,128]{2,1,0:T(8,128)S(1)}, f32[14,32,128]{2,1,0:T(8,128)S(1)}, u32[]{:S(2)}, u32[]{:S(2)}) collective-permute-start(f32[14,32,128]{2,1,0:T(8,128)S(1)} %get-tuple-element.171), channel_id=1, source_target_pairs={{0,8},{8,16},{16,24},{24,0},{1,9},{9,17},{17,25},{25,1},{2,10},{10... | collective-permute-start | bytes 688136 | tf_op jit(solution)/shard_map/ppermute | solution.py:614
  9.8 20.8 %collective-permute-start.7 = (f32[14,32,128]{2,1,0:T(8,128)S(1)}, f32[14,32,128]{2,1,0:T(8,128)S(1)}, u32[]{:S(2)}, u32[]{:S(2)}) collective-permute-start(f32[14,32,128]{2,1,0:T(8,128)S(1)} %get-tuple-element.172), channel_id=1, source_target_pairs={{0,16},{8,24},{16,0},{24,8},{1,17},{9,25},{17,1},{25,9},{2,18},{10... | collective-permute-start | bytes 688136 | tf_op jit(solution)/shard_map/ppermute | solution.py:614
  11.0 55.4 %collective-permute-start.8 = (f32[14,32,128]{2,1,0:T(8,128)S(1)}, f32[14,32,128]{2,1,0:T(8,128)S(1)}, u32[]{:S(2)}, u32[]{:S(2)}) collective-permute-start(f32[14,32,128]{2,1,0:T(8,128)S(1)} %get-tuple-element.173), channel_id=1, source_target_pairs={{0,24},{8,0},{16,8},{24,16},{1,25},{9,1},{17,9},{25,17},{2,26},{10... | collective-permute-start | bytes 688136 | tf_op jit(solution)/shard_map/ppermute | solution.py:614
  20.6 101.7 %collective-permute-start.16 = (f32[50,32,128]{2,1,0:T(8,128)}, f32[50,32,128]{2,1,0:T(8,128)S(1)}, u32[]{:S(2)}, u32[]{:S(2)}) collective-permute-start(f32[50,32,128]{2,1,0:T(8,128)} %get-tuple-element.181), channel_id=1, source_target_pairs={{0,8},{8,16},{16,24},{24,0},{1,9},{9,17},{17,25},{25,1},{2,10},{10... | collective-permute-start | bytes 2457608 | tf_op jit(solution)/shard_map/ppermute | solution.py:614
  21.9 103.8 %collective-permute-start.17 = (f32[50,32,128]{2,1,0:T(8,128)}, f32[50,32,128]{2,1,0:T(8,128)}, u32[]{:S(2)}, u32[]{:S(2)}) collective-permute-start(f32[50,32,128]{2,1,0:T(8,128)} %get-tuple-element.182), channel_id=1, source_target_pairs={{0,16},{8,24},{16,0},{24,8},{1,17},{9,25},{17,1},{25,9},{2,18},{10... | collective-permute-start | bytes 2457608 | tf_op jit(solution)/shard_map/ppermute | solution.py:614
  71.4 5.8 %copy-start.12 = (f32[240,128]{1,0:T(8,128)}, f32[240,128]{1,0:T(8,128)S(1)}, u32[]{:S(2)}) copy-start(f32[240,128]{1,0:T(8,128)S(1)} %get-tuple-element.177) | copy-start | bytes 368644
  77.2 0.8 copy-start.7
  78.0 0.9 copy-start.8
  78.8 0.8 copy-start.9
  91.1 34.6 %collective-permute-start.18 = (f32[50,32,128]{2,1,0:T(8,128)}, f32[50,32,128]{2,1,0:T(8,128)}, u32[]{:S(2)}, u32[]{:S(2)}) collective-permute-start(f32[50,32,128]{2,1,0:T(8,128)} %get-tuple-element.183), channel_id=1, source_target_pairs={{0,24},{8,0},{16,8},{24,16},{1,25},{9,1},{17,9},{25,17},{2,26},{10... | collective-permute-start | bytes 2457608 | tf_op jit(solution)/shard_map/ppermute | solution.py:614
  92.1 5.8 %copy-start.2 = (f32[128,512]{1,0:T(8,128)S(1)}, f32[128,512]{1,0:T(8,128)}, u32[]{:S(2)}) copy-start(f32[128,512]{1,0:T(8,128)} %refs_8_.1) | copy-start | bytes 786436
  103.6 1.3 copy-start.17
  107.0 3.0 %copy-start.1 = (s32[128,512]{1,0:T(8,128)S(1)}, s32[128,512]{1,0:T(8,128)}, u32[]{:S(2)}) copy-start(s32[128,512]{1,0:T(8,128)} %refs_0_.3) | copy-start | bytes 786436
  110.9 8.7 %collective-permute-start.10 = (f32[2,8,512]{2,1,0:T(8,128)S(1)}, f32[2,8,512]{2,1,0:T(8,128)S(1)}, u32[]{:S(2)}, u32[]{:S(2)}) collective-permute-start(f32[2,8,512]{2,1,0:T(8,128)S(1)} %fusion.1), channel_id=1, source_target_pairs={{4,0},{5,1},{6,2},{7,3},{12,8},{13,9},{14,10},{15,11},{20,16},{21,... | collective-permute-start | bytes 98312 | tf_op jit(solution)/shard_map/ppermute | solution.py:614
  115.1 6.7 %collective-permute-start.9 = (f32[2,8,512]{2,1,0:T(8,128)S(1)}, f32[2,8,512]{2,1,0:T(8,128)S(1)}, u32[]{:S(2)}, u32[]{:S(2)}) collective-permute-start(f32[2,8,512]{2,1,0:T(8,128)S(1)} %pad_maximum_fusion), channel_id=1, source_target_pairs={{0,4},{1,5},{2,6},{3,7},{8,12},{9,13},{10,14},{11,15},{16,20},{17,... | collective-permute-start | bytes 98312 | tf_op jit(solution)/shard_map/ppermute | solution.py:614
  119.8 58.2 %collective-permute-start.22 = (f32[33,32,128]{2,1,0:T(8,128)}, f32[33,32,128]{2,1,0:T(8,128)}, u32[]{:S(2)}, u32[]{:S(2)}) collective-permute-start(f32[33,32,128]{2,1,0:T(8,128)} %copy-done.9), channel_id=1, source_target_pairs={{0,8},{8,16},{16,24},{24,0},{1,9},{9,17},{17,25},{25,1},{2,10},{10... | collective-permute-start | bytes 1622024 | tf_op jit(solution)/shard_map/ppermute | solution.py:614
  121.9 71.7 %collective-permute-start.23 = (f32[33,32,128]{2,1,0:T(8,128)}, f32[33,32,128]{2,1,0:T(8,128)}, u32[]{:S(2)}, u32[]{:S(2)}) collective-permute-start(f32[33,32,128]{2,1,0:T(8,128)} %copy-done.8), channel_id=1, source_target_pairs={{0,16},{8,24},{16,0},{24,8},{1,17},{9,25},{17,1},{25,9},{2,18},{10... | collective-permute-start | bytes 1622024 | tf_op jit(solution)/shard_map/ppermute | solution.py:614
  122.3 0.9 copy-start.5
  123.2 70.4 %collective-permute-start.24 = (f32[33,32,128]{2,1,0:T(8,128)}, f32[33,32,128]{2,1,0:T(8,128)}, u32[]{:S(2)}, u32[]{:S(2)}) collective-permute-start(f32[33,32,128]{2,1,0:T(8,128)} %copy-done.7), channel_id=1, source_target_pairs={{0,24},{8,0},{16,8},{24,16},{1,25},{9,1},{17,9},{25,17},{2,26},{10... | collective-permute-start | bytes 1622024 | tf_op jit(solution)/shard_map/ppermute | solution.py:614
  125.7 19.3 %collective-permute-start.11 = (f32[3,8,128]{2,1,0:T(8,128)S(1)}, f32[3,8,128]{2,1,0:T(8,128)S(1)}, u32[]{:S(2)}, u32[]{:S(2)}) collective-permute-start(f32[3,8,128]{2,1,0:T(8,128)S(1)} %pad_maximum_fusion.2), channel_id=1, source_target_pairs={{0,1},{1,2},{2,3},{3,0},{4,5},{5,6},{6,7},{7,4},{8,9},{9,10},{10,1... | collective-permute-start | bytes 36872 | tf_op jit(solution)/shard_map/ppermute | solution.py:614
  125.7 19.4 %collective-permute-start.12 = (f32[3,8,128]{2,1,0:T(8,128)S(1)}, f32[3,8,128]{2,1,0:T(8,128)S(1)}, u32[]{:S(2)}, u32[]{:S(2)}) collective-permute-start(f32[3,8,128]{2,1,0:T(8,128)S(1)} %pad_maximum_fusion.3), channel_id=1, source_target_pairs={{0,3},{1,0},{2,1},{3,2},{4,7},{5,4},{6,5},{7,6},{8,11},{9,8},{10,9... | collective-permute-start | bytes 36872 | tf_op jit(solution)/shard_map/ppermute | solution.py:614
  127.4 1.1 copy-start.6
  128.6 16.5 %copy-start.13 = (f32[240,128]{1,0:T(8,128)S(1)}, f32[240,128]{1,0:T(8,128)}, u32[]{:S(2)}) copy-start(f32[240,128]{1,0:T(8,128)} %copy-done.12) | copy-start | bytes 368644
  143.4 0.8 copy-start.10
  144.2 0.7 copy-start.11
  145.0 65.6 %collective-permute-start.19 = (f32[856,128]{1,0:T(8,128)}, f32[856,128]{1,0:T(8,128)S(1)}, u32[]{:S(2)}, u32[]{:S(2)}) collective-permute-start(f32[856,128]{1,0:T(8,128)} %get-tuple-element.185), channel_id=1, source_target_pairs={{0,8},{8,16},{16,24},{24,0},{1,9},{9,17},{17,25},{25,1},{2,10},{10... | collective-permute-start | bytes 1314824 | tf_op jit(solution)/shard_map/ppermute | solution.py:614
  145.1 32.6 %collective-permute-start.13 = (f32[240,128]{1,0:T(8,128)S(1)}, f32[240,128]{1,0:T(8,128)S(1)}, u32[]{:S(2)}, u32[]{:S(2)}) collective-permute-start(f32[240,128]{1,0:T(8,128)S(1)} %copy-done.13), channel_id=1, source_target_pairs={{0,8},{8,16},{16,24},{24,0},{1,9},{9,17},{17,25},{25,1},{2,10},{10... | collective-permute-start | bytes 368648 | tf_op jit(solution)/shard_map/ppermute | solution.py:614
  177.7 26.3 %collective-permute-start.14 = (f32[240,128]{1,0:T(8,128)}, f32[240,128]{1,0:T(8,128)S(1)}, u32[]{:S(2)}, u32[]{:S(2)}) collective-permute-start(f32[240,128]{1,0:T(8,128)} %get-tuple-element.178), channel_id=1, source_target_pairs={{0,16},{8,24},{16,0},{24,8},{1,17},{9,25},{17,1},{25,9},{2,18},{10... | collective-permute-start | bytes 368648 | tf_op jit(solution)/shard_map/ppermute | solution.py:614
  178.0 32.2 %collective-permute-start.15 = (f32[240,128]{1,0:T(8,128)S(1)}, f32[240,128]{1,0:T(8,128)S(1)}, u32[]{:S(2)}, u32[]{:S(2)}) collective-permute-start(f32[240,128]{1,0:T(8,128)S(1)} %get-tuple-element.179), channel_id=1, source_target_pairs={{0,24},{8,0},{16,8},{24,16},{1,25},{9,1},{17,9},{25,17},{2,26},{10... | collective-permute-start | bytes 368648 | tf_op jit(solution)/shard_map/ppermute | solution.py:614
  193.6 35.2 %collective-permute-start.20 = (f32[856,128]{1,0:T(8,128)}, f32[856,128]{1,0:T(8,128)S(1)}, u32[]{:S(2)}, u32[]{:S(2)}) collective-permute-start(f32[856,128]{1,0:T(8,128)} %copy-done.11), channel_id=1, source_target_pairs={{0,16},{8,24},{16,0},{24,8},{1,17},{9,25},{17,1},{25,9},{2,18},{10... | collective-permute-start | bytes 1314824 | tf_op jit(solution)/shard_map/ppermute | solution.py:614
  193.6 38.8 %collective-permute-start.21 = (f32[856,128]{1,0:T(8,128)}, f32[856,128]{1,0:T(8,128)S(1)}, u32[]{:S(2)}, u32[]{:S(2)}) collective-permute-start(f32[856,128]{1,0:T(8,128)} %copy-done.10), channel_id=1, source_target_pairs={{0,24},{8,0},{16,8},{24,16},{1,25},{9,1},{17,9},{25,17},{2,26},{10... | collective-permute-start | bytes 1314824 | tf_op jit(solution)/shard_map/ppermute | solution.py:614
  193.7 19.0 %slice-start = ((s8[6291456]{0:T(1024)(128)(4,1)}), s8[4194304]{0:T(1024)(128)(4,1)S(1)}, s32[]{:S(2)}) async-start(s8[6291456]{0:T(1024)(128)(4,1)} %bitcast.58), calls=%async_computation | async-start | bytes 8388608
  193.7 19.0 %slice-start.1 = ((s8[6291456]{0:T(1024)(128)(4,1)}), s8[2097152]{0:T(1024)(128)(4,1)S(1)}, s32[]{:S(2)}) async-start(s8[6291456]{0:T(1024)(128)(4,1)} %bitcast.58), calls=%async_computation.1 | async-start | bytes 4194304
  204.0 41.1 %collective-permute-start.25 = (f32[568,128]{1,0:T(8,128)S(1)}, f32[568,128]{1,0:T(8,128)S(1)}, u32[]{:S(2)}, u32[]{:S(2)}) collective-permute-start(f32[568,128]{1,0:T(8,128)S(1)} %get-tuple-element.193), channel_id=1, source_target_pairs={{0,8},{8,16},{16,24},{24,0},{1,9},{9,17},{17,25},{25,1},{2,10},{10... | collective-permute-start | bytes 872456 | tf_op jit(solution)/shard_map/ppermute | solution.py:614
  210.1 35.0 %collective-permute-start.26 = (f32[568,128]{1,0:T(8,128)S(1)}, f32[568,128]{1,0:T(8,128)S(1)}, u32[]{:S(2)}, u32[]{:S(2)}) collective-permute-start(f32[568,128]{1,0:T(8,128)S(1)} %get-tuple-element.194), channel_id=1, source_target_pairs={{0,16},{8,24},{16,0},{24,8},{1,17},{9,25},{17,1},{25,9},{2,18},{10... | collective-permute-start | bytes 872456 | tf_op jit(solution)/shard_map/ppermute | solution.py:614
  210.6 34.6 %collective-permute-start.27 = (f32[568,128]{1,0:T(8,128)S(1)}, f32[568,128]{1,0:T(8,128)S(1)}, u32[]{:S(2)}, u32[]{:S(2)}) collective-permute-start(f32[568,128]{1,0:T(8,128)S(1)} %get-tuple-element.195), channel_id=1, source_target_pairs={{0,24},{8,0},{16,8},{24,16},{1,25},{9,1},{17,9},{25,17},{2,26},{10... | collective-permute-start | bytes 872456 | tf_op jit(solution)/shard_map/ppermute | solution.py:614
  212.7 19.7 %copy-start.3 = (f32[128,512]{1,0:T(8,128)S(1)}, f32[128,512]{1,0:T(8,128)}, u32[]{:S(2)}) copy-start(f32[128,512]{1,0:T(8,128)} %refs_1_.8) | copy-start | bytes 786436
  212.8 19.7 %copy-start.4 = (s32[8,640]{1,0:T(8,128)S(1)}, s32[8,640]{1,0:T(8,128)}, u32[]{:S(2)}) copy-start(s32[8,640]{1,0:T(8,128)} %constant.92.clone.table_ref) | copy-start | bytes 61444
  232.4 12.7 %copy-start.16 = (f32[4,544,128]{2,1,0:T(8,128)S(1)}, f32[4,544,128]{2,1,0:T(8,128)}, u32[]{:S(2)}) copy-start(f32[4,544,128]{2,1,0:T(8,128)} %get-tuple-element.196) | copy-start | bytes 3342340

commit v5 on v4

--- a/solution.py
+++ b/solution.py
@@ -19,9 +19,10 @@
 OMEGA_STEP = 0.25
 SPEED_SOFT = 0.01
 VMEM_BYTES = 48 * 1024 * 1024
-CHUNK_SHARES = (14, 50, 33)
+CHUNK_SHARES = (16, 48, 33)
 SHARE_UNITS = 128
 LOOP_TILES = 8
+PACK_COST = 16384
 
 
 def split_table():
@@ -41,16 +42,19 @@
     return high, low
 
 
-def friction_kernel(groups, coefs, tiles, place_ref, synth_ref, analyse_ref, *refs):
-    flow_refs, out_refs, token_ref = refs[:groups], refs[groups:-1], refs[-1]
+def friction_kernel(groups, coefs, chunk_tiles, place_ref, synth_ref, analyse_ref, *refs):
+    parts = len(chunk_tiles)
+    tiles = sum(chunk_tiles)
+    out_refs, token_ref = refs[groups * parts : -1], refs[-1]
     token_ref[...] = jnp.zeros_like(token_ref)
     columns = 2 * NCON
 
-    def block(tile, count):
+    def block(flow_refs, first, at, count):
+        tile = first + at
         loaded = []
         for source in range(groups):
-            parts = [flow_refs[source][tile + i] for i in range(count)]
-            loaded.append(jnp.concatenate(parts, axis=1))
+            several = [flow_refs[source][at + i] for i in range(count)]
+            loaded.append(jnp.concatenate(several, axis=1))
         series = []
         for field in range(4):
             rows = slice(field * coefs, (field + 1) * coefs)
@@ -90,13 +94,18 @@
                 at = tiles * 2 * coefs + tile + part
                 out_refs[target][pl.ds(at, 1), :] = mean[:, lanes]
 
-    def body(step, carry):
-        block(step * 2, 2)
-        return carry
-
-    lax.fori_loop(0, tiles // 2, body, 0)
-    if tiles % 2:
-        block(tiles - 1, 1)
+    first = 0
+    for part, here in enumerate(chunk_tiles):
+        flow_refs = refs[part * groups : (part + 1) * groups]
+
+        def body(step, carry, flow_refs=flow_refs, first=first):
+            block(flow_refs, first, step * 2, 2)
+            return carry
+
+        lax.fori_loop(0, here // 2, body, 0)
+        if here % 2:
+            block(flow_refs, first, here - 1, 1)
+        first += here
 
 
 def placed_tables(groups, coefs):
@@ -118,8 +127,9 @@
 
 
 def friction_call(place, flows, coefs):
-    groups = len(flows)
-    tiles = flows[0].shape[0]
+    groups = len(flows[0])
+    chunk_tiles = [chunk[0].shape[0] for chunk in flows]
+    tiles = sum(chunk_tiles)
     synth, analyse = placed_tables(groups, coefs)
     cells = groups * tiles * LANES
     out_shape = (piece_rows(tiles, coefs), LANES)
@@ -130,21 +140,25 @@
             pl.BlockSpec((1,) + synth.shape[1:], lambda i, place: (place[0], 0, 0)),
             pl.BlockSpec((1,) + analyse.shape[1:], lambda i, place: (place[0], 0, 0)),
         ]
-        + [pl.BlockSpec(flows[0].shape, lambda i, place: (0, 0, 0))] * groups,
+        + [
+            pl.BlockSpec(block.shape, lambda i, place: (0, 0, 0))
+            for chunk in flows
+            for block in chunk
+        ],
         out_specs=[pl.BlockSpec(out_shape, lambda i, place: (0, 0))] * groups
         + [pl.BlockSpec((SUB, LANES), lambda i, place: (0, 0))],
     )
     return pl.pallas_call(
-        lambda *refs: friction_kernel(groups, coefs, tiles, *refs),
+        lambda *refs: friction_kernel(groups, coefs, chunk_tiles, *refs),
         out_shape=[jax.ShapeDtypeStruct(out_shape, jnp.float32)] * groups
         + [jax.ShapeDtypeStruct((SUB, LANES), jnp.int32)],
         grid_spec=grid_spec,
         compiler_params=pltpu.CompilerParams(vmem_limit_bytes=VMEM_BYTES),
         cost_estimate=pl.CostEstimate(
-            flops=cells * NTIME * 512, bytes_accessed=cells * 128, transcendentals=0
+            flops=cells * NTIME, bytes_accessed=0, transcendentals=0
         ),
         name="friction",
-    )(place, jnp.asarray(synth), jnp.asarray(analyse), *flows)
+    )(place, jnp.asarray(synth), jnp.asarray(analyse), *[b for chunk in flows for b in chunk])
 
 
 def index_kernel(wet_ref, index_ref, place_ref, offset_ref, scratch):
@@ -207,7 +221,8 @@
     )(wet_mask)
 
 
-def pack_kernel(groups, coefs, tiles, params_ref, offset_ref, index_ref, base_ref, step_ref, *refs):
+def pack_kernel(groups, coefs, tiles, waited, params_ref, offset_ref, index_ref, base_ref, step_ref, *refs):
+    refs = refs[waited:]
     out_refs = refs[:groups]
     token_ref, held, stage, in_sem, out_sem = refs[groups:]
     token_ref[...] = jnp.zeros_like(token_ref)
@@ -305,14 +320,15 @@
         copy.wait()
 
 
-def pack_call(params, offset, index, base_flow, direction, groups, tiles):
+def pack_call(params, offset, index, base_flow, direction, groups, tiles, waited):
     coefs, _, columns = direction.shape[1:]
     shape = (tiles, 4 * coefs, LANES)
     anywhere = pl.BlockSpec(memory_space=pl.ANY)
     grid_spec = pltpu.PrefetchScalarGridSpec(
         num_scalar_prefetch=2,
         grid=(1,),
-        in_specs=[pl.BlockSpec(index.shape, lambda i, p, o: (0, 0)), anywhere, anywhere],
+        in_specs=[pl.BlockSpec(index.shape, lambda i, p, o: (0, 0))]
+        + [anywhere] * (2 + len(waited)),
         out_specs=[anywhere] * groups + [pl.BlockSpec((SUB, LANES), lambda i, p, o: (0, 0))],
         scratch_shapes=[
             pltpu.VMEM((2, 4, coefs, SUB, columns), jnp.float32),
@@ -322,21 +338,22 @@
         ],
     )
     return pl.pallas_call(
-        lambda *refs: pack_kernel(groups, coefs, tiles, *refs),
+        lambda *refs: pack_kernel(groups, coefs, tiles, len(waited), *refs),
         out_shape=[jax.ShapeDtypeStruct(shape, jnp.float32)] * groups
         + [jax.ShapeDtypeStruct((SUB, LANES), jnp.int32)],
         grid_spec=grid_spec,
         compiler_params=pltpu.CompilerParams(vmem_limit_bytes=VMEM_BYTES),
         cost_estimate=pl.CostEstimate(
-            flops=0, bytes_accessed=groups * tiles * coefs * 4096, transcendentals=0
+            flops=0, bytes_accessed=groups * tiles * coefs * PACK_COST, transcendentals=0
         ),
         name="pack",
-    )(params, offset, index, base_flow, direction)
+    )(params, offset, index, base_flow, direction, *waited)
 
 
 def prepare_kernel(coefs, scalars_ref, *refs):
     (here_ref, prev_ref, next_ref, wet_ref, wet_prev_ref, wet_next_ref, depth_ref, depth_prev_ref,
-     above_ref, below_ref, slab_ref, out_ref) = refs
+     above_ref, below_ref, slab_ref, out_ref, token_ref) = refs
+    token_ref[...] = jnp.zeros_like(token_ref)
     columns = here_ref.shape[-1]
     row_block = pl.program_id(0)
     at_top = row_block == 0
@@ -444,7 +461,10 @@
     edge = pl.BlockSpec((2, coefs, columns), lambda i: (0, 0, 0))
     return pl.pallas_call(
         lambda *refs: prepare_kernel(coefs, *refs),
-        out_shape=jax.ShapeDtypeStruct(direction.shape, jnp.float32),
+        out_shape=[
+            jax.ShapeDtypeStruct(direction.shape, jnp.float32),
+            jax.ShapeDtypeStruct((SUB, LANES), jnp.int32),
+        ],
         grid=(rows // SUB,),
         in_specs=[
             pl.BlockSpec(memory_space=pltpu.SMEM),
@@ -460,10 +480,10 @@
             edge,
             pl.BlockSpec((6, coefs, SUB, LANES), lambda i: (0, 0, i, 0)),
         ],
-        out_specs=planes,
+        out_specs=[planes, pl.BlockSpec((SUB, LANES), lambda i: (0, 0))],
         compiler_params=pltpu.CompilerParams(vmem_limit_bytes=VMEM_BYTES),
         cost_estimate=pl.CostEstimate(
-            flops=0, bytes_accessed=rows * columns * coefs * 48, transcendentals=0
+            flops=rows * columns * coefs, bytes_accessed=0, transcendentals=0
         ),
         name="prepare",
     )(
@@ -614,17 +634,70 @@
     return lax.ppermute(block, axis, pairs)
 
 
-def halo(direction, wet, depth):
-    height, east, north = direction[0], direction[1], direction[2]
-    last = north[:, -1] * wet[-1]
-    above = shifted(jnp.stack([last, last * depth[-1]]), "lat", 1, False)
-    below = shifted(direction[:2, :, 0] * wet[0], "lat", -1, False)
-    east_col = east[:, :, -1] * wet[:, -1]
-    east_below = jnp.concatenate([east_col[:, 1:], below[1, :, -1:]], axis=1)
-    north_col = north[:, :, 0] * wet[:, 0]
-    north_above = jnp.concatenate([above[0, :, :1], north_col[:, :-1]], axis=1)
-    to_right = jnp.stack([east_col, east_below, east_col * depth[:, -1]])
-    to_left = jnp.stack([height[:, :, 0] * wet[:, 0], north_col, north_above])
+def edge_kernel(coefs, east_ref, height_ref, north_ref, last_ref, first_ref, wet_ref, depth_ref, *refs):
+    up_ref, down_ref, right_ref, left_ref = refs[-4:]
+    rows, columns = wet_ref.shape
+    wet = wet_ref[...].astype(jnp.float32)
+    end = slice(columns - LANES, columns)
+    wet_end = wet[:, end]
+    wet_start = wet[:, :LANES]
+    depth_end = depth_ref[:, end]
+    wet_last = wet[rows - 1 :, :]
+    depth_last = depth_ref[rows - 1 :, :]
+    for c in range(coefs):
+        at = slice(c, c + 1)
+        north_row = last_ref[0, c, SUB - 1 :, :] * wet_last
+        up_ref[0, at, :] = north_row
+        up_ref[1, at, :] = north_row * depth_last
+        down_ref[0, at, :] = first_ref[0, c, :1, :] * wet[:1, :]
+        down_ref[1, at, :] = first_ref[1, c, :1, :] * wet[:1, :]
+        east = east_ref[0, c] * wet_end
+        right_ref[0, at, :] = jnp.transpose(east)[LANES - 1 :, :]
+        right_ref[1, at, :] = jnp.transpose(east * depth_end)[LANES - 1 :, :]
+        left_ref[0, at, :] = jnp.transpose(height_ref[0, c] * wet_start)[:1, :]
+        left_ref[1, at, :] = jnp.transpose(north_ref[0, c] * wet_start)[:1, :]
+
+
+def edge_call(direction, wet_mask, depth, waited):
+    _, coefs, rows, columns = direction.shape
+    last_tile = columns // LANES - 1
+    last_block = rows // SUB - 1
+    tall = (1, coefs, rows, LANES)
+    whole = pl.BlockSpec((rows, columns), lambda i: (0, 0))
+    row_out = (2, coefs, columns)
+    col_out = (2, coefs, rows)
+    shapes = [row_out, row_out, col_out, col_out]
+    return pl.pallas_call(
+        lambda *refs: edge_kernel(coefs, *refs),
+        out_shape=[jax.ShapeDtypeStruct(shape, jnp.float32) for shape in shapes],
+        grid=(1,),
+        in_specs=[
+            pl.BlockSpec(tall, lambda i: (1, 0, 0, last_tile)),
+            pl.BlockSpec(tall, lambda i: (0, 0, 0, 0)),
+            pl.BlockSpec(tall, lambda i: (2, 0, 0, 0)),
+            pl.BlockSpec((1, coefs, SUB, columns), lambda i: (2, 0, last_block, 0)),
+            pl.BlockSpec((2, coefs, SUB, columns), lambda i: (0, 0, 0, 0)),
+            whole,
+            whole,
+        ]
+        + [pl.BlockSpec(memory_space=pl.ANY)] * len(waited),
+        out_specs=[pl.BlockSpec(shape, lambda i: (0, 0, 0)) for shape in shapes],
+        compiler_params=pltpu.CompilerParams(vmem_limit_bytes=VMEM_BYTES),
+        cost_estimate=pl.CostEstimate(
+            flops=rows * columns, bytes_accessed=0, transcendentals=0
+        ),
+        name="edges",
+    )(direction, direction, direction, direction, direction, wet_mask, depth, *waited)
+
+
+def halo(direction, wet_mask, depth, waited):
+    up, down, right, left = edge_call(direction, wet_mask, depth, waited)
+    above = shifted(up, "lat", 1, False)
+    below = shifted(down, "lat", -1, False)
+    east_below = jnp.concatenate([right[0, :, 1:], below[1, :, -1:]], axis=1)
+    north_above = jnp.concatenate([above[0, :, :1], left[1, :, :-1]], axis=1)
+    to_right = jnp.stack([right[0], east_below, right[1]])
+    to_left = jnp.stack([left[0], left[1], north_above])
     cols = jnp.concatenate(
         [shifted(to_right, "lon", 1, True), shifted(to_left, "lon", -1, True)], axis=0
     )
@@ -639,21 +712,24 @@
     ]
 
 
-def tile_table(groups, coefs, chunk_tiles, steps, blocks):
-    places = list(chunk_tiles) + [LOOP_TILES] * steps
+def tile_table(groups, coefs, back_chunks, blocks):
     table = np.zeros((2 * groups, blocks + LANES), np.int32)
     for member in range(groups):
         tile = 0
         row = 0
-        for tiles in places:
-            for band in range(groups):
-                start = row + (member - band) % groups * piece_rows(tiles, coefs)
-                for i in range(tiles):
-                    if tile < blocks:
-                        table[2 * member, tile] = start + i * 2 * coefs
-                        table[2 * member + 1, tile] = start + tiles * 2 * coefs + i
-                    tile += 1
-            row += groups * piece_rows(tiles, coefs)
+        for chunk_tiles in back_chunks:
+            together = sum(chunk_tiles)
+            before = 0
+            for tiles in chunk_tiles:
+                for band in range(groups):
+                    start = row + (member - band) % groups * piece_rows(together, coefs)
+                    for i in range(before, before + tiles):
+                        if tile < blocks:
+                            table[2 * member, tile] = start + i * 2 * coefs
+                            table[2 * member + 1, tile] = start + together * 2 * coefs + i
+                        tile += 1
+                before += tiles
+            row += groups * piece_rows(together, coefs)
     return table
 
 
@@ -677,48 +753,49 @@
     chunk_tiles = [share * blocks // (groups * SHARE_UNITS) for share in CHUNK_SHARES]
     fixed = groups * sum(chunk_tiles)
     steps = -(-(blocks - fixed) // (groups * LOOP_TILES))
-    table = jnp.asarray(tile_table(groups, coefs, chunk_tiles, steps, blocks))
+    back_chunks = [chunk_tiles[:-1], chunk_tiles[-1:]]
+    table = jnp.asarray(
+        tile_table(groups, coefs, back_chunks + [[LOOP_TILES]] * steps, blocks)
+    )
     index, cells, offset = index_call(wet_mask)
     offsets = offset.reshape(-1)
     ends = offsets[SUB * lane_tiles : blocks + 1 : SUB * lane_tiles]
 
-    def packed(first_tile, tiles, token):
+    def packed(first_tile, tiles, token, waited=()):
         params = jnp.stack([place[0], first_tile + token])
         *flows, token = pack_call(
-            params, offset, index, base_flow, direction, groups, tiles
+            params, offset, index, base_flow, direction, groups, tiles, waited
         )
         return spread_out(flows), token[0, 0]
 
-    def through(flows):
-        *back, token = friction_call(place, flows, coefs)
+    def through(flows, token):
+        *back, token = friction_call(place + token, flows, coefs)
         return spread_out(back), token[0, 0]
 
     flows = []
-    backs = []
     tile = 0
     token = jnp.int32(0)
     for chunk, tiles in enumerate(chunk_tiles):
-        flow, token = packed(tile, tiles, token)
+        waited = flows[0][1:] if chunk == 2 else ()
+        flow, token = packed(tile, tiles, token, waited)
         flows.append(flow)
-        if chunk >= 1:
-            back, token_back = through(flows[chunk - 1])
-            backs.append(back)
-            if chunk == 1:
-                token = token + token_back
         tile += groups * tiles
-    backs.append(through(flows[-1])[0])
-    later_mask = wet_mask + token
-    wet = later_mask.astype(jnp.float32)
-    above, below, slabs = halo(direction, wet, water_depth)
-    result = prepare_call(scalars, direction, later_mask, water_depth, above, below, slabs)
-
-    largest = lax.pmax(offsets[blocks] + token, ("lat", "lon"))
+    above, below, slabs = halo(direction, wet_mask, water_depth, flows[-1][:1])
+    result, prepared = prepare_call(
+        scalars, direction, wet_mask, water_depth, above, below, slabs
+    )
+    back, token = through(flows[:-1], prepared[0, 0])
+    backs = [back]
+    back, token = through(flows[-1:], token)
+    backs.append(back)
     loop_cells = groups * LOOP_TILES * LANES
-    loops = jnp.maximum(largest - fixed * LANES + loop_cells - 1, 0) // loop_cells
+    beyond = offsets[blocks] + token - fixed * LANES
+    loops = jnp.maximum(beyond + loop_cells - 1, 0) // loop_cells
 
     def more(state):
         done, held = state
-        back = through(packed(fixed + done * groups * LOOP_TILES, LOOP_TILES, 0)[0])[0]
+        flow, _ = packed(fixed + done * groups * LOOP_TILES, LOOP_TILES, 0)
+        back, _ = through([flow], 0)
         held = lax.dynamic_update_slice_in_dim(
             held, jnp.concatenate(back, axis=0)[None], done, 0
         )
@@ -730,19 +807,18 @@
 
     arrays = (wet_mask, drag_factor, cells)
     pieces = []
-    back_rows = rows * steps + groups * sum(piece_rows(tiles, coefs) for tiles in chunk_tiles)
+    back_rows = rows * steps
+    back_rows += groups * sum(piece_rows(sum(several), coefs) for several in back_chunks)
     begin = jnp.int32(0)
     tile = 0
-    for chunk, tiles in enumerate(chunk_tiles):
-        pieces += backs[chunk]
-        tile += groups * tiles
-        if chunk == len(chunk_tiles) - 1:
+    for last, several in enumerate(back_chunks):
+        pieces += backs[last]
+        tile += groups * sum(several)
+        if last:
             end = jnp.int32(row_blocks)
             pieces.append(extra.reshape(-1, LANES))
-        elif chunk == len(chunk_tiles) - 2:
+        else:
             end = jnp.sum((ends <= tile * LANES).astype(jnp.int32))
-        else:
-            continue
         first = jnp.stack([begin, place[0], end - begin])
         result = finish_call(
             first, offset, table, scalars, arrays, list(pieces), back_rows, result

time: 256 us -> 235 us (0.918)
  waiting for transfers between devices: 85.6 us -> 110 us
  local copies, waits for them, and re-layouts: 31 us -> 10.2 us
  starting transfers between devices: 40.6 us -> 22.9 us
  blocking collectives: 7.9 us -> 0 us
  Pallas kernels: 79.9 us -> 84.4 us
  other arithmetic: 5.13 us -> 1.83 us
    ppermute x22 -> x19, waiting for transfers between devices: 85.6 us -> 110 us  [shifted(): return lax.ppermute(block, axis, pairs)]
    ppermute x22 -> x19, starting transfers between devices: 40.6 us -> 22.9 us  [shifted(): return lax.ppermute(block, axis, pairs)]
    unnamed x43 -> x46, local copies, waits for them, and re-layouts: 17 us -> 4.84 us
    slice x9 -> x3, local copies, waits for them, and re-layouts: 9.66 us -> 1 us  [the longest x1 0.52 us: local(): beyond = offsets[blocks] + token - fixed * LANES]
    pmax x1 -> x0, blocking collectives: 7.9 us -> none  [local(): largest = lax.pmax(offsets[blocks] + token, ('lat', 'lon'))]
    pallas_call x7, Pallas kernels: 56.6 us -> 63.1 us  [the longest x2 28.2 us: friction_call(): pl.pallas_call(lambda *refs: friction_kernel(groups, coefs, chunk_tiles,...]
    mul x6 -> x0, other arithmetic: 2.76 us -> none  [the longest x1 0.72 us: halo(): above = shifted(jnp.stack([last, last * depth[-1]]), 'lat', 1, False)]
  transfers between devices with their start and end apart: 22 -> 19, of which waited for: 6 -> 11; matrix products, arithmetic and copies ran while one was open for 11% -> 3% of each run, Pallas kernels for 25% -> 30%
where the time goes in v5:
time: 235 us; the launch traced here: 234 us
  waiting for transfers between devices  110 us (47%)
  Pallas kernels  84.4 us (36%)
  starting transfers between devices  22.9 us (10%)
  local copies, waits for them, and re-layouts  10.2 us (4%)
  between operations  4.66 us (2%)
    ppermute x19, waiting for transfers between devices, shifted(): return lax.ppermute(block, axis, pairs)  110 us
    pallas_call x2, Pallas kernels, friction_call(): pl.pallas_call(lambda *refs: friction_kernel(groups, coefs, chunk_tiles,...  28.2 us
    ppermute x19, starting transfers between devices, shifted(): return lax.ppermute(block, axis, pairs)  22.9 us
    pallas_call x2, Pallas kernels, finish_call(): pl.pallas_call(kernel, out_shape=jax.ShapeDtypeStruct(result.shape, jnp.f...  20.3 us
    pallas_call x3, Pallas kernels, pack_call(): pl.pallas_call(lambda *refs: pack_kernel(groups, coefs, tiles, len(waited...  20 us
    pallas_call x1, Pallas kernels, prepare_call(): pl.pallas_call(lambda *refs: prepare_kernel(coefs, *refs), out_shape=[jax...  14.3 us
    unnamed x46, local copies, waits for them, and re-layouts  4.84 us
  transfers between devices with their start and end apart: 19, of which 11 were waited for; matrix products, arithmetic and copies ran while one was open for 3% of the time, Pallas kernels for 30%

profile of v5, /device:TPU:12, one launch (start us, length us, event | category | flops | bytes accessed | tf_op | source)
XLA Modules:
  0.0 234.1 jit_solution(3019929783172141005)
XLA Ops:
  0.0 0.9 copy-done
  1.0 1.0 index.1
  2.0 4.0 %pack.7 = (f32[16,32,128]{2,1,0:T(8,128)S(1)}, f32[16,32,128]{2,1,0:T(8,128)S(1)}, f32[16,32,128]{2,1,0:T(8,128)S(1)}, f32[16,32,128]{2,1,0:T(8,128)S(1)}, s32[8,128]{1,0:T(8,128)S(1)}) custom-call(s32[2]{0:T(128)S(1)} %pad_add_fusion.3.refs_0_, s32[8,128]{1,0:T(8,128)S(1)} %get-tuple-element.337.refs_1_.offset_ref, ...), custom_call_target="tpu_custom_call" | custom-call | bytes 8388608 | tf_op jit(solution)/shard_map/pack/pallas_call | solution.py:340
  6.0 1.6 collective-permute-start.6
  7.7 1.2 collective-permute-start.7
  8.9 1.8 collective-permute-start.8
  10.7 0.5 slice.43
  11.9 8.8 %pack.8 = (f32[48,32,128]{2,1,0:T(8,128)S(1)}, f32[48,32,128]{2,1,0:T(8,128)S(1)}, f32[48,32,128]{2,1,0:T(8,128)}, f32[48,32,128]{2,1,0:T(8,128)}, s32[8,128]{1,0:T(8,128)S(1)}) custom-call(s32[2]{0:T(128)S(1)} %pad_add_fusion.4.refs_0_, s32[8,128]{1,0:T(8,128)S(1)} %get-tuple-element.337.refs_1_.offset_ref, s32[512,128]{1,0:T(8,128)S(1)} %get-tuple-element.338.refs_2_, ...), custom_call_target="tpu_custom_call" | custom-call | bytes 25165824 | tf_op jit(solution)/shard_map/pack/pallas_call | solution.py:340
  20.8 0.3 collective-permute-start.13
  21.1 0.5 slice.44
  22.3 3.5 %collective-permute-start.14 = (f32[48,32,128]{2,1,0:T(8,128)}, f32[48,32,128]{2,1,0:T(8,128)}, u32[]{:S(2)}, u32[]{:S(2)}) collective-permute-start(f32[48,32,128]{2,1,0:T(8,128)} %get-tuple-element.185), channel_id=1, source_target_pairs={{0,16},{8,24},{16,0},{24,8},{1,17},{9,25},{17,1},{25,9},{2,18},{10... | collective-permute-start | bytes 2359304 | tf_op jit(solution)/shard_map/ppermute | solution.py:634
  25.8 5.5 %collective-permute-done.7.refs_6_.refs_5_ = f32[16,32,128]{2,1,0:T(8,128)S(1)} collective-permute-done((f32[16,32,128]{2,1,0:T(8,128)S(1)}, f32[16,32,128]{2,1,0:T(8,128)S(1)}, u32[]{:S(2)}, u32[]{:S(2)}) %collective-permute-start.7) | collective-permute-done | bytes 262176 | tf_op jit(solution)/shard_map/ppermute | solution.py:634
  31.3 34.4 %collective-permute-done.8.refs_7_.refs_6_ = f32[16,32,128]{2,1,0:T(8,128)S(1)} collective-permute-done((f32[16,32,128]{2,1,0:T(8,128)S(1)}, f32[16,32,128]{2,1,0:T(8,128)S(1)}, u32[]{:S(2)}, u32[]{:S(2)}) %collective-permute-start.8) | collective-permute-done | bytes 262176 | tf_op jit(solution)/shard_map/ppermute | solution.py:634
  65.7 7.2 %pack.9 = (f32[33,32,128]{2,1,0:T(8,128)S(1)}, f32[33,32,128]{2,1,0:T(8,128)}, f32[33,32,128]{2,1,0:T(8,128)}, f32[33,32,128]{2,1,0:T(8,128)}, s32[8,128]{1,0:T(8,128)}) custom-call(s32[2]{0:T(128)S(1)} %pad_add_fusion.5.refs_0_, s32[8,128]{1,0:T(8,128)S(1)} %get-tuple-element.337.refs_1_.offset_ref, s32[512,128]{1,0:T(8,128)S(1)} %get-tuple-element.338.refs_2_, ...), custom_call_target="tpu_custom_call" | custom-call | bytes 17301504 | tf_op jit(solution)/shard_map/pack/pallas_call | solution.py:340
  72.9 0.6 edges.1
  73.5 1.3 collective-permute-start.10
  74.8 4.5 %collective-permute-start.9 = (f32[2,8,512]{2,1,0:T(8,128)S(1)}, f32[2,8,512]{2,1,0:T(8,128)S(1)}, u32[]{:S(2)}, u32[]{:S(2)}) collective-permute-start(f32[2,8,512]{2,1,0:T(8,128)S(1)} %get-tuple-element.176), channel_id=1, source_target_pairs={{0,4},{1,5},{2,6},{3,7},{8,12},{9,13},{10,14},{11,15},{16,20},{17,... | collective-permute-start | bytes 98312 | tf_op jit(solution)/shard_map/ppermute | solution.py:634
  79.6 1.4 collective-permute-done.9.refs_9_
  81.1 0.3 collective-permute-start.12
  81.4 1.3 collective-permute-done.11
  82.8 0.9 copy-done.6
  83.7 1.9 collective-permute-start.21
  85.6 0.5 slice.53
  86.3 0.9 broadcast_in_dim.15.refs_11_
  87.2 14.3 %prepare.1 = (f32[3,8,128,512]{3,2,1,0:T(8,128)}, s32[8,128]{1,0:T(8,128)S(1)}) custom-call(f32[6]{0:T(128)S(1)} %pad_maximum_fusion.3.refs_0_.scalars_ref, f32[3,8,128,512]{3,2,1,0:T(8,128)} %refs_3_.9, f32[3,8,128,512]{3,2,1,0:T(8,128)} %refs_3_.9, f32[3,8,128,512]{3,2,1,0:T(8,128)} %refs_3_.9, s32[128,512]{1,0:T(8,128)S(1)} %copy-done.1, ...), custom_call_target="tpu_custom_call" | custom-call | flops 524288 | tf_op jit(solution)/shard_map/prepare/pallas_call | solution.py:462
  101.5 0.5 slice.51
  102.5 19.5 %collective-permute-done.14.refs_9_ = f32[48,32,128]{2,1,0:T(8,128)} collective-permute-done((f32[48,32,128]{2,1,0:T(8,128)}, f32[48,32,128]{2,1,0:T(8,128)}, u32[]{:S(2)}, u32[]{:S(2)}) %collective-permute-start.14) | collective-permute-done | bytes 786464 | tf_op jit(solution)/shard_map/ppermute | solution.py:634
  122.0 0.7 collective-permute-done.15.refs_10_
  122.7 18.5 %friction.6 = (f32[1088,128]{1,0:T(8,128)S(1)}, f32[1088,128]{1,0:T(8,128)}, f32[1088,128]{1,0:T(8,128)}, f32[1088,128]{1,0:T(8,128)S(1)}, s32[8,128]{1,0:T(8,128)S(1)}) custom-call(s32[1]{0:T(128)S(6)} %add.47.refs_0_, bf16[4,256,96]{2,1,0:T(8,128)(2,1)S(1)} %copy-done.18, bf16[4,64,256]{2,1,0:T(8,128)(2,1)S(1)} %copy-done.20, ...), custom_call_target="tpu_custom_call" | custom-call | flops 8388608 | tf_op jit(solution)/shard_map/friction/pallas_call | solution.py:151
  141.2 0.6 slice.52
  142.5 2.8 %collective-permute-start.17 = (f32[1088,128]{1,0:T(8,128)}, f32[1088,128]{1,0:T(8,128)S(1)}, u32[]{:S(2)}, u32[]{:S(2)}) collective-permute-start(f32[1088,128]{1,0:T(8,128)} %get-tuple-element.189), channel_id=1, source_target_pairs={{0,16},{8,24},{16,0},{24,8},{1,17},{9,25},{17,1},{25,9},{2,18},{10... | collective-permute-start | bytes 1671176 | tf_op jit(solution)/shard_map/ppermute | solution.py:634
  145.3 24.4 %collective-permute-done.21.refs_6_ = f32[33,32,128]{2,1,0:T(8,128)} collective-permute-done((f32[33,32,128]{2,1,0:T(8,128)}, f32[33,32,128]{2,1,0:T(8,128)}, u32[]{:S(2)}, u32[]{:S(2)}) %collective-permute-start.21) | collective-permute-done | bytes 540704 | tf_op jit(solution)/shard_map/ppermute | solution.py:634
  169.7 9.7 %friction.7 = (f32[568,128]{1,0:T(8,128)S(1)}, f32[568,128]{1,0:T(8,128)S(1)}, f32[568,128]{1,0:T(8,128)S(1)}, f32[568,128]{1,0:T(8,128)S(1)}, s32[8,128]{1,0:T(8,128)S(1)}) custom-call(s32[1]{0:T(128)S(6)} %add.48.refs_0_, bf16[4,256,96]{2,1,0:T(8,128)(2,1)S(1)} %copy-done.18, bf16[4,64,256]{2,1,0:T(8,128)(2,1)S(1)} %copy-done.20, ...), custom_call_target="tpu_custom_call" | custom-call | flops 4325376 | tf_op jit(solution)/shard_map/friction/pallas_call | solution.py:151
  179.4 0.8 copy-done.8
  180.2 0.7 copy-done.14
  180.9 0.7 copy-done.15
  181.6 0.7 copy-done.16
  182.3 0.5 slice.54
  184.1 1.1 broadcast_in_dim.16
  185.4 2.0 collective-permute-start.22
  187.4 1.5 collective-permute-start.24
  188.9 0.7 fusion.1
  190.2 0.7 pad_add_fusion.1
  190.9 1.7 collective-permute-done.17.refs_6_
  192.6 20.9 %collective-permute-done.18.refs_7_ = f32[1088,128]{1,0:T(8,128)S(1)} collective-permute-done((f32[1088,128]{1,0:T(8,128)}, f32[1088,128]{1,0:T(8,128)S(1)}, u32[]{:S(2)}, u32[]{:S(2)}) %collective-permute-start.18) | collective-permute-done | bytes 557088 | tf_op jit(solution)/shard_map/ppermute | solution.py:634
  213.6 11.3 %finish.2.refs_3_ = f32[3,8,128,512]{3,2,1,0:T(8,128)} custom-call(s32[3]{0:T(128)S(1)} %get-tuple-element.266.first_ref, s32[8,128]{1,0:T(8,128)S(1)} %get-tuple-element.409, s32[8,640]{1,0:T(8,128)S(1)} %copy-done.10, f32[6]{0:T(128)S(1)} %copy-done.12, s32[128,512]{1,0:T(8,128)S(1)} %copy-done.1, ...), custom_call_target="tpu_custom_call", output_to_operand_aliasing={{}: (7, {})} | custom-call | bytes 9437184 | tf_op jit(solution)/shard_map/finish/pallas_call | solution.py:611
  224.9 0.2 collective-permute-done.24.refs_11_
  225.0 9.0 %finish.3 = f32[3,8,128,512]{3,2,1,0:T(8,128)} custom-call(s32[3]{0:T(128)S(1)} %get-tuple-element.265.first_ref, s32[8,128]{1,0:T(8,128)S(1)} %get-tuple-element.409, s32[8,640]{1,0:T(8,128)S(1)} %copy-done.10, f32[6]{0:T(128)S(1)} %copy-done.12, s32[128,512]{1,0:T(8,128)S(1)} %copy-done.1, ...), custom_call_target="tpu_custom_call", output_to_operand_aliasing={{}: (7, {})} | custom-call | bytes 9437184 | tf_op jit(solution)/shard_map/finish/pallas_call | solution.py:611
  (73 shorter events, 1.1 us)
Async XLA Ops:
  0.0 0.9 copy-start
  2.0 9.9 %copy-start.17 = (f32[3,8,128,512]{3,2,1,0:T(8,128)S(1)}, f32[3,8,128,512]{3,2,1,0:T(8,128)}, u32[]{:S(2)}) copy-start(f32[3,8,128,512]{3,2,1,0:T(8,128)} %refs_3_.9) | copy-start | bytes 18874372
  6.0 19.8 %collective-permute-start.6 = (f32[16,32,128]{2,1,0:T(8,128)S(1)}, f32[16,32,128]{2,1,0:T(8,128)S(1)}, u32[]{:S(2)}, u32[]{:S(2)}) collective-permute-start(f32[16,32,128]{2,1,0:T(8,128)S(1)} %get-tuple-element.172), channel_id=1, source_target_pairs={{0,8},{8,16},{16,24},{24,0},{1,9},{9,17},{17,25},{25,1},{2,10},{10... | collective-permute-start | bytes 786440 | tf_op jit(solution)/shard_map/ppermute | solution.py:634
  7.7 23.6 %collective-permute-start.7 = (f32[16,32,128]{2,1,0:T(8,128)S(1)}, f32[16,32,128]{2,1,0:T(8,128)S(1)}, u32[]{:S(2)}, u32[]{:S(2)}) collective-permute-start(f32[16,32,128]{2,1,0:T(8,128)S(1)} %get-tuple-element.173), channel_id=1, source_target_pairs={{0,16},{8,24},{16,0},{24,8},{1,17},{9,25},{17,1},{25,9},{2,18},{10... | collective-permute-start | bytes 786440 | tf_op jit(solution)/shard_map/ppermute | solution.py:634
  8.9 56.8 %collective-permute-start.8 = (f32[16,32,128]{2,1,0:T(8,128)S(1)}, f32[16,32,128]{2,1,0:T(8,128)S(1)}, u32[]{:S(2)}, u32[]{:S(2)}) collective-permute-start(f32[16,32,128]{2,1,0:T(8,128)S(1)} %get-tuple-element.174), channel_id=1, source_target_pairs={{0,24},{8,0},{16,8},{24,16},{1,25},{9,1},{17,9},{25,17},{2,26},{10... | collective-permute-start | bytes 786440 | tf_op jit(solution)/shard_map/ppermute | solution.py:634
  20.8 52.1 %copy-start.4 = (f32[48,32,128]{2,1,0:T(8,128)}, f32[48,32,128]{2,1,0:T(8,128)S(1)}, u32[]{:S(2)}) copy-start(f32[48,32,128]{2,1,0:T(8,128)S(1)} %get-tuple-element.183.refs_7_) | copy-start | bytes 2359300
  20.8 62.0 %collective-permute-start.13 = (f32[48,32,128]{2,1,0:T(8,128)S(1)}, f32[48,32,128]{2,1,0:T(8,128)S(1)}, u32[]{:S(2)}, u32[]{:S(2)}) collective-permute-start(f32[48,32,128]{2,1,0:T(8,128)S(1)} %get-tuple-element.184), channel_id=1, source_target_pairs={{0,8},{8,16},{16,24},{24,0},{1,9},{9,17},{17,25},{25,1},{2,10},{10... | collective-permute-start | bytes 2359304 | tf_op jit(solution)/shard_map/ppermute | solution.py:634
  22.3 99.7 %collective-permute-start.14 = (f32[48,32,128]{2,1,0:T(8,128)}, f32[48,32,128]{2,1,0:T(8,128)}, u32[]{:S(2)}, u32[]{:S(2)}) collective-permute-start(f32[48,32,128]{2,1,0:T(8,128)} %get-tuple-element.185), channel_id=1, source_target_pairs={{0,16},{8,24},{16,0},{24,8},{1,17},{9,25},{17,1},{25,9},{2,18},{10... | collective-permute-start | bytes 2359304 | tf_op jit(solution)/shard_map/ppermute | solution.py:634
  25.8 47.0 %copy-start.1 = (s32[128,512]{1,0:T(8,128)S(1)}, s32[128,512]{1,0:T(8,128)}, u32[]{:S(2)}) copy-start(s32[128,512]{1,0:T(8,128)} %refs_0_.5) | copy-start | bytes 786436
  25.8 47.1 %copy-start.2 = (f32[128,512]{1,0:T(8,128)S(1)}, f32[128,512]{1,0:T(8,128)}, u32[]{:S(2)}) copy-start(f32[128,512]{1,0:T(8,128)} %refs_8_.1) | copy-start | bytes 786436
  25.8 96.9 %collective-permute-start.15 = (f32[48,32,128]{2,1,0:T(8,128)}, f32[48,32,128]{2,1,0:T(8,128)}, u32[]{:S(2)}, u32[]{:S(2)}) collective-permute-start(f32[48,32,128]{2,1,0:T(8,128)} %get-tuple-element.186), channel_id=1, source_target_pairs={{0,24},{8,0},{16,8},{24,16},{1,25},{9,1},{17,9},{25,17},{2,26},{10... | collective-permute-start | bytes 2359304 | tf_op jit(solution)/shard_map/ppermute | solution.py:634
  73.5 5.9 %collective-permute-start.10 = (f32[2,8,512]{2,1,0:T(8,128)S(1)}, f32[2,8,512]{2,1,0:T(8,128)S(1)}, u32[]{:S(2)}, u32[]{:S(2)}) collective-permute-start(f32[2,8,512]{2,1,0:T(8,128)S(1)} %get-tuple-element.177), channel_id=1, source_target_pairs={{4,0},{5,1},{6,2},{7,3},{12,8},{13,9},{14,10},{15,11},{20,16},{21,... | collective-permute-start | bytes 98312 | tf_op jit(solution)/shard_map/ppermute | solution.py:634
  74.8 6.1 %collective-permute-start.9 = (f32[2,8,512]{2,1,0:T(8,128)S(1)}, f32[2,8,512]{2,1,0:T(8,128)S(1)}, u32[]{:S(2)}, u32[]{:S(2)}) collective-permute-start(f32[2,8,512]{2,1,0:T(8,128)S(1)} %get-tuple-element.176), channel_id=1, source_target_pairs={{0,4},{1,5},{2,6},{3,7},{8,12},{9,13},{10,14},{11,15},{16,20},{17,... | collective-permute-start | bytes 98312 | tf_op jit(solution)/shard_map/ppermute | solution.py:634
  79.6 3.1 %collective-permute-start.11 = (f32[3,8,128]{2,1,0:T(8,128)S(1)}, f32[3,8,128]{2,1,0:T(8,128)S(1)}, u32[]{:S(2)}, u32[]{:S(2)}) collective-permute-start(f32[3,8,128]{2,1,0:T(8,128)S(1)} %pad_maximum_fusion.1), channel_id=1, source_target_pairs={{0,1},{1,2},{2,3},{3,0},{4,5},{5,6},{6,7},{7,4},{8,9},{9,10},{10,1... | collective-permute-start | bytes 36872 | tf_op jit(solution)/shard_map/ppermute | solution.py:634
  81.1 1.7 collective-permute-start.12
  82.7 62.6 %collective-permute-start.19 = (f32[33,32,128]{2,1,0:T(8,128)}, f32[33,32,128]{2,1,0:T(8,128)S(1)}, u32[]{:S(2)}, u32[]{:S(2)}) collective-permute-start(f32[33,32,128]{2,1,0:T(8,128)} %get-tuple-element.192), channel_id=1, source_target_pairs={{0,8},{8,16},{16,24},{24,0},{1,9},{9,17},{17,25},{25,1},{2,10},{10... | collective-permute-start | bytes 1622024 | tf_op jit(solution)/shard_map/ppermute | solution.py:634
  82.8 62.5 %collective-permute-start.20 = (f32[33,32,128]{2,1,0:T(8,128)}, f32[33,32,128]{2,1,0:T(8,128)}, u32[]{:S(2)}, u32[]{:S(2)}) collective-permute-start(f32[33,32,128]{2,1,0:T(8,128)} %get-tuple-element.193), channel_id=1, source_target_pairs={{0,16},{8,24},{16,0},{24,8},{1,17},{9,25},{17,1},{25,9},{2,18},{10... | collective-permute-start | bytes 1622024 | tf_op jit(solution)/shard_map/ppermute | solution.py:634
  82.8 0.9 copy-start.6
  83.7 86.0 %collective-permute-start.21 = (f32[33,32,128]{2,1,0:T(8,128)}, f32[33,32,128]{2,1,0:T(8,128)}, u32[]{:S(2)}, u32[]{:S(2)}) collective-permute-start(f32[33,32,128]{2,1,0:T(8,128)} %get-tuple-element.194), channel_id=1, source_target_pairs={{0,24},{8,0},{16,8},{24,16},{1,25},{9,1},{17,9},{25,17},{2,26},{10... | collective-permute-start | bytes 1622024 | tf_op jit(solution)/shard_map/ppermute | solution.py:634
  86.2 0.9 copy-start.11
  87.1 35.5 %copy-start.5 = (f32[48,32,128]{2,1,0:T(8,128)S(1)}, f32[48,32,128]{2,1,0:T(8,128)}, u32[]{:S(2)}) copy-start(f32[48,32,128]{2,1,0:T(8,128)} %copy-done.4) | copy-start | bytes 2359300
  87.1 35.5 %copy-start.7 = (f32[48,32,128]{2,1,0:T(8,128)S(1)}, f32[48,32,128]{2,1,0:T(8,128)}, u32[]{:S(2)}) copy-start(f32[48,32,128]{2,1,0:T(8,128)} %copy-done.6) | copy-start | bytes 2359300
  87.2 35.5 %copy-start.18 = (bf16[4,256,96]{2,1,0:T(8,128)(2,1)S(1)}, bf16[4,256,96]{2,1,0:T(8,128)(2,1)}, u32[]{:S(2)}) copy-start(bf16[4,256,96]{2,1,0:T(8,128)(2,1)} %constant.93.clone.refs_1_) | copy-start | bytes 589828
  87.2 35.5 %copy-start.20 = (bf16[4,64,256]{2,1,0:T(8,128)(2,1)S(1)}, bf16[4,64,256]{2,1,0:T(8,128)(2,1)}, u32[]{:S(2)}) copy-start(bf16[4,64,256]{2,1,0:T(8,128)(2,1)} %constant.94.clone.refs_2_) | copy-start | bytes 393220
  141.2 38.2 %copy-start.13 = (f32[1088,128]{1,0:T(8,128)}, f32[1088,128]{1,0:T(8,128)S(1)}, u32[]{:S(2)}) copy-start(f32[1088,128]{1,0:T(8,128)S(1)} %get-tuple-element.190) | copy-start | bytes 1671172
  142.4 44.9 %collective-permute-start.16 = (f32[1088,128]{1,0:T(8,128)}, f32[1088,128]{1,0:T(8,128)S(1)}, u32[]{:S(2)}, u32[]{:S(2)}) collective-permute-start(f32[1088,128]{1,0:T(8,128)} %get-tuple-element.188), channel_id=1, source_target_pairs={{0,8},{8,16},{16,24},{24,0},{1,9},{9,17},{17,25},{25,1},{2,10},{10... | collective-permute-start | bytes 1671176 | tf_op jit(solution)/shard_map/ppermute | solution.py:634
  142.5 50.1 %collective-permute-start.17 = (f32[1088,128]{1,0:T(8,128)}, f32[1088,128]{1,0:T(8,128)S(1)}, u32[]{:S(2)}, u32[]{:S(2)}) collective-permute-start(f32[1088,128]{1,0:T(8,128)} %get-tuple-element.189), channel_id=1, source_target_pairs={{0,16},{8,24},{16,0},{24,8},{1,17},{9,25},{17,1},{25,9},{2,18},{10... | collective-permute-start | bytes 1671176 | tf_op jit(solution)/shard_map/ppermute | solution.py:634
  179.4 0.8 copy-start.8
  180.2 0.7 copy-start.14
  180.9 0.7 copy-start.15
  181.6 0.7 copy-start.16
  182.3 2.9 %copy-start.19 = (bf16[4,256,96]{2,1,0:T(8,128)(2,1)S(1)}, bf16[4,256,96]{2,1,0:T(8,128)(2,1)}, u32[]{:S(2)}) copy-start(bf16[4,256,96]{2,1,0:T(8,128)(2,1)} %constant.93.clone.refs_1_) | copy-start | bytes 589828
  182.3 2.9 %copy-start.21 = (bf16[4,64,256]{2,1,0:T(8,128)(2,1)S(1)}, bf16[4,64,256]{2,1,0:T(8,128)(2,1)}, u32[]{:S(2)}) copy-start(bf16[4,64,256]{2,1,0:T(8,128)(2,1)} %constant.94.clone.refs_2_) | copy-start | bytes 393220
  185.3 28.3 %copy-start.3 = (f32[128,512]{1,0:T(8,128)S(1)}, f32[128,512]{1,0:T(8,128)}, u32[]{:S(2)}) copy-start(f32[128,512]{1,0:T(8,128)} %refs_1_.9) | copy-start | bytes 786436
  185.3 28.3 %copy-start.10 = (s32[8,640]{1,0:T(8,128)S(1)}, s32[8,640]{1,0:T(8,128)}, u32[]{:S(2)}) copy-start(s32[8,640]{1,0:T(8,128)} %constant.92.clone.table_ref) | copy-start | bytes 61444
  185.3 28.3 %copy-start.12 = (f32[6]{0:T(128)S(1)}, f32[6]{0:T(128)}, u32[]{:S(2)}) copy-start(f32[6]{0:T(128)} %copy-done.11) | copy-start | bytes 76
  185.3 28.2 %collective-permute-start.18 = (f32[1088,128]{1,0:T(8,128)}, f32[1088,128]{1,0:T(8,128)S(1)}, u32[]{:S(2)}, u32[]{:S(2)}) collective-permute-start(f32[1088,128]{1,0:T(8,128)} %copy-done.13), channel_id=1, source_target_pairs={{0,24},{8,0},{16,8},{24,16},{1,25},{9,1},{17,9},{25,17},{2,26},{10... | collective-permute-start | bytes 1671176 | tf_op jit(solution)/shard_map/ppermute | solution.py:634
  185.4 39.5 %collective-permute-start.22 = (f32[568,128]{1,0:T(8,128)}, f32[568,128]{1,0:T(8,128)S(1)}, u32[]{:S(2)}, u32[]{:S(2)}) collective-permute-start(f32[568,128]{1,0:T(8,128)} %copy-done.16), channel_id=1, source_target_pairs={{0,8},{8,16},{16,24},{24,0},{1,9},{9,17},{17,25},{25,1},{2,10},{10... | collective-permute-start | bytes 872456 | tf_op jit(solution)/shard_map/ppermute | solution.py:634
  187.4 37.5 %collective-permute-start.23 = (f32[568,128]{1,0:T(8,128)}, f32[568,128]{1,0:T(8,128)}, u32[]{:S(2)}, u32[]{:S(2)}) collective-permute-start(f32[568,128]{1,0:T(8,128)} %copy-done.15), channel_id=1, source_target_pairs={{0,16},{8,24},{16,0},{24,8},{1,17},{9,25},{17,1},{25,9},{2,18},{10... | collective-permute-start | bytes 872456 | tf_op jit(solution)/shard_map/ppermute | solution.py:634
  187.4 37.7 %collective-permute-start.24 = (f32[568,128]{1,0:T(8,128)}, f32[568,128]{1,0:T(8,128)}, u32[]{:S(2)}, u32[]{:S(2)}) collective-permute-start(f32[568,128]{1,0:T(8,128)} %copy-done.14), channel_id=1, source_target_pairs={{0,24},{8,0},{16,8},{24,16},{1,25},{9,1},{17,9},{25,17},{2,26},{10... | collective-permute-start | bytes 872456 | tf_op jit(solution)/shard_map/ppermute | solution.py:634
  213.5 11.5 %copy-start.9 = (f32[568,128]{1,0:T(8,128)S(1)}, f32[568,128]{1,0:T(8,128)}, u32[]{:S(2)}) copy-start(f32[568,128]{1,0:T(8,128)} %copy-done.8) | copy-start | bytes 872452
  213.5 11.5 %copy-start.22 = (f32[4,544,128]{2,1,0:T(8,128)S(1)}, f32[4,544,128]{2,1,0:T(8,128)}, u32[]{:S(2)}) copy-start(f32[4,544,128]{2,1,0:T(8,128)} %get-tuple-element.200) | copy-start | bytes 3342340

commit v6 on v5

--- a/solution.py
+++ b/solution.py
@@ -19,10 +19,11 @@
 OMEGA_STEP = 0.25
 SPEED_SOFT = 0.01
 VMEM_BYTES = 48 * 1024 * 1024
-CHUNK_SHARES = (16, 48, 33)
+CHUNK_SHARES = (12, 60, 25)
 SHARE_UNITS = 128
 LOOP_TILES = 8
 PACK_COST = 16384
+LATE_WEIGHT = 2048
 
 
 def split_table():
@@ -126,7 +127,7 @@
     return tiles * 2 * coefs + -(-tiles // SUB) * SUB
 
 
-def friction_call(place, flows, coefs):
+def friction_call(place, flows, coefs, weight):
     groups = len(flows[0])
     chunk_tiles = [chunk[0].shape[0] for chunk in flows]
     tiles = sum(chunk_tiles)
@@ -155,7 +156,7 @@
         grid_spec=grid_spec,
         compiler_params=pltpu.CompilerParams(vmem_limit_bytes=VMEM_BYTES),
         cost_estimate=pl.CostEstimate(
-            flops=cells * NTIME, bytes_accessed=0, transcendentals=0
+            flops=cells * NTIME * weight, bytes_accessed=0, transcendentals=0
         ),
         name="friction",
     )(place, jnp.asarray(synth), jnp.asarray(analyse), *[b for chunk in flows for b in chunk])
@@ -236,7 +237,7 @@
     high = low + count * LANES
 
     def offset_of(block):
-        return offset_ref[block // LANES, block % LANES]
+        return offset_ref[block >> 7, block & (LANES - 1)]
 
     begin = jnp.int32(0)
     end = jnp.int32(0)
@@ -246,7 +247,7 @@
     end = jnp.maximum(end, begin)
 
     def copies(block):
-        slot = block % 2
+        slot = block & 1
         rows = pl.ds(pl.multiple_of(block * SUB, SUB), SUB)
         return (
             pltpu.make_async_copy(
@@ -275,7 +276,7 @@
 
         for copy in copies(block):
             copy.wait()
-        slot = block % 2
+        slot = block & 1
         for lane_tile in range(lane_tiles):
             lanes = slice(lane_tile * LANES, (lane_tile + 1) * LANES)
             turned = [
@@ -283,8 +284,9 @@
             ]
             start = block * per_block + lane_tile * SUB
             index = index_ref[pl.ds(pl.multiple_of(start, SUB), SUB), :]
+            following = offset_of(start)
             for r in range(SUB):
-                offset = offset_of(start + r)
+                offset = following
                 following = offset_of(start + r + 1)
                 shift = offset & (LANES - 1)
                 crossing = (following >> 7) > (offset >> 7)
@@ -514,7 +516,7 @@
         speeds = [[], []]
         for r in range(SUB):
             at = (row_block * lane_tiles + lane_tile) * SUB + r
-            tile = offset_ref[at // LANES, at % LANES] >> 7
+            tile = offset_ref[at >> 7, at & (LANES - 1)] >> 7
             found = []
             for which in range(2):
                 start = pl.multiple_of(table_ref[first_ref[1] * 2, tile + which], SUB)
@@ -768,26 +770,18 @@
         )
         return spread_out(flows), token[0, 0]
 
-    def through(flows, token):
-        *back, token = friction_call(place + token, flows, coefs)
+    def through(flows, token, weight):
+        *back, token = friction_call(place + token, flows, coefs, weight)
         return spread_out(back), token[0, 0]
 
     flows = []
     tile = 0
     token = jnp.int32(0)
-    for chunk, tiles in enumerate(chunk_tiles):
-        waited = flows[0][1:] if chunk == 2 else ()
-        flow, token = packed(tile, tiles, token, waited)
+    for tiles in chunk_tiles[:-1]:
+        flow, token = packed(tile, tiles, token)
         flows.append(flow)
         tile += groups * tiles
-    above, below, slabs = halo(direction, wet_mask, water_depth, flows[-1][:1])
-    result, prepared = prepare_call(
-        scalars, direction, wet_mask, water_depth, above, below, slabs
-    )
-    back, token = through(flows[:-1], prepared[0, 0])
-    backs = [back]
-    back, token = through(flows[-1:], token)
-    backs.append(back)
+
     loop_cells = groups * LOOP_TILES * LANES
     beyond = offsets[blocks] + token - fixed * LANES
     loops = jnp.maximum(beyond + loop_cells - 1, 0) // loop_cells
@@ -795,7 +789,7 @@
     def more(state):
         done, held = state
         flow, _ = packed(fixed + done * groups * LOOP_TILES, LOOP_TILES, 0)
-        back, _ = through([flow], 0)
+        back, _ = through([flow], 0, 1)
         held = lax.dynamic_update_slice_in_dim(
             held, jnp.concatenate(back, axis=0)[None], done, 0
         )
@@ -803,7 +797,18 @@
 
     rows = groups * piece_rows(LOOP_TILES, coefs)
     extra = jnp.zeros((steps, rows, LANES), jnp.float32)
-    _, extra = lax.while_loop(lambda state: state[0] < loops, more, (jnp.int32(0), extra))
+    done, extra = lax.while_loop(lambda state: state[0] < loops, more, (jnp.int32(0), extra))
+
+    token = token + jnp.minimum(done, 0)
+    flows.append(packed(tile, chunk_tiles[-1], token, flows[0][1:])[0])
+    above, below, slabs = halo(direction, wet_mask, water_depth, flows[-1][:1])
+    result, prepared = prepare_call(
+        scalars, direction, wet_mask, water_depth, above, below, slabs
+    )
+    back, token = through(flows[:-1], prepared[0, 0], 1)
+    backs = [back]
+    back, token = through(flows[-1:], token, LATE_WEIGHT)
+    backs.append(back)
 
     arrays = (wet_mask, drag_factor, cells)
     pieces = []

time: 235 us -> 246 us (1.047)
  waiting for transfers between devices: 110 us -> 120 us
  Pallas kernels: 84.4 us -> 88 us
    ppermute x19, waiting for transfers between devices: 110 us -> 120 us  [shifted(): return lax.ppermute(block, axis, pairs)]
    pallas_call x3, Pallas kernels: 20 us -> 22.6 us  [pack_call(): pl.pallas_call(lambda *refs: pack_kernel(groups, coefs, tiles, len(waited...]
  transfers between devices with their start and end apart: 19 -> 19, of which waited for: 11 -> 8; matrix products, arithmetic and copies ran while one was open for 3% -> 3% of each run, Pallas kernels for 30% -> 31%
where the time goes in v6:
time: 246 us; the launch traced here: 244 us
  waiting for transfers between devices  120 us (49%)
  Pallas kernels  88 us (36%)
  starting transfers between devices  21 us (9%)
  local copies, waits for them, and re-layouts  8.68 us (4%)
  between operations  4.63 us (2%)
    ppermute x19, waiting for transfers between devices, shifted(): return lax.ppermute(block, axis, pairs)  120 us
    pallas_call x2, Pallas kernels, friction_call(): pl.pallas_call(lambda *refs: friction_kernel(groups, coefs, chunk_tiles,...  29.6 us
    pallas_call x3, Pallas kernels, pack_call(): pl.pallas_call(lambda *refs: pack_kernel(groups, coefs, tiles, len(waited...  22.6 us
    ppermute x19, starting transfers between devices, shifted(): return lax.ppermute(block, axis, pairs)  21 us
    pallas_call x2, Pallas kernels, finish_call(): pl.pallas_call(kernel, out_shape=jax.ShapeDtypeStruct(result.shape, jnp.f...  19.9 us
    pallas_call x1, Pallas kernels, prepare_call(): pl.pallas_call(lambda *refs: prepare_kernel(coefs, *refs), out_shape=[jax...  14.3 us
  transfers between devices with their start and end apart: 19, of which 8 were waited for; matrix products, arithmetic and copies ran while one was open for 3% of the time, Pallas kernels for 31%

profile of v6, /device:TPU:12, one launch (start us, length us, event | category | flops | bytes accessed | tf_op | source)
XLA Modules:
  0.0 244.2 jit_solution(5490450198891492699)
XLA Ops:
  0.0 0.9 copy-done
  1.0 1.0 index.1
  2.0 0.1 pad_add_fusion.3.refs_0_
  2.0 4.7 %pack.7 = (f32[12,32,128]{2,1,0:T(8,128)S(1)}, f32[12,32,128]{2,1,0:T(8,128)S(1)}, f32[12,32,128]{2,1,0:T(8,128)}, f32[12,32,128]{2,1,0:T(8,128)}, s32[8,128]{1,0:T(8,128)S(1)}) custom-call(s32[2]{0:T(128)S(1)} %pad_add_fusion.3.refs_0_, s32[8,128]{1,0:T(8,128)S(1)} %get-tuple-element.337.refs_1_.offset_ref, s32[512,128]{1,0:T(8,128)S(1)} %get-tuple-element.338.refs_2_, ...), custom_call_target="tpu_custom_call" | custom-call | bytes 6291456 | tf_op jit(solution)/shard_map/pack/pallas_call | solution.py:342
  6.8 0.7 copy-done.8
  7.4 1.6 collective-permute-start.6
  9.0 1.2 collective-permute-start.7
  10.2 0.5 slice.42
  10.8 0.5 slice.40
  12.0 11.0 %pack.8 = (f32[60,32,128]{2,1,0:T(8,128)S(1)}, f32[60,32,128]{2,1,0:T(8,128)S(1)}, f32[60,32,128]{2,1,0:T(8,128)S(1)}, f32[60,32,128]{2,1,0:T(8,128)S(1)}, s32[8,128]{1,0:T(8,128)S(1)}) custom-call(s32[2]{0:T(128)S(1)} %pad_add_fusion.4.refs_0_, s32[8,128]{1,0:T(8,128)S(1)} %get-tuple-element.337.refs_1_.offset_ref, s32[512,128]{1,0:T(8,128)} %copy-done.15, ...), custom_call_target="tpu_custom_call" | custom-call | bytes 31457280 | tf_op jit(solution)/shard_map/pack/pallas_call | solution.py:342
  23.1 1.0 copy-done.11
  24.0 0.9 copy-done.12
  25.0 0.5 slice.41
  26.7 1.1 broadcast_in_dim.15
  27.8 1.8 collective-permute-start.8
  29.6 0.2 collective-permute-start.13
  29.8 3.5 %collective-permute-start.14 = (f32[60,32,128]{2,1,0:T(8,128)}, f32[60,32,128]{2,1,0:T(8,128)}, u32[]{:S(2)}, u32[]{:S(2)}) collective-permute-start(f32[60,32,128]{2,1,0:T(8,128)} %copy-done.12), channel_id=1, source_target_pairs={{0,16},{8,24},{16,0},{24,8},{1,17},{9,25},{17,1},{25,9},{2,18},{10... | collective-permute-start | bytes 2949128 | tf_op jit(solution)/shard_map/ppermute | solution.py:636
  34.0 43.6 %collective-permute-done.8.refs_7_.refs_6_ = f32[12,32,128]{2,1,0:T(8,128)} collective-permute-done((f32[12,32,128]{2,1,0:T(8,128)}, f32[12,32,128]{2,1,0:T(8,128)}, u32[]{:S(2)}, u32[]{:S(2)}) %collective-permute-start.8) | collective-permute-done | bytes 196640 | tf_op jit(solution)/shard_map/ppermute | solution.py:636
  77.7 6.9 %pack.9 = (f32[25,32,128]{2,1,0:T(8,128)S(1)}, f32[25,32,128]{2,1,0:T(8,128)}, f32[25,32,128]{2,1,0:T(8,128)}, f32[25,32,128]{2,1,0:T(8,128)}, s32[8,128]{1,0:T(8,128)}) custom-call(s32[2]{0:T(128)S(1)} %pad_add_fusion.5.refs_0_, s32[8,128]{1,0:T(8,128)S(1)} %get-tuple-element.410, s32[512,128]{1,0:T(8,128)} %get-tuple-element.404, ...), custom_call_target="tpu_custom_call" | custom-call | bytes 13107200 | tf_op jit(solution)/shard_map/pack/pallas_call | solution.py:342
  84.6 0.6 edges.1
  85.2 0.2 copy-done.6
  85.5 3.7 %collective-permute-start.9 = (f32[2,8,512]{2,1,0:T(8,128)S(1)}, f32[2,8,512]{2,1,0:T(8,128)S(1)}, u32[]{:S(2)}, u32[]{:S(2)}) collective-permute-start(f32[2,8,512]{2,1,0:T(8,128)S(1)} %get-tuple-element.177), channel_id=1, source_target_pairs={{0,4},{1,5},{2,6},{3,7},{8,12},{9,13},{10,14},{11,15},{16,20},{17,... | collective-permute-start | bytes 98312 | tf_op jit(solution)/shard_map/ppermute | solution.py:636
  89.1 1.3 collective-permute-start.10
  90.4 0.3 collective-permute-done.9.refs_9_
  90.7 0.1 maximum_bitcast_fusion.2
  90.8 4.2 %collective-permute-done.10.refs_10_ = f32[2,8,512]{2,1,0:T(8,128)S(1)} collective-permute-done((f32[2,8,512]{2,1,0:T(8,128)S(1)}, f32[2,8,512]{2,1,0:T(8,128)S(1)}, u32[]{:S(2)}, u32[]{:S(2)}) %collective-permute-start.10) | collective-permute-done | bytes 32800 | tf_op jit(solution)/shard_map/ppermute | solution.py:636
  95.0 0.1 maximum_bitcast_fusion.1
  95.2 3.0 %collective-permute-done.11 = f32[3,8,128]{2,1,0:T(8,128)S(1)} collective-permute-done((f32[3,8,128]{2,1,0:T(8,128)S(1)}, f32[3,8,128]{2,1,0:T(8,128)S(1)}, u32[]{:S(2)}, u32[]{:S(2)}) %collective-permute-start.11) | collective-permute-done | bytes 12320 | tf_op jit(solution)/shard_map/ppermute | solution.py:636
  98.2 0.7 collective-permute-start.21
  98.9 0.1 slice.39
  99.1 0.9 broadcast_in_dim.16.refs_11_
  100.0 14.3 %prepare.1 = (f32[3,8,128,512]{3,2,1,0:T(8,128)}, s32[8,128]{1,0:T(8,128)S(1)}) custom-call(f32[6]{0:T(128)S(1)} %pad_maximum_fusion.3.refs_0_.scalars_ref, f32[3,8,128,512]{3,2,1,0:T(8,128)} %get-tuple-element.402, f32[3,8,128,512]{3,2,1,0:T(8,128)} %get-tuple-element.402, f32[3,8,128,512]{3,2,1,0:T(8,128)} %get-tuple-element.402, ...), custom_call_target="tpu_custom_call" | custom-call | flops 524288 | tf_op jit(solution)/shard_map/prepare/pallas_call | solution.py:464
  114.3 0.6 slice.49
  115.6 20.2 %collective-permute-done.14.refs_9_ = f32[60,32,128]{2,1,0:T(8,128)} collective-permute-done((f32[60,32,128]{2,1,0:T(8,128)}, f32[60,32,128]{2,1,0:T(8,128)}, u32[]{:S(2)}, u32[]{:S(2)}) %collective-permute-start.14) | collective-permute-done | bytes 983072 | tf_op jit(solution)/shard_map/ppermute | solution.py:636
  135.8 1.7 collective-permute-done.15.refs_10_
  137.4 21.0 %friction.6 = (f32[1224,128]{1,0:T(8,128)S(1)}, f32[1224,128]{1,0:T(8,128)S(1)}, f32[1224,128]{1,0:T(8,128)}, f32[1224,128]{1,0:T(8,128)}, s32[8,128]{1,0:T(8,128)S(1)}) custom-call(s32[1]{0:T(128)S(6)} %add.52.refs_0_, bf16[4,256,96]{2,1,0:T(8,128)(2,1)S(1)} %copy-done.17, bf16[4,64,256]{2,1,0:T(8,128)(2,1)S(1)} %copy-done.19, ...), custom_call_target="tpu_custom_call" | custom-call | flops 9437184 | tf_op jit(solution)/shard_map/friction/pallas_call | solution.py:152
  158.5 0.6 slice.50
  159.8 1.8 collective-permute-start.17
  161.6 1.9 collective-permute-start.18
  163.5 8.6 %friction.7 = (f32[432,128]{1,0:T(8,128)S(1)}, f32[432,128]{1,0:T(8,128)}, f32[432,128]{1,0:T(8,128)}, f32[432,128]{1,0:T(8,128)}, s32[8,128]{1,0:T(8,128)}) custom-call(s32[1]{0:T(128)S(6)} %add.53.refs_0_, bf16[4,256,96]{2,1,0:T(8,128)(2,1)S(1)} %copy-done.17, bf16[4,64,256]{2,1,0:T(8,128)(2,1)S(1)} %copy-done.19, f32[25,32,128]{2,1,0:T(8,128)S(1)} %copy-done.7, ...), custom_call_target="tpu_custom_call" | custom-call | flops 6710886400 | tf_op jit(solution)/shard_map/friction/pallas_call | solution.py:152
  172.1 0.1 collective-permute-start.22
  172.2 3.0 %collective-permute-start.23 = (f32[432,128]{1,0:T(8,128)}, f32[432,128]{1,0:T(8,128)}, u32[]{:S(2)}, u32[]{:S(2)}) collective-permute-start(f32[432,128]{1,0:T(8,128)} %get-tuple-element.198), channel_id=1, source_target_pairs={{0,16},{8,24},{16,0},{24,8},{1,17},{9,25},{17,1},{25,9},{2,18},{10... | collective-permute-start | bytes 663560 | tf_op jit(solution)/shard_map/ppermute | solution.py:636
  175.2 28.1 %collective-permute-done.16.refs_5_ = f32[1224,128]{1,0:T(8,128)S(1)} collective-permute-done((f32[1224,128]{1,0:T(8,128)S(1)}, f32[1224,128]{1,0:T(8,128)S(1)}, u32[]{:S(2)}, u32[]{:S(2)}) %collective-permute-start.16) | collective-permute-done | bytes 626720 | tf_op jit(solution)/shard_map/ppermute | solution.py:636
  203.3 0.6 fusion.1
  204.5 0.6 pad_add_fusion.1
  205.1 19.1 %collective-permute-done.17.refs_6_ = f32[1224,128]{1,0:T(8,128)S(1)} collective-permute-done((f32[1224,128]{1,0:T(8,128)}, f32[1224,128]{1,0:T(8,128)S(1)}, u32[]{:S(2)}, u32[]{:S(2)}) %collective-permute-start.17) | collective-permute-done | bytes 626720 | tf_op jit(solution)/shard_map/ppermute | solution.py:636
  224.2 12.4 %finish.2.refs_3_ = f32[3,8,128,512]{3,2,1,0:T(8,128)} custom-call(s32[3]{0:T(128)S(1)} %get-tuple-element.266.first_ref, s32[8,128]{1,0:T(8,128)S(1)} %get-tuple-element.410, s32[8,640]{1,0:T(8,128)S(1)} %copy-done.10, f32[6]{0:T(128)S(1)} %pad_maximum_fusion.3.refs_0_.scalars_ref, s32[128,512]{1,0:T(8,128)S(1)} %copy-done.1, ...), custom_call_target="tpu_custom_call", output_to_operand_aliasing={{}: (7, {})} | custom-call | bytes 9437184 | tf_op jit(solution)/shard_map/finish/pallas_call | solution.py:613
  236.6 7.5 %finish.3 = f32[3,8,128,512]{3,2,1,0:T(8,128)} custom-call(s32[3]{0:T(128)S(1)} %get-tuple-element.265.first_ref, s32[8,128]{1,0:T(8,128)S(1)} %get-tuple-element.410, s32[8,640]{1,0:T(8,128)S(1)} %copy-done.10, f32[6]{0:T(128)S(1)} %pad_maximum_fusion.3.refs_0_.scalars_ref, s32[128,512]{1,0:T(8,128)S(1)} %copy-done.1, ...), custom_call_target="tpu_custom_call", output_to_operand_aliasing={{}: (7, {})} | custom-call | bytes 9437184 | tf_op jit(solution)/shard_map/finish/pallas_call | solution.py:613
  (66 shorter events, 0.7 us)
Async XLA Ops:
  0.0 0.9 copy-start
  2.0 4.8 %copy-start.15 = (s32[512,128]{1,0:T(8,128)}, s32[512,128]{1,0:T(8,128)S(1)}, u32[]{:S(2)}) copy-start(s32[512,128]{1,0:T(8,128)S(1)} %get-tuple-element.338.refs_2_) | copy-start | bytes 786436
  6.7 0.7 copy-start.8
  7.4 26.5 %collective-permute-start.6 = (f32[12,32,128]{2,1,0:T(8,128)S(1)}, f32[12,32,128]{2,1,0:T(8,128)S(1)}, u32[]{:S(2)}, u32[]{:S(2)}) collective-permute-start(f32[12,32,128]{2,1,0:T(8,128)S(1)} %get-tuple-element.173), channel_id=1, source_target_pairs={{0,8},{8,16},{16,24},{24,0},{1,9},{9,17},{17,25},{25,1},{2,10},{10... | collective-permute-start | bytes 589832 | tf_op jit(solution)/shard_map/ppermute | solution.py:636
  9.0 25.0 %collective-permute-start.7 = (f32[12,32,128]{2,1,0:T(8,128)}, f32[12,32,128]{2,1,0:T(8,128)S(1)}, u32[]{:S(2)}, u32[]{:S(2)}) collective-permute-start(f32[12,32,128]{2,1,0:T(8,128)} %get-tuple-element.174), channel_id=1, source_target_pairs={{0,16},{8,24},{16,0},{24,8},{1,17},{9,25},{17,1},{25,9},{2,18},{10... | collective-permute-start | bytes 589832 | tf_op jit(solution)/shard_map/ppermute | solution.py:636
  23.1 1.0 copy-start.11
  24.0 1.0 copy-start.12
  24.0 3.8 %copy-start.13 = (f32[60,32,128]{2,1,0:T(8,128)}, f32[60,32,128]{2,1,0:T(8,128)S(1)}, u32[]{:S(2)}) copy-start(f32[60,32,128]{2,1,0:T(8,128)S(1)} %get-tuple-element.185) | copy-start | bytes 2949124
  24.0 3.8 %copy-start.18 = (bf16[4,64,256]{2,1,0:T(8,128)(2,1)S(1)}, bf16[4,64,256]{2,1,0:T(8,128)(2,1)}, u32[]{:S(2)}) copy-start(bf16[4,64,256]{2,1,0:T(8,128)(2,1)} %constant.93.clone.refs_2_) | copy-start | bytes 393220
  27.8 49.9 %collective-permute-start.8 = (f32[12,32,128]{2,1,0:T(8,128)}, f32[12,32,128]{2,1,0:T(8,128)}, u32[]{:S(2)}, u32[]{:S(2)}) collective-permute-start(f32[12,32,128]{2,1,0:T(8,128)} %get-tuple-element.175), channel_id=1, source_target_pairs={{0,24},{8,0},{16,8},{24,16},{1,25},{9,1},{17,9},{25,17},{2,26},{10... | collective-permute-start | bytes 589832 | tf_op jit(solution)/shard_map/ppermute | solution.py:636
  29.6 68.6 %collective-permute-start.13 = (f32[60,32,128]{2,1,0:T(8,128)}, f32[60,32,128]{2,1,0:T(8,128)S(1)}, u32[]{:S(2)}, u32[]{:S(2)}) collective-permute-start(f32[60,32,128]{2,1,0:T(8,128)} %copy-done.13), channel_id=1, source_target_pairs={{0,8},{8,16},{16,24},{24,0},{1,9},{9,17},{17,25},{25,1},{2,10},{10... | collective-permute-start | bytes 2949128 | tf_op jit(solution)/shard_map/ppermute | solution.py:636
  29.8 105.9 %collective-permute-start.14 = (f32[60,32,128]{2,1,0:T(8,128)}, f32[60,32,128]{2,1,0:T(8,128)}, u32[]{:S(2)}, u32[]{:S(2)}) collective-permute-start(f32[60,32,128]{2,1,0:T(8,128)} %copy-done.12), channel_id=1, source_target_pairs={{0,16},{8,24},{16,0},{24,8},{1,17},{9,25},{17,1},{25,9},{2,18},{10... | collective-permute-start | bytes 2949128 | tf_op jit(solution)/shard_map/ppermute | solution.py:636
  34.0 50.6 %copy-start.1 = (s32[128,512]{1,0:T(8,128)S(1)}, s32[128,512]{1,0:T(8,128)}, u32[]{:S(2)}) copy-start(s32[128,512]{1,0:T(8,128)} %refs_0_.5) | copy-start | bytes 786436
  34.0 50.6 %copy-start.2 = (f32[128,512]{1,0:T(8,128)S(1)}, f32[128,512]{1,0:T(8,128)}, u32[]{:S(2)}) copy-start(f32[128,512]{1,0:T(8,128)} %refs_8_.1) | copy-start | bytes 786436
  34.0 103.4 %collective-permute-start.15 = (f32[60,32,128]{2,1,0:T(8,128)}, f32[60,32,128]{2,1,0:T(8,128)}, u32[]{:S(2)}, u32[]{:S(2)}) collective-permute-start(f32[60,32,128]{2,1,0:T(8,128)} %copy-done.11), channel_id=1, source_target_pairs={{0,24},{8,0},{16,8},{24,16},{1,25},{9,1},{17,9},{25,17},{2,26},{10... | collective-permute-start | bytes 2949128 | tf_op jit(solution)/shard_map/ppermute | solution.py:636
  34.0 50.5 %copy-start.4 = (f32[12,32,128]{2,1,0:T(8,128)}, f32[12,32,128]{2,1,0:T(8,128)S(1)}, u32[]{:S(2)}) copy-start(f32[12,32,128]{2,1,0:T(8,128)S(1)} %collective-permute-done.7.refs_6_.refs_5_) | copy-start | bytes 589828
  77.7 6.9 %copy-start.14 = (f32[3,8,128,512]{3,2,1,0:T(8,128)S(1)}, f32[3,8,128,512]{3,2,1,0:T(8,128)}, u32[]{:S(2)}) copy-start(f32[3,8,128,512]{3,2,1,0:T(8,128)} %get-tuple-element.402) | copy-start | bytes 18874372
  84.6 0.8 copy-start.6
  85.5 5.2 %collective-permute-start.9 = (f32[2,8,512]{2,1,0:T(8,128)S(1)}, f32[2,8,512]{2,1,0:T(8,128)S(1)}, u32[]{:S(2)}, u32[]{:S(2)}) collective-permute-start(f32[2,8,512]{2,1,0:T(8,128)S(1)} %get-tuple-element.177), channel_id=1, source_target_pairs={{0,4},{1,5},{2,6},{3,7},{8,12},{9,13},{10,14},{11,15},{16,20},{17,... | collective-permute-start | bytes 98312 | tf_op jit(solution)/shard_map/ppermute | solution.py:636
  89.1 5.8 %collective-permute-start.10 = (f32[2,8,512]{2,1,0:T(8,128)S(1)}, f32[2,8,512]{2,1,0:T(8,128)S(1)}, u32[]{:S(2)}, u32[]{:S(2)}) collective-permute-start(f32[2,8,512]{2,1,0:T(8,128)S(1)} %get-tuple-element.178), channel_id=1, source_target_pairs={{4,0},{5,1},{6,2},{7,3},{12,8},{13,9},{14,10},{15,11},{20,16},{21,... | collective-permute-start | bytes 98312 | tf_op jit(solution)/shard_map/ppermute | solution.py:636
  90.8 4.3 %collective-permute-start.12 = (f32[3,8,128]{2,1,0:T(8,128)S(1)}, f32[3,8,128]{2,1,0:T(8,128)S(1)}, u32[]{:S(2)}, u32[]{:S(2)}) collective-permute-start(f32[3,8,128]{2,1,0:T(8,128)S(1)} %pad_maximum_fusion.2), channel_id=1, source_target_pairs={{0,3},{1,0},{2,1},{3,2},{4,7},{5,4},{6,5},{7,6},{8,11},{9,8},{10,9... | collective-permute-start | bytes 36872 | tf_op jit(solution)/shard_map/ppermute | solution.py:636
  95.1 3.1 %collective-permute-start.11 = (f32[3,8,128]{2,1,0:T(8,128)S(1)}, f32[3,8,128]{2,1,0:T(8,128)S(1)}, u32[]{:S(2)}, u32[]{:S(2)}) collective-permute-start(f32[3,8,128]{2,1,0:T(8,128)S(1)} %pad_maximum_fusion.1), channel_id=1, source_target_pairs={{0,1},{1,2},{2,3},{3,0},{4,5},{5,6},{6,7},{7,4},{8,9},{9,10},{10,1... | collective-permute-start | bytes 36872 | tf_op jit(solution)/shard_map/ppermute | solution.py:636
  95.1 66.5 %collective-permute-start.19 = (f32[25,32,128]{2,1,0:T(8,128)}, f32[25,32,128]{2,1,0:T(8,128)}, u32[]{:S(2)}, u32[]{:S(2)}) collective-permute-start(f32[25,32,128]{2,1,0:T(8,128)} %get-tuple-element.193), channel_id=1, source_target_pairs={{0,8},{8,16},{16,24},{24,0},{1,9},{9,17},{17,25},{25,1},{2,10},{10... | collective-permute-start | bytes 1228808 | tf_op jit(solution)/shard_map/ppermute | solution.py:636
  98.2 65.3 %collective-permute-start.20 = (f32[25,32,128]{2,1,0:T(8,128)}, f32[25,32,128]{2,1,0:T(8,128)}, u32[]{:S(2)}, u32[]{:S(2)}) collective-permute-start(f32[25,32,128]{2,1,0:T(8,128)} %get-tuple-element.194), channel_id=1, source_target_pairs={{0,16},{8,24},{16,0},{24,8},{1,17},{9,25},{17,1},{25,9},{2,18},{10... | collective-permute-start | bytes 1228808 | tf_op jit(solution)/shard_map/ppermute | solution.py:636
  98.2 65.3 %collective-permute-start.21 = (f32[25,32,128]{2,1,0:T(8,128)}, f32[25,32,128]{2,1,0:T(8,128)}, u32[]{:S(2)}, u32[]{:S(2)}) collective-permute-start(f32[25,32,128]{2,1,0:T(8,128)} %get-tuple-element.195), channel_id=1, source_target_pairs={{0,24},{8,0},{16,8},{24,16},{1,25},{9,1},{17,9},{25,17},{2,26},{10... | collective-permute-start | bytes 1228808 | tf_op jit(solution)/shard_map/ppermute | solution.py:636
  100.0 37.4 %copy-start.5 = (f32[12,32,128]{2,1,0:T(8,128)S(1)}, f32[12,32,128]{2,1,0:T(8,128)}, u32[]{:S(2)}) copy-start(f32[12,32,128]{2,1,0:T(8,128)} %copy-done.4) | copy-start | bytes 589828
  100.0 37.4 %copy-start.9 = (f32[12,32,128]{2,1,0:T(8,128)S(1)}, f32[12,32,128]{2,1,0:T(8,128)}, u32[]{:S(2)}) copy-start(f32[12,32,128]{2,1,0:T(8,128)} %copy-done.8) | copy-start | bytes 589828
  100.0 37.4 %copy-start.17 = (bf16[4,256,96]{2,1,0:T(8,128)(2,1)S(1)}, bf16[4,256,96]{2,1,0:T(8,128)(2,1)}, u32[]{:S(2)}) copy-start(bf16[4,256,96]{2,1,0:T(8,128)(2,1)} %get-tuple-element.405) | copy-start | bytes 589828
  100.0 37.4 %copy-start.19 = (bf16[4,64,256]{2,1,0:T(8,128)(2,1)S(1)}, bf16[4,64,256]{2,1,0:T(8,128)(2,1)}, u32[]{:S(2)}) copy-start(bf16[4,64,256]{2,1,0:T(8,128)(2,1)} %constant.93.clone.refs_2_) | copy-start | bytes 393220
  137.4 26.1 %copy-start.7 = (f32[25,32,128]{2,1,0:T(8,128)S(1)}, f32[25,32,128]{2,1,0:T(8,128)}, u32[]{:S(2)}) copy-start(f32[25,32,128]{2,1,0:T(8,128)} %copy-done.6) | copy-start | bytes 1228804
  159.7 43.6 %collective-permute-start.16 = (f32[1224,128]{1,0:T(8,128)S(1)}, f32[1224,128]{1,0:T(8,128)S(1)}, u32[]{:S(2)}, u32[]{:S(2)}) collective-permute-start(f32[1224,128]{1,0:T(8,128)S(1)} %get-tuple-element.189), channel_id=1, source_target_pairs={{0,8},{8,16},{16,24},{24,0},{1,9},{9,17},{17,25},{25,1},{2,10},{10... | collective-permute-start | bytes 1880072 | tf_op jit(solution)/shard_map/ppermute | solution.py:636
  159.8 64.4 %collective-permute-start.17 = (f32[1224,128]{1,0:T(8,128)}, f32[1224,128]{1,0:T(8,128)S(1)}, u32[]{:S(2)}, u32[]{:S(2)}) collective-permute-start(f32[1224,128]{1,0:T(8,128)} %get-tuple-element.190), channel_id=1, source_target_pairs={{0,16},{8,24},{16,0},{24,8},{1,17},{9,25},{17,1},{25,9},{2,18},{10... | collective-permute-start | bytes 1880072 | tf_op jit(solution)/shard_map/ppermute | solution.py:636
  161.6 62.6 %copy-start.3 = (f32[128,512]{1,0:T(8,128)S(1)}, f32[128,512]{1,0:T(8,128)}, u32[]{:S(2)}) copy-start(f32[128,512]{1,0:T(8,128)} %refs_1_.9) | copy-start | bytes 786436
  161.6 62.6 %copy-start.10 = (s32[8,640]{1,0:T(8,128)S(1)}, s32[8,640]{1,0:T(8,128)}, u32[]{:S(2)}) copy-start(s32[8,640]{1,0:T(8,128)} %constant.91.clone.table_ref) | copy-start | bytes 61444
  161.6 62.6 %collective-permute-start.18 = (f32[1224,128]{1,0:T(8,128)}, f32[1224,128]{1,0:T(8,128)S(1)}, u32[]{:S(2)}, u32[]{:S(2)}) collective-permute-start(f32[1224,128]{1,0:T(8,128)} %get-tuple-element.191), channel_id=1, source_target_pairs={{0,24},{8,0},{16,8},{24,16},{1,25},{9,1},{17,9},{25,17},{2,26},{10... | collective-permute-start | bytes 1880072 | tf_op jit(solution)/shard_map/ppermute | solution.py:636
  172.1 64.5 %collective-permute-start.22 = (f32[432,128]{1,0:T(8,128)}, f32[432,128]{1,0:T(8,128)}, u32[]{:S(2)}, u32[]{:S(2)}) collective-permute-start(f32[432,128]{1,0:T(8,128)} %get-tuple-element.197), channel_id=1, source_target_pairs={{0,8},{8,16},{16,24},{24,0},{1,9},{9,17},{17,25},{25,1},{2,10},{10... | collective-permute-start | bytes 663560 | tf_op jit(solution)/shard_map/ppermute | solution.py:636
  172.2 64.4 %collective-permute-start.23 = (f32[432,128]{1,0:T(8,128)}, f32[432,128]{1,0:T(8,128)}, u32[]{:S(2)}, u32[]{:S(2)}) collective-permute-start(f32[432,128]{1,0:T(8,128)} %get-tuple-element.198), channel_id=1, source_target_pairs={{0,16},{8,24},{16,0},{24,8},{1,17},{9,25},{17,1},{25,9},{2,18},{10... | collective-permute-start | bytes 663560 | tf_op jit(solution)/shard_map/ppermute | solution.py:636
  203.3 33.3 %collective-permute-start.24 = (f32[432,128]{1,0:T(8,128)}, f32[432,128]{1,0:T(8,128)}, u32[]{:S(2)}, u32[]{:S(2)}) collective-permute-start(f32[432,128]{1,0:T(8,128)} %get-tuple-element.199), channel_id=1, source_target_pairs={{0,24},{8,0},{16,8},{24,16},{1,25},{9,1},{17,9},{25,17},{2,26},{10... | collective-permute-start | bytes 663560 | tf_op jit(solution)/shard_map/ppermute | solution.py:636
  224.2 12.4 %copy-start.20 = (f32[4,544,128]{2,1,0:T(8,128)S(1)}, f32[4,544,128]{2,1,0:T(8,128)}, u32[]{:S(2)}) copy-start(f32[4,544,128]{2,1,0:T(8,128)} %get-tuple-element.200) | copy-start | bytes 3342340

commit v7 on v6

--- a/solution.py
+++ b/solution.py
@@ -19,7 +19,7 @@
 OMEGA_STEP = 0.25
 SPEED_SOFT = 0.01
 VMEM_BYTES = 48 * 1024 * 1024
-CHUNK_SHARES = (12, 60, 25)
+CHUNK_SHARES = (16, 50, 31)
 SHARE_UNITS = 128
 LOOP_TILES = 8
 PACK_COST = 16384
@@ -800,8 +800,8 @@
     done, extra = lax.while_loop(lambda state: state[0] < loops, more, (jnp.int32(0), extra))
 
     token = token + jnp.minimum(done, 0)
-    flows.append(packed(tile, chunk_tiles[-1], token, flows[0][1:])[0])
-    above, below, slabs = halo(direction, wet_mask, water_depth, flows[-1][:1])
+    flows.append(packed(tile, chunk_tiles[-1], token)[0])
+    above, below, slabs = halo(direction, wet_mask, water_depth, flows[0][1:] + flows[-1][:1])
     result, prepared = prepare_call(
         scalars, direction, wet_mask, water_depth, above, below, slabs
     )

time: 246 us -> 231 us (0.939)
  waiting for transfers between devices: 120 us -> 106 us
    ppermute x19, waiting for transfers between devices: 120 us -> 106 us  [shifted(): return lax.ppermute(block, axis, pairs)]
  transfers between devices with their start and end apart: 19 -> 19, of which waited for: 8 -> 8; matrix products, arithmetic and copies ran while one was open for 3% -> 3% of each run, Pallas kernels for 31% -> 32%
where the time goes in v7:
time: 231 us; the launch traced here: 229 us
  waiting for transfers between devices  106 us (46%)
  Pallas kernels  86.6 us (37%)
  starting transfers between devices  20.7 us (9%)
  local copies, waits for them, and re-layouts  8.1 us (4%)
  between operations  4.57 us (2%)
  other arithmetic  2.48 us (1%)
    ppermute x19, waiting for transfers between devices, shifted(): return lax.ppermute(block, axis, pairs)  106 us
    pallas_call x2, Pallas kernels, friction_call(): pl.pallas_call(lambda *refs: friction_kernel(groups, coefs, chunk_tiles,...  29.7 us
    pallas_call x3, Pallas kernels, pack_call(): pl.pallas_call(lambda *refs: pack_kernel(groups, coefs, tiles, len(waited...  21.7 us
    ppermute x19, starting transfers between devices, shifted(): return lax.ppermute(block, axis, pairs)  20.7 us
    pallas_call x2, Pallas kernels, finish_call(): pl.pallas_call(kernel, out_shape=jax.ShapeDtypeStruct(result.shape, jnp.f...  19.3 us
    pallas_call x1, Pallas kernels, prepare_call(): pl.pallas_call(lambda *refs: prepare_kernel(coefs, *refs), out_shape=[jax...  14.2 us
  transfers between devices with their start and end apart: 19, of which 8 were waited for; matrix products, arithmetic and copies ran while one was open for 3% of the time, Pallas kernels for 32%

profile of v7, /device:TPU:12, one launch (start us, length us, event | category | flops | bytes accessed | tf_op | source)
XLA Modules:
  0.0 228.6 jit_solution(8990615772266854883)
XLA Ops:
  0.0 0.9 copy-done
  1.0 1.0 index.1
  2.0 4.3 %pack.7 = (f32[16,32,128]{2,1,0:T(8,128)S(1)}, f32[16,32,128]{2,1,0:T(8,128)}, f32[16,32,128]{2,1,0:T(8,128)}, f32[16,32,128]{2,1,0:T(8,128)}, s32[8,128]{1,0:T(8,128)S(1)}) custom-call(s32[2]{0:T(128)S(1)} %pad_add_fusion.3.refs_0_, s32[8,128]{1,0:T(8,128)S(1)} %get-tuple-element.337.refs_1_.offset_ref, s32[512,128]{1,0:T(8,128)S(1)} %get-tuple-element.338.refs_2_, ...), custom_call_target="tpu_custom_call" | custom-call | bytes 8388608 | tf_op jit(solution)/shard_map/pack/pallas_call | solution.py:342
  6.4 1.6 collective-permute-start.6
  8.0 1.2 collective-permute-start.7
  9.2 0.5 slice.42
  9.7 0.5 slice.40
  11.0 9.1 %pack.8 = (f32[50,32,128]{2,1,0:T(8,128)S(1)}, f32[50,32,128]{2,1,0:T(8,128)S(1)}, f32[50,32,128]{2,1,0:T(8,128)S(1)}, f32[50,32,128]{2,1,0:T(8,128)}, s32[8,128]{1,0:T(8,128)S(1)}) custom-call(s32[2]{0:T(128)S(1)} %pad_add_fusion.4.refs_0_, s32[8,128]{1,0:T(8,128)S(1)} %get-tuple-element.337.refs_1_.offset_ref, s32[512,128]{1,0:T(8,128)S(1)} %get-tuple-element.338.refs_2_, ...), custom_call_target="tpu_custom_call" | custom-call | bytes 26214400 | tf_op jit(solution)/shard_map/pack/pallas_call | solution.py:342
  20.1 0.9 copy-done.7
  21.0 0.6 slice.41
  22.8 1.1 broadcast_in_dim.15
  23.9 0.7 copy-done.9
  24.6 1.8 collective-permute-start.8
  26.4 0.2 collective-permute-start.13
  26.7 3.5 %collective-permute-start.14 = (f32[50,32,128]{2,1,0:T(8,128)S(1)}, f32[50,32,128]{2,1,0:T(8,128)}, u32[]{:S(2)}, u32[]{:S(2)}) collective-permute-start(f32[50,32,128]{2,1,0:T(8,128)S(1)} %get-tuple-element.186), channel_id=1, source_target_pairs={{0,16},{8,24},{16,0},{24,8},{1,17},{9,25},{17,1},{25,9},{2,18},{10... | collective-permute-start | bytes 2457608 | tf_op jit(solution)/shard_map/ppermute | solution.py:636
  30.9 8.2 %pack.9 = (f32[31,32,128]{2,1,0:T(8,128)S(1)}, f32[31,32,128]{2,1,0:T(8,128)}, f32[31,32,128]{2,1,0:T(8,128)}, f32[31,32,128]{2,1,0:T(8,128)}, s32[8,128]{1,0:T(8,128)}) custom-call(s32[2]{0:T(128)S(1)} %pad_add_fusion.5.refs_0_, s32[8,128]{1,0:T(8,128)S(1)} %get-tuple-element.407, s32[512,128]{1,0:T(8,128)} %copy-done.9, ...), custom_call_target="tpu_custom_call" | custom-call | bytes 16252928 | tf_op jit(solution)/shard_map/pack/pallas_call | solution.py:342
  39.2 29.8 %collective-permute-done.8.refs_9_.refs_6_ = f32[16,32,128]{2,1,0:T(8,128)S(1)} collective-permute-done((f32[16,32,128]{2,1,0:T(8,128)}, f32[16,32,128]{2,1,0:T(8,128)S(1)}, u32[]{:S(2)}, u32[]{:S(2)}) %collective-permute-start.8) | collective-permute-done | bytes 262176 | tf_op jit(solution)/shard_map/ppermute | solution.py:636
  69.0 0.6 edges.1
  69.7 3.4 %collective-permute-start.9 = (f32[2,8,512]{2,1,0:T(8,128)S(1)}, f32[2,8,512]{2,1,0:T(8,128)S(1)}, u32[]{:S(2)}, u32[]{:S(2)}) collective-permute-start(f32[2,8,512]{2,1,0:T(8,128)S(1)} %get-tuple-element.177), channel_id=1, source_target_pairs={{0,4},{1,5},{2,6},{3,7},{8,12},{9,13},{10,14},{11,15},{16,20},{17,... | collective-permute-start | bytes 98312 | tf_op jit(solution)/shard_map/ppermute | solution.py:636
  73.1 1.3 collective-permute-start.10
  74.4 0.3 collective-permute-done.9.refs_9_
  74.7 0.1 maximum_bitcast_fusion.2
  74.8 4.2 %collective-permute-done.10.refs_10_ = f32[2,8,512]{2,1,0:T(8,128)S(1)} collective-permute-done((f32[2,8,512]{2,1,0:T(8,128)S(1)}, f32[2,8,512]{2,1,0:T(8,128)S(1)}, u32[]{:S(2)}, u32[]{:S(2)}) %collective-permute-start.10) | collective-permute-done | bytes 32800 | tf_op jit(solution)/shard_map/ppermute | solution.py:636
  79.0 0.1 maximum_bitcast_fusion.1
  79.2 3.0 %collective-permute-done.11 = f32[3,8,128]{2,1,0:T(8,128)S(1)} collective-permute-done((f32[3,8,128]{2,1,0:T(8,128)S(1)}, f32[3,8,128]{2,1,0:T(8,128)S(1)}, u32[]{:S(2)}, u32[]{:S(2)}) %collective-permute-start.11) | collective-permute-done | bytes 12320 | tf_op jit(solution)/shard_map/ppermute | solution.py:636
  82.2 0.6 copy-done.16
  82.8 0.6 collective-permute-start.21
  83.4 0.1 pad_maximum_fusion.3.refs_0_.scalars_ref
  83.5 0.7 pad_maximum_fusion
  84.3 0.9 broadcast_in_dim.16.refs_11_
  85.1 14.2 %prepare.1 = (f32[3,8,128,512]{3,2,1,0:T(8,128)}, s32[8,128]{1,0:T(8,128)S(1)}) custom-call(f32[6]{0:T(128)S(1)} %pad_maximum_fusion.3.refs_0_.scalars_ref, f32[3,8,128,512]{3,2,1,0:T(8,128)} %get-tuple-element.400, f32[3,8,128,512]{3,2,1,0:T(8,128)} %get-tuple-element.400, f32[3,8,128,512]{3,2,1,0:T(8,128)} %get-tuple-element.400, ...), custom_call_target="tpu_custom_call" | custom-call | flops 524288 | tf_op jit(solution)/shard_map/prepare/pallas_call | solution.py:464
  99.4 0.6 slice.49
  100.6 23.6 %collective-permute-done.14.refs_9_ = f32[50,32,128]{2,1,0:T(8,128)} collective-permute-done((f32[50,32,128]{2,1,0:T(8,128)S(1)}, f32[50,32,128]{2,1,0:T(8,128)}, u32[]{:S(2)}, u32[]{:S(2)}) %collective-permute-start.14) | collective-permute-done | bytes 819232 | tf_op jit(solution)/shard_map/ppermute | solution.py:636
  124.2 2.0 collective-permute-done.15.refs_10_
  126.2 19.5 %friction.6 = (f32[1128,128]{1,0:T(8,128)S(1)}, f32[1128,128]{1,0:T(8,128)S(1)}, f32[1128,128]{1,0:T(8,128)}, f32[1128,128]{1,0:T(8,128)}, s32[8,128]{1,0:T(8,128)S(1)}) custom-call(s32[1]{0:T(128)S(6)} %add.52.refs_0_, bf16[4,256,96]{2,1,0:T(8,128)(2,1)S(1)} %copy-done.11, bf16[4,64,256]{2,1,0:T(8,128)(2,1)S(1)} %copy-done.13, ...), custom_call_target="tpu_custom_call" | custom-call | flops 8650752 | tf_op jit(solution)/shard_map/friction/pallas_call | solution.py:152
  145.6 0.5 slice.50
  146.9 1.6 collective-permute-start.17
  148.4 1.9 collective-permute-start.18
  150.4 10.3 %friction.7 = (f32[528,128]{1,0:T(8,128)S(1)}, f32[528,128]{1,0:T(8,128)}, f32[528,128]{1,0:T(8,128)}, f32[528,128]{1,0:T(8,128)}, s32[8,128]{1,0:T(8,128)}) custom-call(s32[1]{0:T(128)S(6)} %add.53.refs_0_, bf16[4,256,96]{2,1,0:T(8,128)(2,1)S(1)} %copy-done.11, bf16[4,64,256]{2,1,0:T(8,128)(2,1)S(1)} %copy-done.13, f32[31,32,128]{2,1,0:T(8,128)S(1)} %copy-done.5, ...), custom_call_target="tpu_custom_call" | custom-call | flops 8321499136 | tf_op jit(solution)/shard_map/friction/pallas_call | solution.py:152
  160.7 0.1 collective-permute-start.22
  160.7 3.2 %collective-permute-start.23 = (f32[528,128]{1,0:T(8,128)}, f32[528,128]{1,0:T(8,128)}, u32[]{:S(2)}, u32[]{:S(2)}) collective-permute-start(f32[528,128]{1,0:T(8,128)} %get-tuple-element.198), channel_id=1, source_target_pairs={{0,16},{8,24},{16,0},{24,8},{1,17},{9,25},{17,1},{25,9},{2,18},{10... | collective-permute-start | bytes 811016 | tf_op jit(solution)/shard_map/ppermute | solution.py:636
  164.0 19.2 %collective-permute-done.16.refs_5_ = f32[1128,128]{1,0:T(8,128)S(1)} collective-permute-done((f32[1128,128]{1,0:T(8,128)S(1)}, f32[1128,128]{1,0:T(8,128)S(1)}, u32[]{:S(2)}, u32[]{:S(2)}) %collective-permute-start.16) | collective-permute-done | bytes 577568 | tf_op jit(solution)/shard_map/ppermute | solution.py:636
  183.1 0.1 slice.39
  183.2 0.6 fusion.1
  184.4 0.6 pad_add_fusion.1
  185.1 24.1 %collective-permute-done.17.refs_6_ = f32[1128,128]{1,0:T(8,128)S(1)} collective-permute-done((f32[1128,128]{1,0:T(8,128)}, f32[1128,128]{1,0:T(8,128)S(1)}, u32[]{:S(2)}, u32[]{:S(2)}) %collective-permute-start.17) | collective-permute-done | bytes 577568 | tf_op jit(solution)/shard_map/ppermute | solution.py:636
  209.2 11.4 %finish.2.refs_3_ = f32[3,8,128,512]{3,2,1,0:T(8,128)} custom-call(s32[3]{0:T(128)S(1)} %get-tuple-element.266.first_ref, s32[8,128]{1,0:T(8,128)S(1)} %get-tuple-element.407, s32[8,640]{1,0:T(8,128)S(1)} %copy-done.6, f32[6]{0:T(128)S(1)} %pad_maximum_fusion.3.refs_0_.scalars_ref, s32[128,512]{1,0:T(8,128)S(1)} %copy-done.1, ...), custom_call_target="tpu_custom_call", output_to_operand_aliasing={{}: (7, {})} | custom-call | bytes 9437184 | tf_op jit(solution)/shard_map/finish/pallas_call | solution.py:613
  220.7 7.9 %finish.3 = f32[3,8,128,512]{3,2,1,0:T(8,128)} custom-call(s32[3]{0:T(128)S(1)} %get-tuple-element.265.first_ref, s32[8,128]{1,0:T(8,128)S(1)} %get-tuple-element.407, s32[8,640]{1,0:T(8,128)S(1)} %copy-done.6, f32[6]{0:T(128)S(1)} %pad_maximum_fusion.3.refs_0_.scalars_ref, s32[128,512]{1,0:T(8,128)S(1)} %copy-done.1, ...), custom_call_target="tpu_custom_call", output_to_operand_aliasing={{}: (7, {})} | custom-call | bytes 9437184 | tf_op jit(solution)/shard_map/finish/pallas_call | solution.py:613
  (58 shorter events, 0.7 us)
Async XLA Ops:
  0.0 0.9 copy-start
  6.4 32.8 %collective-permute-start.6 = (f32[16,32,128]{2,1,0:T(8,128)}, f32[16,32,128]{2,1,0:T(8,128)S(1)}, u32[]{:S(2)}, u32[]{:S(2)}) collective-permute-start(f32[16,32,128]{2,1,0:T(8,128)} %get-tuple-element.170), channel_id=1, source_target_pairs={{0,8},{8,16},{16,24},{24,0},{1,9},{9,17},{17,25},{25,1},{2,10},{10... | collective-permute-start | bytes 786440 | tf_op jit(solution)/shard_map/ppermute | solution.py:636
  8.0 31.2 %collective-permute-start.7 = (f32[16,32,128]{2,1,0:T(8,128)}, f32[16,32,128]{2,1,0:T(8,128)S(1)}, u32[]{:S(2)}, u32[]{:S(2)}) collective-permute-start(f32[16,32,128]{2,1,0:T(8,128)} %get-tuple-element.171), channel_id=1, source_target_pairs={{0,16},{8,24},{16,0},{24,8},{1,17},{9,25},{17,1},{25,9},{2,18},{10... | collective-permute-start | bytes 786440 | tf_op jit(solution)/shard_map/ppermute | solution.py:636
  20.1 0.9 copy-start.7
  21.0 2.9 %copy-start.12 = (bf16[4,64,256]{2,1,0:T(8,128)(2,1)S(1)}, bf16[4,64,256]{2,1,0:T(8,128)(2,1)}, u32[]{:S(2)}) copy-start(bf16[4,64,256]{2,1,0:T(8,128)(2,1)} %constant.93.clone.refs_2_) | copy-start | bytes 393220
  23.9 0.7 copy-start.9
  24.6 44.4 %collective-permute-start.8 = (f32[16,32,128]{2,1,0:T(8,128)}, f32[16,32,128]{2,1,0:T(8,128)S(1)}, u32[]{:S(2)}, u32[]{:S(2)}) collective-permute-start(f32[16,32,128]{2,1,0:T(8,128)} %get-tuple-element.172), channel_id=1, source_target_pairs={{0,24},{8,0},{16,8},{24,16},{1,25},{9,1},{17,9},{25,17},{2,26},{10... | collective-permute-start | bytes 786440 | tf_op jit(solution)/shard_map/ppermute | solution.py:636
  26.4 56.4 %collective-permute-start.13 = (f32[50,32,128]{2,1,0:T(8,128)}, f32[50,32,128]{2,1,0:T(8,128)}, u32[]{:S(2)}, u32[]{:S(2)}) collective-permute-start(f32[50,32,128]{2,1,0:T(8,128)} %copy-done.7), channel_id=1, source_target_pairs={{0,8},{8,16},{16,24},{24,0},{1,9},{9,17},{17,25},{25,1},{2,10},{10... | collective-permute-start | bytes 2457608 | tf_op jit(solution)/shard_map/ppermute | solution.py:636
  26.7 97.5 %collective-permute-start.14 = (f32[50,32,128]{2,1,0:T(8,128)S(1)}, f32[50,32,128]{2,1,0:T(8,128)}, u32[]{:S(2)}, u32[]{:S(2)}) collective-permute-start(f32[50,32,128]{2,1,0:T(8,128)S(1)} %get-tuple-element.186), channel_id=1, source_target_pairs={{0,16},{8,24},{16,0},{24,8},{1,17},{9,25},{17,1},{25,9},{2,18},{10... | collective-permute-start | bytes 2457608 | tf_op jit(solution)/shard_map/ppermute | solution.py:636
  30.9 38.2 %copy-start.1 = (s32[128,512]{1,0:T(8,128)S(1)}, s32[128,512]{1,0:T(8,128)}, u32[]{:S(2)}) copy-start(s32[128,512]{1,0:T(8,128)} %refs_0_.5) | copy-start | bytes 786436
  30.9 38.2 %copy-start.2 = (f32[128,512]{1,0:T(8,128)S(1)}, f32[128,512]{1,0:T(8,128)}, u32[]{:S(2)}) copy-start(f32[128,512]{1,0:T(8,128)} %refs_8_.1) | copy-start | bytes 786436
  30.9 38.2 %copy-start.8 = (f32[3,8,128,512]{3,2,1,0:T(8,128)S(1)}, f32[3,8,128,512]{3,2,1,0:T(8,128)}, u32[]{:S(2)}) copy-start(f32[3,8,128,512]{3,2,1,0:T(8,128)} %get-tuple-element.400) | copy-start | bytes 18874372
  39.1 30.5 %copy-start.4 = (f32[31,32,128]{2,1,0:T(8,128)}, f32[31,32,128]{2,1,0:T(8,128)S(1)}, u32[]{:S(2)}) copy-start(f32[31,32,128]{2,1,0:T(8,128)S(1)} %get-tuple-element.176.refs_10_.refs_3_) | copy-start | bytes 1523716
  39.1 87.0 %collective-permute-start.15 = (f32[50,32,128]{2,1,0:T(8,128)}, f32[50,32,128]{2,1,0:T(8,128)}, u32[]{:S(2)}, u32[]{:S(2)}) collective-permute-start(f32[50,32,128]{2,1,0:T(8,128)} %get-tuple-element.187), channel_id=1, source_target_pairs={{0,24},{8,0},{16,8},{24,16},{1,25},{9,1},{17,9},{25,17},{2,26},{10... | collective-permute-start | bytes 2457608 | tf_op jit(solution)/shard_map/ppermute | solution.py:636
  69.7 5.0 %collective-permute-start.9 = (f32[2,8,512]{2,1,0:T(8,128)S(1)}, f32[2,8,512]{2,1,0:T(8,128)S(1)}, u32[]{:S(2)}, u32[]{:S(2)}) collective-permute-start(f32[2,8,512]{2,1,0:T(8,128)S(1)} %get-tuple-element.177), channel_id=1, source_target_pairs={{0,4},{1,5},{2,6},{3,7},{8,12},{9,13},{10,14},{11,15},{16,20},{17,... | collective-permute-start | bytes 98312 | tf_op jit(solution)/shard_map/ppermute | solution.py:636
  73.1 5.8 %collective-permute-start.10 = (f32[2,8,512]{2,1,0:T(8,128)S(1)}, f32[2,8,512]{2,1,0:T(8,128)S(1)}, u32[]{:S(2)}, u32[]{:S(2)}) collective-permute-start(f32[2,8,512]{2,1,0:T(8,128)S(1)} %get-tuple-element.178), channel_id=1, source_target_pairs={{4,0},{5,1},{6,2},{7,3},{12,8},{13,9},{14,10},{15,11},{20,16},{21,... | collective-permute-start | bytes 98312 | tf_op jit(solution)/shard_map/ppermute | solution.py:636
  74.8 4.3 %collective-permute-start.12 = (f32[3,8,128]{2,1,0:T(8,128)S(1)}, f32[3,8,128]{2,1,0:T(8,128)S(1)}, u32[]{:S(2)}, u32[]{:S(2)}) collective-permute-start(f32[3,8,128]{2,1,0:T(8,128)S(1)} %pad_maximum_fusion.2), channel_id=1, source_target_pairs={{0,3},{1,0},{2,1},{3,2},{4,7},{5,4},{6,5},{7,6},{8,11},{9,8},{10,9... | collective-permute-start | bytes 36872 | tf_op jit(solution)/shard_map/ppermute | solution.py:636
  79.1 3.1 %collective-permute-start.11 = (f32[3,8,128]{2,1,0:T(8,128)S(1)}, f32[3,8,128]{2,1,0:T(8,128)S(1)}, u32[]{:S(2)}, u32[]{:S(2)}) collective-permute-start(f32[3,8,128]{2,1,0:T(8,128)S(1)} %pad_maximum_fusion.1), channel_id=1, source_target_pairs={{0,1},{1,2},{2,3},{3,0},{4,5},{5,6},{6,7},{7,4},{8,9},{9,10},{10,1... | collective-permute-start | bytes 36872 | tf_op jit(solution)/shard_map/ppermute | solution.py:636
  79.1 3.1 %copy-start.15 = (f32[3,8,128]{2,1,0:T(8,128)}, f32[3,8,128]{2,1,0:T(8,128)S(1)}, u32[]{:S(2)}) copy-start(f32[3,8,128]{2,1,0:T(8,128)S(1)} %collective-permute-done.12) | copy-start | bytes 36868
  79.1 69.3 %collective-permute-start.19 = (f32[31,32,128]{2,1,0:T(8,128)}, f32[31,32,128]{2,1,0:T(8,128)}, u32[]{:S(2)}, u32[]{:S(2)}) collective-permute-start(f32[31,32,128]{2,1,0:T(8,128)} %get-tuple-element.193), channel_id=1, source_target_pairs={{0,8},{8,16},{16,24},{24,0},{1,9},{9,17},{17,25},{25,1},{2,10},{10... | collective-permute-start | bytes 1523720 | tf_op jit(solution)/shard_map/ppermute | solution.py:636
  82.2 0.6 copy-start.16
  82.8 67.6 %collective-permute-start.20 = (f32[31,32,128]{2,1,0:T(8,128)}, f32[31,32,128]{2,1,0:T(8,128)}, u32[]{:S(2)}, u32[]{:S(2)}) collective-permute-start(f32[31,32,128]{2,1,0:T(8,128)} %get-tuple-element.194), channel_id=1, source_target_pairs={{0,16},{8,24},{16,0},{24,8},{1,17},{9,25},{17,1},{25,9},{2,18},{10... | collective-permute-start | bytes 1523720 | tf_op jit(solution)/shard_map/ppermute | solution.py:636
  82.8 67.6 %collective-permute-start.21 = (f32[31,32,128]{2,1,0:T(8,128)}, f32[31,32,128]{2,1,0:T(8,128)}, u32[]{:S(2)}, u32[]{:S(2)}) collective-permute-start(f32[31,32,128]{2,1,0:T(8,128)} %get-tuple-element.195), channel_id=1, source_target_pairs={{0,24},{8,0},{16,8},{24,16},{1,25},{9,1},{17,9},{25,17},{2,26},{10... | collective-permute-start | bytes 1523720 | tf_op jit(solution)/shard_map/ppermute | solution.py:636
  85.1 41.1 %copy-start.11 = (bf16[4,256,96]{2,1,0:T(8,128)(2,1)S(1)}, bf16[4,256,96]{2,1,0:T(8,128)(2,1)}, u32[]{:S(2)}) copy-start(bf16[4,256,96]{2,1,0:T(8,128)(2,1)} %get-tuple-element.403) | copy-start | bytes 589828
  85.1 41.1 %copy-start.13 = (bf16[4,64,256]{2,1,0:T(8,128)(2,1)S(1)}, bf16[4,64,256]{2,1,0:T(8,128)(2,1)}, u32[]{:S(2)}) copy-start(bf16[4,64,256]{2,1,0:T(8,128)(2,1)} %constant.93.clone.refs_2_) | copy-start | bytes 393220
  126.2 24.2 %copy-start.5 = (f32[31,32,128]{2,1,0:T(8,128)S(1)}, f32[31,32,128]{2,1,0:T(8,128)}, u32[]{:S(2)}) copy-start(f32[31,32,128]{2,1,0:T(8,128)} %copy-done.4) | copy-start | bytes 1523716
  146.8 36.3 %collective-permute-start.16 = (f32[1128,128]{1,0:T(8,128)S(1)}, f32[1128,128]{1,0:T(8,128)S(1)}, u32[]{:S(2)}, u32[]{:S(2)}) collective-permute-start(f32[1128,128]{1,0:T(8,128)S(1)} %get-tuple-element.189), channel_id=1, source_target_pairs={{0,8},{8,16},{16,24},{24,0},{1,9},{9,17},{17,25},{25,1},{2,10},{10... | collective-permute-start | bytes 1732616 | tf_op jit(solution)/shard_map/ppermute | solution.py:636
  146.9 62.3 %collective-permute-start.17 = (f32[1128,128]{1,0:T(8,128)}, f32[1128,128]{1,0:T(8,128)S(1)}, u32[]{:S(2)}, u32[]{:S(2)}) collective-permute-start(f32[1128,128]{1,0:T(8,128)} %get-tuple-element.190), channel_id=1, source_target_pairs={{0,16},{8,24},{16,0},{24,8},{1,17},{9,25},{17,1},{25,9},{2,18},{10... | collective-permute-start | bytes 1732616 | tf_op jit(solution)/shard_map/ppermute | solution.py:636
  148.4 60.8 %copy-start.3 = (f32[128,512]{1,0:T(8,128)S(1)}, f32[128,512]{1,0:T(8,128)}, u32[]{:S(2)}) copy-start(f32[128,512]{1,0:T(8,128)} %refs_1_.9) | copy-start | bytes 786436
  148.4 60.8 %copy-start.6 = (s32[8,640]{1,0:T(8,128)S(1)}, s32[8,640]{1,0:T(8,128)}, u32[]{:S(2)}) copy-start(s32[8,640]{1,0:T(8,128)} %constant.91.clone.table_ref) | copy-start | bytes 61444
  148.4 60.8 %collective-permute-start.18 = (f32[1128,128]{1,0:T(8,128)}, f32[1128,128]{1,0:T(8,128)S(1)}, u32[]{:S(2)}, u32[]{:S(2)}) collective-permute-start(f32[1128,128]{1,0:T(8,128)} %get-tuple-element.191), channel_id=1, source_target_pairs={{0,24},{8,0},{16,8},{24,16},{1,25},{9,1},{17,9},{25,17},{2,26},{10... | collective-permute-start | bytes 1732616 | tf_op jit(solution)/shard_map/ppermute | solution.py:636
  160.7 60.0 %collective-permute-start.22 = (f32[528,128]{1,0:T(8,128)}, f32[528,128]{1,0:T(8,128)}, u32[]{:S(2)}, u32[]{:S(2)}) collective-permute-start(f32[528,128]{1,0:T(8,128)} %get-tuple-element.197), channel_id=1, source_target_pairs={{0,8},{8,16},{16,24},{24,0},{1,9},{9,17},{17,25},{25,1},{2,10},{10... | collective-permute-start | bytes 811016 | tf_op jit(solution)/shard_map/ppermute | solution.py:636
  160.7 59.9 %collective-permute-start.23 = (f32[528,128]{1,0:T(8,128)}, f32[528,128]{1,0:T(8,128)}, u32[]{:S(2)}, u32[]{:S(2)}) collective-permute-start(f32[528,128]{1,0:T(8,128)} %get-tuple-element.198), channel_id=1, source_target_pairs={{0,16},{8,24},{16,0},{24,8},{1,17},{9,25},{17,1},{25,9},{2,18},{10... | collective-permute-start | bytes 811016 | tf_op jit(solution)/shard_map/ppermute | solution.py:636
  183.1 37.6 %collective-permute-start.24 = (f32[528,128]{1,0:T(8,128)}, f32[528,128]{1,0:T(8,128)}, u32[]{:S(2)}, u32[]{:S(2)}) collective-permute-start(f32[528,128]{1,0:T(8,128)} %get-tuple-element.199), channel_id=1, source_target_pairs={{0,24},{8,0},{16,8},{24,16},{1,25},{9,1},{17,9},{25,17},{2,26},{10... | collective-permute-start | bytes 811016 | tf_op jit(solution)/shard_map/ppermute | solution.py:636
  209.2 11.5 %copy-start.14 = (f32[4,544,128]{2,1,0:T(8,128)S(1)}, f32[4,544,128]{2,1,0:T(8,128)}, u32[]{:S(2)}) copy-start(f32[4,544,128]{2,1,0:T(8,128)} %get-tuple-element.200) | copy-start | bytes 3342340

commit v8 on v7

--- a/solution.py
+++ b/solution.py
@@ -227,8 +227,7 @@
     out_refs = refs[:groups]
     token_ref, held, stage, in_sem, out_sem = refs[groups:]
     token_ref[...] = jnp.zeros_like(token_ref)
-    columns = held.shape[-1]
-    lane_tiles = columns // LANES
+    lane_tiles = held.shape[1]
     per_block = SUB * lane_tiles
     row_blocks = index_ref.shape[0] // per_block
     count = groups * tiles
@@ -249,14 +248,25 @@
     def copies(block):
         slot = block & 1
         rows = pl.ds(pl.multiple_of(block * SUB, SUB), SUB)
-        return (
-            pltpu.make_async_copy(
-                base_ref.at[:, :, rows, :], held.at[slot, pl.ds(0, 2)], in_sem.at[slot, 0]
-            ),
-            pltpu.make_async_copy(
-                step_ref.at[pl.ds(1, 2), :, rows, :], held.at[slot, pl.ds(2, 2)], in_sem.at[slot, 1]
-            ),
-        )
+        started = []
+        for lane_tile in range(lane_tiles):
+            lanes = pl.ds(lane_tile * LANES, LANES)
+            landing = held.at[slot, lane_tile]
+            started.append(
+                pltpu.make_async_copy(
+                    base_ref.at[:, :, rows, lanes],
+                    landing.at[pl.ds(0, 2)],
+                    in_sem.at[slot, 2 * lane_tile],
+                )
+            )
+            started.append(
+                pltpu.make_async_copy(
+                    step_ref.at[pl.ds(1, 2), :, rows, lanes],
+                    landing.at[pl.ds(2, 2)],
+                    in_sem.at[slot, 2 * lane_tile + 1],
+                )
+            )
+        return started
 
     @pl.when(begin < end)
     def _():
@@ -278,9 +288,8 @@
             copy.wait()
         slot = block & 1
         for lane_tile in range(lane_tiles):
-            lanes = slice(lane_tile * LANES, (lane_tile + 1) * LANES)
-            turned = [
-                jnp.swapaxes(held[slot, field, :, :, lanes], 0, 1) for field in range(4)
+            fields = [
+                held.at[slot, lane_tile, field].reshape(coefs * SUB, LANES) for field in range(4)
             ]
             start = block * per_block + lane_tile * SUB
             index = index_ref[pl.ds(pl.multiple_of(start, SUB), SUB), :]
@@ -295,7 +304,10 @@
                 renewed = []
                 for field in range(4):
                     got = jnp.take_along_axis(
-                        turned[field][r], source, axis=1, mode="promise_in_bounds"
+                        fields[field][pl.ds(r, coefs, stride=SUB), :],
+                        source,
+                        axis=1,
+                        mode="promise_in_bounds",
                     )
                     full = jnp.where(lane >= shift, got, current[field])
                     stage[to, field * coefs : (field + 1) * coefs, :] = full
@@ -333,9 +345,9 @@
         + [anywhere] * (2 + len(waited)),
         out_specs=[anywhere] * groups + [pl.BlockSpec((SUB, LANES), lambda i, p, o: (0, 0))],
         scratch_shapes=[
-            pltpu.VMEM((2, 4, coefs, SUB, columns), jnp.float32),
+            pltpu.VMEM((2, columns // LANES, 4, coefs, SUB, LANES), jnp.float32),
             pltpu.VMEM((groups * tiles + 2, 4 * coefs, LANES), jnp.float32),
-            pltpu.SemaphoreType.DMA((2, 2)),
+            pltpu.SemaphoreType.DMA((2, 2 * (columns // LANES))),
             pltpu.SemaphoreType.DMA((groups,)),
         ],
     )
@@ -494,7 +506,7 @@
     )
 
 
-def finish_kernel(coefs, lane_tiles, row_block, first_ref, offset_ref, table_ref, scalars_ref, back, refs):
+def finish_kernel(coefs, lane_tiles, row_block, first_ref, offset_ref, table_ref, scalars_ref, back, spread_ref, refs):
     wet_ref, drag_ref, cell_ref, east_ref, north_ref, east_out, north_out = refs
     columns = lane_tiles * LANES
     wet = wet_ref[...].astype(jnp.float32)
@@ -508,11 +520,10 @@
         second = jnp.take_along_axis(after, index, axis=1, mode="promise_in_bounds")
         return jnp.where(over, second, first)
 
-    spread = []
     speed = []
     for lane_tile in range(lane_tiles):
         places = cell_ref[lane_tile * SUB : (lane_tile + 1) * SUB, :]
-        rows = []
+        turned = spread_ref.at[lane_tile].reshape(2 * coefs * SUB, LANES)
         speeds = [[], []]
         for r in range(SUB):
             at = (row_block * lane_tiles + lane_tile) * SUB + r
@@ -524,8 +535,9 @@
                 start = table_ref[first_ref[1] * 2 + 1, tile + which]
                 speeds[which].append(back[pl.ds(start, 1), :])
             place = jnp.broadcast_to(places[r : r + 1], (2 * coefs, LANES))
-            rows.append(gathered(found[0], found[1], place & (LANES - 1), place >= LANES))
-        spread.append(jnp.swapaxes(jnp.stack(rows, axis=0), 0, 1))
+            turned[pl.ds(r, 2 * coefs, stride=SUB), :] = gathered(
+                found[0], found[1], place & (LANES - 1), place >= LANES
+            )
         speed.append(
             gathered(
                 jnp.concatenate(speeds[0], axis=0),
@@ -537,7 +549,9 @@
     is_wet = wet > 0.5
     friction = [
         jnp.where(
-            is_wet, jnp.concatenate([part[index] for part in spread], axis=1) * drag, 0.0
+            is_wet,
+            jnp.concatenate([spread_ref[n, index] for n in range(lane_tiles)], axis=1) * drag,
+            0.0,
         )
         for index in range(2 * coefs)
     ]
@@ -571,15 +585,15 @@
 
     def kernel(first_ref, offset_ref, table_ref, scalars_ref, *refs):
         array_refs = refs[:3]
-        piece_refs = refs[4:-3]
-        out_ref, back, sem = refs[-3:]
+        piece_refs = refs[4:-4]
+        out_ref, back, spread_ref, sem = refs[-4:]
         first = first_ref[0]
         count = first_ref[2]
 
         def body(*block_refs):
             finish_kernel(
                 coefs, lane_tiles, first + pl.program_id(0), first_ref, offset_ref, table_ref,
-                scalars_ref, back, block_refs,
+                scalars_ref, back, spread_ref, block_refs,
             )
 
         @pl.when(count > 0)
@@ -617,6 +631,7 @@
         out_specs=anywhere,
         scratch_shapes=[
             pltpu.VMEM((rows, LANES), jnp.float32),
+            pltpu.VMEM((lane_tiles, 2 * coefs, SUB, LANES), jnp.float32),
             pltpu.SemaphoreType.DMA((len(pieces),)),
         ],
         input_output_aliases={7: 0},

time: 231 us -> 231 us (level)
  no operation moved by 1% of the time
where the time goes in v8:
time: 231 us; the launch traced here: 229 us
  waiting for transfers between devices  106 us (46%)
  Pallas kernels  87.1 us (38%)
  starting transfers between devices  20.7 us (9%)
  local copies, waits for them, and re-layouts  8.1 us (4%)
  between operations  4.57 us (2%)
  other arithmetic  2.48 us (1%)
    ppermute x19, waiting for transfers between devices, shifted(): return lax.ppermute(block, axis, pairs)  106 us
    pallas_call x2, Pallas kernels, friction_call(): pl.pallas_call(lambda *refs: friction_kernel(groups, coefs, chunk_tiles,...  29.7 us
    pallas_call x3, Pallas kernels, pack_call(): pl.pallas_call(lambda *refs: pack_kernel(groups, coefs, tiles, len(waited...  22.1 us
    ppermute x19, starting transfers between devices, shifted(): return lax.ppermute(block, axis, pairs)  20.7 us
    pallas_call x2, Pallas kernels, finish_call(): pl.pallas_call(kernel, out_shape=jax.ShapeDtypeStruct(result.shape, jnp.f...  19.5 us
    pallas_call x1, Pallas kernels, prepare_call(): pl.pallas_call(lambda *refs: prepare_kernel(coefs, *refs), out_shape=[jax...  14.2 us
  transfers between devices with their start and end apart: 19, of which 8 were waited for; matrix products, arithmetic and copies ran while one was open for 3% of the time, Pallas kernels for 32%

profile of v8, /device:TPU:12, one launch (start us, length us, event | category | flops | bytes accessed | tf_op | source)
XLA Modules:
  0.0 228.9 jit_solution(12254705093370778293)
XLA Ops:
  0.0 0.9 copy-done
  1.0 1.0 index.1
  2.0 4.5 %pack.7 = (f32[16,32,128]{2,1,0:T(8,128)S(1)}, f32[16,32,128]{2,1,0:T(8,128)}, f32[16,32,128]{2,1,0:T(8,128)}, f32[16,32,128]{2,1,0:T(8,128)}, s32[8,128]{1,0:T(8,128)S(1)}) custom-call(s32[2]{0:T(128)S(1)} %pad_add_fusion.3.refs_0_, s32[8,128]{1,0:T(8,128)S(1)} %get-tuple-element.337.refs_1_.offset_ref, s32[512,128]{1,0:T(8,128)S(1)} %get-tuple-element.338.refs_2_, ...), custom_call_target="tpu_custom_call" | custom-call | bytes 8388608 | tf_op jit(solution)/shard_map/pack/pallas_call | solution.py:354
  6.5 1.6 collective-permute-start.6
  8.2 1.2 collective-permute-start.7
  9.4 0.5 slice.42
  9.9 0.5 slice.40
  11.1 9.2 %pack.8 = (f32[50,32,128]{2,1,0:T(8,128)S(1)}, f32[50,32,128]{2,1,0:T(8,128)S(1)}, f32[50,32,128]{2,1,0:T(8,128)S(1)}, f32[50,32,128]{2,1,0:T(8,128)}, s32[8,128]{1,0:T(8,128)S(1)}) custom-call(s32[2]{0:T(128)S(1)} %pad_add_fusion.4.refs_0_, s32[8,128]{1,0:T(8,128)S(1)} %get-tuple-element.337.refs_1_.offset_ref, s32[512,128]{1,0:T(8,128)S(1)} %get-tuple-element.338.refs_2_, ...), custom_call_target="tpu_custom_call" | custom-call | bytes 26214400 | tf_op jit(solution)/shard_map/pack/pallas_call | solution.py:354
  20.3 0.9 copy-done.7
  21.2 0.6 slice.41
  23.0 1.1 broadcast_in_dim.15
  24.1 0.7 copy-done.9
  24.8 1.8 collective-permute-start.8
  26.6 0.2 collective-permute-start.13
  26.9 3.5 %collective-permute-start.14 = (f32[50,32,128]{2,1,0:T(8,128)S(1)}, f32[50,32,128]{2,1,0:T(8,128)}, u32[]{:S(2)}, u32[]{:S(2)}) collective-permute-start(f32[50,32,128]{2,1,0:T(8,128)S(1)} %get-tuple-element.186), channel_id=1, source_target_pairs={{0,16},{8,24},{16,0},{24,8},{1,17},{9,25},{17,1},{25,9},{2,18},{10... | collective-permute-start | bytes 2457608 | tf_op jit(solution)/shard_map/ppermute | solution.py:651
  31.1 8.4 %pack.9 = (f32[31,32,128]{2,1,0:T(8,128)S(1)}, f32[31,32,128]{2,1,0:T(8,128)}, f32[31,32,128]{2,1,0:T(8,128)}, f32[31,32,128]{2,1,0:T(8,128)}, s32[8,128]{1,0:T(8,128)}) custom-call(s32[2]{0:T(128)S(1)} %pad_add_fusion.5.refs_0_, s32[8,128]{1,0:T(8,128)S(1)} %get-tuple-element.407, s32[512,128]{1,0:T(8,128)} %copy-done.9, ...), custom_call_target="tpu_custom_call" | custom-call | bytes 16252928 | tf_op jit(solution)/shard_map/pack/pallas_call | solution.py:354
  39.6 29.7 %collective-permute-done.8.refs_9_.refs_6_ = f32[16,32,128]{2,1,0:T(8,128)S(1)} collective-permute-done((f32[16,32,128]{2,1,0:T(8,128)}, f32[16,32,128]{2,1,0:T(8,128)S(1)}, u32[]{:S(2)}, u32[]{:S(2)}) %collective-permute-start.8) | collective-permute-done | bytes 262176 | tf_op jit(solution)/shard_map/ppermute | solution.py:651
  69.2 0.6 edges.1
  69.9 3.4 %collective-permute-start.9 = (f32[2,8,512]{2,1,0:T(8,128)S(1)}, f32[2,8,512]{2,1,0:T(8,128)S(1)}, u32[]{:S(2)}, u32[]{:S(2)}) collective-permute-start(f32[2,8,512]{2,1,0:T(8,128)S(1)} %get-tuple-element.177), channel_id=1, source_target_pairs={{0,4},{1,5},{2,6},{3,7},{8,12},{9,13},{10,14},{11,15},{16,20},{17,... | collective-permute-start | bytes 98312 | tf_op jit(solution)/shard_map/ppermute | solution.py:651
  73.3 1.3 collective-permute-start.10
  74.6 0.3 collective-permute-done.9.refs_9_
  74.9 0.1 maximum_bitcast_fusion.2
  75.0 4.2 %collective-permute-done.10.refs_10_ = f32[2,8,512]{2,1,0:T(8,128)S(1)} collective-permute-done((f32[2,8,512]{2,1,0:T(8,128)S(1)}, f32[2,8,512]{2,1,0:T(8,128)S(1)}, u32[]{:S(2)}, u32[]{:S(2)}) %collective-permute-start.10) | collective-permute-done | bytes 32800 | tf_op jit(solution)/shard_map/ppermute | solution.py:651
  79.2 0.1 maximum_bitcast_fusion.1
  79.4 3.0 %collective-permute-done.11 = f32[3,8,128]{2,1,0:T(8,128)S(1)} collective-permute-done((f32[3,8,128]{2,1,0:T(8,128)S(1)}, f32[3,8,128]{2,1,0:T(8,128)S(1)}, u32[]{:S(2)}, u32[]{:S(2)}) %collective-permute-start.11) | collective-permute-done | bytes 12320 | tf_op jit(solution)/shard_map/ppermute | solution.py:651
  82.4 0.6 copy-done.16
  83.0 0.6 collective-permute-start.21
  83.6 0.1 pad_maximum_fusion.3.refs_0_.scalars_ref
  83.7 0.7 pad_maximum_fusion
  84.4 0.9 broadcast_in_dim.16.refs_11_
  85.3 14.2 %prepare.1 = (f32[3,8,128,512]{3,2,1,0:T(8,128)}, s32[8,128]{1,0:T(8,128)S(1)}) custom-call(f32[6]{0:T(128)S(1)} %pad_maximum_fusion.3.refs_0_.scalars_ref, f32[3,8,128,512]{3,2,1,0:T(8,128)} %get-tuple-element.400, f32[3,8,128,512]{3,2,1,0:T(8,128)} %get-tuple-element.400, f32[3,8,128,512]{3,2,1,0:T(8,128)} %get-tuple-element.400, ...), custom_call_target="tpu_custom_call" | custom-call | flops 524288 | tf_op jit(solution)/shard_map/prepare/pallas_call | solution.py:476
  99.6 0.6 slice.49
  100.8 23.7 %collective-permute-done.14.refs_9_ = f32[50,32,128]{2,1,0:T(8,128)} collective-permute-done((f32[50,32,128]{2,1,0:T(8,128)S(1)}, f32[50,32,128]{2,1,0:T(8,128)}, u32[]{:S(2)}, u32[]{:S(2)}) %collective-permute-start.14) | collective-permute-done | bytes 819232 | tf_op jit(solution)/shard_map/ppermute | solution.py:651
  124.5 1.9 collective-permute-done.15.refs_10_
  126.4 19.5 %friction.6 = (f32[1128,128]{1,0:T(8,128)S(1)}, f32[1128,128]{1,0:T(8,128)S(1)}, f32[1128,128]{1,0:T(8,128)}, f32[1128,128]{1,0:T(8,128)}, s32[8,128]{1,0:T(8,128)S(1)}) custom-call(s32[1]{0:T(128)S(6)} %add.52.refs_0_, bf16[4,256,96]{2,1,0:T(8,128)(2,1)S(1)} %copy-done.11, bf16[4,64,256]{2,1,0:T(8,128)(2,1)S(1)} %copy-done.13, ...), custom_call_target="tpu_custom_call" | custom-call | flops 8650752 | tf_op jit(solution)/shard_map/friction/pallas_call | solution.py:152
  145.8 0.5 slice.50
  147.1 1.7 collective-permute-start.17
  148.8 1.9 collective-permute-start.18
  150.7 10.3 %friction.7 = (f32[528,128]{1,0:T(8,128)S(1)}, f32[528,128]{1,0:T(8,128)}, f32[528,128]{1,0:T(8,128)}, f32[528,128]{1,0:T(8,128)}, s32[8,128]{1,0:T(8,128)}) custom-call(s32[1]{0:T(128)S(6)} %add.53.refs_0_, bf16[4,256,96]{2,1,0:T(8,128)(2,1)S(1)} %copy-done.11, bf16[4,64,256]{2,1,0:T(8,128)(2,1)S(1)} %copy-done.13, f32[31,32,128]{2,1,0:T(8,128)S(1)} %copy-done.5, ...), custom_call_target="tpu_custom_call" | custom-call | flops 8321499136 | tf_op jit(solution)/shard_map/friction/pallas_call | solution.py:152
  161.0 0.1 collective-permute-start.22
  161.0 3.1 %collective-permute-start.23 = (f32[528,128]{1,0:T(8,128)}, f32[528,128]{1,0:T(8,128)}, u32[]{:S(2)}, u32[]{:S(2)}) collective-permute-start(f32[528,128]{1,0:T(8,128)} %get-tuple-element.198), channel_id=1, source_target_pairs={{0,16},{8,24},{16,0},{24,8},{1,17},{9,25},{17,1},{25,9},{2,18},{10... | collective-permute-start | bytes 811016 | tf_op jit(solution)/shard_map/ppermute | solution.py:651
  164.2 19.2 %collective-permute-done.16.refs_5_ = f32[1128,128]{1,0:T(8,128)S(1)} collective-permute-done((f32[1128,128]{1,0:T(8,128)S(1)}, f32[1128,128]{1,0:T(8,128)S(1)}, u32[]{:S(2)}, u32[]{:S(2)}) %collective-permute-start.16) | collective-permute-done | bytes 577568 | tf_op jit(solution)/shard_map/ppermute | solution.py:651
  183.3 0.1 slice.39
  183.4 0.6 fusion.1
  184.6 0.6 pad_add_fusion.1
  185.3 24.1 %collective-permute-done.17.refs_6_ = f32[1128,128]{1,0:T(8,128)S(1)} collective-permute-done((f32[1128,128]{1,0:T(8,128)}, f32[1128,128]{1,0:T(8,128)S(1)}, u32[]{:S(2)}, u32[]{:S(2)}) %collective-permute-start.17) | collective-permute-done | bytes 577568 | tf_op jit(solution)/shard_map/ppermute | solution.py:651
  209.4 11.5 %finish.2.refs_3_ = f32[3,8,128,512]{3,2,1,0:T(8,128)} custom-call(s32[3]{0:T(128)S(1)} %get-tuple-element.266.first_ref, s32[8,128]{1,0:T(8,128)S(1)} %get-tuple-element.407, s32[8,640]{1,0:T(8,128)S(1)} %copy-done.6, f32[6]{0:T(128)S(1)} %pad_maximum_fusion.3.refs_0_.scalars_ref, s32[128,512]{1,0:T(8,128)S(1)} %copy-done.1, ...), custom_call_target="tpu_custom_call", output_to_operand_aliasing={{}: (7, {})} | custom-call | bytes 9437184 | tf_op jit(solution)/shard_map/finish/pallas_call | solution.py:627
  221.0 7.9 %finish.3 = f32[3,8,128,512]{3,2,1,0:T(8,128)} custom-call(s32[3]{0:T(128)S(1)} %get-tuple-element.265.first_ref, s32[8,128]{1,0:T(8,128)S(1)} %get-tuple-element.407, s32[8,640]{1,0:T(8,128)S(1)} %copy-done.6, f32[6]{0:T(128)S(1)} %pad_maximum_fusion.3.refs_0_.scalars_ref, s32[128,512]{1,0:T(8,128)S(1)} %copy-done.1, ...), custom_call_target="tpu_custom_call", output_to_operand_aliasing={{}: (7, {})} | custom-call | bytes 9437184 | tf_op jit(solution)/shard_map/finish/pallas_call | solution.py:627
  (58 shorter events, 0.7 us)
Async XLA Ops:
  0.0 0.9 copy-start
  6.5 33.0 %collective-permute-start.6 = (f32[16,32,128]{2,1,0:T(8,128)}, f32[16,32,128]{2,1,0:T(8,128)S(1)}, u32[]{:S(2)}, u32[]{:S(2)}) collective-permute-start(f32[16,32,128]{2,1,0:T(8,128)} %get-tuple-element.170), channel_id=1, source_target_pairs={{0,8},{8,16},{16,24},{24,0},{1,9},{9,17},{17,25},{25,1},{2,10},{10... | collective-permute-start | bytes 786440 | tf_op jit(solution)/shard_map/ppermute | solution.py:651
  8.2 31.4 %collective-permute-start.7 = (f32[16,32,128]{2,1,0:T(8,128)}, f32[16,32,128]{2,1,0:T(8,128)S(1)}, u32[]{:S(2)}, u32[]{:S(2)}) collective-permute-start(f32[16,32,128]{2,1,0:T(8,128)} %get-tuple-element.171), channel_id=1, source_target_pairs={{0,16},{8,24},{16,0},{24,8},{1,17},{9,25},{17,1},{25,9},{2,18},{10... | collective-permute-start | bytes 786440 | tf_op jit(solution)/shard_map/ppermute | solution.py:651
  20.3 0.9 copy-start.7
  21.2 2.9 %copy-start.12 = (bf16[4,64,256]{2,1,0:T(8,128)(2,1)S(1)}, bf16[4,64,256]{2,1,0:T(8,128)(2,1)}, u32[]{:S(2)}) copy-start(bf16[4,64,256]{2,1,0:T(8,128)(2,1)} %constant.93.clone.refs_2_) | copy-start | bytes 393220
  24.1 0.7 copy-start.9
  24.8 44.4 %collective-permute-start.8 = (f32[16,32,128]{2,1,0:T(8,128)}, f32[16,32,128]{2,1,0:T(8,128)S(1)}, u32[]{:S(2)}, u32[]{:S(2)}) collective-permute-start(f32[16,32,128]{2,1,0:T(8,128)} %get-tuple-element.172), channel_id=1, source_target_pairs={{0,24},{8,0},{16,8},{24,16},{1,25},{9,1},{17,9},{25,17},{2,26},{10... | collective-permute-start | bytes 786440 | tf_op jit(solution)/shard_map/ppermute | solution.py:651
  26.6 56.4 %collective-permute-start.13 = (f32[50,32,128]{2,1,0:T(8,128)}, f32[50,32,128]{2,1,0:T(8,128)}, u32[]{:S(2)}, u32[]{:S(2)}) collective-permute-start(f32[50,32,128]{2,1,0:T(8,128)} %copy-done.7), channel_id=1, source_target_pairs={{0,8},{8,16},{16,24},{24,0},{1,9},{9,17},{17,25},{25,1},{2,10},{10... | collective-permute-start | bytes 2457608 | tf_op jit(solution)/shard_map/ppermute | solution.py:651
  26.9 97.6 %collective-permute-start.14 = (f32[50,32,128]{2,1,0:T(8,128)S(1)}, f32[50,32,128]{2,1,0:T(8,128)}, u32[]{:S(2)}, u32[]{:S(2)}) collective-permute-start(f32[50,32,128]{2,1,0:T(8,128)S(1)} %get-tuple-element.186), channel_id=1, source_target_pairs={{0,16},{8,24},{16,0},{24,8},{1,17},{9,25},{17,1},{25,9},{2,18},{10... | collective-permute-start | bytes 2457608 | tf_op jit(solution)/shard_map/ppermute | solution.py:651
  31.1 38.2 %copy-start.1 = (s32[128,512]{1,0:T(8,128)S(1)}, s32[128,512]{1,0:T(8,128)}, u32[]{:S(2)}) copy-start(s32[128,512]{1,0:T(8,128)} %refs_0_.5) | copy-start | bytes 786436
  31.1 38.2 %copy-start.2 = (f32[128,512]{1,0:T(8,128)S(1)}, f32[128,512]{1,0:T(8,128)}, u32[]{:S(2)}) copy-start(f32[128,512]{1,0:T(8,128)} %refs_8_.1) | copy-start | bytes 786436
  31.1 38.2 %copy-start.8 = (f32[3,8,128,512]{3,2,1,0:T(8,128)S(1)}, f32[3,8,128,512]{3,2,1,0:T(8,128)}, u32[]{:S(2)}) copy-start(f32[3,8,128,512]{3,2,1,0:T(8,128)} %get-tuple-element.400) | copy-start | bytes 18874372
  39.5 30.4 %copy-start.4 = (f32[31,32,128]{2,1,0:T(8,128)}, f32[31,32,128]{2,1,0:T(8,128)S(1)}, u32[]{:S(2)}) copy-start(f32[31,32,128]{2,1,0:T(8,128)S(1)} %get-tuple-element.176.refs_10_.refs_3_) | copy-start | bytes 1523716
  39.5 86.9 %collective-permute-start.15 = (f32[50,32,128]{2,1,0:T(8,128)}, f32[50,32,128]{2,1,0:T(8,128)}, u32[]{:S(2)}, u32[]{:S(2)}) collective-permute-start(f32[50,32,128]{2,1,0:T(8,128)} %get-tuple-element.187), channel_id=1, source_target_pairs={{0,24},{8,0},{16,8},{24,16},{1,25},{9,1},{17,9},{25,17},{2,26},{10... | collective-permute-start | bytes 2457608 | tf_op jit(solution)/shard_map/ppermute | solution.py:651
  69.9 5.0 %collective-permute-start.9 = (f32[2,8,512]{2,1,0:T(8,128)S(1)}, f32[2,8,512]{2,1,0:T(8,128)S(1)}, u32[]{:S(2)}, u32[]{:S(2)}) collective-permute-start(f32[2,8,512]{2,1,0:T(8,128)S(1)} %get-tuple-element.177), channel_id=1, source_target_pairs={{0,4},{1,5},{2,6},{3,7},{8,12},{9,13},{10,14},{11,15},{16,20},{17,... | collective-permute-start | bytes 98312 | tf_op jit(solution)/shard_map/ppermute | solution.py:651
  73.3 5.8 %collective-permute-start.10 = (f32[2,8,512]{2,1,0:T(8,128)S(1)}, f32[2,8,512]{2,1,0:T(8,128)S(1)}, u32[]{:S(2)}, u32[]{:S(2)}) collective-permute-start(f32[2,8,512]{2,1,0:T(8,128)S(1)} %get-tuple-element.178), channel_id=1, source_target_pairs={{4,0},{5,1},{6,2},{7,3},{12,8},{13,9},{14,10},{15,11},{20,16},{21,... | collective-permute-start | bytes 98312 | tf_op jit(solution)/shard_map/ppermute | solution.py:651
  75.0 4.3 %collective-permute-start.12 = (f32[3,8,128]{2,1,0:T(8,128)S(1)}, f32[3,8,128]{2,1,0:T(8,128)S(1)}, u32[]{:S(2)}, u32[]{:S(2)}) collective-permute-start(f32[3,8,128]{2,1,0:T(8,128)S(1)} %pad_maximum_fusion.2), channel_id=1, source_target_pairs={{0,3},{1,0},{2,1},{3,2},{4,7},{5,4},{6,5},{7,6},{8,11},{9,8},{10,9... | collective-permute-start | bytes 36872 | tf_op jit(solution)/shard_map/ppermute | solution.py:651
  79.3 3.1 %collective-permute-start.11 = (f32[3,8,128]{2,1,0:T(8,128)S(1)}, f32[3,8,128]{2,1,0:T(8,128)S(1)}, u32[]{:S(2)}, u32[]{:S(2)}) collective-permute-start(f32[3,8,128]{2,1,0:T(8,128)S(1)} %pad_maximum_fusion.1), channel_id=1, source_target_pairs={{0,1},{1,2},{2,3},{3,0},{4,5},{5,6},{6,7},{7,4},{8,9},{9,10},{10,1... | collective-permute-start | bytes 36872 | tf_op jit(solution)/shard_map/ppermute | solution.py:651
  79.3 3.1 %copy-start.15 = (f32[3,8,128]{2,1,0:T(8,128)}, f32[3,8,128]{2,1,0:T(8,128)S(1)}, u32[]{:S(2)}) copy-start(f32[3,8,128]{2,1,0:T(8,128)S(1)} %collective-permute-done.12) | copy-start | bytes 36868
  79.3 69.4 %collective-permute-start.19 = (f32[31,32,128]{2,1,0:T(8,128)}, f32[31,32,128]{2,1,0:T(8,128)}, u32[]{:S(2)}, u32[]{:S(2)}) collective-permute-start(f32[31,32,128]{2,1,0:T(8,128)} %get-tuple-element.193), channel_id=1, source_target_pairs={{0,8},{8,16},{16,24},{24,0},{1,9},{9,17},{17,25},{25,1},{2,10},{10... | collective-permute-start | bytes 1523720 | tf_op jit(solution)/shard_map/ppermute | solution.py:651
  82.4 0.6 copy-start.16
  83.0 67.7 %collective-permute-start.20 = (f32[31,32,128]{2,1,0:T(8,128)}, f32[31,32,128]{2,1,0:T(8,128)}, u32[]{:S(2)}, u32[]{:S(2)}) collective-permute-start(f32[31,32,128]{2,1,0:T(8,128)} %get-tuple-element.194), channel_id=1, source_target_pairs={{0,16},{8,24},{16,0},{24,8},{1,17},{9,25},{17,1},{25,9},{2,18},{10... | collective-permute-start | bytes 1523720 | tf_op jit(solution)/shard_map/ppermute | solution.py:651
  83.0 67.7 %collective-permute-start.21 = (f32[31,32,128]{2,1,0:T(8,128)}, f32[31,32,128]{2,1,0:T(8,128)}, u32[]{:S(2)}, u32[]{:S(2)}) collective-permute-start(f32[31,32,128]{2,1,0:T(8,128)} %get-tuple-element.195), channel_id=1, source_target_pairs={{0,24},{8,0},{16,8},{24,16},{1,25},{9,1},{17,9},{25,17},{2,26},{10... | collective-permute-start | bytes 1523720 | tf_op jit(solution)/shard_map/ppermute | solution.py:651
  85.3 41.1 %copy-start.11 = (bf16[4,256,96]{2,1,0:T(8,128)(2,1)S(1)}, bf16[4,256,96]{2,1,0:T(8,128)(2,1)}, u32[]{:S(2)}) copy-start(bf16[4,256,96]{2,1,0:T(8,128)(2,1)} %get-tuple-element.403) | copy-start | bytes 589828
  85.3 41.1 %copy-start.13 = (bf16[4,64,256]{2,1,0:T(8,128)(2,1)S(1)}, bf16[4,64,256]{2,1,0:T(8,128)(2,1)}, u32[]{:S(2)}) copy-start(bf16[4,64,256]{2,1,0:T(8,128)(2,1)} %constant.93.clone.refs_2_) | copy-start | bytes 393220
  126.4 24.3 %copy-start.5 = (f32[31,32,128]{2,1,0:T(8,128)S(1)}, f32[31,32,128]{2,1,0:T(8,128)}, u32[]{:S(2)}) copy-start(f32[31,32,128]{2,1,0:T(8,128)} %copy-done.4) | copy-start | bytes 1523716
  147.0 36.3 %collective-permute-start.16 = (f32[1128,128]{1,0:T(8,128)S(1)}, f32[1128,128]{1,0:T(8,128)S(1)}, u32[]{:S(2)}, u32[]{:S(2)}) collective-permute-start(f32[1128,128]{1,0:T(8,128)S(1)} %get-tuple-element.189), channel_id=1, source_target_pairs={{0,8},{8,16},{16,24},{24,0},{1,9},{9,17},{17,25},{25,1},{2,10},{10... | collective-permute-start | bytes 1732616 | tf_op jit(solution)/shard_map/ppermute | solution.py:651
  147.1 62.3 %collective-permute-start.17 = (f32[1128,128]{1,0:T(8,128)}, f32[1128,128]{1,0:T(8,128)S(1)}, u32[]{:S(2)}, u32[]{:S(2)}) collective-permute-start(f32[1128,128]{1,0:T(8,128)} %get-tuple-element.190), channel_id=1, source_target_pairs={{0,16},{8,24},{16,0},{24,8},{1,17},{9,25},{17,1},{25,9},{2,18},{10... | collective-permute-start | bytes 1732616 | tf_op jit(solution)/shard_map/ppermute | solution.py:651
  148.7 60.6 %copy-start.3 = (f32[128,512]{1,0:T(8,128)S(1)}, f32[128,512]{1,0:T(8,128)}, u32[]{:S(2)}) copy-start(f32[128,512]{1,0:T(8,128)} %refs_1_.9) | copy-start | bytes 786436
  148.8 60.6 %copy-start.6 = (s32[8,640]{1,0:T(8,128)S(1)}, s32[8,640]{1,0:T(8,128)}, u32[]{:S(2)}) copy-start(s32[8,640]{1,0:T(8,128)} %constant.91.clone.table_ref) | copy-start | bytes 61444
  148.8 60.6 %collective-permute-start.18 = (f32[1128,128]{1,0:T(8,128)}, f32[1128,128]{1,0:T(8,128)S(1)}, u32[]{:S(2)}, u32[]{:S(2)}) collective-permute-start(f32[1128,128]{1,0:T(8,128)} %get-tuple-element.191), channel_id=1, source_target_pairs={{0,24},{8,0},{16,8},{24,16},{1,25},{9,1},{17,9},{25,17},{2,26},{10... | collective-permute-start | bytes 1732616 | tf_op jit(solution)/shard_map/ppermute | solution.py:651
  161.0 60.0 %collective-permute-start.22 = (f32[528,128]{1,0:T(8,128)}, f32[528,128]{1,0:T(8,128)}, u32[]{:S(2)}, u32[]{:S(2)}) collective-permute-start(f32[528,128]{1,0:T(8,128)} %get-tuple-element.197), channel_id=1, source_target_pairs={{0,8},{8,16},{16,24},{24,0},{1,9},{9,17},{17,25},{25,1},{2,10},{10... | collective-permute-start | bytes 811016 | tf_op jit(solution)/shard_map/ppermute | solution.py:651
  161.0 59.9 %collective-permute-start.23 = (f32[528,128]{1,0:T(8,128)}, f32[528,128]{1,0:T(8,128)}, u32[]{:S(2)}, u32[]{:S(2)}) collective-permute-start(f32[528,128]{1,0:T(8,128)} %get-tuple-element.198), channel_id=1, source_target_pairs={{0,16},{8,24},{16,0},{24,8},{1,17},{9,25},{17,1},{25,9},{2,18},{10... | collective-permute-start | bytes 811016 | tf_op jit(solution)/shard_map/ppermute | solution.py:651
  183.3 37.7 %collective-permute-start.24 = (f32[528,128]{1,0:T(8,128)}, f32[528,128]{1,0:T(8,128)}, u32[]{:S(2)}, u32[]{:S(2)}) collective-permute-start(f32[528,128]{1,0:T(8,128)} %get-tuple-element.199), channel_id=1, source_target_pairs={{0,24},{8,0},{16,8},{24,16},{1,25},{9,1},{17,9},{25,17},{2,26},{10... | collective-permute-start | bytes 811016 | tf_op jit(solution)/shard_map/ppermute | solution.py:651
  209.4 11.6 %copy-start.14 = (f32[4,544,128]{2,1,0:T(8,128)S(1)}, f32[4,544,128]{2,1,0:T(8,128)}, u32[]{:S(2)}) copy-start(f32[4,544,128]{2,1,0:T(8,128)} %get-tuple-element.200) | copy-start | bytes 3342340

commit v9 on v8

--- a/solution.py
+++ b/solution.py
@@ -23,6 +23,7 @@
 SHARE_UNITS = 128
 LOOP_TILES = 8
 PACK_COST = 16384
+AHEAD = 4
 LATE_WEIGHT = 2048
 
 
@@ -246,7 +247,7 @@
     end = jnp.maximum(end, begin)
 
     def copies(block):
-        slot = block & 1
+        slot = lax.rem(block, AHEAD)
         rows = pl.ds(pl.multiple_of(block * SUB, SUB), SUB)
         started = []
         for lane_tile in range(lane_tiles):
@@ -268,10 +269,12 @@
             )
         return started
 
-    @pl.when(begin < end)
-    def _():
-        for copy in copies(begin):
-            copy.start()
+    for step in range(AHEAD - 1):
+
+        @pl.when(begin + step < end)
+        def _():
+            for copy in copies(begin + step):
+                copy.start()
 
     lane = lax.broadcasted_iota(jnp.int32, (coefs, LANES), 1)
 
@@ -279,14 +282,14 @@
         return jnp.clip((offset >> 7) - first_tile + 1, 0, count + 1)
 
     def body(block, current):
-        @pl.when(block + 1 < end)
+        @pl.when(block + AHEAD - 1 < end)
         def _():
-            for copy in copies(block + 1):
+            for copy in copies(block + AHEAD - 1):
                 copy.start()
 
         for copy in copies(block):
             copy.wait()
-        slot = block & 1
+        slot = lax.rem(block, AHEAD)
         for lane_tile in range(lane_tiles):
             fields = [
                 held.at[slot, lane_tile, field].reshape(coefs * SUB, LANES) for field in range(4)
@@ -345,9 +348,9 @@
         + [anywhere] * (2 + len(waited)),
         out_specs=[anywhere] * groups + [pl.BlockSpec((SUB, LANES), lambda i, p, o: (0, 0))],
         scratch_shapes=[
-            pltpu.VMEM((2, columns // LANES, 4, coefs, SUB, LANES), jnp.float32),
+            pltpu.VMEM((AHEAD, columns // LANES, 4, coefs, SUB, LANES), jnp.float32),
             pltpu.VMEM((groups * tiles + 2, 4 * coefs, LANES), jnp.float32),
-            pltpu.SemaphoreType.DMA((2, 2 * (columns // LANES))),
+            pltpu.SemaphoreType.DMA((AHEAD, 2 * (columns // LANES))),
             pltpu.SemaphoreType.DMA((groups,)),
         ],
     )
@@ -610,15 +613,29 @@
                 copy.start()
             for copy in copies:
                 copy.wait()
-            flat = pl.BlockSpec((SUB, columns), lambda i: (first + i, 0))
-            east = pl.BlockSpec((1, coefs, SUB, columns), lambda i: (1, 0, first + i, 0))
-            north = pl.BlockSpec((1, coefs, SUB, columns), lambda i: (2, 0, first + i, 0))
-            cells = pl.BlockSpec((SUB * lane_tiles, LANES), lambda i: (first + i, 0))
+            deep = pl.Buffered(3)
+
+            def flat(rows, width):
+                return pl.BlockSpec(
+                    (rows, width), lambda i: (first + i, 0), pipeline_mode=deep
+                )
+
+            def plane(p, mode):
+                return pl.BlockSpec(
+                    (1, coefs, SUB, columns), lambda i: (p, 0, first + i, 0), pipeline_mode=mode
+                )
+
             pltpu.emit_pipeline(
                 body,
                 grid=(count,),
-                in_specs=[flat, flat, cells, east, north],
-                out_specs=[east, north],
+                in_specs=[
+                    flat(SUB, columns),
+                    flat(SUB, columns),
+                    flat(SUB * lane_tiles, LANES),
+                    plane(1, deep),
+                    plane(2, deep),
+                ],
+                out_specs=[plane(1, None), plane(2, None)],
             )(*array_refs, out_ref, out_ref, out_ref, out_ref)
 
     anywhere = pl.BlockSpec(memory_space=pl.ANY)

time: 231 us -> 228 us (0.987)
  Pallas kernels: 87.1 us -> 80.2 us
  waiting for transfers between devices: 106 us -> 110 us
    pallas_call x3, Pallas kernels: 22.1 us -> 17.6 us  [pack_call(): pl.pallas_call(lambda *refs: pack_kernel(groups, coefs, tiles, len(waited...]
    ppermute x19, waiting for transfers between devices: 106 us -> 110 us  [shifted(): return lax.ppermute(block, axis, pairs)]
    pallas_call x2, Pallas kernels: 19.5 us -> 17 us  [finish_call(): pl.pallas_call(kernel, out_shape=jax.ShapeDtypeStruct(result.shape, jnp.f...]
  transfers between devices with their start and end apart: 19 -> 19, of which waited for: 8 -> 11; matrix products, arithmetic and copies ran while one was open for 3% -> 3% of each run, Pallas kernels for 32% -> 30%
where the time goes in v9:
time: 228 us; the launch traced here: 226 us
  waiting for transfers between devices  110 us (48%)
  Pallas kernels  80.2 us (35%)
  starting transfers between devices  21.2 us (9%)
  local copies, waits for them, and re-layouts  8.1 us (4%)
  between operations  4.54 us (2%)
  other arithmetic  2.48 us (1%)
    ppermute x19, waiting for transfers between devices, shifted(): return lax.ppermute(block, axis, pairs)  110 us
    pallas_call x2, Pallas kernels, friction_call(): pl.pallas_call(lambda *refs: friction_kernel(groups, coefs, chunk_tiles,...  29.7 us
    ppermute x19, starting transfers between devices, shifted(): return lax.ppermute(block, axis, pairs)  21.2 us
    pallas_call x3, Pallas kernels, pack_call(): pl.pallas_call(lambda *refs: pack_kernel(groups, coefs, tiles, len(waited...  17.6 us
    pallas_call x2, Pallas kernels, finish_call(): pl.pallas_call(kernel, out_shape=jax.ShapeDtypeStruct(result.shape, jnp.f...  17 us
    pallas_call x1, Pallas kernels, prepare_call(): pl.pallas_call(lambda *refs: prepare_kernel(coefs, *refs), out_shape=[jax...  14.2 us
  transfers between devices with their start and end apart: 19, of which 11 were waited for; matrix products, arithmetic and copies ran while one was open for 3% of the time, Pallas kernels for 30%

profile of v9, /device:TPU:12, one launch (start us, length us, event | category | flops | bytes accessed | tf_op | source)
XLA Modules:
  0.0 226.3 jit_solution(17429507741113938575)
XLA Ops:
  0.0 0.9 copy-done
  1.0 1.0 index.1
  2.0 3.9 %pack.7 = (f32[16,32,128]{2,1,0:T(8,128)S(1)}, f32[16,32,128]{2,1,0:T(8,128)}, f32[16,32,128]{2,1,0:T(8,128)}, f32[16,32,128]{2,1,0:T(8,128)}, s32[8,128]{1,0:T(8,128)S(1)}) custom-call(s32[2]{0:T(128)S(1)} %pad_add_fusion.3.refs_0_, s32[8,128]{1,0:T(8,128)S(1)} %get-tuple-element.337.refs_1_.offset_ref, s32[512,128]{1,0:T(8,128)S(1)} %get-tuple-element.338.refs_2_, ...), custom_call_target="tpu_custom_call" | custom-call | bytes 8388608 | tf_op jit(solution)/shard_map/pack/pallas_call | solution.py:357
  6.0 1.6 collective-permute-start.6
  7.6 1.2 collective-permute-start.7
  8.8 0.5 slice.42
  9.3 0.5 slice.40
  10.6 6.6 %pack.8 = (f32[50,32,128]{2,1,0:T(8,128)S(1)}, f32[50,32,128]{2,1,0:T(8,128)S(1)}, f32[50,32,128]{2,1,0:T(8,128)S(1)}, f32[50,32,128]{2,1,0:T(8,128)}, s32[8,128]{1,0:T(8,128)S(1)}) custom-call(s32[2]{0:T(128)S(1)} %pad_add_fusion.4.refs_0_, s32[8,128]{1,0:T(8,128)S(1)} %get-tuple-element.337.refs_1_.offset_ref, s32[512,128]{1,0:T(8,128)S(1)} %get-tuple-element.338.refs_2_, ...), custom_call_target="tpu_custom_call" | custom-call | bytes 26214400 | tf_op jit(solution)/shard_map/pack/pallas_call | solution.py:357
  17.1 0.9 copy-done.7
  18.0 0.6 slice.41
  19.8 1.1 broadcast_in_dim.15
  20.9 0.7 copy-done.9
  21.6 1.8 collective-permute-start.8
  23.4 0.2 collective-permute-start.13
  23.7 3.5 %collective-permute-start.14 = (f32[50,32,128]{2,1,0:T(8,128)S(1)}, f32[50,32,128]{2,1,0:T(8,128)}, u32[]{:S(2)}, u32[]{:S(2)}) collective-permute-start(f32[50,32,128]{2,1,0:T(8,128)S(1)} %get-tuple-element.186), channel_id=1, source_target_pairs={{0,16},{8,24},{16,0},{24,8},{1,17},{9,25},{17,1},{25,9},{2,18},{10... | collective-permute-start | bytes 2457608 | tf_op jit(solution)/shard_map/ppermute | solution.py:668
  27.9 7.1 %pack.9 = (f32[31,32,128]{2,1,0:T(8,128)S(1)}, f32[31,32,128]{2,1,0:T(8,128)}, f32[31,32,128]{2,1,0:T(8,128)}, f32[31,32,128]{2,1,0:T(8,128)}, s32[8,128]{1,0:T(8,128)}) custom-call(s32[2]{0:T(128)S(1)} %pad_add_fusion.5.refs_0_, s32[8,128]{1,0:T(8,128)S(1)} %get-tuple-element.407, s32[512,128]{1,0:T(8,128)} %copy-done.9, ...), custom_call_target="tpu_custom_call" | custom-call | bytes 16252928 | tf_op jit(solution)/shard_map/pack/pallas_call | solution.py:357
  35.1 32.1 %collective-permute-done.8.refs_9_.refs_6_ = f32[16,32,128]{2,1,0:T(8,128)S(1)} collective-permute-done((f32[16,32,128]{2,1,0:T(8,128)}, f32[16,32,128]{2,1,0:T(8,128)S(1)}, u32[]{:S(2)}, u32[]{:S(2)}) %collective-permute-start.8) | collective-permute-done | bytes 262176 | tf_op jit(solution)/shard_map/ppermute | solution.py:668
  67.2 0.6 edges.1
  67.9 3.4 %collective-permute-start.9 = (f32[2,8,512]{2,1,0:T(8,128)S(1)}, f32[2,8,512]{2,1,0:T(8,128)S(1)}, u32[]{:S(2)}, u32[]{:S(2)}) collective-permute-start(f32[2,8,512]{2,1,0:T(8,128)S(1)} %get-tuple-element.177), channel_id=1, source_target_pairs={{0,4},{1,5},{2,6},{3,7},{8,12},{9,13},{10,14},{11,15},{16,20},{17,... | collective-permute-start | bytes 98312 | tf_op jit(solution)/shard_map/ppermute | solution.py:668
  71.3 1.3 collective-permute-start.10
  72.6 0.3 collective-permute-done.9.refs_9_
  73.0 4.2 %collective-permute-done.10.refs_10_ = f32[2,8,512]{2,1,0:T(8,128)S(1)} collective-permute-done((f32[2,8,512]{2,1,0:T(8,128)S(1)}, f32[2,8,512]{2,1,0:T(8,128)S(1)}, u32[]{:S(2)}, u32[]{:S(2)}) %collective-permute-start.10) | collective-permute-done | bytes 32800 | tf_op jit(solution)/shard_map/ppermute | solution.py:668
  77.4 3.0 %collective-permute-done.11 = f32[3,8,128]{2,1,0:T(8,128)S(1)} collective-permute-done((f32[3,8,128]{2,1,0:T(8,128)S(1)}, f32[3,8,128]{2,1,0:T(8,128)S(1)}, u32[]{:S(2)}, u32[]{:S(2)}) %collective-permute-start.11) | collective-permute-done | bytes 12320 | tf_op jit(solution)/shard_map/ppermute | solution.py:668
  80.4 0.6 copy-done.16
  81.0 2.8 %collective-permute-done.13.refs_8_ = f32[50,32,128]{2,1,0:T(8,128)} collective-permute-done((f32[50,32,128]{2,1,0:T(8,128)}, f32[50,32,128]{2,1,0:T(8,128)}, u32[]{:S(2)}, u32[]{:S(2)}) %collective-permute-start.13) | collective-permute-done | bytes 819232 | tf_op jit(solution)/shard_map/ppermute | solution.py:668
  83.8 0.1 pad_maximum_fusion.3.refs_0_.scalars_ref
  83.9 0.7 pad_maximum_fusion
  84.6 0.9 broadcast_in_dim.16.refs_11_
  85.5 14.2 %prepare.1 = (f32[3,8,128,512]{3,2,1,0:T(8,128)}, s32[8,128]{1,0:T(8,128)S(1)}) custom-call(f32[6]{0:T(128)S(1)} %pad_maximum_fusion.3.refs_0_.scalars_ref, f32[3,8,128,512]{3,2,1,0:T(8,128)} %get-tuple-element.400, f32[3,8,128,512]{3,2,1,0:T(8,128)} %get-tuple-element.400, f32[3,8,128,512]{3,2,1,0:T(8,128)} %get-tuple-element.400, ...), custom_call_target="tpu_custom_call" | custom-call | flops 524288 | tf_op jit(solution)/shard_map/prepare/pallas_call | solution.py:479
  99.8 0.6 slice.49
  101.0 22.4 %collective-permute-done.14.refs_9_ = f32[50,32,128]{2,1,0:T(8,128)} collective-permute-done((f32[50,32,128]{2,1,0:T(8,128)S(1)}, f32[50,32,128]{2,1,0:T(8,128)}, u32[]{:S(2)}, u32[]{:S(2)}) %collective-permute-start.14) | collective-permute-done | bytes 819232 | tf_op jit(solution)/shard_map/ppermute | solution.py:668
  123.4 0.8 collective-permute-done.15.refs_10_
  124.3 19.5 %friction.6 = (f32[1128,128]{1,0:T(8,128)S(1)}, f32[1128,128]{1,0:T(8,128)S(1)}, f32[1128,128]{1,0:T(8,128)}, f32[1128,128]{1,0:T(8,128)}, s32[8,128]{1,0:T(8,128)S(1)}) custom-call(s32[1]{0:T(128)S(6)} %add.52.refs_0_, bf16[4,256,96]{2,1,0:T(8,128)(2,1)S(1)} %copy-done.11, bf16[4,64,256]{2,1,0:T(8,128)(2,1)S(1)} %copy-done.13, ...), custom_call_target="tpu_custom_call" | custom-call | flops 8650752 | tf_op jit(solution)/shard_map/friction/pallas_call | solution.py:153
  143.7 0.5 slice.50
  144.9 2.7 %collective-permute-start.17 = (f32[1128,128]{1,0:T(8,128)}, f32[1128,128]{1,0:T(8,128)S(1)}, u32[]{:S(2)}, u32[]{:S(2)}) collective-permute-start(f32[1128,128]{1,0:T(8,128)} %get-tuple-element.190), channel_id=1, source_target_pairs={{0,16},{8,24},{16,0},{24,8},{1,17},{9,25},{17,1},{25,9},{2,18},{10... | collective-permute-start | bytes 1732616 | tf_op jit(solution)/shard_map/ppermute | solution.py:668
  147.7 1.9 collective-permute-start.18
  149.6 10.3 %friction.7 = (f32[528,128]{1,0:T(8,128)S(1)}, f32[528,128]{1,0:T(8,128)}, f32[528,128]{1,0:T(8,128)}, f32[528,128]{1,0:T(8,128)}, s32[8,128]{1,0:T(8,128)}) custom-call(s32[1]{0:T(128)S(6)} %add.53.refs_0_, bf16[4,256,96]{2,1,0:T(8,128)(2,1)S(1)} %copy-done.11, bf16[4,64,256]{2,1,0:T(8,128)(2,1)S(1)} %copy-done.13, f32[31,32,128]{2,1,0:T(8,128)S(1)} %copy-done.5, ...), custom_call_target="tpu_custom_call" | custom-call | flops 8321499136 | tf_op jit(solution)/shard_map/friction/pallas_call | solution.py:153
  159.9 2.3 %collective-permute-start.23 = (f32[528,128]{1,0:T(8,128)}, f32[528,128]{1,0:T(8,128)}, u32[]{:S(2)}, u32[]{:S(2)}) collective-permute-start(f32[528,128]{1,0:T(8,128)} %get-tuple-element.198), channel_id=1, source_target_pairs={{0,16},{8,24},{16,0},{24,8},{1,17},{9,25},{17,1},{25,9},{2,18},{10... | collective-permute-start | bytes 811016 | tf_op jit(solution)/shard_map/ppermute | solution.py:668
  162.3 0.9 collective-permute-start.24
  163.2 0.1 slice.39
  163.3 0.6 fusion.1
  164.5 0.6 pad_add_fusion.1
  165.1 42.1 %collective-permute-done.17.refs_6_ = f32[1128,128]{1,0:T(8,128)S(1)} collective-permute-done((f32[1128,128]{1,0:T(8,128)}, f32[1128,128]{1,0:T(8,128)S(1)}, u32[]{:S(2)}, u32[]{:S(2)}) %collective-permute-start.17) | collective-permute-done | bytes 577568 | tf_op jit(solution)/shard_map/ppermute | solution.py:668
  207.2 0.3 collective-permute-done.18.refs_7_
  207.5 9.8 %finish.2.refs_3_ = f32[3,8,128,512]{3,2,1,0:T(8,128)} custom-call(s32[3]{0:T(128)S(1)} %get-tuple-element.266.first_ref, s32[8,128]{1,0:T(8,128)S(1)} %get-tuple-element.407, s32[8,640]{1,0:T(8,128)S(1)} %copy-done.6, f32[6]{0:T(128)S(1)} %pad_maximum_fusion.3.refs_0_.scalars_ref, s32[128,512]{1,0:T(8,128)S(1)} %copy-done.1, ...), custom_call_target="tpu_custom_call", output_to_operand_aliasing={{}: (7, {})} | custom-call | bytes 9437184 | tf_op jit(solution)/shard_map/finish/pallas_call | solution.py:644
  217.3 0.7 collective-permute-done.23.refs_10_
  218.0 1.1 collective-permute-done.24.refs_11_
  219.1 7.2 %finish.3 = f32[3,8,128,512]{3,2,1,0:T(8,128)} custom-call(s32[3]{0:T(128)S(1)} %get-tuple-element.265.first_ref, s32[8,128]{1,0:T(8,128)S(1)} %get-tuple-element.407, s32[8,640]{1,0:T(8,128)S(1)} %copy-done.6, f32[6]{0:T(128)S(1)} %pad_maximum_fusion.3.refs_0_.scalars_ref, s32[128,512]{1,0:T(8,128)S(1)} %copy-done.1, ...), custom_call_target="tpu_custom_call", output_to_operand_aliasing={{}: (7, {})} | custom-call | bytes 9437184 | tf_op jit(solution)/shard_map/finish/pallas_call | solution.py:644
  (58 shorter events, 0.9 us)
Async XLA Ops:
  0.0 0.9 copy-start
  6.0 29.1 %collective-permute-start.6 = (f32[16,32,128]{2,1,0:T(8,128)}, f32[16,32,128]{2,1,0:T(8,128)S(1)}, u32[]{:S(2)}, u32[]{:S(2)}) collective-permute-start(f32[16,32,128]{2,1,0:T(8,128)} %get-tuple-element.170), channel_id=1, source_target_pairs={{0,8},{8,16},{16,24},{24,0},{1,9},{9,17},{17,25},{25,1},{2,10},{10... | collective-permute-start | bytes 786440 | tf_op jit(solution)/shard_map/ppermute | solution.py:668
  7.6 27.5 %collective-permute-start.7 = (f32[16,32,128]{2,1,0:T(8,128)}, f32[16,32,128]{2,1,0:T(8,128)S(1)}, u32[]{:S(2)}, u32[]{:S(2)}) collective-permute-start(f32[16,32,128]{2,1,0:T(8,128)} %get-tuple-element.171), channel_id=1, source_target_pairs={{0,16},{8,24},{16,0},{24,8},{1,17},{9,25},{17,1},{25,9},{2,18},{10... | collective-permute-start | bytes 786440 | tf_op jit(solution)/shard_map/ppermute | solution.py:668
  17.1 0.9 copy-start.7
  18.0 2.9 %copy-start.12 = (bf16[4,64,256]{2,1,0:T(8,128)(2,1)S(1)}, bf16[4,64,256]{2,1,0:T(8,128)(2,1)}, u32[]{:S(2)}) copy-start(bf16[4,64,256]{2,1,0:T(8,128)(2,1)} %constant.93.clone.refs_2_) | copy-start | bytes 393220
  20.9 0.7 copy-start.9
  21.6 45.6 %collective-permute-start.8 = (f32[16,32,128]{2,1,0:T(8,128)}, f32[16,32,128]{2,1,0:T(8,128)S(1)}, u32[]{:S(2)}, u32[]{:S(2)}) collective-permute-start(f32[16,32,128]{2,1,0:T(8,128)} %get-tuple-element.172), channel_id=1, source_target_pairs={{0,24},{8,0},{16,8},{24,16},{1,25},{9,1},{17,9},{25,17},{2,26},{10... | collective-permute-start | bytes 786440 | tf_op jit(solution)/shard_map/ppermute | solution.py:668
  23.4 60.4 %collective-permute-start.13 = (f32[50,32,128]{2,1,0:T(8,128)}, f32[50,32,128]{2,1,0:T(8,128)}, u32[]{:S(2)}, u32[]{:S(2)}) collective-permute-start(f32[50,32,128]{2,1,0:T(8,128)} %copy-done.7), channel_id=1, source_target_pairs={{0,8},{8,16},{16,24},{24,0},{1,9},{9,17},{17,25},{25,1},{2,10},{10... | collective-permute-start | bytes 2457608 | tf_op jit(solution)/shard_map/ppermute | solution.py:668
  23.7 99.7 %collective-permute-start.14 = (f32[50,32,128]{2,1,0:T(8,128)S(1)}, f32[50,32,128]{2,1,0:T(8,128)}, u32[]{:S(2)}, u32[]{:S(2)}) collective-permute-start(f32[50,32,128]{2,1,0:T(8,128)S(1)} %get-tuple-element.186), channel_id=1, source_target_pairs={{0,16},{8,24},{16,0},{24,8},{1,17},{9,25},{17,1},{25,9},{2,18},{10... | collective-permute-start | bytes 2457608 | tf_op jit(solution)/shard_map/ppermute | solution.py:668
  27.9 39.4 %copy-start.1 = (s32[128,512]{1,0:T(8,128)S(1)}, s32[128,512]{1,0:T(8,128)}, u32[]{:S(2)}) copy-start(s32[128,512]{1,0:T(8,128)} %refs_0_.5) | copy-start | bytes 786436
  27.9 39.4 %copy-start.2 = (f32[128,512]{1,0:T(8,128)S(1)}, f32[128,512]{1,0:T(8,128)}, u32[]{:S(2)}) copy-start(f32[128,512]{1,0:T(8,128)} %refs_8_.1) | copy-start | bytes 786436
  27.9 39.4 %copy-start.8 = (f32[3,8,128,512]{3,2,1,0:T(8,128)S(1)}, f32[3,8,128,512]{3,2,1,0:T(8,128)}, u32[]{:S(2)}) copy-start(f32[3,8,128,512]{3,2,1,0:T(8,128)} %get-tuple-element.400) | copy-start | bytes 18874372
  35.0 32.8 %copy-start.4 = (f32[31,32,128]{2,1,0:T(8,128)}, f32[31,32,128]{2,1,0:T(8,128)S(1)}, u32[]{:S(2)}) copy-start(f32[31,32,128]{2,1,0:T(8,128)S(1)} %get-tuple-element.176.refs_10_.refs_3_) | copy-start | bytes 1523716
  35.0 89.2 %collective-permute-start.15 = (f32[50,32,128]{2,1,0:T(8,128)}, f32[50,32,128]{2,1,0:T(8,128)}, u32[]{:S(2)}, u32[]{:S(2)}) collective-permute-start(f32[50,32,128]{2,1,0:T(8,128)} %get-tuple-element.187), channel_id=1, source_target_pairs={{0,24},{8,0},{16,8},{24,16},{1,25},{9,1},{17,9},{25,17},{2,26},{10... | collective-permute-start | bytes 2457608 | tf_op jit(solution)/shard_map/ppermute | solution.py:668
  67.9 5.0 %collective-permute-start.9 = (f32[2,8,512]{2,1,0:T(8,128)S(1)}, f32[2,8,512]{2,1,0:T(8,128)S(1)}, u32[]{:S(2)}, u32[]{:S(2)}) collective-permute-start(f32[2,8,512]{2,1,0:T(8,128)S(1)} %get-tuple-element.177), channel_id=1, source_target_pairs={{0,4},{1,5},{2,6},{3,7},{8,12},{9,13},{10,14},{11,15},{16,20},{17,... | collective-permute-start | bytes 98312 | tf_op jit(solution)/shard_map/ppermute | solution.py:668
  71.3 5.8 %collective-permute-start.10 = (f32[2,8,512]{2,1,0:T(8,128)S(1)}, f32[2,8,512]{2,1,0:T(8,128)S(1)}, u32[]{:S(2)}, u32[]{:S(2)}) collective-permute-start(f32[2,8,512]{2,1,0:T(8,128)S(1)} %get-tuple-element.178), channel_id=1, source_target_pairs={{4,0},{5,1},{6,2},{7,3},{12,8},{13,9},{14,10},{15,11},{20,16},{21,... | collective-permute-start | bytes 98312 | tf_op jit(solution)/shard_map/ppermute | solution.py:668
  73.0 4.3 %collective-permute-start.12 = (f32[3,8,128]{2,1,0:T(8,128)S(1)}, f32[3,8,128]{2,1,0:T(8,128)S(1)}, u32[]{:S(2)}, u32[]{:S(2)}) collective-permute-start(f32[3,8,128]{2,1,0:T(8,128)S(1)} %pad_maximum_fusion.2), channel_id=1, source_target_pairs={{0,3},{1,0},{2,1},{3,2},{4,7},{5,4},{6,5},{7,6},{8,11},{9,8},{10,9... | collective-permute-start | bytes 36872 | tf_op jit(solution)/shard_map/ppermute | solution.py:668
  77.3 3.1 %collective-permute-start.11 = (f32[3,8,128]{2,1,0:T(8,128)S(1)}, f32[3,8,128]{2,1,0:T(8,128)S(1)}, u32[]{:S(2)}, u32[]{:S(2)}) collective-permute-start(f32[3,8,128]{2,1,0:T(8,128)S(1)} %pad_maximum_fusion.1), channel_id=1, source_target_pairs={{0,1},{1,2},{2,3},{3,0},{4,5},{5,6},{6,7},{7,4},{8,9},{9,10},{10,1... | collective-permute-start | bytes 36872 | tf_op jit(solution)/shard_map/ppermute | solution.py:668
  77.3 3.1 %copy-start.15 = (f32[3,8,128]{2,1,0:T(8,128)}, f32[3,8,128]{2,1,0:T(8,128)S(1)}, u32[]{:S(2)}) copy-start(f32[3,8,128]{2,1,0:T(8,128)S(1)} %collective-permute-done.12) | copy-start | bytes 36868
  77.3 70.3 %collective-permute-start.19 = (f32[31,32,128]{2,1,0:T(8,128)}, f32[31,32,128]{2,1,0:T(8,128)}, u32[]{:S(2)}, u32[]{:S(2)}) collective-permute-start(f32[31,32,128]{2,1,0:T(8,128)} %get-tuple-element.193), channel_id=1, source_target_pairs={{0,8},{8,16},{16,24},{24,0},{1,9},{9,17},{17,25},{25,1},{2,10},{10... | collective-permute-start | bytes 1523720 | tf_op jit(solution)/shard_map/ppermute | solution.py:668
  80.4 0.6 copy-start.16
  81.0 68.6 %collective-permute-start.20 = (f32[31,32,128]{2,1,0:T(8,128)}, f32[31,32,128]{2,1,0:T(8,128)}, u32[]{:S(2)}, u32[]{:S(2)}) collective-permute-start(f32[31,32,128]{2,1,0:T(8,128)} %get-tuple-element.194), channel_id=1, source_target_pairs={{0,16},{8,24},{16,0},{24,8},{1,17},{9,25},{17,1},{25,9},{2,18},{10... | collective-permute-start | bytes 1523720 | tf_op jit(solution)/shard_map/ppermute | solution.py:668
  83.8 65.8 %collective-permute-start.21 = (f32[31,32,128]{2,1,0:T(8,128)}, f32[31,32,128]{2,1,0:T(8,128)}, u32[]{:S(2)}, u32[]{:S(2)}) collective-permute-start(f32[31,32,128]{2,1,0:T(8,128)} %get-tuple-element.195), channel_id=1, source_target_pairs={{0,24},{8,0},{16,8},{24,16},{1,25},{9,1},{17,9},{25,17},{2,26},{10... | collective-permute-start | bytes 1523720 | tf_op jit(solution)/shard_map/ppermute | solution.py:668
  85.5 38.7 %copy-start.11 = (bf16[4,256,96]{2,1,0:T(8,128)(2,1)S(1)}, bf16[4,256,96]{2,1,0:T(8,128)(2,1)}, u32[]{:S(2)}) copy-start(bf16[4,256,96]{2,1,0:T(8,128)(2,1)} %get-tuple-element.403) | copy-start | bytes 589828
  85.5 38.7 %copy-start.13 = (bf16[4,64,256]{2,1,0:T(8,128)(2,1)S(1)}, bf16[4,64,256]{2,1,0:T(8,128)(2,1)}, u32[]{:S(2)}) copy-start(bf16[4,64,256]{2,1,0:T(8,128)(2,1)} %constant.93.clone.refs_2_) | copy-start | bytes 393220
  124.2 25.4 %copy-start.5 = (f32[31,32,128]{2,1,0:T(8,128)S(1)}, f32[31,32,128]{2,1,0:T(8,128)}, u32[]{:S(2)}) copy-start(f32[31,32,128]{2,1,0:T(8,128)} %copy-done.4) | copy-start | bytes 1523716
  144.9 17.4 %collective-permute-start.16 = (f32[1128,128]{1,0:T(8,128)S(1)}, f32[1128,128]{1,0:T(8,128)S(1)}, u32[]{:S(2)}, u32[]{:S(2)}) collective-permute-start(f32[1128,128]{1,0:T(8,128)S(1)} %get-tuple-element.189), channel_id=1, source_target_pairs={{0,8},{8,16},{16,24},{24,0},{1,9},{9,17},{17,25},{25,1},{2,10},{10... | collective-permute-start | bytes 1732616 | tf_op jit(solution)/shard_map/ppermute | solution.py:668
  144.9 62.2 %collective-permute-start.17 = (f32[1128,128]{1,0:T(8,128)}, f32[1128,128]{1,0:T(8,128)S(1)}, u32[]{:S(2)}, u32[]{:S(2)}) collective-permute-start(f32[1128,128]{1,0:T(8,128)} %get-tuple-element.190), channel_id=1, source_target_pairs={{0,16},{8,24},{16,0},{24,8},{1,17},{9,25},{17,1},{25,9},{2,18},{10... | collective-permute-start | bytes 1732616 | tf_op jit(solution)/shard_map/ppermute | solution.py:668
  147.7 59.9 %copy-start.3 = (f32[128,512]{1,0:T(8,128)S(1)}, f32[128,512]{1,0:T(8,128)}, u32[]{:S(2)}) copy-start(f32[128,512]{1,0:T(8,128)} %refs_1_.9) | copy-start | bytes 786436
  147.7 59.9 %copy-start.6 = (s32[8,640]{1,0:T(8,128)S(1)}, s32[8,640]{1,0:T(8,128)}, u32[]{:S(2)}) copy-start(s32[8,640]{1,0:T(8,128)} %constant.91.clone.table_ref) | copy-start | bytes 61444
  147.7 59.9 %collective-permute-start.18 = (f32[1128,128]{1,0:T(8,128)}, f32[1128,128]{1,0:T(8,128)S(1)}, u32[]{:S(2)}, u32[]{:S(2)}) collective-permute-start(f32[1128,128]{1,0:T(8,128)} %get-tuple-element.191), channel_id=1, source_target_pairs={{0,24},{8,0},{16,8},{24,16},{1,25},{9,1},{17,9},{25,17},{2,26},{10... | collective-permute-start | bytes 1732616 | tf_op jit(solution)/shard_map/ppermute | solution.py:668
  159.9 57.4 %collective-permute-start.22 = (f32[528,128]{1,0:T(8,128)}, f32[528,128]{1,0:T(8,128)}, u32[]{:S(2)}, u32[]{:S(2)}) collective-permute-start(f32[528,128]{1,0:T(8,128)} %get-tuple-element.197), channel_id=1, source_target_pairs={{0,8},{8,16},{16,24},{24,0},{1,9},{9,17},{17,25},{25,1},{2,10},{10... | collective-permute-start | bytes 811016 | tf_op jit(solution)/shard_map/ppermute | solution.py:668
  159.9 58.1 %collective-permute-start.23 = (f32[528,128]{1,0:T(8,128)}, f32[528,128]{1,0:T(8,128)}, u32[]{:S(2)}, u32[]{:S(2)}) collective-permute-start(f32[528,128]{1,0:T(8,128)} %get-tuple-element.198), channel_id=1, source_target_pairs={{0,16},{8,24},{16,0},{24,8},{1,17},{9,25},{17,1},{25,9},{2,18},{10... | collective-permute-start | bytes 811016 | tf_op jit(solution)/shard_map/ppermute | solution.py:668
  162.3 56.8 %collective-permute-start.24 = (f32[528,128]{1,0:T(8,128)}, f32[528,128]{1,0:T(8,128)}, u32[]{:S(2)}, u32[]{:S(2)}) collective-permute-start(f32[528,128]{1,0:T(8,128)} %get-tuple-element.199), channel_id=1, source_target_pairs={{0,24},{8,0},{16,8},{24,16},{1,25},{9,1},{17,9},{25,17},{2,26},{10... | collective-permute-start | bytes 811016 | tf_op jit(solution)/shard_map/ppermute | solution.py:668
  207.5 11.6 %copy-start.14 = (f32[4,544,128]{2,1,0:T(8,128)S(1)}, f32[4,544,128]{2,1,0:T(8,128)}, u32[]{:S(2)}) copy-start(f32[4,544,128]{2,1,0:T(8,128)} %get-tuple-element.200) | copy-start | bytes 3342340

commit v10 on v9

--- a/solution.py
+++ b/solution.py
@@ -19,7 +19,7 @@
 OMEGA_STEP = 0.25
 SPEED_SOFT = 0.01
 VMEM_BYTES = 48 * 1024 * 1024
-CHUNK_SHARES = (16, 50, 31)
+CHUNK_SHARES = (12, 55, 30)
 SHARE_UNITS = 128
 LOOP_TILES = 8
 PACK_COST = 16384
@@ -582,7 +582,7 @@
         north_out[0, sin_at] = -(num_north_re * inv_imag + num_north_im * inv_real)
 
 
-def finish_call(first, offset, table, scalars, arrays, pieces, rows, result):
+def finish_call(first, offset, table, scalars, arrays, pieces, rows, result, groups, early):
     _, coefs, _, columns = result.shape
     lane_tiles = columns // LANES
 
@@ -593,26 +593,41 @@
         first = first_ref[0]
         count = first_ref[2]
 
-        def body(*block_refs):
-            finish_kernel(
-                coefs, lane_tiles, first + pl.program_id(0), first_ref, offset_ref, table_ref,
-                scalars_ref, back, spread_ref, block_refs,
-            )
-
         @pl.when(count > 0)
         def _():
+            at = 0
             copies = []
-            at = 0
             for n, piece in enumerate(piece_refs):
                 rows = piece.shape[0]
-                copies.append(
-                    pltpu.make_async_copy(piece, back.at[pl.ds(at, rows)], sem.at[n])
+                copy = pltpu.make_async_copy(piece, back.at[pl.ds(at, rows)], sem.at[n])
+                needed = True
+                if n < early[0]:
+                    source = lax.rem(first_ref[1] + groups - n % groups, groups)
+                    needed = source >= groups - early[1]
+                elif n >= early[0] + groups:
+                    needed = first_ref[3] > 0
+                copies.append((copy, needed))
+                at += rows
+
+            def each(act):
+                for copy, needed in copies:
+                    if needed is True:
+                        act(copy)
+                    else:
+                        pl.when(needed)(lambda copy=copy: act(copy))
+
+            each(lambda copy: copy.start())
+
+            def body(*block_refs):
+                @pl.when(pl.program_id(0) == 0)
+                def _():
+                    each(lambda copy: copy.wait())
+
+                finish_kernel(
+                    coefs, lane_tiles, first + pl.program_id(0), first_ref, offset_ref,
+                    table_ref, scalars_ref, back, spread_ref, block_refs,
                 )
-                at += rows
-            for copy in copies:
-                copy.start()
-            for copy in copies:
-                copy.wait()
+
             deep = pl.Buffered(3)
 
             def flat(rows, width):
@@ -856,9 +871,10 @@
             pieces.append(extra.reshape(-1, LANES))
         else:
             end = jnp.sum((ends <= tile * LANES).astype(jnp.int32))
-        first = jnp.stack([begin, place[0], end - begin])
+        first = jnp.stack([begin, place[0], end - begin, loops])
         result = finish_call(
-            first, offset, table, scalars, arrays, list(pieces), back_rows, result
+            first, offset, table, scalars, arrays, list(pieces), back_rows, result, groups,
+            (groups, -(-SUB * lane_tiles // chunk_tiles[-2])) if last else (0, 0),
         )
         begin = end
     return result

time: 228 us -> 231 us (1.013)
  waiting for transfers between devices: 110 us -> 116 us
    ppermute x19, waiting for transfers between devices: 110 us -> 116 us  [shifted(): return lax.ppermute(block, axis, pairs)]
  transfers between devices with their start and end apart: 19 -> 19, of which waited for: 11 -> 10; matrix products, arithmetic and copies ran while one was open for 3% -> 3% of each run, Pallas kernels for 30% -> 30%
where the time goes in v10:
time: 231 us; the launch traced here: 230 us
  waiting for transfers between devices  116 us (50%)
  Pallas kernels  79.3 us (34%)
  starting transfers between devices  20.7 us (9%)
  local copies, waits for them, and re-layouts  7.59 us (3%)
  between operations  4.78 us (2%)
    ppermute x19, waiting for transfers between devices, shifted(): return lax.ppermute(block, axis, pairs)  116 us
    pallas_call x2, Pallas kernels, friction_call(): pl.pallas_call(lambda *refs: friction_kernel(groups, coefs, chunk_tiles,...  29.5 us
    ppermute x19, starting transfers between devices, shifted(): return lax.ppermute(block, axis, pairs)  20.7 us
    pallas_call x3, Pallas kernels, pack_call(): pl.pallas_call(lambda *refs: pack_kernel(groups, coefs, tiles, len(waited...  18.1 us
    pallas_call x2, Pallas kernels, finish_call(): pl.pallas_call(kernel, out_shape=jax.ShapeDtypeStruct(result.shape, jnp.f...  15.9 us
    pallas_call x1, Pallas kernels, prepare_call(): pl.pallas_call(lambda *refs: prepare_kernel(coefs, *refs), out_shape=[jax...  14.2 us
  transfers between devices with their start and end apart: 19, of which 10 were waited for; matrix products, arithmetic and copies ran while one was open for 3% of the time, Pallas kernels for 30%

profile of v10, /device:TPU:12, one launch (start us, length us, event | category | flops | bytes accessed | tf_op | source)
XLA Modules:
  0.0 229.8 jit_solution(8245372530010909349)
XLA Ops:
  0.0 0.9 copy-done
  1.0 1.0 index.1
  2.0 3.7 %pack.7 = (f32[12,32,128]{2,1,0:T(8,128)S(1)}, f32[12,32,128]{2,1,0:T(8,128)}, f32[12,32,128]{2,1,0:T(8,128)}, f32[12,32,128]{2,1,0:T(8,128)S(1)}, s32[8,128]{1,0:T(8,128)S(1)}) custom-call(s32[2]{0:T(128)S(1)} %pad_add_fusion.1.refs_0_, s32[8,128]{1,0:T(8,128)S(1)} %get-tuple-element.337.refs_1_.offset_ref, s32[512,128]{1,0:T(8,128)S(1)} %get-tuple-element.338.refs_2_, ...), custom_call_target="tpu_custom_call" | custom-call | bytes 6291456 | tf_op jit(solution)/shard_map/pack/pallas_call | solution.py:357
  5.7 0.7 copy-done.6
  6.4 1.6 collective-permute-start.6
  8.0 1.2 collective-permute-start.7
  9.2 0.5 slice.40
  9.7 0.5 slice.41
  11.0 7.3 %pack.8 = (f32[55,32,128]{2,1,0:T(8,128)S(1)}, f32[55,32,128]{2,1,0:T(8,128)S(1)}, f32[55,32,128]{2,1,0:T(8,128)S(1)}, f32[55,32,128]{2,1,0:T(8,128)}, s32[8,128]{1,0:T(8,128)S(1)}) custom-call(s32[2]{0:T(128)S(1)} %pad_add_fusion.2.refs_0_, s32[8,128]{1,0:T(8,128)S(1)} %get-tuple-element.337.refs_1_.offset_ref, s32[512,128]{1,0:T(8,128)S(1)} %get-tuple-element.338.refs_2_, ...), custom_call_target="tpu_custom_call" | custom-call | bytes 28835840 | tf_op jit(solution)/shard_map/pack/pallas_call | solution.py:357
  18.3 0.9 copy-done.9
  19.2 0.6 slice.42
  21.0 1.1 broadcast_in_dim.15
  22.1 1.9 collective-permute-start.8
  24.0 0.2 collective-permute-start.13
  24.2 3.5 %collective-permute-start.14 = (f32[55,32,128]{2,1,0:T(8,128)}, f32[55,32,128]{2,1,0:T(8,128)}, u32[]{:S(2)}, u32[]{:S(2)}) collective-permute-start(f32[55,32,128]{2,1,0:T(8,128)} %copy-done.9), channel_id=1, source_target_pairs={{0,16},{8,24},{16,0},{24,8},{1,17},{9,25},{17,1},{25,9},{2,18},{10... | collective-permute-start | bytes 2703368 | tf_op jit(solution)/shard_map/ppermute | solution.py:683
  28.4 7.1 %pack.9 = (f32[30,32,128]{2,1,0:T(8,128)S(1)}, f32[30,32,128]{2,1,0:T(8,128)}, f32[30,32,128]{2,1,0:T(8,128)}, f32[30,32,128]{2,1,0:T(8,128)}, s32[8,128]{1,0:T(8,128)}) custom-call(s32[2]{0:T(128)S(1)} %pad_add_fusion.3.refs_0_, s32[8,128]{1,0:T(8,128)S(1)} %get-tuple-element.410, s32[512,128]{1,0:T(8,128)} %copy-done.12, ...), custom_call_target="tpu_custom_call" | custom-call | bytes 15728640 | tf_op jit(solution)/shard_map/pack/pallas_call | solution.py:357
  35.6 32.7 %collective-permute-done.8.refs_9_.refs_6_ = f32[12,32,128]{2,1,0:T(8,128)S(1)} collective-permute-done((f32[12,32,128]{2,1,0:T(8,128)S(1)}, f32[12,32,128]{2,1,0:T(8,128)S(1)}, u32[]{:S(2)}, u32[]{:S(2)}) %collective-permute-start.8) | collective-permute-done | bytes 196640 | tf_op jit(solution)/shard_map/ppermute | solution.py:683
  68.3 0.6 edges.1
  69.0 3.4 %collective-permute-start.9 = (f32[2,8,512]{2,1,0:T(8,128)S(1)}, f32[2,8,512]{2,1,0:T(8,128)S(1)}, u32[]{:S(2)}, u32[]{:S(2)}) collective-permute-start(f32[2,8,512]{2,1,0:T(8,128)S(1)} %get-tuple-element.177), channel_id=1, source_target_pairs={{0,4},{1,5},{2,6},{3,7},{8,12},{9,13},{10,14},{11,15},{16,20},{17,... | collective-permute-start | bytes 98312 | tf_op jit(solution)/shard_map/ppermute | solution.py:683
  72.3 1.3 collective-permute-start.10
  73.6 0.3 collective-permute-done.9.refs_9_
  73.9 0.1 maximum_bitcast_fusion.2
  74.0 4.2 %collective-permute-done.10.refs_10_ = f32[2,8,512]{2,1,0:T(8,128)S(1)} collective-permute-done((f32[2,8,512]{2,1,0:T(8,128)S(1)}, f32[2,8,512]{2,1,0:T(8,128)S(1)}, u32[]{:S(2)}, u32[]{:S(2)}) %collective-permute-start.10) | collective-permute-done | bytes 32800 | tf_op jit(solution)/shard_map/ppermute | solution.py:683
  78.2 0.1 maximum_bitcast_fusion.1
  78.4 3.0 %collective-permute-done.11 = f32[3,8,128]{2,1,0:T(8,128)S(1)} collective-permute-done((f32[3,8,128]{2,1,0:T(8,128)S(1)}, f32[3,8,128]{2,1,0:T(8,128)S(1)}, u32[]{:S(2)}, u32[]{:S(2)}) %collective-permute-start.11) | collective-permute-done | bytes 12320 | tf_op jit(solution)/shard_map/ppermute | solution.py:683
  81.4 0.6 collective-permute-start.21
  82.1 0.1 pad_maximum_fusion.3.refs_0_.scalars_ref
  82.2 0.9 broadcast_in_dim.16.refs_11_
  83.1 14.2 %prepare.1 = (f32[3,8,128,512]{3,2,1,0:T(8,128)}, s32[8,128]{1,0:T(8,128)S(1)}) custom-call(f32[6]{0:T(128)S(1)} %pad_maximum_fusion.3.refs_0_.scalars_ref, f32[3,8,128,512]{3,2,1,0:T(8,128)} %get-tuple-element.402, f32[3,8,128,512]{3,2,1,0:T(8,128)} %get-tuple-element.402, f32[3,8,128,512]{3,2,1,0:T(8,128)} %get-tuple-element.402, ...), custom_call_target="tpu_custom_call" | custom-call | flops 524288 | tf_op jit(solution)/shard_map/prepare/pallas_call | solution.py:479
  97.3 0.6 slice.49
  98.6 28.4 %collective-permute-done.14.refs_9_ = f32[55,32,128]{2,1,0:T(8,128)} collective-permute-done((f32[55,32,128]{2,1,0:T(8,128)}, f32[55,32,128]{2,1,0:T(8,128)}, u32[]{:S(2)}, u32[]{:S(2)}) %collective-permute-start.14) | collective-permute-done | bytes 901152 | tf_op jit(solution)/shard_map/ppermute | solution.py:683
  127.0 1.1 collective-permute-done.15.refs_10_
  128.1 19.7 %friction.6 = (f32[1144,128]{1,0:T(8,128)S(1)}, f32[1144,128]{1,0:T(8,128)S(1)}, f32[1144,128]{1,0:T(8,128)}, f32[1144,128]{1,0:T(8,128)}, s32[8,128]{1,0:T(8,128)S(1)}) custom-call(s32[1]{0:T(128)S(6)} %add.52.refs_0_, bf16[4,256,96]{2,1,0:T(8,128)(2,1)S(1)} %copy-done.14, bf16[4,64,256]{2,1,0:T(8,128)(2,1)S(1)} %copy-done.16, ...), custom_call_target="tpu_custom_call" | custom-call | flops 8781824 | tf_op jit(solution)/shard_map/friction/pallas_call | solution.py:153
  147.8 0.6 slice.50
  149.1 2.3 %collective-permute-start.17 = (f32[1144,128]{1,0:T(8,128)}, f32[1144,128]{1,0:T(8,128)S(1)}, u32[]{:S(2)}, u32[]{:S(2)}) collective-permute-start(f32[1144,128]{1,0:T(8,128)} %get-tuple-element.190), channel_id=1, source_target_pairs={{0,16},{8,24},{16,0},{24,8},{1,17},{9,25},{17,1},{25,9},{2,18},{10... | collective-permute-start | bytes 1757192 | tf_op jit(solution)/shard_map/ppermute | solution.py:683
  151.5 1.9 collective-permute-start.18
  153.4 9.8 %friction.7 = (f32[512,128]{1,0:T(8,128)S(1)}, f32[512,128]{1,0:T(8,128)}, f32[512,128]{1,0:T(8,128)}, f32[512,128]{1,0:T(8,128)}, s32[8,128]{1,0:T(8,128)}) custom-call(s32[1]{0:T(128)S(6)} %add.53.refs_0_, bf16[4,256,96]{2,1,0:T(8,128)(2,1)S(1)} %copy-done.14, bf16[4,64,256]{2,1,0:T(8,128)(2,1)S(1)} %copy-done.16, f32[30,32,128]{2,1,0:T(8,128)S(1)} %copy-done.5, ...), custom_call_target="tpu_custom_call" | custom-call | flops 8053063680 | tf_op jit(solution)/shard_map/friction/pallas_call | solution.py:153
  163.2 0.1 collective-permute-start.22
  163.3 2.5 %collective-permute-start.23 = (f32[512,128]{1,0:T(8,128)}, f32[512,128]{1,0:T(8,128)}, u32[]{:S(2)}, u32[]{:S(2)}) collective-permute-start(f32[512,128]{1,0:T(8,128)} %get-tuple-element.198), channel_id=1, source_target_pairs={{0,16},{8,24},{16,0},{24,8},{1,17},{9,25},{17,1},{25,9},{2,18},{10... | collective-permute-start | bytes 786440 | tf_op jit(solution)/shard_map/ppermute | solution.py:683
  165.8 20.1 %collective-permute-done.16.refs_5_ = f32[1144,128]{1,0:T(8,128)S(1)} collective-permute-done((f32[1144,128]{1,0:T(8,128)S(1)}, f32[1144,128]{1,0:T(8,128)S(1)}, u32[]{:S(2)}, u32[]{:S(2)}) %collective-permute-start.16) | collective-permute-done | bytes 585760 | tf_op jit(solution)/shard_map/ppermute | solution.py:683
  185.9 0.1 slice.39
  186.0 0.7 fusion.1
  187.4 0.7 add_add_fusion
  188.2 23.7 %collective-permute-done.17.refs_6_ = f32[1144,128]{1,0:T(8,128)S(1)} collective-permute-done((f32[1144,128]{1,0:T(8,128)}, f32[1144,128]{1,0:T(8,128)S(1)}, u32[]{:S(2)}, u32[]{:S(2)}) %collective-permute-start.17) | collective-permute-done | bytes 585760 | tf_op jit(solution)/shard_map/ppermute | solution.py:683
  211.8 0.7 collective-permute-done.18.refs_7_
  212.5 9.9 %finish.2.refs_3_ = f32[3,8,128,512]{3,2,1,0:T(8,128)} custom-call(s32[4]{0:T(128)S(1)} %get-tuple-element.266.first_ref, s32[8,128]{1,0:T(8,128)S(1)} %get-tuple-element.410, s32[8,640]{1,0:T(8,128)S(1)} %copy-done.8, f32[6]{0:T(128)S(1)} %pad_maximum_fusion.3.refs_0_.scalars_ref, s32[128,512]{1,0:T(8,128)S(1)} %copy-done.1, ...), custom_call_target="tpu_custom_call", output_to_operand_aliasing={{}: (7, {})} | custom-call | bytes 9437184 | tf_op jit(solution)/shard_map/finish/pallas_call | solution.py:659
  222.4 1.4 collective-permute-done.24.refs_11_
  223.8 6.1 %finish.3 = f32[3,8,128,512]{3,2,1,0:T(8,128)} custom-call(s32[4]{0:T(128)S(1)} %get-tuple-element.265.first_ref, s32[8,128]{1,0:T(8,128)S(1)} %get-tuple-element.410, s32[8,640]{1,0:T(8,128)S(1)} %copy-done.8, f32[6]{0:T(128)S(1)} %pad_maximum_fusion.3.refs_0_.scalars_ref, s32[128,512]{1,0:T(8,128)S(1)} %copy-done.1, ...), custom_call_target="tpu_custom_call", output_to_operand_aliasing={{}: (7, {})} | custom-call | bytes 9437184 | tf_op jit(solution)/shard_map/finish/pallas_call | solution.py:659
  (60 shorter events, 0.7 us)
Async XLA Ops:
  0.0 0.9 copy-start
  5.7 0.7 copy-start.6
  6.4 29.1 %collective-permute-start.6 = (f32[12,32,128]{2,1,0:T(8,128)}, f32[12,32,128]{2,1,0:T(8,128)S(1)}, u32[]{:S(2)}, u32[]{:S(2)}) collective-permute-start(f32[12,32,128]{2,1,0:T(8,128)} %get-tuple-element.172), channel_id=1, source_target_pairs={{0,8},{8,16},{16,24},{24,0},{1,9},{9,17},{17,25},{25,1},{2,10},{10... | collective-permute-start | bytes 589832 | tf_op jit(solution)/shard_map/ppermute | solution.py:683
  8.0 27.6 %collective-permute-start.7 = (f32[12,32,128]{2,1,0:T(8,128)}, f32[12,32,128]{2,1,0:T(8,128)S(1)}, u32[]{:S(2)}, u32[]{:S(2)}) collective-permute-start(f32[12,32,128]{2,1,0:T(8,128)} %get-tuple-element.173), channel_id=1, source_target_pairs={{0,16},{8,24},{16,0},{24,8},{1,17},{9,25},{17,1},{25,9},{2,18},{10... | collective-permute-start | bytes 589832 | tf_op jit(solution)/shard_map/ppermute | solution.py:683
  18.3 0.9 copy-start.9
  19.2 2.9 %copy-start.10 = (f32[55,32,128]{2,1,0:T(8,128)}, f32[55,32,128]{2,1,0:T(8,128)S(1)}, u32[]{:S(2)}) copy-start(f32[55,32,128]{2,1,0:T(8,128)S(1)} %get-tuple-element.185) | copy-start | bytes 2703364
  19.2 2.9 %copy-start.15 = (bf16[4,64,256]{2,1,0:T(8,128)(2,1)S(1)}, bf16[4,64,256]{2,1,0:T(8,128)(2,1)}, u32[]{:S(2)}) copy-start(bf16[4,64,256]{2,1,0:T(8,128)(2,1)} %constant.93.clone.refs_2_) | copy-start | bytes 393220
  22.1 6.2 %copy-start.12 = (s32[512,128]{1,0:T(8,128)}, s32[512,128]{1,0:T(8,128)S(1)}, u32[]{:S(2)}) copy-start(s32[512,128]{1,0:T(8,128)S(1)} %get-tuple-element.404) | copy-start | bytes 786436
  22.1 46.1 %collective-permute-start.8 = (f32[12,32,128]{2,1,0:T(8,128)S(1)}, f32[12,32,128]{2,1,0:T(8,128)S(1)}, u32[]{:S(2)}, u32[]{:S(2)}) collective-permute-start(f32[12,32,128]{2,1,0:T(8,128)S(1)} %get-tuple-element.174), channel_id=1, source_target_pairs={{0,24},{8,0},{16,8},{24,16},{1,25},{9,1},{17,9},{25,17},{2,26},{10... | collective-permute-start | bytes 589832 | tf_op jit(solution)/shard_map/ppermute | solution.py:683
  24.0 57.5 %collective-permute-start.13 = (f32[55,32,128]{2,1,0:T(8,128)}, f32[55,32,128]{2,1,0:T(8,128)S(1)}, u32[]{:S(2)}, u32[]{:S(2)}) collective-permute-start(f32[55,32,128]{2,1,0:T(8,128)} %copy-done.10), channel_id=1, source_target_pairs={{0,8},{8,16},{16,24},{24,0},{1,9},{9,17},{17,25},{25,1},{2,10},{10... | collective-permute-start | bytes 2703368 | tf_op jit(solution)/shard_map/ppermute | solution.py:683
  24.2 102.8 %collective-permute-start.14 = (f32[55,32,128]{2,1,0:T(8,128)}, f32[55,32,128]{2,1,0:T(8,128)}, u32[]{:S(2)}, u32[]{:S(2)}) collective-permute-start(f32[55,32,128]{2,1,0:T(8,128)} %copy-done.9), channel_id=1, source_target_pairs={{0,16},{8,24},{16,0},{24,8},{1,17},{9,25},{17,1},{25,9},{2,18},{10... | collective-permute-start | bytes 2703368 | tf_op jit(solution)/shard_map/ppermute | solution.py:683
  28.4 39.9 %copy-start.1 = (s32[128,512]{1,0:T(8,128)S(1)}, s32[128,512]{1,0:T(8,128)}, u32[]{:S(2)}) copy-start(s32[128,512]{1,0:T(8,128)} %refs_0_.5) | copy-start | bytes 786436
  28.4 39.9 %copy-start.2 = (f32[128,512]{1,0:T(8,128)S(1)}, f32[128,512]{1,0:T(8,128)}, u32[]{:S(2)}) copy-start(f32[128,512]{1,0:T(8,128)} %refs_8_.1) | copy-start | bytes 786436
  28.4 39.9 %copy-start.11 = (f32[3,8,128,512]{3,2,1,0:T(8,128)S(1)}, f32[3,8,128,512]{3,2,1,0:T(8,128)}, u32[]{:S(2)}) copy-start(f32[3,8,128,512]{3,2,1,0:T(8,128)} %get-tuple-element.402) | copy-start | bytes 18874372
  35.5 33.4 %copy-start.4 = (f32[30,32,128]{2,1,0:T(8,128)}, f32[30,32,128]{2,1,0:T(8,128)S(1)}, u32[]{:S(2)}) copy-start(f32[30,32,128]{2,1,0:T(8,128)S(1)} %get-tuple-element.176.refs_10_.refs_3_) | copy-start | bytes 1474564
  35.5 92.6 %collective-permute-start.15 = (f32[55,32,128]{2,1,0:T(8,128)}, f32[55,32,128]{2,1,0:T(8,128)}, u32[]{:S(2)}, u32[]{:S(2)}) collective-permute-start(f32[55,32,128]{2,1,0:T(8,128)} %get-tuple-element.187), channel_id=1, source_target_pairs={{0,24},{8,0},{16,8},{24,16},{1,25},{9,1},{17,9},{25,17},{2,26},{10... | collective-permute-start | bytes 2703368 | tf_op jit(solution)/shard_map/ppermute | solution.py:683
  69.0 5.0 %collective-permute-start.9 = (f32[2,8,512]{2,1,0:T(8,128)S(1)}, f32[2,8,512]{2,1,0:T(8,128)S(1)}, u32[]{:S(2)}, u32[]{:S(2)}) collective-permute-start(f32[2,8,512]{2,1,0:T(8,128)S(1)} %get-tuple-element.177), channel_id=1, source_target_pairs={{0,4},{1,5},{2,6},{3,7},{8,12},{9,13},{10,14},{11,15},{16,20},{17,... | collective-permute-start | bytes 98312 | tf_op jit(solution)/shard_map/ppermute | solution.py:683
  72.3 5.8 %collective-permute-start.10 = (f32[2,8,512]{2,1,0:T(8,128)S(1)}, f32[2,8,512]{2,1,0:T(8,128)S(1)}, u32[]{:S(2)}, u32[]{:S(2)}) collective-permute-start(f32[2,8,512]{2,1,0:T(8,128)S(1)} %get-tuple-element.178), channel_id=1, source_target_pairs={{4,0},{5,1},{6,2},{7,3},{12,8},{13,9},{14,10},{15,11},{20,16},{21,... | collective-permute-start | bytes 98312 | tf_op jit(solution)/shard_map/ppermute | solution.py:683
  74.0 4.3 %collective-permute-start.12 = (f32[3,8,128]{2,1,0:T(8,128)S(1)}, f32[3,8,128]{2,1,0:T(8,128)S(1)}, u32[]{:S(2)}, u32[]{:S(2)}) collective-permute-start(f32[3,8,128]{2,1,0:T(8,128)S(1)} %pad_maximum_fusion.2), channel_id=1, source_target_pairs={{0,3},{1,0},{2,1},{3,2},{4,7},{5,4},{6,5},{7,6},{8,11},{9,8},{10,9... | collective-permute-start | bytes 36872 | tf_op jit(solution)/shard_map/ppermute | solution.py:683
  78.3 3.1 %collective-permute-start.11 = (f32[3,8,128]{2,1,0:T(8,128)S(1)}, f32[3,8,128]{2,1,0:T(8,128)S(1)}, u32[]{:S(2)}, u32[]{:S(2)}) collective-permute-start(f32[3,8,128]{2,1,0:T(8,128)S(1)} %pad_maximum_fusion.1), channel_id=1, source_target_pairs={{0,1},{1,2},{2,3},{3,0},{4,5},{5,6},{6,7},{7,4},{8,9},{9,10},{10,1... | collective-permute-start | bytes 36872 | tf_op jit(solution)/shard_map/ppermute | solution.py:683
  78.3 73.1 %collective-permute-start.19 = (f32[30,32,128]{2,1,0:T(8,128)}, f32[30,32,128]{2,1,0:T(8,128)}, u32[]{:S(2)}, u32[]{:S(2)}) collective-permute-start(f32[30,32,128]{2,1,0:T(8,128)} %get-tuple-element.193), channel_id=1, source_target_pairs={{0,8},{8,16},{16,24},{24,0},{1,9},{9,17},{17,25},{25,1},{2,10},{10... | collective-permute-start | bytes 1474568 | tf_op jit(solution)/shard_map/ppermute | solution.py:683
  81.4 72.0 %collective-permute-start.20 = (f32[30,32,128]{2,1,0:T(8,128)}, f32[30,32,128]{2,1,0:T(8,128)}, u32[]{:S(2)}, u32[]{:S(2)}) collective-permute-start(f32[30,32,128]{2,1,0:T(8,128)} %get-tuple-element.194), channel_id=1, source_target_pairs={{0,16},{8,24},{16,0},{24,8},{1,17},{9,25},{17,1},{25,9},{2,18},{10... | collective-permute-start | bytes 1474568 | tf_op jit(solution)/shard_map/ppermute | solution.py:683
  81.4 72.0 %collective-permute-start.21 = (f32[30,32,128]{2,1,0:T(8,128)}, f32[30,32,128]{2,1,0:T(8,128)}, u32[]{:S(2)}, u32[]{:S(2)}) collective-permute-start(f32[30,32,128]{2,1,0:T(8,128)} %get-tuple-element.195), channel_id=1, source_target_pairs={{0,24},{8,0},{16,8},{24,16},{1,25},{9,1},{17,9},{25,17},{2,26},{10... | collective-permute-start | bytes 1474568 | tf_op jit(solution)/shard_map/ppermute | solution.py:683
  83.0 45.1 %copy-start.7 = (f32[12,32,128]{2,1,0:T(8,128)S(1)}, f32[12,32,128]{2,1,0:T(8,128)}, u32[]{:S(2)}) copy-start(f32[12,32,128]{2,1,0:T(8,128)} %copy-done.6) | copy-start | bytes 589828
  83.0 45.1 %copy-start.14 = (bf16[4,256,96]{2,1,0:T(8,128)(2,1)S(1)}, bf16[4,256,96]{2,1,0:T(8,128)(2,1)}, u32[]{:S(2)}) copy-start(bf16[4,256,96]{2,1,0:T(8,128)(2,1)} %get-tuple-element.405) | copy-start | bytes 589828
  83.0 45.0 %copy-start.16 = (bf16[4,64,256]{2,1,0:T(8,128)(2,1)S(1)}, bf16[4,64,256]{2,1,0:T(8,128)(2,1)}, u32[]{:S(2)}) copy-start(bf16[4,64,256]{2,1,0:T(8,128)(2,1)} %constant.93.clone.refs_2_) | copy-start | bytes 393220
  128.1 25.3 %copy-start.5 = (f32[30,32,128]{2,1,0:T(8,128)S(1)}, f32[30,32,128]{2,1,0:T(8,128)}, u32[]{:S(2)}) copy-start(f32[30,32,128]{2,1,0:T(8,128)} %copy-done.4) | copy-start | bytes 1474564
  149.1 36.9 %collective-permute-start.16 = (f32[1144,128]{1,0:T(8,128)S(1)}, f32[1144,128]{1,0:T(8,128)S(1)}, u32[]{:S(2)}, u32[]{:S(2)}) collective-permute-start(f32[1144,128]{1,0:T(8,128)S(1)} %get-tuple-element.189), channel_id=1, source_target_pairs={{0,8},{8,16},{16,24},{24,0},{1,9},{9,17},{17,25},{25,1},{2,10},{10... | collective-permute-start | bytes 1757192 | tf_op jit(solution)/shard_map/ppermute | solution.py:683
  149.1 62.7 %collective-permute-start.17 = (f32[1144,128]{1,0:T(8,128)}, f32[1144,128]{1,0:T(8,128)S(1)}, u32[]{:S(2)}, u32[]{:S(2)}) collective-permute-start(f32[1144,128]{1,0:T(8,128)} %get-tuple-element.190), channel_id=1, source_target_pairs={{0,16},{8,24},{16,0},{24,8},{1,17},{9,25},{17,1},{25,9},{2,18},{10... | collective-permute-start | bytes 1757192 | tf_op jit(solution)/shard_map/ppermute | solution.py:683
  151.5 61.0 %copy-start.3 = (f32[128,512]{1,0:T(8,128)S(1)}, f32[128,512]{1,0:T(8,128)}, u32[]{:S(2)}) copy-start(f32[128,512]{1,0:T(8,128)} %refs_1_.9) | copy-start | bytes 786436
  151.5 61.0 %copy-start.8 = (s32[8,640]{1,0:T(8,128)S(1)}, s32[8,640]{1,0:T(8,128)}, u32[]{:S(2)}) copy-start(s32[8,640]{1,0:T(8,128)} %constant.91.clone.table_ref) | copy-start | bytes 61444
  151.5 61.0 %collective-permute-start.18 = (f32[1144,128]{1,0:T(8,128)}, f32[1144,128]{1,0:T(8,128)S(1)}, u32[]{:S(2)}, u32[]{:S(2)}) collective-permute-start(f32[1144,128]{1,0:T(8,128)} %get-tuple-element.191), channel_id=1, source_target_pairs={{0,24},{8,0},{16,8},{24,16},{1,25},{9,1},{17,9},{25,17},{2,26},{10... | collective-permute-start | bytes 1757192 | tf_op jit(solution)/shard_map/ppermute | solution.py:683
  163.2 59.2 %collective-permute-start.22 = (f32[512,128]{1,0:T(8,128)}, f32[512,128]{1,0:T(8,128)}, u32[]{:S(2)}, u32[]{:S(2)}) collective-permute-start(f32[512,128]{1,0:T(8,128)} %get-tuple-element.197), channel_id=1, source_target_pairs={{0,8},{8,16},{16,24},{24,0},{1,9},{9,17},{17,25},{25,1},{2,10},{10... | collective-permute-start | bytes 786440 | tf_op jit(solution)/shard_map/ppermute | solution.py:683
  163.3 59.1 %collective-permute-start.23 = (f32[512,128]{1,0:T(8,128)}, f32[512,128]{1,0:T(8,128)}, u32[]{:S(2)}, u32[]{:S(2)}) collective-permute-start(f32[512,128]{1,0:T(8,128)} %get-tuple-element.198), channel_id=1, source_target_pairs={{0,16},{8,24},{16,0},{24,8},{1,17},{9,25},{17,1},{25,9},{2,18},{10... | collective-permute-start | bytes 786440 | tf_op jit(solution)/shard_map/ppermute | solution.py:683
  185.9 37.8 %collective-permute-start.24 = (f32[512,128]{1,0:T(8,128)}, f32[512,128]{1,0:T(8,128)}, u32[]{:S(2)}, u32[]{:S(2)}) collective-permute-start(f32[512,128]{1,0:T(8,128)} %get-tuple-element.199), channel_id=1, source_target_pairs={{0,24},{8,0},{16,8},{24,16},{1,25},{9,1},{17,9},{25,17},{2,26},{10... | collective-permute-start | bytes 786440 | tf_op jit(solution)/shard_map/ppermute | solution.py:683
  212.5 11.2 %copy-start.17 = (f32[4,544,128]{2,1,0:T(8,128)S(1)}, f32[4,544,128]{2,1,0:T(8,128)}, u32[]{:S(2)}) copy-start(f32[4,544,128]{2,1,0:T(8,128)} %get-tuple-element.200) | copy-start | bytes 3342340

commit v11 on v10

--- a/solution.py
+++ b/solution.py
@@ -19,7 +19,7 @@
 OMEGA_STEP = 0.25
 SPEED_SOFT = 0.01
 VMEM_BYTES = 48 * 1024 * 1024
-CHUNK_SHARES = (12, 55, 30)
+CHUNK_SHARES = (18, 49, 30)
 SHARE_UNITS = 128
 LOOP_TILES = 8
 PACK_COST = 16384

time: 231 us -> 228 us (0.987)
  waiting for transfers between devices: 116 us -> 111 us
    ppermute x19, waiting for transfers between devices: 116 us -> 111 us  [shifted(): return lax.ppermute(block, axis, pairs)]
where the time goes in v11:
time: 228 us; the launch traced here: 226 us
  waiting for transfers between devices  111 us (49%)
  Pallas kernels  78.6 us (34%)
  starting transfers between devices  22.3 us (10%)
  local copies, waits for them, and re-layouts  7.67 us (3%)
  between operations  4.68 us (2%)
    ppermute x19, waiting for transfers between devices, shifted(): return lax.ppermute(block, axis, pairs)  111 us
    pallas_call x2, Pallas kernels, friction_call(): pl.pallas_call(lambda *refs: friction_kernel(groups, coefs, chunk_tiles,...  29.6 us
    ppermute x19, starting transfers between devices, shifted(): return lax.ppermute(block, axis, pairs)  22.3 us
    pallas_call x3, Pallas kernels, pack_call(): pl.pallas_call(lambda *refs: pack_kernel(groups, coefs, tiles, len(waited...  17.4 us
    pallas_call x2, Pallas kernels, finish_call(): pl.pallas_call(kernel, out_shape=jax.ShapeDtypeStruct(result.shape, jnp.f...  15.9 us
    pallas_call x1, Pallas kernels, prepare_call(): pl.pallas_call(lambda *refs: prepare_kernel(coefs, *refs), out_shape=[jax...  14.2 us
  transfers between devices with their start and end apart: 19, of which 10 were waited for; matrix products, arithmetic and copies ran while one was open for 3% of the time, Pallas kernels for 30%

profile of v11, /device:TPU:12, one launch (start us, length us, event | category | flops | bytes accessed | tf_op | source)
XLA Modules:
  0.0 225.7 jit_solution(2712937504236445459)
XLA Ops:
  0.0 0.9 copy-done
  1.0 1.0 index.1
  2.0 4.1 %pack.7 = (f32[18,32,128]{2,1,0:T(8,128)S(1)}, f32[18,32,128]{2,1,0:T(8,128)}, f32[18,32,128]{2,1,0:T(8,128)S(1)}, f32[18,32,128]{2,1,0:T(8,128)S(1)}, s32[8,128]{1,0:T(8,128)S(1)}) custom-call(s32[2]{0:T(128)S(1)} %pad_add_fusion.1.refs_0_, s32[8,128]{1,0:T(8,128)S(1)} %get-tuple-element.337.refs_1_.offset_ref, s32[512,128]{1,0:T(8,128)S(1)} %get-tuple-element.338.refs_2_, ...), custom_call_target="tpu_custom_call" | custom-call | bytes 9437184 | tf_op jit(solution)/shard_map/pack/pallas_call | solution.py:357
  6.2 1.6 collective-permute-start.6
  7.8 1.2 collective-permute-start.7
  9.0 0.5 slice.40
  9.6 0.5 slice.41
  10.8 6.2 %pack.8 = (f32[49,32,128]{2,1,0:T(8,128)S(1)}, f32[49,32,128]{2,1,0:T(8,128)S(1)}, f32[49,32,128]{2,1,0:T(8,128)S(1)}, f32[49,32,128]{2,1,0:T(8,128)}, s32[8,128]{1,0:T(8,128)S(1)}) custom-call(s32[2]{0:T(128)S(1)} %pad_add_fusion.2.refs_0_, s32[8,128]{1,0:T(8,128)S(1)} %get-tuple-element.337.refs_1_.offset_ref, s32[512,128]{1,0:T(8,128)S(1)} %get-tuple-element.338.refs_2_, ...), custom_call_target="tpu_custom_call" | custom-call | bytes 25690112 | tf_op jit(solution)/shard_map/pack/pallas_call | solution.py:357
  17.0 0.9 copy-done.7
  17.9 0.9 copy-done.8
  18.8 0.5 slice.42
  20.6 1.1 broadcast_in_dim.15
  21.7 1.9 collective-permute-start.8
  23.5 0.2 collective-permute-start.13
  23.7 3.5 %collective-permute-start.14 = (f32[49,32,128]{2,1,0:T(8,128)}, f32[49,32,128]{2,1,0:T(8,128)}, u32[]{:S(2)}, u32[]{:S(2)}) collective-permute-start(f32[49,32,128]{2,1,0:T(8,128)} %copy-done.7), channel_id=1, source_target_pairs={{0,16},{8,24},{16,0},{24,8},{1,17},{9,25},{17,1},{25,9},{2,18},{10... | collective-permute-start | bytes 2408456 | tf_op jit(solution)/shard_map/ppermute | solution.py:683
  27.9 7.1 %pack.9 = (f32[30,32,128]{2,1,0:T(8,128)S(1)}, f32[30,32,128]{2,1,0:T(8,128)}, f32[30,32,128]{2,1,0:T(8,128)}, f32[30,32,128]{2,1,0:T(8,128)}, s32[8,128]{1,0:T(8,128)}) custom-call(s32[2]{0:T(128)S(1)} %pad_add_fusion.3.refs_0_, s32[8,128]{1,0:T(8,128)S(1)} %get-tuple-element.410, s32[512,128]{1,0:T(8,128)} %copy-done.10, ...), custom_call_target="tpu_custom_call" | custom-call | bytes 15728640 | tf_op jit(solution)/shard_map/pack/pallas_call | solution.py:357
  35.1 34.1 %collective-permute-done.8.refs_9_.refs_6_ = f32[18,32,128]{2,1,0:T(8,128)S(1)} collective-permute-done((f32[18,32,128]{2,1,0:T(8,128)S(1)}, f32[18,32,128]{2,1,0:T(8,128)S(1)}, u32[]{:S(2)}, u32[]{:S(2)}) %collective-permute-start.8) | collective-permute-done | bytes 294944 | tf_op jit(solution)/shard_map/ppermute | solution.py:683
  69.2 0.6 edges.1
  69.9 3.4 %collective-permute-start.9 = (f32[2,8,512]{2,1,0:T(8,128)S(1)}, f32[2,8,512]{2,1,0:T(8,128)S(1)}, u32[]{:S(2)}, u32[]{:S(2)}) collective-permute-start(f32[2,8,512]{2,1,0:T(8,128)S(1)} %get-tuple-element.177), channel_id=1, source_target_pairs={{0,4},{1,5},{2,6},{3,7},{8,12},{9,13},{10,14},{11,15},{16,20},{17,... | collective-permute-start | bytes 98312 | tf_op jit(solution)/shard_map/ppermute | solution.py:683
  73.3 1.3 collective-permute-start.10
  74.6 0.3 collective-permute-done.9.refs_9_
  74.9 0.1 maximum_bitcast_fusion.2
  75.0 4.2 %collective-permute-done.10.refs_10_ = f32[2,8,512]{2,1,0:T(8,128)S(1)} collective-permute-done((f32[2,8,512]{2,1,0:T(8,128)S(1)}, f32[2,8,512]{2,1,0:T(8,128)S(1)}, u32[]{:S(2)}, u32[]{:S(2)}) %collective-permute-start.10) | collective-permute-done | bytes 32800 | tf_op jit(solution)/shard_map/ppermute | solution.py:683
  79.2 0.1 maximum_bitcast_fusion.1
  79.4 3.0 %collective-permute-done.11 = f32[3,8,128]{2,1,0:T(8,128)S(1)} collective-permute-done((f32[3,8,128]{2,1,0:T(8,128)S(1)}, f32[3,8,128]{2,1,0:T(8,128)S(1)}, u32[]{:S(2)}, u32[]{:S(2)}) %collective-permute-start.11) | collective-permute-done | bytes 12320 | tf_op jit(solution)/shard_map/ppermute | solution.py:683
  82.4 3.8 %collective-permute-done.13.refs_8_ = f32[49,32,128]{2,1,0:T(8,128)} collective-permute-done((f32[49,32,128]{2,1,0:T(8,128)}, f32[49,32,128]{2,1,0:T(8,128)}, u32[]{:S(2)}, u32[]{:S(2)}) %collective-permute-start.13) | collective-permute-done | bytes 802848 | tf_op jit(solution)/shard_map/ppermute | solution.py:683
  86.2 0.1 pad_maximum_fusion.3.refs_0_.scalars_ref
  86.3 0.9 broadcast_in_dim.16.refs_11_
  87.2 14.2 %prepare.1 = (f32[3,8,128,512]{3,2,1,0:T(8,128)}, s32[8,128]{1,0:T(8,128)S(1)}) custom-call(f32[6]{0:T(128)S(1)} %pad_maximum_fusion.3.refs_0_.scalars_ref, f32[3,8,128,512]{3,2,1,0:T(8,128)} %get-tuple-element.402, f32[3,8,128,512]{3,2,1,0:T(8,128)} %get-tuple-element.402, f32[3,8,128,512]{3,2,1,0:T(8,128)} %get-tuple-element.402, ...), custom_call_target="tpu_custom_call" | custom-call | flops 524288 | tf_op jit(solution)/shard_map/prepare/pallas_call | solution.py:479
  101.4 0.6 slice.49
  102.6 21.9 %collective-permute-done.14.refs_9_ = f32[49,32,128]{2,1,0:T(8,128)} collective-permute-done((f32[49,32,128]{2,1,0:T(8,128)}, f32[49,32,128]{2,1,0:T(8,128)}, u32[]{:S(2)}, u32[]{:S(2)}) %collective-permute-start.14) | collective-permute-done | bytes 802848 | tf_op jit(solution)/shard_map/ppermute | solution.py:683
  124.5 0.3 collective-permute-done.15.refs_10_
  124.8 19.8 %friction.6 = (f32[1144,128]{1,0:T(8,128)S(1)}, f32[1144,128]{1,0:T(8,128)S(1)}, f32[1144,128]{1,0:T(8,128)}, f32[1144,128]{1,0:T(8,128)}, s32[8,128]{1,0:T(8,128)S(1)}) custom-call(s32[1]{0:T(128)S(6)} %add.52.refs_0_, bf16[4,256,96]{2,1,0:T(8,128)(2,1)S(1)} %copy-done.12, bf16[4,64,256]{2,1,0:T(8,128)(2,1)S(1)} %get-tuple-element.406, ...), custom_call_target="tpu_custom_call" | custom-call | flops 8781824 | tf_op jit(solution)/shard_map/friction/pallas_call | solution.py:153
  144.6 0.5 slice.50
  145.8 3.1 %collective-permute-start.17 = (f32[1144,128]{1,0:T(8,128)}, f32[1144,128]{1,0:T(8,128)S(1)}, u32[]{:S(2)}, u32[]{:S(2)}) collective-permute-start(f32[1144,128]{1,0:T(8,128)} %get-tuple-element.190), channel_id=1, source_target_pairs={{0,16},{8,24},{16,0},{24,8},{1,17},{9,25},{17,1},{25,9},{2,18},{10... | collective-permute-start | bytes 1757192 | tf_op jit(solution)/shard_map/ppermute | solution.py:683
  149.0 2.0 collective-permute-start.18
  151.0 9.8 %friction.7 = (f32[512,128]{1,0:T(8,128)S(1)}, f32[512,128]{1,0:T(8,128)}, f32[512,128]{1,0:T(8,128)}, f32[512,128]{1,0:T(8,128)}, s32[8,128]{1,0:T(8,128)}) custom-call(s32[1]{0:T(128)S(6)} %add.53.refs_0_, bf16[4,256,96]{2,1,0:T(8,128)(2,1)S(1)} %copy-done.12, bf16[4,64,256]{2,1,0:T(8,128)(2,1)S(1)} %get-tuple-element.406, f32[30,32,128]{2,1,0:T(8,128)S(1)} %copy-done.5, ...), custom_call_target="tpu_custom_call" | custom-call | flops 8053063680 | tf_op jit(solution)/shard_map/friction/pallas_call | solution.py:153
  160.8 0.1 collective-permute-start.22
  160.9 2.3 %collective-permute-start.23 = (f32[512,128]{1,0:T(8,128)}, f32[512,128]{1,0:T(8,128)}, u32[]{:S(2)}, u32[]{:S(2)}) collective-permute-start(f32[512,128]{1,0:T(8,128)} %get-tuple-element.198), channel_id=1, source_target_pairs={{0,16},{8,24},{16,0},{24,8},{1,17},{9,25},{17,1},{25,9},{2,18},{10... | collective-permute-start | bytes 786440 | tf_op jit(solution)/shard_map/ppermute | solution.py:683
  163.2 1.5 collective-permute-start.24
  164.6 0.1 slice.39
  164.7 0.7 fusion.1
  166.1 0.7 add_add_fusion
  166.8 41.6 %collective-permute-done.17.refs_6_ = f32[1144,128]{1,0:T(8,128)S(1)} collective-permute-done((f32[1144,128]{1,0:T(8,128)}, f32[1144,128]{1,0:T(8,128)S(1)}, u32[]{:S(2)}, u32[]{:S(2)}) %collective-permute-start.17) | collective-permute-done | bytes 585760 | tf_op jit(solution)/shard_map/ppermute | solution.py:683
  208.4 9.9 %finish.2.refs_3_ = f32[3,8,128,512]{3,2,1,0:T(8,128)} custom-call(s32[4]{0:T(128)S(1)} %get-tuple-element.266.first_ref, s32[8,128]{1,0:T(8,128)S(1)} %copy-done.16, s32[8,640]{1,0:T(8,128)S(1)} %copy-done.6, f32[6]{0:T(128)S(1)} %pad_maximum_fusion.3.refs_0_.scalars_ref, s32[128,512]{1,0:T(8,128)S(1)} %copy-done.1, ...), custom_call_target="tpu_custom_call", output_to_operand_aliasing={{}: (7, {})} | custom-call | bytes 9437184 | tf_op jit(solution)/shard_map/finish/pallas_call | solution.py:659
  218.3 0.6 collective-permute-done.23.refs_10_
  218.9 0.7 collective-permute-done.24.refs_11_
  219.7 6.1 %finish.3 = f32[3,8,128,512]{3,2,1,0:T(8,128)} custom-call(s32[4]{0:T(128)S(1)} %get-tuple-element.265.first_ref, s32[8,128]{1,0:T(8,128)S(1)} %copy-done.16, s32[8,640]{1,0:T(8,128)S(1)} %copy-done.6, f32[6]{0:T(128)S(1)} %pad_maximum_fusion.3.refs_0_.scalars_ref, s32[128,512]{1,0:T(8,128)S(1)} %copy-done.1, ...), custom_call_target="tpu_custom_call", output_to_operand_aliasing={{}: (7, {})} | custom-call | bytes 9437184 | tf_op jit(solution)/shard_map/finish/pallas_call | solution.py:659
  (58 shorter events, 0.7 us)
Async XLA Ops:
  0.0 0.9 copy-start
  6.2 28.9 %collective-permute-start.6 = (f32[18,32,128]{2,1,0:T(8,128)}, f32[18,32,128]{2,1,0:T(8,128)S(1)}, u32[]{:S(2)}, u32[]{:S(2)}) collective-permute-start(f32[18,32,128]{2,1,0:T(8,128)} %get-tuple-element.172), channel_id=1, source_target_pairs={{0,8},{8,16},{16,24},{24,0},{1,9},{9,17},{17,25},{25,1},{2,10},{10... | collective-permute-start | bytes 884744 | tf_op jit(solution)/shard_map/ppermute | solution.py:683
  7.8 27.3 %collective-permute-start.7 = (f32[18,32,128]{2,1,0:T(8,128)S(1)}, f32[18,32,128]{2,1,0:T(8,128)S(1)}, u32[]{:S(2)}, u32[]{:S(2)}) collective-permute-start(f32[18,32,128]{2,1,0:T(8,128)S(1)} %get-tuple-element.173), channel_id=1, source_target_pairs={{0,16},{8,24},{16,0},{24,8},{1,17},{9,25},{17,1},{25,9},{2,18},{10... | collective-permute-start | bytes 884744 | tf_op jit(solution)/shard_map/ppermute | solution.py:683
  17.0 0.9 copy-start.7
  17.9 0.9 copy-start.8
  17.9 3.8 %copy-start.13 = (bf16[4,64,256]{2,1,0:T(8,128)(2,1)S(1)}, bf16[4,64,256]{2,1,0:T(8,128)(2,1)}, u32[]{:S(2)}) copy-start(bf16[4,64,256]{2,1,0:T(8,128)(2,1)} %constant.93.clone.refs_2_) | copy-start | bytes 393220
  21.7 6.2 %copy-start.10 = (s32[512,128]{1,0:T(8,128)}, s32[512,128]{1,0:T(8,128)S(1)}, u32[]{:S(2)}) copy-start(s32[512,128]{1,0:T(8,128)S(1)} %get-tuple-element.404) | copy-start | bytes 786436
  21.7 13.4 %copy-start.15 = (s32[8,128]{1,0:T(8,128)}, s32[8,128]{1,0:T(8,128)S(1)}, u32[]{:S(2)}) copy-start(s32[8,128]{1,0:T(8,128)S(1)} %get-tuple-element.410) | copy-start | bytes 12292
  21.7 47.6 %collective-permute-start.8 = (f32[18,32,128]{2,1,0:T(8,128)S(1)}, f32[18,32,128]{2,1,0:T(8,128)S(1)}, u32[]{:S(2)}, u32[]{:S(2)}) collective-permute-start(f32[18,32,128]{2,1,0:T(8,128)S(1)} %get-tuple-element.174), channel_id=1, source_target_pairs={{0,24},{8,0},{16,8},{24,16},{1,25},{9,1},{17,9},{25,17},{2,26},{10... | collective-permute-start | bytes 884744 | tf_op jit(solution)/shard_map/ppermute | solution.py:683
  23.5 62.7 %collective-permute-start.13 = (f32[49,32,128]{2,1,0:T(8,128)}, f32[49,32,128]{2,1,0:T(8,128)}, u32[]{:S(2)}, u32[]{:S(2)}) collective-permute-start(f32[49,32,128]{2,1,0:T(8,128)} %copy-done.8), channel_id=1, source_target_pairs={{0,8},{8,16},{16,24},{24,0},{1,9},{9,17},{17,25},{25,1},{2,10},{10... | collective-permute-start | bytes 2408456 | tf_op jit(solution)/shard_map/ppermute | solution.py:683
  23.7 100.8 %collective-permute-start.14 = (f32[49,32,128]{2,1,0:T(8,128)}, f32[49,32,128]{2,1,0:T(8,128)}, u32[]{:S(2)}, u32[]{:S(2)}) collective-permute-start(f32[49,32,128]{2,1,0:T(8,128)} %copy-done.7), channel_id=1, source_target_pairs={{0,16},{8,24},{16,0},{24,8},{1,17},{9,25},{17,1},{25,9},{2,18},{10... | collective-permute-start | bytes 2408456 | tf_op jit(solution)/shard_map/ppermute | solution.py:683
  27.9 41.3 %copy-start.1 = (s32[128,512]{1,0:T(8,128)S(1)}, s32[128,512]{1,0:T(8,128)}, u32[]{:S(2)}) copy-start(s32[128,512]{1,0:T(8,128)} %refs_0_.5) | copy-start | bytes 786436
  27.9 41.3 %copy-start.2 = (f32[128,512]{1,0:T(8,128)S(1)}, f32[128,512]{1,0:T(8,128)}, u32[]{:S(2)}) copy-start(f32[128,512]{1,0:T(8,128)} %refs_8_.1) | copy-start | bytes 786436
  27.9 41.3 %copy-start.9 = (f32[3,8,128,512]{3,2,1,0:T(8,128)S(1)}, f32[3,8,128,512]{3,2,1,0:T(8,128)}, u32[]{:S(2)}) copy-start(f32[3,8,128,512]{3,2,1,0:T(8,128)} %get-tuple-element.402) | copy-start | bytes 18874372
  35.0 34.8 %copy-start.4 = (f32[30,32,128]{2,1,0:T(8,128)}, f32[30,32,128]{2,1,0:T(8,128)S(1)}, u32[]{:S(2)}) copy-start(f32[30,32,128]{2,1,0:T(8,128)S(1)} %get-tuple-element.176.refs_10_.refs_3_) | copy-start | bytes 1474564
  35.1 89.8 %collective-permute-start.15 = (f32[49,32,128]{2,1,0:T(8,128)}, f32[49,32,128]{2,1,0:T(8,128)}, u32[]{:S(2)}, u32[]{:S(2)}) collective-permute-start(f32[49,32,128]{2,1,0:T(8,128)} %get-tuple-element.187), channel_id=1, source_target_pairs={{0,24},{8,0},{16,8},{24,16},{1,25},{9,1},{17,9},{25,17},{2,26},{10... | collective-permute-start | bytes 2408456 | tf_op jit(solution)/shard_map/ppermute | solution.py:683
  69.9 5.0 %collective-permute-start.9 = (f32[2,8,512]{2,1,0:T(8,128)S(1)}, f32[2,8,512]{2,1,0:T(8,128)S(1)}, u32[]{:S(2)}, u32[]{:S(2)}) collective-permute-start(f32[2,8,512]{2,1,0:T(8,128)S(1)} %get-tuple-element.177), channel_id=1, source_target_pairs={{0,4},{1,5},{2,6},{3,7},{8,12},{9,13},{10,14},{11,15},{16,20},{17,... | collective-permute-start | bytes 98312 | tf_op jit(solution)/shard_map/ppermute | solution.py:683
  73.3 5.8 %collective-permute-start.10 = (f32[2,8,512]{2,1,0:T(8,128)S(1)}, f32[2,8,512]{2,1,0:T(8,128)S(1)}, u32[]{:S(2)}, u32[]{:S(2)}) collective-permute-start(f32[2,8,512]{2,1,0:T(8,128)S(1)} %get-tuple-element.178), channel_id=1, source_target_pairs={{4,0},{5,1},{6,2},{7,3},{12,8},{13,9},{14,10},{15,11},{20,16},{21,... | collective-permute-start | bytes 98312 | tf_op jit(solution)/shard_map/ppermute | solution.py:683
  75.0 4.3 %collective-permute-start.12 = (f32[3,8,128]{2,1,0:T(8,128)S(1)}, f32[3,8,128]{2,1,0:T(8,128)S(1)}, u32[]{:S(2)}, u32[]{:S(2)}) collective-permute-start(f32[3,8,128]{2,1,0:T(8,128)S(1)} %pad_maximum_fusion.2), channel_id=1, source_target_pairs={{0,3},{1,0},{2,1},{3,2},{4,7},{5,4},{6,5},{7,6},{8,11},{9,8},{10,9... | collective-permute-start | bytes 36872 | tf_op jit(solution)/shard_map/ppermute | solution.py:683
  79.3 3.1 %collective-permute-start.11 = (f32[3,8,128]{2,1,0:T(8,128)S(1)}, f32[3,8,128]{2,1,0:T(8,128)S(1)}, u32[]{:S(2)}, u32[]{:S(2)}) collective-permute-start(f32[3,8,128]{2,1,0:T(8,128)S(1)} %pad_maximum_fusion.1), channel_id=1, source_target_pairs={{0,1},{1,2},{2,3},{3,0},{4,5},{5,6},{6,7},{7,4},{8,9},{9,10},{10,1... | collective-permute-start | bytes 36872 | tf_op jit(solution)/shard_map/ppermute | solution.py:683
  79.3 69.7 %collective-permute-start.19 = (f32[30,32,128]{2,1,0:T(8,128)}, f32[30,32,128]{2,1,0:T(8,128)}, u32[]{:S(2)}, u32[]{:S(2)}) collective-permute-start(f32[30,32,128]{2,1,0:T(8,128)} %get-tuple-element.193), channel_id=1, source_target_pairs={{0,8},{8,16},{16,24},{24,0},{1,9},{9,17},{17,25},{25,1},{2,10},{10... | collective-permute-start | bytes 1474568 | tf_op jit(solution)/shard_map/ppermute | solution.py:683
  82.4 68.6 %collective-permute-start.20 = (f32[30,32,128]{2,1,0:T(8,128)}, f32[30,32,128]{2,1,0:T(8,128)}, u32[]{:S(2)}, u32[]{:S(2)}) collective-permute-start(f32[30,32,128]{2,1,0:T(8,128)} %get-tuple-element.194), channel_id=1, source_target_pairs={{0,16},{8,24},{16,0},{24,8},{1,17},{9,25},{17,1},{25,9},{2,18},{10... | collective-permute-start | bytes 1474568 | tf_op jit(solution)/shard_map/ppermute | solution.py:683
  86.2 64.8 %collective-permute-start.21 = (f32[30,32,128]{2,1,0:T(8,128)}, f32[30,32,128]{2,1,0:T(8,128)}, u32[]{:S(2)}, u32[]{:S(2)}) collective-permute-start(f32[30,32,128]{2,1,0:T(8,128)} %get-tuple-element.195), channel_id=1, source_target_pairs={{0,24},{8,0},{16,8},{24,16},{1,25},{9,1},{17,9},{25,17},{2,26},{10... | collective-permute-start | bytes 1474568 | tf_op jit(solution)/shard_map/ppermute | solution.py:683
  87.2 37.7 %copy-start.12 = (bf16[4,256,96]{2,1,0:T(8,128)(2,1)S(1)}, bf16[4,256,96]{2,1,0:T(8,128)(2,1)}, u32[]{:S(2)}) copy-start(bf16[4,256,96]{2,1,0:T(8,128)(2,1)} %get-tuple-element.405) | copy-start | bytes 589828
  124.8 26.1 %copy-start.5 = (f32[30,32,128]{2,1,0:T(8,128)S(1)}, f32[30,32,128]{2,1,0:T(8,128)}, u32[]{:S(2)}) copy-start(f32[30,32,128]{2,1,0:T(8,128)} %copy-done.4) | copy-start | bytes 1474564
  145.8 17.4 %collective-permute-start.16 = (f32[1144,128]{1,0:T(8,128)S(1)}, f32[1144,128]{1,0:T(8,128)S(1)}, u32[]{:S(2)}, u32[]{:S(2)}) collective-permute-start(f32[1144,128]{1,0:T(8,128)S(1)} %get-tuple-element.189), channel_id=1, source_target_pairs={{0,8},{8,16},{16,24},{24,0},{1,9},{9,17},{17,25},{25,1},{2,10},{10... | collective-permute-start | bytes 1757192 | tf_op jit(solution)/shard_map/ppermute | solution.py:683
  145.8 62.6 %collective-permute-start.17 = (f32[1144,128]{1,0:T(8,128)}, f32[1144,128]{1,0:T(8,128)S(1)}, u32[]{:S(2)}, u32[]{:S(2)}) collective-permute-start(f32[1144,128]{1,0:T(8,128)} %get-tuple-element.190), channel_id=1, source_target_pairs={{0,16},{8,24},{16,0},{24,8},{1,17},{9,25},{17,1},{25,9},{2,18},{10... | collective-permute-start | bytes 1757192 | tf_op jit(solution)/shard_map/ppermute | solution.py:683
  149.0 15.7 %copy-start.16 = (s32[8,128]{1,0:T(8,128)S(1)}, s32[8,128]{1,0:T(8,128)}, u32[]{:S(2)}) copy-start(s32[8,128]{1,0:T(8,128)} %copy-done.15) | copy-start | bytes 12292
  149.0 59.5 %copy-start.3 = (f32[128,512]{1,0:T(8,128)S(1)}, f32[128,512]{1,0:T(8,128)}, u32[]{:S(2)}) copy-start(f32[128,512]{1,0:T(8,128)} %refs_1_.9) | copy-start | bytes 786436
  149.0 59.5 %copy-start.6 = (s32[8,640]{1,0:T(8,128)S(1)}, s32[8,640]{1,0:T(8,128)}, u32[]{:S(2)}) copy-start(s32[8,640]{1,0:T(8,128)} %constant.91.clone.table_ref) | copy-start | bytes 61444
  149.0 59.4 %collective-permute-start.18 = (f32[1144,128]{1,0:T(8,128)}, f32[1144,128]{1,0:T(8,128)S(1)}, u32[]{:S(2)}, u32[]{:S(2)}) collective-permute-start(f32[1144,128]{1,0:T(8,128)} %get-tuple-element.191), channel_id=1, source_target_pairs={{0,24},{8,0},{16,8},{24,16},{1,25},{9,1},{17,9},{25,17},{2,26},{10... | collective-permute-start | bytes 1757192 | tf_op jit(solution)/shard_map/ppermute | solution.py:683
  160.8 57.5 %collective-permute-start.22 = (f32[512,128]{1,0:T(8,128)}, f32[512,128]{1,0:T(8,128)}, u32[]{:S(2)}, u32[]{:S(2)}) collective-permute-start(f32[512,128]{1,0:T(8,128)} %get-tuple-element.197), channel_id=1, source_target_pairs={{0,8},{8,16},{16,24},{24,0},{1,9},{9,17},{17,25},{25,1},{2,10},{10... | collective-permute-start | bytes 786440 | tf_op jit(solution)/shard_map/ppermute | solution.py:683
  160.9 58.1 %collective-permute-start.23 = (f32[512,128]{1,0:T(8,128)}, f32[512,128]{1,0:T(8,128)}, u32[]{:S(2)}, u32[]{:S(2)}) collective-permute-start(f32[512,128]{1,0:T(8,128)} %get-tuple-element.198), channel_id=1, source_target_pairs={{0,16},{8,24},{16,0},{24,8},{1,17},{9,25},{17,1},{25,9},{2,18},{10... | collective-permute-start | bytes 786440 | tf_op jit(solution)/shard_map/ppermute | solution.py:683
  163.2 56.5 %collective-permute-start.24 = (f32[512,128]{1,0:T(8,128)}, f32[512,128]{1,0:T(8,128)}, u32[]{:S(2)}, u32[]{:S(2)}) collective-permute-start(f32[512,128]{1,0:T(8,128)} %get-tuple-element.199), channel_id=1, source_target_pairs={{0,24},{8,0},{16,8},{24,16},{1,25},{9,1},{17,9},{25,17},{2,26},{10... | collective-permute-start | bytes 786440 | tf_op jit(solution)/shard_map/ppermute | solution.py:683
  208.4 11.2 %copy-start.14 = (f32[4,544,128]{2,1,0:T(8,128)S(1)}, f32[4,544,128]{2,1,0:T(8,128)}, u32[]{:S(2)}) copy-start(f32[4,544,128]{2,1,0:T(8,128)} %get-tuple-element.200) | copy-start | bytes 3342340

commit v12 on v11

--- a/solution.py
+++ b/solution.py
@@ -19,7 +19,7 @@
 OMEGA_STEP = 0.25
 SPEED_SOFT = 0.01
 VMEM_BYTES = 48 * 1024 * 1024
-CHUNK_SHARES = (18, 49, 30)
+CHUNK_SHARES = (16, 50, 31)
 SHARE_UNITS = 128
 LOOP_TILES = 8
 PACK_COST = 16384

time: 228 us -> 227 us (level)
  transfers between devices with their start and end apart: 19 -> 19, of which waited for: 10 -> 11; matrix products, arithmetic and copies ran while one was open for 3% -> 3% of each run, Pallas kernels for 30% -> 30%
where the time goes in v12:
time: 227 us; the launch traced here: 226 us
  waiting for transfers between devices  110 us (48%)
  Pallas kernels  79 us (35%)
  starting transfers between devices  21.2 us (9%)
  local copies, waits for them, and re-layouts  8.1 us (4%)
  between operations  4.54 us (2%)
  other arithmetic  2.48 us (1%)
    ppermute x19, waiting for transfers between devices, shifted(): return lax.ppermute(block, axis, pairs)  110 us
    pallas_call x2, Pallas kernels, friction_call(): pl.pallas_call(lambda *refs: friction_kernel(groups, coefs, chunk_tiles,...  29.7 us
    ppermute x19, starting transfers between devices, shifted(): return lax.ppermute(block, axis, pairs)  21.2 us
    pallas_call x3, Pallas kernels, pack_call(): pl.pallas_call(lambda *refs: pack_kernel(groups, coefs, tiles, len(waited...  17.6 us
    pallas_call x2, Pallas kernels, finish_call(): pl.pallas_call(kernel, out_shape=jax.ShapeDtypeStruct(result.shape, jnp.f...  15.9 us
    pallas_call x1, Pallas kernels, prepare_call(): pl.pallas_call(lambda *refs: prepare_kernel(coefs, *refs), out_shape=[jax...  14.2 us
  transfers between devices with their start and end apart: 19, of which 11 were waited for; matrix products, arithmetic and copies ran while one was open for 3% of the time, Pallas kernels for 30%

profile of v12, /device:TPU:12, one launch (start us, length us, event | category | flops | bytes accessed | tf_op | source)
XLA Modules:
  0.0 225.8 jit_solution(3657837734641380491)
XLA Ops:
  0.0 0.9 copy-done
  1.0 1.0 index.1
  2.0 3.9 %pack.7 = (f32[16,32,128]{2,1,0:T(8,128)S(1)}, f32[16,32,128]{2,1,0:T(8,128)}, f32[16,32,128]{2,1,0:T(8,128)}, f32[16,32,128]{2,1,0:T(8,128)}, s32[8,128]{1,0:T(8,128)S(1)}) custom-call(s32[2]{0:T(128)S(1)} %pad_add_fusion.1.refs_0_, s32[8,128]{1,0:T(8,128)S(1)} %get-tuple-element.337.refs_1_.offset_ref, s32[512,128]{1,0:T(8,128)S(1)} %get-tuple-element.338.refs_2_, ...), custom_call_target="tpu_custom_call" | custom-call | bytes 8388608 | tf_op jit(solution)/shard_map/pack/pallas_call | solution.py:357
  6.0 1.6 collective-permute-start.6
  7.6 1.2 collective-permute-start.7
  8.8 0.5 slice.40
  9.3 0.5 slice.41
  10.6 6.2 %pack.8 = (f32[50,32,128]{2,1,0:T(8,128)S(1)}, f32[50,32,128]{2,1,0:T(8,128)S(1)}, f32[50,32,128]{2,1,0:T(8,128)S(1)}, f32[50,32,128]{2,1,0:T(8,128)}, s32[8,128]{1,0:T(8,128)S(1)}) custom-call(s32[2]{0:T(128)S(1)} %pad_add_fusion.2.refs_0_, s32[8,128]{1,0:T(8,128)S(1)} %get-tuple-element.337.refs_1_.offset_ref, s32[512,128]{1,0:T(8,128)S(1)} %get-tuple-element.338.refs_2_, ...), custom_call_target="tpu_custom_call" | custom-call | bytes 26214400 | tf_op jit(solution)/shard_map/pack/pallas_call | solution.py:357
  16.8 0.9 copy-done.7
  17.7 0.6 slice.42
  19.5 1.1 broadcast_in_dim.15
  20.6 0.7 copy-done.9
  21.3 1.8 collective-permute-start.8
  23.1 0.2 collective-permute-start.13
  23.3 3.5 %collective-permute-start.14 = (f32[50,32,128]{2,1,0:T(8,128)S(1)}, f32[50,32,128]{2,1,0:T(8,128)}, u32[]{:S(2)}, u32[]{:S(2)}) collective-permute-start(f32[50,32,128]{2,1,0:T(8,128)S(1)} %get-tuple-element.186), channel_id=1, source_target_pairs={{0,16},{8,24},{16,0},{24,8},{1,17},{9,25},{17,1},{25,9},{2,18},{10... | collective-permute-start | bytes 2457608 | tf_op jit(solution)/shard_map/ppermute | solution.py:683
  27.5 7.5 %pack.9 = (f32[31,32,128]{2,1,0:T(8,128)S(1)}, f32[31,32,128]{2,1,0:T(8,128)}, f32[31,32,128]{2,1,0:T(8,128)}, f32[31,32,128]{2,1,0:T(8,128)}, s32[8,128]{1,0:T(8,128)}) custom-call(s32[2]{0:T(128)S(1)} %pad_add_fusion.3.refs_0_, s32[8,128]{1,0:T(8,128)S(1)} %get-tuple-element.407, s32[512,128]{1,0:T(8,128)} %copy-done.9, ...), custom_call_target="tpu_custom_call" | custom-call | bytes 16252928 | tf_op jit(solution)/shard_map/pack/pallas_call | solution.py:357
  35.1 32.1 %collective-permute-done.8.refs_9_.refs_6_ = f32[16,32,128]{2,1,0:T(8,128)S(1)} collective-permute-done((f32[16,32,128]{2,1,0:T(8,128)}, f32[16,32,128]{2,1,0:T(8,128)S(1)}, u32[]{:S(2)}, u32[]{:S(2)}) %collective-permute-start.8) | collective-permute-done | bytes 262176 | tf_op jit(solution)/shard_map/ppermute | solution.py:683
  67.2 0.6 edges.1
  67.9 3.4 %collective-permute-start.9 = (f32[2,8,512]{2,1,0:T(8,128)S(1)}, f32[2,8,512]{2,1,0:T(8,128)S(1)}, u32[]{:S(2)}, u32[]{:S(2)}) collective-permute-start(f32[2,8,512]{2,1,0:T(8,128)S(1)} %get-tuple-element.177), channel_id=1, source_target_pairs={{0,4},{1,5},{2,6},{3,7},{8,12},{9,13},{10,14},{11,15},{16,20},{17,... | collective-permute-start | bytes 98312 | tf_op jit(solution)/shard_map/ppermute | solution.py:683
  71.3 1.3 collective-permute-start.10
  72.6 0.3 collective-permute-done.9.refs_9_
  73.0 4.2 %collective-permute-done.10.refs_10_ = f32[2,8,512]{2,1,0:T(8,128)S(1)} collective-permute-done((f32[2,8,512]{2,1,0:T(8,128)S(1)}, f32[2,8,512]{2,1,0:T(8,128)S(1)}, u32[]{:S(2)}, u32[]{:S(2)}) %collective-permute-start.10) | collective-permute-done | bytes 32800 | tf_op jit(solution)/shard_map/ppermute | solution.py:683
  77.4 3.0 %collective-permute-done.11 = f32[3,8,128]{2,1,0:T(8,128)S(1)} collective-permute-done((f32[3,8,128]{2,1,0:T(8,128)S(1)}, f32[3,8,128]{2,1,0:T(8,128)S(1)}, u32[]{:S(2)}, u32[]{:S(2)}) %collective-permute-start.11) | collective-permute-done | bytes 12320 | tf_op jit(solution)/shard_map/ppermute | solution.py:683
  80.4 0.6 copy-done.16
  81.0 3.0 %collective-permute-done.13.refs_8_ = f32[50,32,128]{2,1,0:T(8,128)} collective-permute-done((f32[50,32,128]{2,1,0:T(8,128)}, f32[50,32,128]{2,1,0:T(8,128)}, u32[]{:S(2)}, u32[]{:S(2)}) %collective-permute-start.13) | collective-permute-done | bytes 819232 | tf_op jit(solution)/shard_map/ppermute | solution.py:683
  84.0 0.1 pad_maximum_fusion.3.refs_0_.scalars_ref
  84.1 0.7 pad_maximum_fusion
  84.9 0.9 broadcast_in_dim.16.refs_11_
  85.7 14.2 %prepare.1 = (f32[3,8,128,512]{3,2,1,0:T(8,128)}, s32[8,128]{1,0:T(8,128)S(1)}) custom-call(f32[6]{0:T(128)S(1)} %pad_maximum_fusion.3.refs_0_.scalars_ref, f32[3,8,128,512]{3,2,1,0:T(8,128)} %get-tuple-element.400, f32[3,8,128,512]{3,2,1,0:T(8,128)} %get-tuple-element.400, f32[3,8,128,512]{3,2,1,0:T(8,128)} %get-tuple-element.400, ...), custom_call_target="tpu_custom_call" | custom-call | flops 524288 | tf_op jit(solution)/shard_map/prepare/pallas_call | solution.py:479
  100.0 0.6 slice.49
  101.2 22.2 %collective-permute-done.14.refs_9_ = f32[50,32,128]{2,1,0:T(8,128)} collective-permute-done((f32[50,32,128]{2,1,0:T(8,128)S(1)}, f32[50,32,128]{2,1,0:T(8,128)}, u32[]{:S(2)}, u32[]{:S(2)}) %collective-permute-start.14) | collective-permute-done | bytes 819232 | tf_op jit(solution)/shard_map/ppermute | solution.py:683
  123.4 0.8 collective-permute-done.15.refs_10_
  124.3 19.5 %friction.6 = (f32[1128,128]{1,0:T(8,128)S(1)}, f32[1128,128]{1,0:T(8,128)S(1)}, f32[1128,128]{1,0:T(8,128)}, f32[1128,128]{1,0:T(8,128)}, s32[8,128]{1,0:T(8,128)S(1)}) custom-call(s32[1]{0:T(128)S(6)} %add.52.refs_0_, bf16[4,256,96]{2,1,0:T(8,128)(2,1)S(1)} %copy-done.11, bf16[4,64,256]{2,1,0:T(8,128)(2,1)S(1)} %copy-done.13, ...), custom_call_target="tpu_custom_call" | custom-call | flops 8650752 | tf_op jit(solution)/shard_map/friction/pallas_call | solution.py:153
  143.7 0.5 slice.50
  144.9 2.7 %collective-permute-start.17 = (f32[1128,128]{1,0:T(8,128)}, f32[1128,128]{1,0:T(8,128)S(1)}, u32[]{:S(2)}, u32[]{:S(2)}) collective-permute-start(f32[1128,128]{1,0:T(8,128)} %get-tuple-element.190), channel_id=1, source_target_pairs={{0,16},{8,24},{16,0},{24,8},{1,17},{9,25},{17,1},{25,9},{2,18},{10... | collective-permute-start | bytes 1732616 | tf_op jit(solution)/shard_map/ppermute | solution.py:683
  147.7 1.9 collective-permute-start.18
  149.6 10.3 %friction.7 = (f32[528,128]{1,0:T(8,128)S(1)}, f32[528,128]{1,0:T(8,128)}, f32[528,128]{1,0:T(8,128)}, f32[528,128]{1,0:T(8,128)}, s32[8,128]{1,0:T(8,128)}) custom-call(s32[1]{0:T(128)S(6)} %add.53.refs_0_, bf16[4,256,96]{2,1,0:T(8,128)(2,1)S(1)} %copy-done.11, bf16[4,64,256]{2,1,0:T(8,128)(2,1)S(1)} %copy-done.13, f32[31,32,128]{2,1,0:T(8,128)S(1)} %copy-done.5, ...), custom_call_target="tpu_custom_call" | custom-call | flops 8321499136 | tf_op jit(solution)/shard_map/friction/pallas_call | solution.py:153
  159.9 2.3 %collective-permute-start.23 = (f32[528,128]{1,0:T(8,128)}, f32[528,128]{1,0:T(8,128)}, u32[]{:S(2)}, u32[]{:S(2)}) collective-permute-start(f32[528,128]{1,0:T(8,128)} %get-tuple-element.198), channel_id=1, source_target_pairs={{0,16},{8,24},{16,0},{24,8},{1,17},{9,25},{17,1},{25,9},{2,18},{10... | collective-permute-start | bytes 811016 | tf_op jit(solution)/shard_map/ppermute | solution.py:683
  162.3 0.9 collective-permute-start.24
  163.2 0.1 slice.39
  163.2 0.6 fusion.1
  164.5 0.6 add_add_fusion
  165.1 42.1 %collective-permute-done.17.refs_6_ = f32[1128,128]{1,0:T(8,128)S(1)} collective-permute-done((f32[1128,128]{1,0:T(8,128)}, f32[1128,128]{1,0:T(8,128)S(1)}, u32[]{:S(2)}, u32[]{:S(2)}) %collective-permute-start.17) | collective-permute-done | bytes 577568 | tf_op jit(solution)/shard_map/ppermute | solution.py:683
  207.2 0.3 collective-permute-done.18.refs_7_
  207.5 9.2 %finish.2.refs_3_ = f32[3,8,128,512]{3,2,1,0:T(8,128)} custom-call(s32[4]{0:T(128)S(1)} %get-tuple-element.266.first_ref, s32[8,128]{1,0:T(8,128)S(1)} %get-tuple-element.407, s32[8,640]{1,0:T(8,128)S(1)} %copy-done.6, f32[6]{0:T(128)S(1)} %pad_maximum_fusion.3.refs_0_.scalars_ref, s32[128,512]{1,0:T(8,128)S(1)} %copy-done.1, ...), custom_call_target="tpu_custom_call", output_to_operand_aliasing={{}: (7, {})} | custom-call | bytes 9437184 | tf_op jit(solution)/shard_map/finish/pallas_call | solution.py:659
  216.7 1.3 collective-permute-done.23.refs_10_
  218.0 1.1 collective-permute-done.24.refs_11_
  219.1 6.7 %finish.3 = f32[3,8,128,512]{3,2,1,0:T(8,128)} custom-call(s32[4]{0:T(128)S(1)} %get-tuple-element.265.first_ref, s32[8,128]{1,0:T(8,128)S(1)} %get-tuple-element.407, s32[8,640]{1,0:T(8,128)S(1)} %copy-done.6, f32[6]{0:T(128)S(1)} %pad_maximum_fusion.3.refs_0_.scalars_ref, s32[128,512]{1,0:T(8,128)S(1)} %copy-done.1, ...), custom_call_target="tpu_custom_call", output_to_operand_aliasing={{}: (7, {})} | custom-call | bytes 9437184 | tf_op jit(solution)/shard_map/finish/pallas_call | solution.py:659
  (58 shorter events, 0.9 us)
Async XLA Ops:
  0.0 0.9 copy-start
  6.0 29.1 %collective-permute-start.6 = (f32[16,32,128]{2,1,0:T(8,128)}, f32[16,32,128]{2,1,0:T(8,128)S(1)}, u32[]{:S(2)}, u32[]{:S(2)}) collective-permute-start(f32[16,32,128]{2,1,0:T(8,128)} %get-tuple-element.172), channel_id=1, source_target_pairs={{0,8},{8,16},{16,24},{24,0},{1,9},{9,17},{17,25},{25,1},{2,10},{10... | collective-permute-start | bytes 786440 | tf_op jit(solution)/shard_map/ppermute | solution.py:683
  7.6 27.5 %collective-permute-start.7 = (f32[16,32,128]{2,1,0:T(8,128)}, f32[16,32,128]{2,1,0:T(8,128)S(1)}, u32[]{:S(2)}, u32[]{:S(2)}) collective-permute-start(f32[16,32,128]{2,1,0:T(8,128)} %get-tuple-element.173), channel_id=1, source_target_pairs={{0,16},{8,24},{16,0},{24,8},{1,17},{9,25},{17,1},{25,9},{2,18},{10... | collective-permute-start | bytes 786440 | tf_op jit(solution)/shard_map/ppermute | solution.py:683
  16.8 0.9 copy-start.7
  17.7 2.9 %copy-start.12 = (bf16[4,64,256]{2,1,0:T(8,128)(2,1)S(1)}, bf16[4,64,256]{2,1,0:T(8,128)(2,1)}, u32[]{:S(2)}) copy-start(bf16[4,64,256]{2,1,0:T(8,128)(2,1)} %constant.93.clone.refs_2_) | copy-start | bytes 393220
  20.6 0.7 copy-start.9
  21.3 45.9 %collective-permute-start.8 = (f32[16,32,128]{2,1,0:T(8,128)}, f32[16,32,128]{2,1,0:T(8,128)S(1)}, u32[]{:S(2)}, u32[]{:S(2)}) collective-permute-start(f32[16,32,128]{2,1,0:T(8,128)} %get-tuple-element.174), channel_id=1, source_target_pairs={{0,24},{8,0},{16,8},{24,16},{1,25},{9,1},{17,9},{25,17},{2,26},{10... | collective-permute-start | bytes 786440 | tf_op jit(solution)/shard_map/ppermute | solution.py:683
  23.1 60.9 %collective-permute-start.13 = (f32[50,32,128]{2,1,0:T(8,128)}, f32[50,32,128]{2,1,0:T(8,128)}, u32[]{:S(2)}, u32[]{:S(2)}) collective-permute-start(f32[50,32,128]{2,1,0:T(8,128)} %copy-done.7), channel_id=1, source_target_pairs={{0,8},{8,16},{16,24},{24,0},{1,9},{9,17},{17,25},{25,1},{2,10},{10... | collective-permute-start | bytes 2457608 | tf_op jit(solution)/shard_map/ppermute | solution.py:683
  23.3 100.1 %collective-permute-start.14 = (f32[50,32,128]{2,1,0:T(8,128)S(1)}, f32[50,32,128]{2,1,0:T(8,128)}, u32[]{:S(2)}, u32[]{:S(2)}) collective-permute-start(f32[50,32,128]{2,1,0:T(8,128)S(1)} %get-tuple-element.186), channel_id=1, source_target_pairs={{0,16},{8,24},{16,0},{24,8},{1,17},{9,25},{17,1},{25,9},{2,18},{10... | collective-permute-start | bytes 2457608 | tf_op jit(solution)/shard_map/ppermute | solution.py:683
  27.5 39.7 %copy-start.1 = (s32[128,512]{1,0:T(8,128)S(1)}, s32[128,512]{1,0:T(8,128)}, u32[]{:S(2)}) copy-start(s32[128,512]{1,0:T(8,128)} %refs_0_.5) | copy-start | bytes 786436
  27.5 39.7 %copy-start.2 = (f32[128,512]{1,0:T(8,128)S(1)}, f32[128,512]{1,0:T(8,128)}, u32[]{:S(2)}) copy-start(f32[128,512]{1,0:T(8,128)} %refs_8_.1) | copy-start | bytes 786436
  27.5 39.7 %copy-start.8 = (f32[3,8,128,512]{3,2,1,0:T(8,128)S(1)}, f32[3,8,128,512]{3,2,1,0:T(8,128)}, u32[]{:S(2)}) copy-start(f32[3,8,128,512]{3,2,1,0:T(8,128)} %get-tuple-element.400) | copy-start | bytes 18874372
  35.0 32.8 %copy-start.4 = (f32[31,32,128]{2,1,0:T(8,128)}, f32[31,32,128]{2,1,0:T(8,128)S(1)}, u32[]{:S(2)}) copy-start(f32[31,32,128]{2,1,0:T(8,128)S(1)} %get-tuple-element.176.refs_10_.refs_3_) | copy-start | bytes 1523716
  35.0 89.2 %collective-permute-start.15 = (f32[50,32,128]{2,1,0:T(8,128)}, f32[50,32,128]{2,1,0:T(8,128)}, u32[]{:S(2)}, u32[]{:S(2)}) collective-permute-start(f32[50,32,128]{2,1,0:T(8,128)} %get-tuple-element.187), channel_id=1, source_target_pairs={{0,24},{8,0},{16,8},{24,16},{1,25},{9,1},{17,9},{25,17},{2,26},{10... | collective-permute-start | bytes 2457608 | tf_op jit(solution)/shard_map/ppermute | solution.py:683
  67.9 5.0 %collective-permute-start.9 = (f32[2,8,512]{2,1,0:T(8,128)S(1)}, f32[2,8,512]{2,1,0:T(8,128)S(1)}, u32[]{:S(2)}, u32[]{:S(2)}) collective-permute-start(f32[2,8,512]{2,1,0:T(8,128)S(1)} %get-tuple-element.177), channel_id=1, source_target_pairs={{0,4},{1,5},{2,6},{3,7},{8,12},{9,13},{10,14},{11,15},{16,20},{17,... | collective-permute-start | bytes 98312 | tf_op jit(solution)/shard_map/ppermute | solution.py:683
  71.3 5.8 %collective-permute-start.10 = (f32[2,8,512]{2,1,0:T(8,128)S(1)}, f32[2,8,512]{2,1,0:T(8,128)S(1)}, u32[]{:S(2)}, u32[]{:S(2)}) collective-permute-start(f32[2,8,512]{2,1,0:T(8,128)S(1)} %get-tuple-element.178), channel_id=1, source_target_pairs={{4,0},{5,1},{6,2},{7,3},{12,8},{13,9},{14,10},{15,11},{20,16},{21,... | collective-permute-start | bytes 98312 | tf_op jit(solution)/shard_map/ppermute | solution.py:683
  73.0 4.3 %collective-permute-start.12 = (f32[3,8,128]{2,1,0:T(8,128)S(1)}, f32[3,8,128]{2,1,0:T(8,128)S(1)}, u32[]{:S(2)}, u32[]{:S(2)}) collective-permute-start(f32[3,8,128]{2,1,0:T(8,128)S(1)} %pad_maximum_fusion.2), channel_id=1, source_target_pairs={{0,3},{1,0},{2,1},{3,2},{4,7},{5,4},{6,5},{7,6},{8,11},{9,8},{10,9... | collective-permute-start | bytes 36872 | tf_op jit(solution)/shard_map/ppermute | solution.py:683
  77.3 3.1 %collective-permute-start.11 = (f32[3,8,128]{2,1,0:T(8,128)S(1)}, f32[3,8,128]{2,1,0:T(8,128)S(1)}, u32[]{:S(2)}, u32[]{:S(2)}) collective-permute-start(f32[3,8,128]{2,1,0:T(8,128)S(1)} %pad_maximum_fusion.1), channel_id=1, source_target_pairs={{0,1},{1,2},{2,3},{3,0},{4,5},{5,6},{6,7},{7,4},{8,9},{9,10},{10,1... | collective-permute-start | bytes 36872 | tf_op jit(solution)/shard_map/ppermute | solution.py:683
  77.3 3.1 %copy-start.15 = (f32[3,8,128]{2,1,0:T(8,128)}, f32[3,8,128]{2,1,0:T(8,128)S(1)}, u32[]{:S(2)}) copy-start(f32[3,8,128]{2,1,0:T(8,128)S(1)} %collective-permute-done.12) | copy-start | bytes 36868
  77.3 70.3 %collective-permute-start.19 = (f32[31,32,128]{2,1,0:T(8,128)}, f32[31,32,128]{2,1,0:T(8,128)}, u32[]{:S(2)}, u32[]{:S(2)}) collective-permute-start(f32[31,32,128]{2,1,0:T(8,128)} %get-tuple-element.193), channel_id=1, source_target_pairs={{0,8},{8,16},{16,24},{24,0},{1,9},{9,17},{17,25},{25,1},{2,10},{10... | collective-permute-start | bytes 1523720 | tf_op jit(solution)/shard_map/ppermute | solution.py:683
  80.4 0.6 copy-start.16
  81.0 68.6 %collective-permute-start.20 = (f32[31,32,128]{2,1,0:T(8,128)}, f32[31,32,128]{2,1,0:T(8,128)}, u32[]{:S(2)}, u32[]{:S(2)}) collective-permute-start(f32[31,32,128]{2,1,0:T(8,128)} %get-tuple-element.194), channel_id=1, source_target_pairs={{0,16},{8,24},{16,0},{24,8},{1,17},{9,25},{17,1},{25,9},{2,18},{10... | collective-permute-start | bytes 1523720 | tf_op jit(solution)/shard_map/ppermute | solution.py:683
  84.0 65.6 %collective-permute-start.21 = (f32[31,32,128]{2,1,0:T(8,128)}, f32[31,32,128]{2,1,0:T(8,128)}, u32[]{:S(2)}, u32[]{:S(2)}) collective-permute-start(f32[31,32,128]{2,1,0:T(8,128)} %get-tuple-element.195), channel_id=1, source_target_pairs={{0,24},{8,0},{16,8},{24,16},{1,25},{9,1},{17,9},{25,17},{2,26},{10... | collective-permute-start | bytes 1523720 | tf_op jit(solution)/shard_map/ppermute | solution.py:683
  85.7 38.5 %copy-start.11 = (bf16[4,256,96]{2,1,0:T(8,128)(2,1)S(1)}, bf16[4,256,96]{2,1,0:T(8,128)(2,1)}, u32[]{:S(2)}) copy-start(bf16[4,256,96]{2,1,0:T(8,128)(2,1)} %get-tuple-element.403) | copy-start | bytes 589828
  85.7 38.5 %copy-start.13 = (bf16[4,64,256]{2,1,0:T(8,128)(2,1)S(1)}, bf16[4,64,256]{2,1,0:T(8,128)(2,1)}, u32[]{:S(2)}) copy-start(bf16[4,64,256]{2,1,0:T(8,128)(2,1)} %constant.93.clone.refs_2_) | copy-start | bytes 393220
  124.2 25.4 %copy-start.5 = (f32[31,32,128]{2,1,0:T(8,128)S(1)}, f32[31,32,128]{2,1,0:T(8,128)}, u32[]{:S(2)}) copy-start(f32[31,32,128]{2,1,0:T(8,128)} %copy-done.4) | copy-start | bytes 1523716
  144.9 17.4 %collective-permute-start.16 = (f32[1128,128]{1,0:T(8,128)S(1)}, f32[1128,128]{1,0:T(8,128)S(1)}, u32[]{:S(2)}, u32[]{:S(2)}) collective-permute-start(f32[1128,128]{1,0:T(8,128)S(1)} %get-tuple-element.189), channel_id=1, source_target_pairs={{0,8},{8,16},{16,24},{24,0},{1,9},{9,17},{17,25},{25,1},{2,10},{10... | collective-permute-start | bytes 1732616 | tf_op jit(solution)/shard_map/ppermute | solution.py:683
  144.9 62.2 %collective-permute-start.17 = (f32[1128,128]{1,0:T(8,128)}, f32[1128,128]{1,0:T(8,128)S(1)}, u32[]{:S(2)}, u32[]{:S(2)}) collective-permute-start(f32[1128,128]{1,0:T(8,128)} %get-tuple-element.190), channel_id=1, source_target_pairs={{0,16},{8,24},{16,0},{24,8},{1,17},{9,25},{17,1},{25,9},{2,18},{10... | collective-permute-start | bytes 1732616 | tf_op jit(solution)/shard_map/ppermute | solution.py:683
  147.6 59.9 %copy-start.3 = (f32[128,512]{1,0:T(8,128)S(1)}, f32[128,512]{1,0:T(8,128)}, u32[]{:S(2)}) copy-start(f32[128,512]{1,0:T(8,128)} %refs_1_.9) | copy-start | bytes 786436
  147.6 59.9 %copy-start.6 = (s32[8,640]{1,0:T(8,128)S(1)}, s32[8,640]{1,0:T(8,128)}, u32[]{:S(2)}) copy-start(s32[8,640]{1,0:T(8,128)} %constant.91.clone.table_ref) | copy-start | bytes 61444
  147.7 59.8 %collective-permute-start.18 = (f32[1128,128]{1,0:T(8,128)}, f32[1128,128]{1,0:T(8,128)S(1)}, u32[]{:S(2)}, u32[]{:S(2)}) collective-permute-start(f32[1128,128]{1,0:T(8,128)} %get-tuple-element.191), channel_id=1, source_target_pairs={{0,24},{8,0},{16,8},{24,16},{1,25},{9,1},{17,9},{25,17},{2,26},{10... | collective-permute-start | bytes 1732616 | tf_op jit(solution)/shard_map/ppermute | solution.py:683
  159.9 56.8 %collective-permute-start.22 = (f32[528,128]{1,0:T(8,128)}, f32[528,128]{1,0:T(8,128)}, u32[]{:S(2)}, u32[]{:S(2)}) collective-permute-start(f32[528,128]{1,0:T(8,128)} %get-tuple-element.197), channel_id=1, source_target_pairs={{0,8},{8,16},{16,24},{24,0},{1,9},{9,17},{17,25},{25,1},{2,10},{10... | collective-permute-start | bytes 811016 | tf_op jit(solution)/shard_map/ppermute | solution.py:683
  159.9 58.1 %collective-permute-start.23 = (f32[528,128]{1,0:T(8,128)}, f32[528,128]{1,0:T(8,128)}, u32[]{:S(2)}, u32[]{:S(2)}) collective-permute-start(f32[528,128]{1,0:T(8,128)} %get-tuple-element.198), channel_id=1, source_target_pairs={{0,16},{8,24},{16,0},{24,8},{1,17},{9,25},{17,1},{25,9},{2,18},{10... | collective-permute-start | bytes 811016 | tf_op jit(solution)/shard_map/ppermute | solution.py:683
  162.3 56.8 %collective-permute-start.24 = (f32[528,128]{1,0:T(8,128)}, f32[528,128]{1,0:T(8,128)}, u32[]{:S(2)}, u32[]{:S(2)}) collective-permute-start(f32[528,128]{1,0:T(8,128)} %get-tuple-element.199), channel_id=1, source_target_pairs={{0,24},{8,0},{16,8},{24,16},{1,25},{9,1},{17,9},{25,17},{2,26},{10... | collective-permute-start | bytes 811016 | tf_op jit(solution)/shard_map/ppermute | solution.py:683
  207.5 11.6 %copy-start.14 = (f32[4,544,128]{2,1,0:T(8,128)S(1)}, f32[4,544,128]{2,1,0:T(8,128)}, u32[]{:S(2)}) copy-start(f32[4,544,128]{2,1,0:T(8,128)} %get-tuple-element.200) | copy-start | bytes 3342340

commit v13 on v12

--- a/solution.py
+++ b/solution.py
@@ -19,7 +19,7 @@
 OMEGA_STEP = 0.25
 SPEED_SOFT = 0.01
 VMEM_BYTES = 48 * 1024 * 1024
-CHUNK_SHARES = (16, 50, 31)
+CHUNK_SHARES = (16, 46, 35)
 SHARE_UNITS = 128
 LOOP_TILES = 8
 PACK_COST = 16384

time: 227 us -> 226 us (level)
  transfers between devices with their start and end apart: 19 -> 19, of which waited for: 11 -> 12; matrix products, arithmetic and copies ran while one was open for 3% -> 3% of each run, Pallas kernels for 30% -> 30%
where the time goes in v13:
time: 226 us; the launch traced here: 225 us
  waiting for transfers between devices  112 us (50%)
  Pallas kernels  79.1 us (35%)
  starting transfers between devices  19.7 us (9%)
  local copies, waits for them, and re-layouts  8.38 us (4%)
  between operations  4.68 us (2%)
    ppermute x19, waiting for transfers between devices, shifted(): return lax.ppermute(block, axis, pairs)  112 us
    pallas_call x2, Pallas kernels, friction_call(): pl.pallas_call(lambda *refs: friction_kernel(groups, coefs, chunk_tiles,...  29.6 us
    ppermute x19, starting transfers between devices, shifted(): return lax.ppermute(block, axis, pairs)  19.7 us
    pallas_call x3, Pallas kernels, pack_call(): pl.pallas_call(lambda *refs: pack_kernel(groups, coefs, tiles, len(waited...  18 us
    pallas_call x2, Pallas kernels, finish_call(): pl.pallas_call(kernel, out_shape=jax.ShapeDtypeStruct(result.shape, jnp.f...  15.7 us
    pallas_call x1, Pallas kernels, prepare_call(): pl.pallas_call(lambda *refs: prepare_kernel(coefs, *refs), out_shape=[jax...  14.2 us
  transfers between devices with their start and end apart: 19, of which 12 were waited for; matrix products, arithmetic and copies ran while one was open for 3% of the time, Pallas kernels for 30%

profile of v13, /device:TPU:12, one launch (start us, length us, event | category | flops | bytes accessed | tf_op | source)
XLA Modules:
  0.0 225.2 jit_solution(18348512776242222797)
XLA Ops:
  0.0 0.9 copy-done
  1.0 1.0 index.1
  2.0 3.8 %pack.7 = (f32[16,32,128]{2,1,0:T(8,128)S(1)}, f32[16,32,128]{2,1,0:T(8,128)}, f32[16,32,128]{2,1,0:T(8,128)}, f32[16,32,128]{2,1,0:T(8,128)S(1)}, s32[8,128]{1,0:T(8,128)S(1)}) custom-call(s32[2]{0:T(128)S(1)} %pad_add_fusion.1.refs_0_, s32[8,128]{1,0:T(8,128)S(1)} %get-tuple-element.337.refs_1_.offset_ref, s32[512,128]{1,0:T(8,128)S(1)} %get-tuple-element.338.refs_2_, ...), custom_call_target="tpu_custom_call" | custom-call | bytes 8388608 | tf_op jit(solution)/shard_map/pack/pallas_call | solution.py:357
  5.9 1.6 collective-permute-start.6
  7.5 1.2 collective-permute-start.7
  8.8 0.5 slice.40
  9.3 0.5 slice.41
  10.5 6.9 %pack.8 = (f32[46,32,128]{2,1,0:T(8,128)S(1)}, f32[46,32,128]{2,1,0:T(8,128)S(1)}, f32[46,32,128]{2,1,0:T(8,128)S(1)}, f32[46,32,128]{2,1,0:T(8,128)}, s32[8,128]{1,0:T(8,128)S(1)}) custom-call(s32[2]{0:T(128)S(1)} %pad_add_fusion.2.refs_0_, s32[8,128]{1,0:T(8,128)S(1)} %get-tuple-element.337.refs_1_.offset_ref, s32[512,128]{1,0:T(8,128)S(1)} %get-tuple-element.338.refs_2_, ...), custom_call_target="tpu_custom_call" | custom-call | bytes 24117248 | tf_op jit(solution)/shard_map/pack/pallas_call | solution.py:357
  17.4 0.9 copy-done.7
  18.3 0.9 copy-done.8
  19.2 0.6 slice.42
  21.1 1.1 broadcast_in_dim.15
  22.2 1.9 collective-permute-start.8
  24.1 0.2 collective-permute-start.13
  24.3 3.5 %collective-permute-start.14 = (f32[46,32,128]{2,1,0:T(8,128)}, f32[46,32,128]{2,1,0:T(8,128)}, u32[]{:S(2)}, u32[]{:S(2)}) collective-permute-start(f32[46,32,128]{2,1,0:T(8,128)} %copy-done.7), channel_id=1, source_target_pairs={{0,16},{8,24},{16,0},{24,8},{1,17},{9,25},{17,1},{25,9},{2,18},{10... | collective-permute-start | bytes 2261000 | tf_op jit(solution)/shard_map/ppermute | solution.py:683
  28.5 7.3 %pack.9 = (f32[35,32,128]{2,1,0:T(8,128)S(1)}, f32[35,32,128]{2,1,0:T(8,128)}, f32[35,32,128]{2,1,0:T(8,128)}, f32[35,32,128]{2,1,0:T(8,128)}, s32[8,128]{1,0:T(8,128)}) custom-call(s32[2]{0:T(128)S(1)} %pad_add_fusion.3.refs_0_, s32[8,128]{1,0:T(8,128)S(1)} %get-tuple-element.410, s32[512,128]{1,0:T(8,128)} %copy-done.10, ...), custom_call_target="tpu_custom_call" | custom-call | bytes 18350080 | tf_op jit(solution)/shard_map/pack/pallas_call | solution.py:357
  35.9 28.4 %collective-permute-done.8.refs_9_.refs_6_ = f32[16,32,128]{2,1,0:T(8,128)S(1)} collective-permute-done((f32[16,32,128]{2,1,0:T(8,128)S(1)}, f32[16,32,128]{2,1,0:T(8,128)S(1)}, u32[]{:S(2)}, u32[]{:S(2)}) %collective-permute-start.8) | collective-permute-done | bytes 262176 | tf_op jit(solution)/shard_map/ppermute | solution.py:683
  64.3 0.6 edges.1
  65.0 3.4 %collective-permute-start.9 = (f32[2,8,512]{2,1,0:T(8,128)S(1)}, f32[2,8,512]{2,1,0:T(8,128)S(1)}, u32[]{:S(2)}, u32[]{:S(2)}) collective-permute-start(f32[2,8,512]{2,1,0:T(8,128)S(1)} %get-tuple-element.177), channel_id=1, source_target_pairs={{0,4},{1,5},{2,6},{3,7},{8,12},{9,13},{10,14},{11,15},{16,20},{17,... | collective-permute-start | bytes 98312 | tf_op jit(solution)/shard_map/ppermute | solution.py:683
  68.4 1.3 collective-permute-start.10
  69.7 0.3 collective-permute-done.9.refs_9_
  70.0 0.1 maximum_bitcast_fusion.2
  70.1 4.2 %collective-permute-done.10.refs_10_ = f32[2,8,512]{2,1,0:T(8,128)S(1)} collective-permute-done((f32[2,8,512]{2,1,0:T(8,128)S(1)}, f32[2,8,512]{2,1,0:T(8,128)S(1)}, u32[]{:S(2)}, u32[]{:S(2)}) %collective-permute-start.10) | collective-permute-done | bytes 32800 | tf_op jit(solution)/shard_map/ppermute | solution.py:683
  74.5 3.0 %collective-permute-done.11 = f32[3,8,128]{2,1,0:T(8,128)S(1)} collective-permute-done((f32[3,8,128]{2,1,0:T(8,128)S(1)}, f32[3,8,128]{2,1,0:T(8,128)S(1)}, u32[]{:S(2)}, u32[]{:S(2)}) %collective-permute-start.11) | collective-permute-done | bytes 12320 | tf_op jit(solution)/shard_map/ppermute | solution.py:683
  77.5 0.9 collective-permute-done.13.refs_8_
  78.5 0.1 pad_maximum_fusion.3.refs_0_.scalars_ref
  78.6 0.9 broadcast_in_dim.16.refs_11_
  79.5 14.2 %prepare.1 = (f32[3,8,128,512]{3,2,1,0:T(8,128)}, s32[8,128]{1,0:T(8,128)S(1)}) custom-call(f32[6]{0:T(128)S(1)} %pad_maximum_fusion.3.refs_0_.scalars_ref, f32[3,8,128,512]{3,2,1,0:T(8,128)} %get-tuple-element.402, f32[3,8,128,512]{3,2,1,0:T(8,128)} %get-tuple-element.402, f32[3,8,128,512]{3,2,1,0:T(8,128)} %get-tuple-element.402, ...), custom_call_target="tpu_custom_call" | custom-call | flops 524288 | tf_op jit(solution)/shard_map/prepare/pallas_call | solution.py:479
  93.7 0.6 slice.49
  95.0 25.2 %collective-permute-done.14.refs_9_ = f32[46,32,128]{2,1,0:T(8,128)} collective-permute-done((f32[46,32,128]{2,1,0:T(8,128)}, f32[46,32,128]{2,1,0:T(8,128)}, u32[]{:S(2)}, u32[]{:S(2)}) %collective-permute-start.14) | collective-permute-done | bytes 753696 | tf_op jit(solution)/shard_map/ppermute | solution.py:683
  120.2 1.1 collective-permute-done.15.refs_10_
  121.4 18.2 %friction.6 = (f32[1056,128]{1,0:T(8,128)S(1)}, f32[1056,128]{1,0:T(8,128)S(1)}, f32[1056,128]{1,0:T(8,128)}, f32[1056,128]{1,0:T(8,128)}, s32[8,128]{1,0:T(8,128)S(1)}) custom-call(s32[1]{0:T(128)S(6)} %add.52.refs_0_, bf16[4,256,96]{2,1,0:T(8,128)(2,1)S(1)} %copy-done.12, bf16[4,64,256]{2,1,0:T(8,128)(2,1)S(1)} %copy-done.14, ...), custom_call_target="tpu_custom_call" | custom-call | flops 8126464 | tf_op jit(solution)/shard_map/friction/pallas_call | solution.py:153
  139.6 0.5 slice.50
  140.7 2.3 %collective-permute-start.17 = (f32[1056,128]{1,0:T(8,128)}, f32[1056,128]{1,0:T(8,128)S(1)}, u32[]{:S(2)}, u32[]{:S(2)}) collective-permute-start(f32[1056,128]{1,0:T(8,128)} %get-tuple-element.190), channel_id=1, source_target_pairs={{0,16},{8,24},{16,0},{24,8},{1,17},{9,25},{17,1},{25,9},{2,18},{10... | collective-permute-start | bytes 1622024 | tf_op jit(solution)/shard_map/ppermute | solution.py:683
  143.1 1.9 collective-permute-start.18
  145.0 24.1 %collective-permute-done.21.refs_6_ = f32[35,32,128]{2,1,0:T(8,128)} collective-permute-done((f32[35,32,128]{2,1,0:T(8,128)}, f32[35,32,128]{2,1,0:T(8,128)}, u32[]{:S(2)}, u32[]{:S(2)}) %collective-permute-start.21) | collective-permute-done | bytes 573472 | tf_op jit(solution)/shard_map/ppermute | solution.py:683
  169.1 11.3 %friction.7 = (f32[600,128]{1,0:T(8,128)S(1)}, f32[600,128]{1,0:T(8,128)}, f32[600,128]{1,0:T(8,128)}, f32[600,128]{1,0:T(8,128)}, s32[8,128]{1,0:T(8,128)}) custom-call(s32[1]{0:T(128)S(6)} %add.53.refs_0_, bf16[4,256,96]{2,1,0:T(8,128)(2,1)S(1)} %copy-done.12, bf16[4,64,256]{2,1,0:T(8,128)(2,1)S(1)} %copy-done.14, ...), custom_call_target="tpu_custom_call" | custom-call | flops 9395240960 | tf_op jit(solution)/shard_map/friction/pallas_call | solution.py:153
  180.4 0.7 copy-done.4
  181.2 2.0 collective-permute-start.24
  183.2 0.1 slice.39
  183.3 0.6 fusion.1
  184.4 0.6 add_add_fusion
  185.1 19.3 %collective-permute-done.17.refs_6_ = f32[1056,128]{1,0:T(8,128)S(1)} collective-permute-done((f32[1056,128]{1,0:T(8,128)}, f32[1056,128]{1,0:T(8,128)S(1)}, u32[]{:S(2)}, u32[]{:S(2)}) %collective-permute-start.17) | collective-permute-done | bytes 540704 | tf_op jit(solution)/shard_map/ppermute | solution.py:683
  204.4 0.9 collective-permute-done.18.refs_7_
  205.4 9.0 %finish.2.refs_3_ = f32[3,8,128,512]{3,2,1,0:T(8,128)} custom-call(s32[4]{0:T(128)S(1)} %get-tuple-element.266.first_ref, s32[8,128]{1,0:T(8,128)S(1)} %get-tuple-element.410, s32[8,640]{1,0:T(8,128)S(1)} %copy-done.6, f32[6]{0:T(128)S(1)} %pad_maximum_fusion.3.refs_0_.scalars_ref, s32[128,512]{1,0:T(8,128)S(1)} %copy-done.1, ...), custom_call_target="tpu_custom_call", output_to_operand_aliasing={{}: (7, {})} | custom-call | bytes 9437184 | tf_op jit(solution)/shard_map/finish/pallas_call | solution.py:659
  214.4 2.5 %collective-permute-done.23.refs_10_ = f32[600,128]{1,0:T(8,128)} collective-permute-done((f32[600,128]{1,0:T(8,128)}, f32[600,128]{1,0:T(8,128)}, u32[]{:S(2)}, u32[]{:S(2)}) %collective-permute-start.23) | collective-permute-done | bytes 307232 | tf_op jit(solution)/shard_map/ppermute | solution.py:683
  216.8 1.7 collective-permute-done.24.refs_11_
  218.5 6.7 %finish.3 = f32[3,8,128,512]{3,2,1,0:T(8,128)} custom-call(s32[4]{0:T(128)S(1)} %get-tuple-element.265.first_ref, s32[8,128]{1,0:T(8,128)S(1)} %get-tuple-element.410, s32[8,640]{1,0:T(8,128)S(1)} %copy-done.6, f32[6]{0:T(128)S(1)} %pad_maximum_fusion.3.refs_0_.scalars_ref, s32[128,512]{1,0:T(8,128)S(1)} %copy-done.1, ...), custom_call_target="tpu_custom_call", output_to_operand_aliasing={{}: (7, {})} | custom-call | bytes 9437184 | tf_op jit(solution)/shard_map/finish/pallas_call | solution.py:659
  (58 shorter events, 0.8 us)
Async XLA Ops:
  0.0 0.9 copy-start
  5.9 29.9 %collective-permute-start.6 = (f32[16,32,128]{2,1,0:T(8,128)}, f32[16,32,128]{2,1,0:T(8,128)S(1)}, u32[]{:S(2)}, u32[]{:S(2)}) collective-permute-start(f32[16,32,128]{2,1,0:T(8,128)} %get-tuple-element.172), channel_id=1, source_target_pairs={{0,8},{8,16},{16,24},{24,0},{1,9},{9,17},{17,25},{25,1},{2,10},{10... | collective-permute-start | bytes 786440 | tf_op jit(solution)/shard_map/ppermute | solution.py:683
  7.5 28.4 %collective-permute-start.7 = (f32[16,32,128]{2,1,0:T(8,128)}, f32[16,32,128]{2,1,0:T(8,128)S(1)}, u32[]{:S(2)}, u32[]{:S(2)}) collective-permute-start(f32[16,32,128]{2,1,0:T(8,128)} %get-tuple-element.173), channel_id=1, source_target_pairs={{0,16},{8,24},{16,0},{24,8},{1,17},{9,25},{17,1},{25,9},{2,18},{10... | collective-permute-start | bytes 786440 | tf_op jit(solution)/shard_map/ppermute | solution.py:683
  17.4 0.9 copy-start.7
  18.3 0.9 copy-start.8
  18.3 3.9 %copy-start.11 = (bf16[4,256,96]{2,1,0:T(8,128)(2,1)S(1)}, bf16[4,256,96]{2,1,0:T(8,128)(2,1)}, u32[]{:S(2)}) copy-start(bf16[4,256,96]{2,1,0:T(8,128)(2,1)} %constant.92.clone.refs_1_) | copy-start | bytes 589828
  18.3 3.9 %copy-start.13 = (bf16[4,64,256]{2,1,0:T(8,128)(2,1)S(1)}, bf16[4,64,256]{2,1,0:T(8,128)(2,1)}, u32[]{:S(2)}) copy-start(bf16[4,64,256]{2,1,0:T(8,128)(2,1)} %constant.93.clone.refs_2_) | copy-start | bytes 393220
  22.2 6.3 %copy-start.10 = (s32[512,128]{1,0:T(8,128)}, s32[512,128]{1,0:T(8,128)S(1)}, u32[]{:S(2)}) copy-start(s32[512,128]{1,0:T(8,128)S(1)} %get-tuple-element.404) | copy-start | bytes 786436
  22.2 42.1 %collective-permute-start.8 = (f32[16,32,128]{2,1,0:T(8,128)S(1)}, f32[16,32,128]{2,1,0:T(8,128)S(1)}, u32[]{:S(2)}, u32[]{:S(2)}) collective-permute-start(f32[16,32,128]{2,1,0:T(8,128)S(1)} %get-tuple-element.174), channel_id=1, source_target_pairs={{0,24},{8,0},{16,8},{24,16},{1,25},{9,1},{17,9},{25,17},{2,26},{10... | collective-permute-start | bytes 786440 | tf_op jit(solution)/shard_map/ppermute | solution.py:683
  24.1 54.3 %collective-permute-start.13 = (f32[46,32,128]{2,1,0:T(8,128)}, f32[46,32,128]{2,1,0:T(8,128)}, u32[]{:S(2)}, u32[]{:S(2)}) collective-permute-start(f32[46,32,128]{2,1,0:T(8,128)} %copy-done.8), channel_id=1, source_target_pairs={{0,8},{8,16},{16,24},{24,0},{1,9},{9,17},{17,25},{25,1},{2,10},{10... | collective-permute-start | bytes 2261000 | tf_op jit(solution)/shard_map/ppermute | solution.py:683
  24.3 95.9 %collective-permute-start.14 = (f32[46,32,128]{2,1,0:T(8,128)}, f32[46,32,128]{2,1,0:T(8,128)}, u32[]{:S(2)}, u32[]{:S(2)}) collective-permute-start(f32[46,32,128]{2,1,0:T(8,128)} %copy-done.7), channel_id=1, source_target_pairs={{0,16},{8,24},{16,0},{24,8},{1,17},{9,25},{17,1},{25,9},{2,18},{10... | collective-permute-start | bytes 2261000 | tf_op jit(solution)/shard_map/ppermute | solution.py:683
  28.5 35.8 %copy-start.1 = (s32[128,512]{1,0:T(8,128)S(1)}, s32[128,512]{1,0:T(8,128)}, u32[]{:S(2)}) copy-start(s32[128,512]{1,0:T(8,128)} %refs_0_.5) | copy-start | bytes 786436
  28.5 35.8 %copy-start.2 = (f32[128,512]{1,0:T(8,128)S(1)}, f32[128,512]{1,0:T(8,128)}, u32[]{:S(2)}) copy-start(f32[128,512]{1,0:T(8,128)} %refs_8_.1) | copy-start | bytes 786436
  28.5 35.8 %copy-start.9 = (f32[3,8,128,512]{3,2,1,0:T(8,128)S(1)}, f32[3,8,128,512]{3,2,1,0:T(8,128)}, u32[]{:S(2)}) copy-start(f32[3,8,128,512]{3,2,1,0:T(8,128)} %get-tuple-element.402) | copy-start | bytes 18874372
  35.8 85.5 %collective-permute-start.15 = (f32[46,32,128]{2,1,0:T(8,128)}, f32[46,32,128]{2,1,0:T(8,128)}, u32[]{:S(2)}, u32[]{:S(2)}) collective-permute-start(f32[46,32,128]{2,1,0:T(8,128)} %get-tuple-element.187), channel_id=1, source_target_pairs={{0,24},{8,0},{16,8},{24,16},{1,25},{9,1},{17,9},{25,17},{2,26},{10... | collective-permute-start | bytes 2261000 | tf_op jit(solution)/shard_map/ppermute | solution.py:683
  65.0 5.0 %collective-permute-start.9 = (f32[2,8,512]{2,1,0:T(8,128)S(1)}, f32[2,8,512]{2,1,0:T(8,128)S(1)}, u32[]{:S(2)}, u32[]{:S(2)}) collective-permute-start(f32[2,8,512]{2,1,0:T(8,128)S(1)} %get-tuple-element.177), channel_id=1, source_target_pairs={{0,4},{1,5},{2,6},{3,7},{8,12},{9,13},{10,14},{11,15},{16,20},{17,... | collective-permute-start | bytes 98312 | tf_op jit(solution)/shard_map/ppermute | solution.py:683
  68.4 5.8 %collective-permute-start.10 = (f32[2,8,512]{2,1,0:T(8,128)S(1)}, f32[2,8,512]{2,1,0:T(8,128)S(1)}, u32[]{:S(2)}, u32[]{:S(2)}) collective-permute-start(f32[2,8,512]{2,1,0:T(8,128)S(1)} %get-tuple-element.178), channel_id=1, source_target_pairs={{4,0},{5,1},{6,2},{7,3},{12,8},{13,9},{14,10},{15,11},{20,16},{21,... | collective-permute-start | bytes 98312 | tf_op jit(solution)/shard_map/ppermute | solution.py:683
  70.1 4.3 %collective-permute-start.12 = (f32[3,8,128]{2,1,0:T(8,128)S(1)}, f32[3,8,128]{2,1,0:T(8,128)S(1)}, u32[]{:S(2)}, u32[]{:S(2)}) collective-permute-start(f32[3,8,128]{2,1,0:T(8,128)S(1)} %pad_maximum_fusion.2), channel_id=1, source_target_pairs={{0,3},{1,0},{2,1},{3,2},{4,7},{5,4},{6,5},{7,6},{8,11},{9,8},{10,9... | collective-permute-start | bytes 36872 | tf_op jit(solution)/shard_map/ppermute | solution.py:683
  74.4 3.1 %collective-permute-start.11 = (f32[3,8,128]{2,1,0:T(8,128)S(1)}, f32[3,8,128]{2,1,0:T(8,128)S(1)}, u32[]{:S(2)}, u32[]{:S(2)}) collective-permute-start(f32[3,8,128]{2,1,0:T(8,128)S(1)} %pad_maximum_fusion.1), channel_id=1, source_target_pairs={{0,1},{1,2},{2,3},{3,0},{4,5},{5,6},{6,7},{7,4},{8,9},{9,10},{10,1... | collective-permute-start | bytes 36872 | tf_op jit(solution)/shard_map/ppermute | solution.py:683
  74.4 68.6 %collective-permute-start.19 = (f32[35,32,128]{2,1,0:T(8,128)}, f32[35,32,128]{2,1,0:T(8,128)}, u32[]{:S(2)}, u32[]{:S(2)}) collective-permute-start(f32[35,32,128]{2,1,0:T(8,128)} %get-tuple-element.193), channel_id=1, source_target_pairs={{0,8},{8,16},{16,24},{24,0},{1,9},{9,17},{17,25},{25,1},{2,10},{10... | collective-permute-start | bytes 1720328 | tf_op jit(solution)/shard_map/ppermute | solution.py:683
  77.5 67.5 %collective-permute-start.20 = (f32[35,32,128]{2,1,0:T(8,128)}, f32[35,32,128]{2,1,0:T(8,128)}, u32[]{:S(2)}, u32[]{:S(2)}) collective-permute-start(f32[35,32,128]{2,1,0:T(8,128)} %get-tuple-element.194), channel_id=1, source_target_pairs={{0,16},{8,24},{16,0},{24,8},{1,17},{9,25},{17,1},{25,9},{2,18},{10... | collective-permute-start | bytes 1720328 | tf_op jit(solution)/shard_map/ppermute | solution.py:683
  78.4 90.7 %collective-permute-start.21 = (f32[35,32,128]{2,1,0:T(8,128)}, f32[35,32,128]{2,1,0:T(8,128)}, u32[]{:S(2)}, u32[]{:S(2)}) collective-permute-start(f32[35,32,128]{2,1,0:T(8,128)} %get-tuple-element.195), channel_id=1, source_target_pairs={{0,24},{8,0},{16,8},{24,16},{1,25},{9,1},{17,9},{25,17},{2,26},{10... | collective-permute-start | bytes 1720328 | tf_op jit(solution)/shard_map/ppermute | solution.py:683
  79.4 41.9 %copy-start.12 = (bf16[4,256,96]{2,1,0:T(8,128)(2,1)S(1)}, bf16[4,256,96]{2,1,0:T(8,128)(2,1)}, u32[]{:S(2)}) copy-start(bf16[4,256,96]{2,1,0:T(8,128)(2,1)} %constant.92.clone.refs_1_) | copy-start | bytes 589828
  79.4 41.9 %copy-start.14 = (bf16[4,64,256]{2,1,0:T(8,128)(2,1)S(1)}, bf16[4,64,256]{2,1,0:T(8,128)(2,1)}, u32[]{:S(2)}) copy-start(bf16[4,64,256]{2,1,0:T(8,128)(2,1)} %constant.93.clone.refs_2_) | copy-start | bytes 393220
  140.7 40.5 %collective-permute-start.16 = (f32[1056,128]{1,0:T(8,128)S(1)}, f32[1056,128]{1,0:T(8,128)S(1)}, u32[]{:S(2)}, u32[]{:S(2)}) collective-permute-start(f32[1056,128]{1,0:T(8,128)S(1)} %get-tuple-element.189), channel_id=1, source_target_pairs={{0,8},{8,16},{16,24},{24,0},{1,9},{9,17},{17,25},{25,1},{2,10},{10... | collective-permute-start | bytes 1622024 | tf_op jit(solution)/shard_map/ppermute | solution.py:683
  140.7 63.7 %collective-permute-start.17 = (f32[1056,128]{1,0:T(8,128)}, f32[1056,128]{1,0:T(8,128)S(1)}, u32[]{:S(2)}, u32[]{:S(2)}) collective-permute-start(f32[1056,128]{1,0:T(8,128)} %get-tuple-element.190), channel_id=1, source_target_pairs={{0,16},{8,24},{16,0},{24,8},{1,17},{9,25},{17,1},{25,9},{2,18},{10... | collective-permute-start | bytes 1622024 | tf_op jit(solution)/shard_map/ppermute | solution.py:683
  143.0 62.3 %copy-start.3 = (f32[128,512]{1,0:T(8,128)S(1)}, f32[128,512]{1,0:T(8,128)}, u32[]{:S(2)}) copy-start(f32[128,512]{1,0:T(8,128)} %refs_1_.9) | copy-start | bytes 786436
  143.0 62.3 %copy-start.6 = (s32[8,640]{1,0:T(8,128)S(1)}, s32[8,640]{1,0:T(8,128)}, u32[]{:S(2)}) copy-start(s32[8,640]{1,0:T(8,128)} %constant.91.clone.table_ref) | copy-start | bytes 61444
  143.1 62.3 %collective-permute-start.18 = (f32[1056,128]{1,0:T(8,128)}, f32[1056,128]{1,0:T(8,128)S(1)}, u32[]{:S(2)}, u32[]{:S(2)}) collective-permute-start(f32[1056,128]{1,0:T(8,128)} %get-tuple-element.191), channel_id=1, source_target_pairs={{0,24},{8,0},{16,8},{24,16},{1,25},{9,1},{17,9},{25,17},{2,26},{10... | collective-permute-start | bytes 1622024 | tf_op jit(solution)/shard_map/ppermute | solution.py:683
  180.4 0.7 copy-start.4
  181.2 33.2 %collective-permute-start.22 = (f32[600,128]{1,0:T(8,128)}, f32[600,128]{1,0:T(8,128)S(1)}, u32[]{:S(2)}, u32[]{:S(2)}) collective-permute-start(f32[600,128]{1,0:T(8,128)} %get-tuple-element.197), channel_id=1, source_target_pairs={{0,8},{8,16},{16,24},{24,0},{1,9},{9,17},{17,25},{25,1},{2,10},{10... | collective-permute-start | bytes 921608 | tf_op jit(solution)/shard_map/ppermute | solution.py:683
  181.2 35.7 %collective-permute-start.23 = (f32[600,128]{1,0:T(8,128)}, f32[600,128]{1,0:T(8,128)}, u32[]{:S(2)}, u32[]{:S(2)}) collective-permute-start(f32[600,128]{1,0:T(8,128)} %get-tuple-element.198), channel_id=1, source_target_pairs={{0,16},{8,24},{16,0},{24,8},{1,17},{9,25},{17,1},{25,9},{2,18},{10... | collective-permute-start | bytes 921608 | tf_op jit(solution)/shard_map/ppermute | solution.py:683
  181.2 37.4 %collective-permute-start.24 = (f32[600,128]{1,0:T(8,128)}, f32[600,128]{1,0:T(8,128)}, u32[]{:S(2)}, u32[]{:S(2)}) collective-permute-start(f32[600,128]{1,0:T(8,128)} %get-tuple-element.199), channel_id=1, source_target_pairs={{0,24},{8,0},{16,8},{24,16},{1,25},{9,1},{17,9},{25,17},{2,26},{10... | collective-permute-start | bytes 921608 | tf_op jit(solution)/shard_map/ppermute | solution.py:683
  205.3 13.2 %copy-start.5 = (f32[600,128]{1,0:T(8,128)S(1)}, f32[600,128]{1,0:T(8,128)}, u32[]{:S(2)}) copy-start(f32[600,128]{1,0:T(8,128)} %copy-done.4) | copy-start | bytes 921604
  205.3 13.2 %copy-start.15 = (f32[4,544,128]{2,1,0:T(8,128)S(1)}, f32[4,544,128]{2,1,0:T(8,128)}, u32[]{:S(2)}) copy-start(f32[4,544,128]{2,1,0:T(8,128)} %get-tuple-element.200) | copy-start | bytes 3342340
